TPU v7x, 256 devices: a whole 4x4x8 slice. The times are simulated.
256 devices in a mesh: ang: 32 (over z_lo, x, core), gz: 8 (over z_hi, y).
Axes of the slice: x: 4, y: 4, z: 8 (z_hi: 2, z_lo: 4; z = z_hi * 4 + z_lo), core: 2. Of those that a mesh axis runs over, the one named last changes fastest.
Arguments:
- projections: bfloat16 [256, 512, 1024], P('ang', 'gz'), may hold values from -6 to 6
- band_weights: bfloat16 [256, 1024, 128], P('ang'), may hold values from -0.03125 to 0.03125
- band_offsets: int32 [256, 64], P('ang'), may hold values from 0 to 896
- phase: int32 [64, 512, 1024], P('ang', 'gz'), may hold values from 0 to 3
- contact: int32 [64, 512, 1024], P('ang', 'gz'), may hold values from 0 to 3
- conductivity_table: float32 [4, 4], replicated, may hold values from 0.1 to 1
Outputs:
- volume: float32 [64, 512, 1024], P('ang', 'gz')
- temperature: float32 [64, 512, 1024], P('ang', 'gz')
Inputs may be any that keep to these rules, and one draw needn't show every extreme that they name: `band_offsets`: each band lies inside the detector.
All inputs are finite; a program needn't handle non-finite values.
Results may differ from a plain program's by a relative error of at most 0.0003.
Values sent between devices are 32-bit elements; how exact they have to be, the bound alone decides.
No kernel may reach another device: no remote copies, remote signals or barrier semaphores. Data moves between devices by JAX's collectives and lax.ppermute only.
A program may use at most 128 MiB of HBM per device.

v0:
```python
import jax
import jax.numpy as jnp
from jax import lax
from jax.sharding import PartitionSpec as P

STEPS = 4


step_size = 0.15


def padded(cells, sides, width):
    for axis, dim in sides:
        count = lax.axis_size(axis)
        ends = count - 1
        head = lax.slice_in_dim(cells, 0, width, axis=dim)
        tail = lax.slice_in_dim(cells, cells.shape[dim] - width, cells.shape[dim], axis=dim)
        cells = jnp.concatenate(
            [
                lax.ppermute(tail, axis, [(i, (i + 1) % count) for i in range(ends)]),
                cells,
                lax.ppermute(head, axis, [((i + 1) % count, i) for i in range(ends)]),
            ],
            axis=dim,
        )
    return cells


def advance(heat_wide, conduct_wide):
    heat_pad = jnp.pad(heat_wide, ((0, 0), (0, 0), (1, 1)))
    conduct_pad = jnp.pad(conduct_wide, ((0, 0), (0, 0), (1, 1)))
    centre = heat_pad[1:-1, 1:-1, 1:-1]
    conduct_mid = conduct_pad[1:-1, 1:-1, 1:-1]
    pieces = [
        (heat_pad[2:, 1:-1, 1:-1], conduct_pad[2:, 1:-1, 1:-1]),
        (heat_pad[:-2, 1:-1, 1:-1], conduct_pad[:-2, 1:-1, 1:-1]),
        (heat_pad[1:-1, 1:-1, 2:], conduct_pad[1:-1, 1:-1, 2:]),
        (heat_pad[1:-1, 1:-1, :-2], conduct_pad[1:-1, 1:-1, :-2]),
        (heat_pad[1:-1, 2:, 1:-1], conduct_pad[1:-1, 2:, 1:-1]),
        (heat_pad[1:-1, :-2, 1:-1], conduct_pad[1:-1, :-2, 1:-1]),
    ]
    flux_sum = jnp.zeros_like(centre)
    for heat_near, conduct_near in pieces:
        denominator = conduct_mid + conduct_near
        positive = denominator > 0.0
        safe_denominator = jnp.where(positive, denominator, 1.0)
        face = jnp.where(positive, 2.0 * conduct_mid * conduct_near / safe_denominator, 0.0)
        flux_sum = flux_sum + face * (heat_near - centre)
    return centre + step_size * flux_sum


def local(projections, band_weights, band_offsets, phase, contact, conductivity_table):
    angle_count = band_weights.shape[0]
    band_width = band_weights.shape[2]
    all_rows = band_offsets.shape[1]
    depth_count = projections.shape[1]
    column_count = projections.shape[2]
    block_count = column_count // band_width
    spread = jnp.arange(band_width, dtype=jnp.int32)
    window_ids = jnp.arange(2 * band_width, dtype=jnp.int32)
    block_ids = jnp.arange(block_count, dtype=jnp.int32)
    column_blocks = projections.reshape(angle_count, depth_count, block_count, band_width)
    following = jnp.concatenate(
        [column_blocks[:, :, 1:, :], jnp.zeros_like(column_blocks[:, :, :1, :])], axis=2
    )
    block_pairs = jnp.concatenate([column_blocks, following], axis=3)
    offsets_block = band_offsets
    block_rows = 8
    groups = all_rows // block_rows
    offsets_block = jnp.moveaxis(offsets_block.reshape(angle_count, groups, block_rows), 1, 0)

    def one_block(offsets_group):
        coarse = offsets_group // band_width
        remainder = offsets_group - coarse * band_width
        chooser = (coarse[:, :, None] == block_ids[None, None, :]).astype(jnp.bfloat16)
        window_rows = jnp.einsum(
            "axk,azkw->axzw", chooser, block_pairs, preferred_element_type=jnp.float32
        ).astype(jnp.bfloat16)
        shifter = (
            window_ids[None, None, :, None]
            == remainder[:, :, None, None] + spread[None, None, None, :]
        ).astype(jnp.bfloat16)
        gathered = jnp.einsum(
            "axzw,axwb->axzb", window_rows, shifter, preferred_element_type=jnp.float32
        ).astype(jnp.bfloat16)
        return jnp.einsum(
            "ayb,axzb->xzy", band_weights, gathered, preferred_element_type=jnp.float32
        )

    blocks = lax.map(one_block, offsets_block)
    partial_value = blocks.reshape((all_rows,) + blocks.shape[2:])
    volume = lax.psum_scatter(partial_value, "ang", scatter_dimension=0, tiled=True)
    label_index = phase * conductivity_table.shape[1] + contact
    flat_table = conductivity_table.reshape(-1)
    conduct = jnp.zeros(phase.shape, jnp.float32)
    for entry in range(flat_table.shape[0]):
        conduct = conduct + jnp.where(label_index == entry, flat_table[entry], 0.0)
    heat_field = volume
    conduct_wide = padded(conduct, (("ang", 0), ("gz", 1)), 1)
    for rounds in range(STEPS):
        heat_wide = padded(heat_field, (("ang", 0), ("gz", 1)), 1)
        heat_field = advance(heat_wide, conduct_wide)
    return (volume, heat_field)


def solution(mesh):
    in_specs = (
        P("ang", "gz", None),
        P("ang", None, None),
        P("ang", None),
        P("ang", "gz", None),
        P("ang", "gz", None),
        P(),
    )
    out_specs = (P("ang", "gz", None), P("ang", "gz", None))
    return jax.shard_map(local, mesh=mesh, in_specs=in_specs, out_specs=out_specs, check_vma=False)
```

profile of v0, /device:TPU:30, one launch (start us, length us, event | category | flops | bytes accessed | tf_op | source)
XLA Modules:
  0.0 367.6 jit_solution(13419702104271659236)
XLA Ops:
  7.2 0.8 reshape.107
  8.0 1.5 copy.15
  9.8 0.4 fusion.29
  10.2 71.7 %while.13 = (s32[]{:T(128)}, f32[8,8,64,1024]{3,2,1,0:T(8,128)}, s32[8,8,8]{2,0,1:T(8,128)S(1)}, bf16[8,64,8,256]{3,2,1,0:T(8,128)(2,1)S(1)}, bf16[8,1024,128]{2,1,0:T(8,128)(2,1)}, /*index=5*/s32[]{:T(128)}) while((s32[]{:T(128)}, f32[8,8,64,1024]{3,2,1,0:T(8,128)}, s32[8,8,8]{2,0,1:T(8,128)S(1)}, ...), condition=%wide.region_1.2_spmd.clone, body=%wide.region_0.1_spmd.clone.sunk | while | flops 1361585664 | bytes 10553173 | solution.py:90
  10.3 2.1 fusion.131
  12.5 6.7 %bitcast_dynamic-update-slice_fusion.2 = f32[8,8,64,1024]{3,2,1,0:T(8,128)} fusion(f32[8,8,64,1024]{3,2,1,0:T(8,128)} %get-tuple-element.219, s32[]{:T(128)S(6)} %copy.43, bf16[8,1024,128]{2,1,0:T(8,128)(2,1)} %get-tuple-element.228, s32[8,8,128]{2,1,0:T(8,128)S(1)} %iota_add_fusion.2, bf16[8,8,64,256]{3,1,2,0:T(8,128)(2,1)} %fusion.131), kind=kOutput, calls=%fused_computation.7.clone.1 | convolution fusion | flops 1344798720 | bytes 6324228 | tf_op jit(solution)/shard_map/while/body/eval_jaxpr/ayb,axzb->xzy/dot_general | solution.py:86
  19.3 2.1 fusion.131
  21.4 6.7 %bitcast_dynamic-update-slice_fusion.2 = f32[8,8,64,1024]{3,2,1,0:T(8,128)} fusion(f32[8,8,64,1024]{3,2,1,0:T(8,128)} %get-tuple-element.219, s32[]{:T(128)S(6)} %copy.43, bf16[8,1024,128]{2,1,0:T(8,128)(2,1)} %get-tuple-element.228, s32[8,8,128]{2,1,0:T(8,128)S(1)} %iota_add_fusion.2, bf16[8,8,64,256]{3,1,2,0:T(8,128)(2,1)} %fusion.131), kind=kOutput, calls=%fused_computation.7.clone.1 | convolution fusion | flops 1344798720 | bytes 6324228 | tf_op jit(solution)/shard_map/while/body/eval_jaxpr/ayb,axzb->xzy/dot_general | solution.py:86
  28.2 2.1 fusion.131
  30.4 6.7 %bitcast_dynamic-update-slice_fusion.2 = f32[8,8,64,1024]{3,2,1,0:T(8,128)} fusion(f32[8,8,64,1024]{3,2,1,0:T(8,128)} %get-tuple-element.219, s32[]{:T(128)S(6)} %copy.43, bf16[8,1024,128]{2,1,0:T(8,128)(2,1)} %get-tuple-element.228, s32[8,8,128]{2,1,0:T(8,128)S(1)} %iota_add_fusion.2, bf16[8,8,64,256]{3,1,2,0:T(8,128)(2,1)} %fusion.131), kind=kOutput, calls=%fused_computation.7.clone.1 | convolution fusion | flops 1344798720 | bytes 6324228 | tf_op jit(solution)/shard_map/while/body/eval_jaxpr/ayb,axzb->xzy/dot_general | solution.py:86
  37.2 2.1 fusion.131
  39.4 6.8 %bitcast_dynamic-update-slice_fusion.2 = f32[8,8,64,1024]{3,2,1,0:T(8,128)} fusion(f32[8,8,64,1024]{3,2,1,0:T(8,128)} %get-tuple-element.219, s32[]{:T(128)S(6)} %copy.43, bf16[8,1024,128]{2,1,0:T(8,128)(2,1)} %get-tuple-element.228, s32[8,8,128]{2,1,0:T(8,128)S(1)} %iota_add_fusion.2, bf16[8,8,64,256]{3,1,2,0:T(8,128)(2,1)} %fusion.131), kind=kOutput, calls=%fused_computation.7.clone.1 | convolution fusion | flops 1344798720 | bytes 6324228 | tf_op jit(solution)/shard_map/while/body/eval_jaxpr/ayb,axzb->xzy/dot_general | solution.py:86
  46.2 2.1 fusion.131
  48.3 6.8 %bitcast_dynamic-update-slice_fusion.2 = f32[8,8,64,1024]{3,2,1,0:T(8,128)} fusion(f32[8,8,64,1024]{3,2,1,0:T(8,128)} %get-tuple-element.219, s32[]{:T(128)S(6)} %copy.43, bf16[8,1024,128]{2,1,0:T(8,128)(2,1)} %get-tuple-element.228, s32[8,8,128]{2,1,0:T(8,128)S(1)} %iota_add_fusion.2, bf16[8,8,64,256]{3,1,2,0:T(8,128)(2,1)} %fusion.131), kind=kOutput, calls=%fused_computation.7.clone.1 | convolution fusion | flops 1344798720 | bytes 6324228 | tf_op jit(solution)/shard_map/while/body/eval_jaxpr/ayb,axzb->xzy/dot_general | solution.py:86
  55.2 2.1 fusion.131
  57.3 6.7 %bitcast_dynamic-update-slice_fusion.2 = f32[8,8,64,1024]{3,2,1,0:T(8,128)} fusion(f32[8,8,64,1024]{3,2,1,0:T(8,128)} %get-tuple-element.219, s32[]{:T(128)S(6)} %copy.43, bf16[8,1024,128]{2,1,0:T(8,128)(2,1)} %get-tuple-element.228, s32[8,8,128]{2,1,0:T(8,128)S(1)} %iota_add_fusion.2, bf16[8,8,64,256]{3,1,2,0:T(8,128)(2,1)} %fusion.131), kind=kOutput, calls=%fused_computation.7.clone.1 | convolution fusion | flops 1344798720 | bytes 6324228 | tf_op jit(solution)/shard_map/while/body/eval_jaxpr/ayb,axzb->xzy/dot_general | solution.py:86
  64.2 2.1 fusion.131
  66.3 6.7 %bitcast_dynamic-update-slice_fusion.2 = f32[8,8,64,1024]{3,2,1,0:T(8,128)} fusion(f32[8,8,64,1024]{3,2,1,0:T(8,128)} %get-tuple-element.219, s32[]{:T(128)S(6)} %copy.43, bf16[8,1024,128]{2,1,0:T(8,128)(2,1)} %get-tuple-element.228, s32[8,8,128]{2,1,0:T(8,128)S(1)} %iota_add_fusion.2, bf16[8,8,64,256]{3,1,2,0:T(8,128)(2,1)} %fusion.131), kind=kOutput, calls=%fused_computation.7.clone.1 | convolution fusion | flops 1344798720 | bytes 6324228 | tf_op jit(solution)/shard_map/while/body/eval_jaxpr/ayb,axzb->xzy/dot_general | solution.py:86
  73.1 2.1 fusion.131
  75.2 6.7 %bitcast_dynamic-update-slice_fusion.2 = f32[8,8,64,1024]{3,2,1,0:T(8,128)} fusion(f32[8,8,64,1024]{3,2,1,0:T(8,128)} %get-tuple-element.219, s32[]{:T(128)S(6)} %copy.43, bf16[8,1024,128]{2,1,0:T(8,128)(2,1)} %get-tuple-element.228, s32[8,8,128]{2,1,0:T(8,128)S(1)} %iota_add_fusion.2, bf16[8,8,64,256]{3,1,2,0:T(8,128)(2,1)} %fusion.131), kind=kOutput, calls=%fused_computation.7.clone.1 | convolution fusion | flops 1344798720 | bytes 6324228 | tf_op jit(solution)/shard_map/while/body/eval_jaxpr/ayb,axzb->xzy/dot_general | solution.py:86
  81.9 0.7 copy-done.3
  82.6 0.7 fusion.115
  83.4 10.7 %select_add_fusion = f32[2,64,1024]{2,1,0:T(8,128)S(1)} fusion(s32[2,64,1024]{2,1,0:T(8,128)S(1)} %copy-done.1, s32[2,64,1024]{2,1,0:T(8,128)S(1)} %copy-done.2, f32[]{:T(128)} %bitcast.17, f32[]{:T(128)} %bitcast.16, f32[]{:T(128)} %bitcast.15, f32[]{:T(128)} %bitcast.14, f32[]{:T(128)} %bitcast.13, f32[]{:T(128)} %bitcast.12, f32[]{:T(128)} %bitcast.11, ...), kind=kLoop, calls=%fused_computation.184 | loop fusion | flops 6422528 | bytes 1572928 | tf_op jit(solution)/shard_map/add | solution.py:97
  94.1 2.2 collective-permute-start
  96.3 2.1 collective-permute-start.2
  98.5 140.1 %reduce-scatter.2.cloned.1.call-done = f32[2,64,1024]{2,1,0:T(8,128)} async-done(((f32[64,64,1024]{2,1,0:T(8,128)}), f32[2,64,1024]{2,1,0:T(8,128)}) %reduce-scatter.2.cloned.1.call-update) | async-done | bytes 524304 | tf_op jit(solution)/shard_map/reduce_scatter | solution.py:92
  238.6 1.1 fusion.114
  239.7 1.9 collective-permute-start.3
  241.6 3.6 collective-permute-start.1
  245.3 2.7 collective-permute-start.5
  248.1 9.1 %collective-permute-start.4 = (f32[4,1,1024]{2,1,0:T(1,128)S(1)}, f32[4,1,1024]{2,1,0:T(1,128)S(1)}, u32[]{:S(2)}, u32[]{:S(2)}) collective-permute-start(f32[4,1,1024]{2,1,0:T(1,128)S(1)} %get-tuple-element.147), channel_id=1, source_target_pairs={{0,1},{1,2},{2,3},{3,4},{4,5},{5,6},{6,7},{8,9},{9,10},{10,11},{11... | collective-permute-start | bytes 49160 | tf_op jit(solution)/shard_map/ppermute | solution.py:20
  257.4 1.9 collective-permute-start.6
  259.3 3.9 %collective-permute-start.7 = (f32[4,1,1024]{2,1,0:T(1,128)S(1)}, f32[4,1,1024]{2,1,0:T(1,128)S(1)}, u32[]{:S(2)}, u32[]{:S(2)}) collective-permute-start(f32[4,1,1024]{2,1,0:T(1,128)S(1)} %get-tuple-element.149), channel_id=1, source_target_pairs={{1,0},{2,1},{3,2},{4,3},{5,4},{6,5},{7,6},{9,8},{10,9},{11,10},{12... | collective-permute-start | bytes 49160 | tf_op jit(solution)/shard_map/ppermute | solution.py:22
  263.2 0.5 select_maximum_fusion.14
  263.8 7.2 %collective-permute-done.7 = f32[4,1,1024]{2,1,0:T(1,128)S(1)} collective-permute-done((f32[4,1,1024]{2,1,0:T(1,128)S(1)}, f32[4,1,1024]{2,1,0:T(1,128)S(1)}, u32[]{:S(2)}, u32[]{:S(2)}) %collective-permute-start.7) | collective-permute-done | bytes 16416 | tf_op jit(solution)/shard_map/ppermute | solution.py:22
  270.9 0.5 select_maximum_fusion.12
  271.4 1.7 fusion.92
  273.2 5.4 %collective-permute-start.8 = (f32[1,64,1024]{2,1,0:T(8,128)S(1)}, f32[1,64,1024]{2,1,0:T(8,128)S(1)}, u32[]{:S(2)}, u32[]{:S(2)}) collective-permute-start(f32[1,64,1024]{2,1,0:T(8,128)S(1)} %get-tuple-element.156), channel_id=1, source_target_pairs={{8,0},{16,8},{24,16},{32,24},{40,32},{48,40},{56,48},{64,56},{72,6... | collective-permute-start | bytes 786440 | tf_op jit(solution)/shard_map/ppermute | solution.py:22
  278.6 1.9 collective-permute-start.9
  280.5 1.9 collective-permute-done.8
  282.4 5.5 %collective-permute-done.9 = f32[1,64,1024]{2,1,0:T(8,128)S(1)} collective-permute-done((f32[1,64,1024]{2,1,0:T(8,128)S(1)}, f32[1,64,1024]{2,1,0:T(8,128)S(1)}, u32[]{:S(2)}, u32[]{:S(2)}) %collective-permute-start.9) | collective-permute-done | bytes 262176 | tf_op jit(solution)/shard_map/ppermute | solution.py:20
  288.0 1.9 collective-permute-start.10
  289.9 3.9 %collective-permute-start.11 = (f32[4,1,1024]{2,1,0:T(1,128)S(1)}, f32[4,1,1024]{2,1,0:T(1,128)S(1)}, u32[]{:S(2)}, u32[]{:S(2)}) collective-permute-start(f32[4,1,1024]{2,1,0:T(1,128)S(1)} %get-tuple-element.145), channel_id=1, source_target_pairs={{1,0},{2,1},{3,2},{4,3},{5,4},{6,5},{7,6},{9,8},{10,9},{11,10},{12... | collective-permute-start | bytes 49160 | tf_op jit(solution)/shard_map/ppermute | solution.py:22
  293.9 7.7 %collective-permute-done.11 = f32[4,1,1024]{2,1,0:T(1,128)S(1)} collective-permute-done((f32[4,1,1024]{2,1,0:T(1,128)S(1)}, f32[4,1,1024]{2,1,0:T(1,128)S(1)}, u32[]{:S(2)}, u32[]{:S(2)}) %collective-permute-start.11) | collective-permute-done | bytes 16416 | tf_op jit(solution)/shard_map/ppermute | solution.py:22
  301.6 0.5 select_maximum_fusion.8
  302.1 0.8 fusion.75
  302.9 1.9 collective-permute-start.12
  304.8 2.4 collective-permute-start.13
  307.2 1.5 collective-permute-done.12
  308.7 9.0 %collective-permute-done.13 = f32[1,64,1024]{2,1,0:T(8,128)S(1)} collective-permute-done((f32[1,64,1024]{2,1,0:T(8,128)S(1)}, f32[1,64,1024]{2,1,0:T(8,128)S(1)}, u32[]{:S(2)}, u32[]{:S(2)}) %collective-permute-start.13) | collective-permute-done | bytes 262176 | tf_op jit(solution)/shard_map/ppermute | solution.py:20
  317.7 1.9 collective-permute-start.14
  319.6 3.9 %collective-permute-start.15 = (f32[4,1,1024]{2,1,0:T(1,128)S(1)}, f32[4,1,1024]{2,1,0:T(1,128)S(1)}, u32[]{:S(2)}, u32[]{:S(2)}) collective-permute-start(f32[4,1,1024]{2,1,0:T(1,128)S(1)} %get-tuple-element.143), channel_id=1, source_target_pairs={{1,0},{2,1},{3,2},{4,3},{5,4},{6,5},{7,6},{9,8},{10,9},{11,10},{12... | collective-permute-start | bytes 49160 | tf_op jit(solution)/shard_map/ppermute | solution.py:22
  323.5 7.7 %collective-permute-done.15 = f32[4,1,1024]{2,1,0:T(1,128)S(1)} collective-permute-done((f32[4,1,1024]{2,1,0:T(1,128)S(1)}, f32[4,1,1024]{2,1,0:T(1,128)S(1)}, u32[]{:S(2)}, u32[]{:S(2)}) %collective-permute-start.15) | collective-permute-done | bytes 16416 | tf_op jit(solution)/shard_map/ppermute | solution.py:22
  331.2 0.5 select_maximum_fusion.4
  331.7 0.8 fusion.58
  332.5 1.9 collective-permute-start.16
  334.5 2.4 collective-permute-start.17
  336.9 1.5 collective-permute-done.16
  338.3 6.8 %collective-permute-done.17 = f32[1,64,1024]{2,1,0:T(8,128)S(1)} collective-permute-done((f32[1,64,1024]{2,1,0:T(8,128)S(1)}, f32[1,64,1024]{2,1,0:T(8,128)S(1)}, u32[]{:S(2)}, u32[]{:S(2)}) %collective-permute-start.17) | collective-permute-done | bytes 262176 | tf_op jit(solution)/shard_map/ppermute | solution.py:20
  345.2 1.9 collective-permute-start.18
  347.1 3.9 %collective-permute-start.19 = (f32[4,1,1024]{2,1,0:T(1,128)S(1)}, f32[4,1,1024]{2,1,0:T(1,128)S(1)}, u32[]{:S(2)}, u32[]{:S(2)}) collective-permute-start(f32[4,1,1024]{2,1,0:T(1,128)S(1)} %get-tuple-element.141), channel_id=1, source_target_pairs={{1,0},{2,1},{3,2},{4,3},{5,4},{6,5},{7,6},{9,8},{10,9},{11,10},{12... | collective-permute-start | bytes 49160 | tf_op jit(solution)/shard_map/ppermute | solution.py:22
  351.0 7.7 %collective-permute-done.19 = f32[4,1,1024]{2,1,0:T(1,128)S(1)} collective-permute-done((f32[4,1,1024]{2,1,0:T(1,128)S(1)}, f32[4,1,1024]{2,1,0:T(1,128)S(1)}, u32[]{:S(2)}, u32[]{:S(2)}) %collective-permute-start.19) | collective-permute-done | bytes 16416 | tf_op jit(solution)/shard_map/ppermute | solution.py:22
  358.7 0.5 select_maximum_fusion
  359.2 1.5 fusion.41
  (58 shorter events, 1.6 us)
Async XLA Ops:
  7.2 231.4 %reduce-scatter.2.cloned.1.call-start = ((), (), s32[]{:S(2)}) async-start(), calls=%async_computation.1 | async-start | bytes 17301504 | tf_op jit(solution)/shard_map/reduce_scatter | solution.py:92
  81.9 0.7 copy-start.3
  81.9 1.5 copy-start.1
  81.9 1.5 copy-start.2
  94.1 151.1 %collective-permute-start = (f32[1,64,1024]{2,1,0:T(8,128)S(1)}, f32[1,64,1024]{2,1,0:T(8,128)S(1)}, u32[]{:S(2)}, u32[]{:S(2)}) collective-permute-start(f32[1,64,1024]{2,1,0:T(8,128)S(1)} %get-tuple-element.158), channel_id=1, source_target_pairs={{8,0},{16,8},{24,16},{32,24},{40,32},{48,40},{56,48},{64,56},{72,6... | collective-permute-start | bytes 786440 | tf_op jit(solution)/shard_map/ppermute | solution.py:22
  96.3 148.9 %collective-permute-start.2 = (f32[1,64,1024]{2,1,0:T(8,128)S(1)}, f32[1,64,1024]{2,1,0:T(8,128)S(1)}, u32[]{:S(2)}, u32[]{:S(2)}) collective-permute-start(f32[1,64,1024]{2,1,0:T(8,128)S(1)} %get-tuple-element.157), channel_id=1, source_target_pairs={{0,8},{8,16},{16,24},{24,32},{32,40},{40,48},{48,56},{56,64},{64,7... | collective-permute-start | bytes 786440 | tf_op jit(solution)/shard_map/ppermute | solution.py:20
  238.6 18.7 %copy-start = (f32[2,64,1024]{2,1,0:T(8,128)S(1)}, f32[2,64,1024]{2,1,0:T(8,128)}, u32[]{:S(2)}) copy-start(f32[2,64,1024]{2,1,0:T(8,128)} %reduce-scatter.2.cloned.1.call-done) | copy-start | bytes 1572868
  239.7 17.5 %collective-permute-start.3 = (f32[1,64,1024]{2,1,0:T(8,128)S(1)}, f32[1,64,1024]{2,1,0:T(8,128)S(1)}, u32[]{:S(2)}, u32[]{:S(2)}) collective-permute-start(f32[1,64,1024]{2,1,0:T(8,128)S(1)} %get-tuple-element.160), channel_id=1, source_target_pairs={{0,8},{8,16},{16,24},{24,32},{32,40},{40,48},{48,56},{56,64},{64,7... | collective-permute-start | bytes 786440 | tf_op jit(solution)/shard_map/ppermute | solution.py:20
  241.6 15.7 %collective-permute-start.1 = (f32[1,64,1024]{2,1,0:T(8,128)S(1)}, f32[1,64,1024]{2,1,0:T(8,128)S(1)}, u32[]{:S(2)}, u32[]{:S(2)}) collective-permute-start(f32[1,64,1024]{2,1,0:T(8,128)S(1)} %get-tuple-element.159), channel_id=1, source_target_pairs={{8,0},{16,8},{24,16},{32,24},{40,32},{48,40},{56,48},{64,56},{72,6... | collective-permute-start | bytes 786440 | tf_op jit(solution)/shard_map/ppermute | solution.py:22
  245.3 17.9 %collective-permute-start.5 = (f32[4,1,1024]{2,1,0:T(1,128)S(1)}, f32[4,1,1024]{2,1,0:T(1,128)S(1)}, u32[]{:S(2)}, u32[]{:S(2)}) collective-permute-start(f32[4,1,1024]{2,1,0:T(1,128)S(1)} %get-tuple-element.148), channel_id=1, source_target_pairs={{1,0},{2,1},{3,2},{4,3},{5,4},{6,5},{7,6},{9,8},{10,9},{11,10},{12... | collective-permute-start | bytes 49160 | tf_op jit(solution)/shard_map/ppermute | solution.py:22
  248.1 15.2 %collective-permute-start.4 = (f32[4,1,1024]{2,1,0:T(1,128)S(1)}, f32[4,1,1024]{2,1,0:T(1,128)S(1)}, u32[]{:S(2)}, u32[]{:S(2)}) collective-permute-start(f32[4,1,1024]{2,1,0:T(1,128)S(1)} %get-tuple-element.147), channel_id=1, source_target_pairs={{0,1},{1,2},{2,3},{3,4},{4,5},{5,6},{6,7},{8,9},{9,10},{10,11},{11... | collective-permute-start | bytes 49160 | tf_op jit(solution)/shard_map/ppermute | solution.py:20
  257.4 6.4 %collective-permute-start.6 = (f32[4,1,1024]{2,1,0:T(1,128)S(1)}, f32[4,1,1024]{2,1,0:T(1,128)S(1)}, u32[]{:S(2)}, u32[]{:S(2)}) collective-permute-start(f32[4,1,1024]{2,1,0:T(1,128)S(1)} %get-tuple-element.150), channel_id=1, source_target_pairs={{0,1},{1,2},{2,3},{3,4},{4,5},{5,6},{6,7},{8,9},{9,10},{10,11},{11... | collective-permute-start | bytes 49160 | tf_op jit(solution)/shard_map/ppermute | solution.py:20
  259.3 11.6 %collective-permute-start.7 = (f32[4,1,1024]{2,1,0:T(1,128)S(1)}, f32[4,1,1024]{2,1,0:T(1,128)S(1)}, u32[]{:S(2)}, u32[]{:S(2)}) collective-permute-start(f32[4,1,1024]{2,1,0:T(1,128)S(1)} %get-tuple-element.149), channel_id=1, source_target_pairs={{1,0},{2,1},{3,2},{4,3},{5,4},{6,5},{7,6},{9,8},{10,9},{11,10},{12... | collective-permute-start | bytes 49160 | tf_op jit(solution)/shard_map/ppermute | solution.py:22
  273.2 9.3 %collective-permute-start.8 = (f32[1,64,1024]{2,1,0:T(8,128)S(1)}, f32[1,64,1024]{2,1,0:T(8,128)S(1)}, u32[]{:S(2)}, u32[]{:S(2)}) collective-permute-start(f32[1,64,1024]{2,1,0:T(8,128)S(1)} %get-tuple-element.156), channel_id=1, source_target_pairs={{8,0},{16,8},{24,16},{32,24},{40,32},{48,40},{56,48},{64,56},{72,6... | collective-permute-start | bytes 786440 | tf_op jit(solution)/shard_map/ppermute | solution.py:22
  278.6 9.4 %collective-permute-start.9 = (f32[1,64,1024]{2,1,0:T(8,128)S(1)}, f32[1,64,1024]{2,1,0:T(8,128)S(1)}, u32[]{:S(2)}, u32[]{:S(2)}) collective-permute-start(f32[1,64,1024]{2,1,0:T(8,128)S(1)} %get-tuple-element.155), channel_id=1, source_target_pairs={{0,8},{8,16},{16,24},{24,32},{32,40},{40,48},{48,56},{56,64},{64,7... | collective-permute-start | bytes 786440 | tf_op jit(solution)/shard_map/ppermute | solution.py:20
  288.0 5.9 %collective-permute-start.10 = (f32[4,1,1024]{2,1,0:T(1,128)S(1)}, f32[4,1,1024]{2,1,0:T(1,128)S(1)}, u32[]{:S(2)}, u32[]{:S(2)}) collective-permute-start(f32[4,1,1024]{2,1,0:T(1,128)S(1)} %get-tuple-element.146), channel_id=1, source_target_pairs={{0,1},{1,2},{2,3},{3,4},{4,5},{5,6},{6,7},{8,9},{9,10},{10,11},{11... | collective-permute-start | bytes 49160 | tf_op jit(solution)/shard_map/ppermute | solution.py:20
  289.9 11.6 %collective-permute-start.11 = (f32[4,1,1024]{2,1,0:T(1,128)S(1)}, f32[4,1,1024]{2,1,0:T(1,128)S(1)}, u32[]{:S(2)}, u32[]{:S(2)}) collective-permute-start(f32[4,1,1024]{2,1,0:T(1,128)S(1)} %get-tuple-element.145), channel_id=1, source_target_pairs={{1,0},{2,1},{3,2},{4,3},{5,4},{6,5},{7,6},{9,8},{10,9},{11,10},{12... | collective-permute-start | bytes 49160 | tf_op jit(solution)/shard_map/ppermute | solution.py:22
  302.9 5.8 %collective-permute-start.12 = (f32[1,64,1024]{2,1,0:T(8,128)S(1)}, f32[1,64,1024]{2,1,0:T(8,128)S(1)}, u32[]{:S(2)}, u32[]{:S(2)}) collective-permute-start(f32[1,64,1024]{2,1,0:T(8,128)S(1)} %get-tuple-element.154), channel_id=1, source_target_pairs={{8,0},{16,8},{24,16},{32,24},{40,32},{48,40},{56,48},{64,56},{72,6... | collective-permute-start | bytes 786440 | tf_op jit(solution)/shard_map/ppermute | solution.py:22
  304.8 12.8 %collective-permute-start.13 = (f32[1,64,1024]{2,1,0:T(8,128)S(1)}, f32[1,64,1024]{2,1,0:T(8,128)S(1)}, u32[]{:S(2)}, u32[]{:S(2)}) collective-permute-start(f32[1,64,1024]{2,1,0:T(8,128)S(1)} %get-tuple-element.153), channel_id=1, source_target_pairs={{0,8},{8,16},{16,24},{24,32},{32,40},{40,48},{48,56},{56,64},{64,7... | collective-permute-start | bytes 786440 | tf_op jit(solution)/shard_map/ppermute | solution.py:20
  317.7 5.9 %collective-permute-start.14 = (f32[4,1,1024]{2,1,0:T(1,128)S(1)}, f32[4,1,1024]{2,1,0:T(1,128)S(1)}, u32[]{:S(2)}, u32[]{:S(2)}) collective-permute-start(f32[4,1,1024]{2,1,0:T(1,128)S(1)} %get-tuple-element.144), channel_id=1, source_target_pairs={{0,1},{1,2},{2,3},{3,4},{4,5},{5,6},{6,7},{8,9},{9,10},{10,11},{11... | collective-permute-start | bytes 49160 | tf_op jit(solution)/shard_map/ppermute | solution.py:20
  319.6 11.6 %collective-permute-start.15 = (f32[4,1,1024]{2,1,0:T(1,128)S(1)}, f32[4,1,1024]{2,1,0:T(1,128)S(1)}, u32[]{:S(2)}, u32[]{:S(2)}) collective-permute-start(f32[4,1,1024]{2,1,0:T(1,128)S(1)} %get-tuple-element.143), channel_id=1, source_target_pairs={{1,0},{2,1},{3,2},{4,3},{5,4},{6,5},{7,6},{9,8},{10,9},{11,10},{12... | collective-permute-start | bytes 49160 | tf_op jit(solution)/shard_map/ppermute | solution.py:22
  332.5 5.8 %collective-permute-start.16 = (f32[1,64,1024]{2,1,0:T(8,128)S(1)}, f32[1,64,1024]{2,1,0:T(8,128)S(1)}, u32[]{:S(2)}, u32[]{:S(2)}) collective-permute-start(f32[1,64,1024]{2,1,0:T(8,128)S(1)} %get-tuple-element.152), channel_id=1, source_target_pairs={{8,0},{16,8},{24,16},{32,24},{40,32},{48,40},{56,48},{64,56},{72,6... | collective-permute-start | bytes 786440 | tf_op jit(solution)/shard_map/ppermute | solution.py:22
  334.5 10.7 %collective-permute-start.17 = (f32[1,64,1024]{2,1,0:T(8,128)S(1)}, f32[1,64,1024]{2,1,0:T(8,128)S(1)}, u32[]{:S(2)}, u32[]{:S(2)}) collective-permute-start(f32[1,64,1024]{2,1,0:T(8,128)S(1)} %get-tuple-element.151), channel_id=1, source_target_pairs={{0,8},{8,16},{16,24},{24,32},{32,40},{40,48},{48,56},{56,64},{64,7... | collective-permute-start | bytes 786440 | tf_op jit(solution)/shard_map/ppermute | solution.py:20
  345.2 5.9 %collective-permute-start.18 = (f32[4,1,1024]{2,1,0:T(1,128)S(1)}, f32[4,1,1024]{2,1,0:T(1,128)S(1)}, u32[]{:S(2)}, u32[]{:S(2)}) collective-permute-start(f32[4,1,1024]{2,1,0:T(1,128)S(1)} %get-tuple-element.142), channel_id=1, source_target_pairs={{0,1},{1,2},{2,3},{3,4},{4,5},{5,6},{6,7},{8,9},{9,10},{10,11},{11... | collective-permute-start | bytes 49160 | tf_op jit(solution)/shard_map/ppermute | solution.py:20
  347.1 11.6 %collective-permute-start.19 = (f32[4,1,1024]{2,1,0:T(1,128)S(1)}, f32[4,1,1024]{2,1,0:T(1,128)S(1)}, u32[]{:S(2)}, u32[]{:S(2)}) collective-permute-start(f32[4,1,1024]{2,1,0:T(1,128)S(1)} %get-tuple-element.141), channel_id=1, source_target_pairs={{1,0},{2,1},{3,2},{4,3},{5,4},{6,5},{7,6},{9,8},{10,9},{11,10},{12... | collective-permute-start | bytes 49160 | tf_op jit(solution)/shard_map/ppermute | solution.py:22
Sparse Core Ops, SparseCore 0:
  82.0 156.4 reduce-scatter.1
where the time goes:
time: 370 us; the launch traced here: 368 us
  waiting for transfers between devices  197 us (53%)
  matrix products  70.8 us (19%)
  starting transfers between devices  61.1 us (17%)
  other arithmetic  19.1 us (5%)
  between operations  14.4 us (4%)
  local copies, waits for them, and re-layouts  5.42 us (1%)
    reduce_scatter x1, waiting for transfers between devices, local(): lax.psum_scatter(partial_value, 'ang', scatter_dimension=0, tiled=True)  140 us
    dot_general x8, matrix products, one_block(): jnp.einsum('ayb,axzb->xzy', band_weights, gathered, preferred_element_typ...  53.8 us
    ppermute x10, waiting for transfers between devices, padded(): lax.ppermute(head, axis, [((i + 1) % count, i) for i in range(ends)])  35.2 us
    ppermute x10, starting transfers between devices, padded(): lax.ppermute(head, axis, [((i + 1) % count, i) for i in range(ends)])  33.5 us
    ppermute x10, starting transfers between devices, padded(): lax.ppermute(tail, axis, [(i, (i + 1) % count) for i in range(ends)])  27.6 us
    ppermute x10, waiting for transfers between devices, padded(): lax.ppermute(tail, axis, [(i, (i + 1) % count) for i in range(ends)])  21.3 us
    dot_general x8, matrix products, one_block(): jnp.einsum('axk,azkw->axzw', chooser, block_pairs, preferred_element_type...  17 us
    add x1, other arithmetic, local(): conduct = conduct + jnp.where(label_index == entry, flat_table[entry], 0.0)  10.7 us
  transfers between devices with their start and end apart: 21, of which 11 were waited for; matrix products, arithmetic and copies ran while one was open for 4% of the time, Pallas kernels for 0%

commit v1 on v0

v1 whole, which is shorter than its diff:
```python
import functools
import jax
import jax.numpy as jnp
from jax import lax
from jax.experimental import pallas as pl
from jax.experimental.pallas import tpu as pltpu
from jax.sharding import PartitionSpec as P

STEPS = 4
STEP_SIZE = 0.15
CHUNKS = 4
ZL, X, C = 4, 4, 2
VMEM_LIMIT = 56 * 1024 * 1024


def shift_ang(value, dz=0, dx=0, dc=0):
    perm = []
    for z in range(ZL):
        for x in range(X):
            for c in range(C):
                src = (z * X + x) * C + c
                dst = (((z + dz) % ZL) * X + (x + dx) % X) * C + (c ^ dc)
                perm.append((src, dst))
    return lax.ppermute(value, "ang", perm)


def shift_line(value, axis, step):
    count = lax.axis_size(axis)
    perm = [(i, i + step) for i in range(count) if 0 <= i + step < count]
    return lax.ppermute(value, axis, perm)


def gather_and_multiply(pos, offsets, proj, weights, wide, bands, core, store):
    angles, depth, columns = proj.shape
    wide[:, :, columns:] = jnp.zeros((angles, depth, 128), jnp.float32)
    for a in range(angles):
        wide[a, :, :columns] = proj[a].astype(jnp.float32)
    lane = lax.broadcasted_iota(jnp.int32, (depth, 128), 1)

    def row_body(row, carry):
        dx, dz, i = row // 8, (row // 2) % 4, row % 2
        owner = (
            ((pos[0] + dz) % ZL) * (X * C * 2) + ((pos[1] + dx) % X) * (C * 2) + core * 2 + i
        )
        for a in range(angles):
            off = offsets[a, owner]
            base = pl.multiple_of((off // 128) * 128, 128)
            rem = off % 128
            low = wide[a, :, pl.ds(base, 128)]
            high = wide[a, :, pl.ds(pl.multiple_of(base + 128, 128), 128)]
            turn = (128 - rem) % 128
            low = pltpu.roll(low, turn, 1)
            high = pltpu.roll(high, turn, 1)
            band = jnp.where(lane < 128 - rem, low, high)
            bands[pl.ds(pl.multiple_of(row * depth, depth), depth), a * 128:(a + 1) * 128] = (
                band.astype(jnp.bfloat16)
            )
        return carry

    lax.fori_loop(0, bands.shape[0] // depth, row_body, 0)
    tile = 256

    def tile_body(n, carry):
        cols = pl.ds(pl.multiple_of(n * tile, tile), tile)
        out = jnp.dot(bands[...], weights[:, cols], preferred_element_type=jnp.float32)
        store(out.reshape(4, 4, 2, depth, tile), cols)
        return carry

    lax.fori_loop(0, weights.shape[1] // tile, tile_body, 0)


def other_kernel(pos, offsets, proj, weights, out, wide, bands):
    def store(value, cols):
        out[:, :, :, :, cols] = value

    gather_and_multiply(pos, offsets, proj, weights, wide, bands, 1 - pos[2], store)


def mine_kernel(pos, offsets, proj, weights, recv, sendp, sendm, holdp, holdm, home, wide, bands):
    def store(value, cols):
        value = value + recv[:, :, :, :, cols]
        sendp[:2, :, :, cols] = value[2, :2]
        sendp[2:, :, :, cols] = value[1, 2:]
        sendm[:2, :, :, cols] = value[2, 2:]
        sendm[2:, :, :, cols] = value[3, :2]
        holdp[:, :, :, cols] = value[1, :2]
        holdm[:, :, :, cols] = value[3, 2:]
        home[:, :, :, cols] = value[0]

    gather_and_multiply(pos, offsets, proj, weights, wide, bands, pos[2], store)


SMEM = pl.BlockSpec(memory_space=pltpu.SMEM)
VMEM = pl.BlockSpec(memory_space=pltpu.VMEM)


def backproject(pos, offsets, proj, weights, chunk, recv=None):
    angles, depth_all, columns = proj.shape
    depth = depth_all // CHUNKS
    wide_y = weights.shape[1]
    proj_spec = pl.BlockSpec((angles, depth, columns), lambda i: (0, chunk, 0))
    full = lambda shape: pl.BlockSpec(shape, lambda i: (0,) * len(shape))
    scratch = [
        pltpu.VMEM((angles, depth, columns + 128), jnp.float32),
        pltpu.VMEM((32 * depth, angles * 128), jnp.bfloat16),
    ]
    flops = 2 * 32 * depth * angles * 128 * wide_y
    params = dict(
        scratch_shapes=scratch,
        grid=(1,),
        compiler_params=pltpu.CompilerParams(vmem_limit_bytes=VMEM_LIMIT),
        cost_estimate=pl.CostEstimate(flops=flops, bytes_accessed=6 * 2**20, transcendentals=0),
    )
    specs = [SMEM, SMEM, proj_spec, full(weights.shape)]
    f32 = lambda *shape: jax.ShapeDtypeStruct(shape, jnp.float32)
    if recv is None:
        shape = (4, 4, 2, depth, wide_y)
        return pl.pallas_call(
            other_kernel, out_shape=f32(*shape), in_specs=specs, out_specs=full(shape), **params
        )(pos, offsets, proj, weights)
    shapes = [(n, 2, depth, wide_y) for n in (4, 4, 2, 2, 4)]
    return pl.pallas_call(
        mine_kernel,
        out_shape=[f32(*s) for s in shapes],
        in_specs=specs + [full(recv.shape)],
        out_specs=[full(s) for s in shapes],
        **params,
    )(pos, offsets, proj, weights, recv)


def conduct_kernel(table, phase, contact, out):
    contacts = table.shape[1]
    index = phase[...] * contacts + contact[...]
    value = jnp.zeros(index.shape, jnp.float32)
    for p in range(table.shape[0]):
        for c in range(contacts):
            value = jnp.where(index == p * contacts + c, table[p, c], value)
    out[...] = value


def conductivities(table, phase, contact):
    rows = phase.shape[1]
    spec = pl.BlockSpec((1, 16, phase.shape[2]), lambda i, j: (i, j, 0))
    return pl.pallas_call(
        conduct_kernel,
        grid=(phase.shape[0], rows // 16),
        out_shape=jax.ShapeDtypeStruct(phase.shape, jnp.float32),
        in_specs=[SMEM, spec, spec],
        out_specs=spec,
    )(table, phase, contact)


def widened(value):
    below = [shift_line(value, "ang", 2), shift_line(value, "ang", 1)]
    above = [shift_line(value, "ang", -1), shift_line(value, "ang", -2)]
    wide = jnp.concatenate([*below, value, *above], axis=0)
    low = shift_line(wide[:, -4:], "gz", 1)
    high = shift_line(wide[:, :4], "gz", -1)
    return wide, low, high


def face_of(a, b):
    total = a + b
    positive = total > 0.0
    return jnp.where(positive, 2.0 * a * b / jnp.where(positive, total, 1.0), 0.0)


def heat_kernel(heat, heat_low, heat_high, cond, cond_low, cond_high, out, field, other, con, fx, fy, fz):
    rows, depth, columns = heat.shape
    tall = depth + 16
    for scratch, value, low, high in (
        (field, heat, heat_low, heat_high),
        (con, cond, cond_low, cond_high),
    ):
        zeros = jnp.zeros((rows, 8, columns), jnp.float32)
        scratch[:, :8] = zeros
        scratch[:, depth + 8:] = zeros
        scratch[:, 4:8] = low[...]
        scratch[:, depth + 8:depth + 12] = high[...]
        scratch[:, 8:depth + 8] = value[...]
    tiles = tall // 8
    lane = lax.broadcasted_iota(jnp.int32, (8, columns), 1)
    sub = lax.broadcasted_iota(jnp.int32, (8, columns), 0)

    def next_z(here, above):
        return jnp.where(sub == 7, pltpu.roll(above, 7, 0), pltpu.roll(here, 7, 0))

    def face_body(r, carry):
        here = con[r, 0:8, :]
        for t in range(tiles):
            z = slice(8 * t, 8 * t + 8)
            above = con[r, 8 * t + 8:8 * t + 16, :] if t + 1 < tiles else jnp.zeros_like(here)
            along_y = pltpu.roll(here, columns - 1, 1)
            fy[r, z, :] = jnp.where(lane == columns - 1, 0.0, face_of(here, along_y))
            fz[r, z, :] = face_of(here, next_z(here, above))
            fx[r, z, :] = face_of(here, con[jnp.minimum(r + 1, rows - 1), z, :])
            here = above
        return carry

    lax.fori_loop(0, rows, face_body, 0)

    source, target = field, other
    for step in range(1, STEPS + 1):
        last = step == STEPS
        first_tile, end_tile = (1, tiles - 1) if last else (0, tiles)

        def row_body(r, carry, source=source, target=target, last=last, first_tile=first_tile, end_tile=end_tile):
            if first_tile:
                before = source[r, 8 * first_tile - 8:8 * first_tile, :]
                here = source[r, 8 * first_tile:8 * first_tile + 8, :]
                flux_before = fz[r, 8 * first_tile - 8:8 * first_tile, :] * (
                    next_z(before, here) - before
                )
            else:
                here = source[r, 0:8, :]
                flux_before = jnp.zeros_like(here)
            for t in range(first_tile, end_tile):
                z = slice(8 * t, 8 * t + 8)
                above = source[r, 8 * t + 8:8 * t + 16, :] if t + 1 < tiles else jnp.zeros_like(here)
                flux_x = fx[r, z, :] * (source[r + 1, z, :] - here)
                flux_x -= fx[r - 1, z, :] * (here - source[r - 1, z, :])
                flux_y = fy[r, z, :] * (pltpu.roll(here, columns - 1, 1) - here)
                flux_y -= pltpu.roll(flux_y, 1, 1)
                flux = fz[r, z, :] * (next_z(here, above) - here)
                flux_z = flux - jnp.where(sub == 0, pltpu.roll(flux_before, 1, 0), pltpu.roll(flux, 1, 0))
                value = here + STEP_SIZE * (flux_x + flux_y + flux_z)
                if last:
                    out[r - STEPS, 8 * t - 8:8 * t, :] = value
                else:
                    target[r, z, :] = value
                here, flux_before = above, flux
            return carry

        lax.fori_loop(step, rows - step, row_body, 0)
        source, target = target, source


def conduct_heat(heat, cond):
    rows, depth, columns = heat[0].shape
    scratch = pltpu.VMEM((rows, depth + 16, columns), jnp.float32)
    return pl.pallas_call(
        heat_kernel,
        out_shape=jax.ShapeDtypeStruct((rows - 2 * STEPS, depth, columns), jnp.float32),
        in_specs=[VMEM] * 6,
        out_specs=VMEM,
        scratch_shapes=[scratch] * 6,
        compiler_params=pltpu.CompilerParams(vmem_limit_bytes=VMEM_LIMIT),
        cost_estimate=pl.CostEstimate(
            flops=200 * 2**20, bytes_accessed=6 * 2**20, transcendentals=0
        ),
    )(*heat, *cond)


def local(projections, band_weights, band_offsets, phase, contact, conductivity_table):
    angles, wide_y, band = band_weights.shape
    ang = lax.axis_index("ang")
    pos = jnp.stack([ang // (X * C), (ang // C) % X, ang % C]).astype(jnp.int32)
    weights = jnp.transpose(band_weights, (0, 2, 1)).reshape(angles * band, wide_y)
    conduct = conductivities(conductivity_table, phase, contact)
    conduct_wide = widened(conduct)

    pieces = []
    for chunk in range(CHUNKS):
        theirs = backproject(pos, band_offsets, projections, weights, chunk)
        recv = shift_ang(theirs, dc=1)
        sendp, sendm, holdp, holdm, home = backproject(
            pos, band_offsets, projections, weights, chunk, recv
        )
        fromp = shift_ang(sendp, dx=1)
        fromm = shift_ang(sendm, dx=-1)
        lastp = shift_ang(holdp + fromp[:2], dx=1)
        lastm = shift_ang(holdm + fromm[:2], dx=-1)
        ring_low = home[:2] + lastp + fromm[2:]
        ring_high = home[2:] + lastm + fromp[2:]
        one = shift_ang(ring_low[1], dz=1)
        two = shift_ang(ring_high[0], dz=2)
        three = shift_ang(ring_high[1], dz=3)
        pieces.append(ring_low[0] + one + two + three)
    volume = jnp.concatenate(pieces, axis=1)
    temperature = conduct_heat(widened(volume), conduct_wide)
    return volume, temperature


def solution(mesh):
    in_specs = (
        P("ang", "gz", None),
        P("ang", None, None),
        P("ang", None),
        P("ang", "gz", None),
        P("ang", "gz", None),
        P(),
    )
    out_specs = (P("ang", "gz", None), P("ang", "gz", None))
    return jax.shard_map(local, mesh=mesh, in_specs=in_specs, out_specs=out_specs, check_vma=False)
```

time: 370 us -> 291 us (0.79)
  waiting for transfers between devices: 197 us -> 85.3 us
  Pallas kernels: 0 us -> 103 us
  matrix products: 70.8 us -> 0 us
  starting transfers between devices: 61.1 us -> 90.4 us
  other arithmetic: 19.1 us -> 4.32 us
  between operations: 14.4 us -> 1.27 us
    reduce_scatter x1 -> x0, waiting for transfers between devices: 140 us -> none  [local(): lax.psum_scatter(partial_value, 'ang', scatter_dimension=0, tiled=True)]
    pallas_call x0 -> x10, Pallas kernels: none -> 103 us  [the longest x4 42.8 us: backproject(): pl.pallas_call(mine_kernel, out_shape=[f32(*s) for s in shapes], in_specs...]
    dot_general x16 -> x0, matrix products: 70.8 us -> none  [the longest x8 53.8 us: one_block(): jnp.einsum('ayb,axzb->xzy', band_weights, gathered, preferred_element_typ...]
    ppermute x20 -> x44, starting transfers between devices: 61.1 us -> 90.4 us  [the longest x32 54.2 us: shift_ang(): return lax.ppermute(value, 'ang', perm)]
    ppermute x20 -> x44, waiting for transfers between devices: 56.5 us -> 85.3 us  [the longest x32 54.3 us: shift_ang(): return lax.ppermute(value, 'ang', perm)]
    add x13 -> x16, other arithmetic: 16 us -> 3.64 us  [the longest x4 2.06 us: local(): lastp = shift_ang(holdp + fromp[:2], dx=1)]
    transpose x0 -> x1, local copies, waits for them, and re-layouts: none -> 3.94 us  [local(): jnp.transpose(band_weights, (0, 2, 1)).reshape(angles * band, wide_y)]
  transfers between devices with their start and end apart: 21 -> 44, of which waited for: 11 -> 19; matrix products, arithmetic and copies ran while one was open for 4% -> 1% of each run, Pallas kernels for 0% -> 27%
where the time goes in v1:
time: 291 us; the launch traced here: 290 us
  Pallas kernels  103 us (35%)
  starting transfers between devices  90.4 us (31%)
  waiting for transfers between devices  85.3 us (29%)
  local copies, waits for them, and re-layouts  5.3 us (2%)
  other arithmetic  4.32 us (1%)
    ppermute x32, waiting for transfers between devices, shift_ang(): return lax.ppermute(value, 'ang', perm)  54.3 us
    ppermute x32, starting transfers between devices, shift_ang(): return lax.ppermute(value, 'ang', perm)  54.2 us
    pallas_call x4, Pallas kernels, backproject(): pl.pallas_call(mine_kernel, out_shape=[f32(*s) for s in shapes], in_specs...  42.8 us
    pallas_call x4, Pallas kernels, backproject(): pl.pallas_call(other_kernel, out_shape=f32(*shape), in_specs=specs, out_s...  40.6 us
    ppermute x12, starting transfers between devices, shift_line(): return lax.ppermute(value, axis, perm)  36.3 us
    ppermute x12, waiting for transfers between devices, shift_line(): return lax.ppermute(value, axis, perm)  30.9 us
    pallas_call x1, Pallas kernels, conduct_heat(): pl.pallas_call(heat_kernel, out_shape=jax.ShapeDtypeStruct((rows - 2 * ST...  14.6 us
  transfers between devices with their start and end apart: 44, of which 19 were waited for; matrix products, arithmetic and copies ran while one was open for 1% of the time, Pallas kernels for 27%

profile of v1, /device:TPU:30, one launch (start us, length us, event | category | flops | bytes accessed | tf_op | source)
XLA Modules:
  0.0 289.8 jit_solution(11324646247589200155)
XLA Ops:
  0.7 3.9 %copy.8 = bf16[8,128,1024]{2,1,0:T(8,128)(2,1)} copy(bf16[8,128,1024]{1,2,0:T(8,128)(2,1)} %bitcast.69) | data formatting | bytes 4194304 | tf_op jit(solution)/shard_map/transpose | solution.py:258
  4.6 0.6 pad_add_fusion.pos
  5.2 10.1 %shard_map.77 = f32[4,4,2,16,1024]{4,3,2,1,0:T(8,128)} custom-call(s32[3]{0:T(128)} %pad_add_fusion.pos, s32[8,64]{1,0:T(8,128)} %offsets.15, bf16[8,64,1024]{2,1,0:T(8,128)(2,1)} %proj.15, bf16[1024,1024]{1,0:T(8,128)(2,1)} %bitcast.61), custom_call_target="tpu_custom_call" | custom-call | flops 1073741824 | bytes 6291456 | tf_op jit(solution)/shard_map/pallas_call | solution.py:118
  15.3 10.2 %shard_map.79 = f32[4,4,2,16,1024]{4,3,2,1,0:T(8,128)} custom-call(s32[3]{0:T(128)} %pad_add_fusion.pos, s32[8,64]{1,0:T(8,128)} %offsets.15, bf16[8,64,1024]{2,1,0:T(8,128)(2,1)} %proj.15, bf16[1024,1024]{1,0:T(8,128)(2,1)} %bitcast.62), custom_call_target="tpu_custom_call" | custom-call | flops 1073741824 | bytes 6291456 | tf_op jit(solution)/shard_map/pallas_call | solution.py:118
  26.0 10.2 %shard_map.81 = f32[4,4,2,16,1024]{4,3,2,1,0:T(8,128)} custom-call(s32[3]{0:T(128)} %pad_add_fusion.pos, s32[8,64]{1,0:T(8,128)} %offsets.15, bf16[8,64,1024]{2,1,0:T(8,128)(2,1)} %proj.15, bf16[1024,1024]{1,0:T(8,128)(2,1)} %bitcast.63), custom_call_target="tpu_custom_call" | custom-call | flops 1073741824 | bytes 6291456 | tf_op jit(solution)/shard_map/pallas_call | solution.py:118
  36.1 10.1 %shard_map.83 = f32[4,4,2,16,1024]{4,3,2,1,0:T(8,128)} custom-call(s32[3]{0:T(128)} %pad_add_fusion.pos, s32[8,64]{1,0:T(8,128)} %offsets.15, bf16[8,64,1024]{2,1,0:T(8,128)(2,1)} %proj.15, bf16[1024,1024]{1,0:T(8,128)(2,1)} %bitcast.64), custom_call_target="tpu_custom_call" | custom-call | flops 1073741824 | bytes 6291456 | tf_op jit(solution)/shard_map/pallas_call | solution.py:118
  46.8 5.2 %shard_map.85 = f32[2,64,1024]{2,1,0:T(8,128)} custom-call(f32[4,4]{1,0:T(4,128)} %table.1, s32[2,64,1024]{2,1,0:T(8,128)} %phase.1, s32[2,64,1024]{2,1,0:T(8,128)} %contact.1), custom_call_target="tpu_custom_call" | custom-call | tf_op jit(solution)/shard_map/pallas_call | solution.py:144
  52.0 3.8 %collective-permute-start.38 = (f32[2,64,1024]{2,1,0:T(8,128)}, f32[2,64,1024]{2,1,0:T(8,128)S(1)}, u32[]{:S(2)}, u32[]{:S(2)}) collective-permute-start(f32[2,64,1024]{2,1,0:T(8,128)} %shard_map.85), channel_id=1, source_target_pairs={{0,16},{8,24},{16,32},{24,40},{32,48},{40,56},{48,64},{56,72},{64,... | collective-permute-start | bytes 1572872 | tf_op jit(solution)/shard_map/ppermute | solution.py:30
  55.9 1.9 collective-permute-start.39
  57.8 10.7 %shard_map.78 = (f32[4,2,16,1024]{3,2,1,0:T(8,128)}, f32[4,2,16,1024]{3,2,1,0:T(8,128)}, f32[2,2,16,1024]{3,2,1,0:T(8,128)}, f32[2,2,16,1024]{3,2,1,0:T(8,128)}, f32[4,2,16,1024]{3,2,1,0:T(8,128)}) custom-call(s32[3]{0:T(128)} %pad_add_fusion.pos, s32[8,64]{1,0:T(8,128)} %offsets.15, bf16[8,64,1024]{2,1,0:T(8,128)(2,1)} %proj.15, ...), custom_call_target="tpu_custom_call" | custom-call | flops 1073741824 | bytes 6291456 | tf_op jit(solution)/shard_map/pallas_call | solution.py:122
  69.1 5.4 %collective-permute-done.39 = f32[2,64,1024]{2,1,0:T(8,128)S(1)} collective-permute-done((f32[2,64,1024]{2,1,0:T(8,128)}, f32[2,64,1024]{2,1,0:T(8,128)S(1)}, u32[]{:S(2)}, u32[]{:S(2)}) %collective-permute-start.39) | collective-permute-done | bytes 524320 | tf_op jit(solution)/shard_map/ppermute | solution.py:30
  74.5 1.9 collective-permute-start.40
  76.5 0.9 collective-permute-start.3
  77.4 10.8 %shard_map.80 = (f32[4,2,16,1024]{3,2,1,0:T(8,128)}, f32[4,2,16,1024]{3,2,1,0:T(8,128)}, f32[2,2,16,1024]{3,2,1,0:T(8,128)}, f32[2,2,16,1024]{3,2,1,0:T(8,128)}, f32[4,2,16,1024]{3,2,1,0:T(8,128)}) custom-call(s32[3]{0:T(128)} %pad_add_fusion.pos, s32[8,64]{1,0:T(8,128)} %offsets.15, bf16[8,64,1024]{2,1,0:T(8,128)(2,1)} %proj.15, ...), custom_call_target="tpu_custom_call" | custom-call | flops 1073741824 | bytes 6291456 | tf_op jit(solution)/shard_map/pallas_call | solution.py:122
  88.1 2.4 collective-permute-start.41
  90.6 10.7 %shard_map.82 = (f32[4,2,16,1024]{3,2,1,0:T(8,128)}, f32[4,2,16,1024]{3,2,1,0:T(8,128)}, f32[2,2,16,1024]{3,2,1,0:T(8,128)}, f32[2,2,16,1024]{3,2,1,0:T(8,128)}, f32[4,2,16,1024]{3,2,1,0:T(8,128)}) custom-call(s32[3]{0:T(128)} %pad_add_fusion.pos, s32[8,64]{1,0:T(8,128)} %offsets.15, bf16[8,64,1024]{2,1,0:T(8,128)(2,1)} %proj.15, ...), custom_call_target="tpu_custom_call" | custom-call | flops 1073741824 | bytes 6291456 | tf_op jit(solution)/shard_map/pallas_call | solution.py:122
  101.3 1.3 collective-permute-start.9
  102.7 10.7 %shard_map.84 = (f32[4,2,16,1024]{3,2,1,0:T(8,128)}, f32[4,2,16,1024]{3,2,1,0:T(8,128)}, f32[2,2,16,1024]{3,2,1,0:T(8,128)}, f32[2,2,16,1024]{3,2,1,0:T(8,128)}, f32[4,2,16,1024]{3,2,1,0:T(8,128)}) custom-call(s32[3]{0:T(128)} %pad_add_fusion.pos, s32[8,64]{1,0:T(8,128)} %offsets.15, bf16[8,64,1024]{2,1,0:T(8,128)(2,1)} %proj.15, ...), custom_call_target="tpu_custom_call" | custom-call | flops 1073741824 | bytes 6291456 | tf_op jit(solution)/shard_map/pallas_call | solution.py:122
  113.3 0.8 collective-permute-start.11
  114.2 1.0 slice_add_fusion.15
  115.2 2.6 collective-permute-start.19
  117.9 1.0 collective-permute-start.17
  118.8 1.0 slice_add_fusion.11
  119.8 9.8 %collective-permute-done.11 = f32[4,2,16,1024]{3,2,1,0:T(8,128)S(1)} collective-permute-done((f32[4,2,16,1024]{3,2,1,0:T(8,128)}, f32[4,2,16,1024]{3,2,1,0:T(8,128)S(1)}, u32[]{:S(2)}, u32[]{:S(2)}) %collective-permute-start.11) | collective-permute-done | bytes 524320 | tf_op jit(solution)/shard_map/ppermute | solution.py:24
  129.6 1.0 slice_add_fusion.9
  130.6 10.2 %collective-permute-done.19 = f32[4,2,16,1024]{3,2,1,0:T(8,128)S(1)} collective-permute-done((f32[4,2,16,1024]{3,2,1,0:T(8,128)}, f32[4,2,16,1024]{3,2,1,0:T(8,128)S(1)}, u32[]{:S(2)}, u32[]{:S(2)}) %collective-permute-start.19) | collective-permute-done | bytes 524320 | tf_op jit(solution)/shard_map/ppermute | solution.py:24
  140.9 1.5 collective-permute-start.25
  142.4 1.3 collective-permute-start.2
  143.7 7.4 %collective-permute-done.27 = f32[4,2,16,1024]{3,2,1,0:T(8,128)S(1)} collective-permute-done((f32[4,2,16,1024]{3,2,1,0:T(8,128)}, f32[4,2,16,1024]{3,2,1,0:T(8,128)S(1)}, u32[]{:S(2)}, u32[]{:S(2)}) %collective-permute-start.27) | collective-permute-done | bytes 524320 | tf_op jit(solution)/shard_map/ppermute | solution.py:24
  151.1 4.6 %collective-permute-done.25 = f32[4,2,16,1024]{3,2,1,0:T(8,128)S(1)} collective-permute-done((f32[4,2,16,1024]{3,2,1,0:T(8,128)S(1)}, f32[4,2,16,1024]{3,2,1,0:T(8,128)S(1)}, u32[]{:S(2)}, u32[]{:S(2)}) %collective-permute-start.25) | collective-permute-done | bytes 524320 | tf_op jit(solution)/shard_map/ppermute | solution.py:24
  155.7 2.4 collective-permute-start.10
  158.2 3.0 %collective-permute-done.2 = f32[2,2,16,1024]{3,2,1,0:T(8,128)S(1)} collective-permute-done((f32[2,2,16,1024]{3,2,1,0:T(8,128)S(1)}, f32[2,2,16,1024]{3,2,1,0:T(8,128)S(1)}, u32[]{:S(2)}, u32[]{:S(2)}) %collective-permute-start.2) | collective-permute-done | bytes 262176 | tf_op jit(solution)/shard_map/ppermute | solution.py:24
  161.4 1.9 collective-permute-start.21
  163.4 0.8 collective-permute-done.10
  164.2 1.8 collective-permute-start.18
  166.1 5.2 %collective-permute-done.13 = f32[2,2,16,1024]{3,2,1,0:T(8,128)S(1)} collective-permute-done((f32[2,2,16,1024]{3,2,1,0:T(8,128)S(1)}, f32[2,2,16,1024]{3,2,1,0:T(8,128)S(1)}, u32[]{:S(2)}, u32[]{:S(2)}) %collective-permute-start.13) | collective-permute-done | bytes 262176 | tf_op jit(solution)/shard_map/ppermute | solution.py:24
  171.4 3.0 %collective-permute-done.21 = f32[2,2,16,1024]{3,2,1,0:T(8,128)S(1)} collective-permute-done((f32[2,2,16,1024]{3,2,1,0:T(8,128)S(1)}, f32[2,2,16,1024]{3,2,1,0:T(8,128)S(1)}, u32[]{:S(2)}, u32[]{:S(2)}) %collective-permute-start.21) | collective-permute-done | bytes 262176 | tf_op jit(solution)/shard_map/ppermute | solution.py:24
  174.7 3.6 %collective-permute-start.6 = (f32[2,16,1024]{2,1,0:T(8,128)S(1)}, f32[2,16,1024]{2,1,0:T(8,128)S(1)}, u32[]{:S(2)}, u32[]{:S(2)}) collective-permute-start(f32[2,16,1024]{2,1,0:T(8,128)S(1)} %get-tuple-element.54), channel_id=1, source_target_pairs={{0,128},{8,136},{16,144},{24,152},{32,160},{40,168},{48,176},{56,1... | collective-permute-start | bytes 393224 | tf_op jit(solution)/shard_map/ppermute | solution.py:24
  178.9 5.0 %collective-permute-start.7 = (f32[2,16,1024]{2,1,0:T(8,128)S(1)}, f32[2,16,1024]{2,1,0:T(8,128)S(1)}, u32[]{:S(2)}, u32[]{:S(2)}) collective-permute-start(f32[2,16,1024]{2,1,0:T(8,128)S(1)} %get-tuple-element.55), channel_id=1, source_target_pairs={{0,192},{8,200},{16,208},{24,216},{32,224},{40,232},{48,240},{56,2... | collective-permute-start | bytes 393224 | tf_op jit(solution)/shard_map/ppermute | solution.py:24
  184.0 2.4 collective-permute-done.6
  187.1 5.8 %collective-permute-start.15 = (f32[2,16,1024]{2,1,0:T(8,128)S(1)}, f32[2,16,1024]{2,1,0:T(8,128)S(1)}, u32[]{:S(2)}, u32[]{:S(2)}) collective-permute-start(f32[2,16,1024]{2,1,0:T(8,128)S(1)} %get-tuple-element.57), channel_id=1, source_target_pairs={{0,192},{8,200},{16,208},{24,216},{32,224},{40,232},{48,240},{56,2... | collective-permute-start | bytes 393224 | tf_op jit(solution)/shard_map/ppermute | solution.py:24
  192.9 5.2 %collective-permute-start.12 = (f32[2,16,1024]{2,1,0:T(8,128)S(1)}, f32[2,16,1024]{2,1,0:T(8,128)S(1)}, u32[]{:S(2)}, u32[]{:S(2)}) collective-permute-start(f32[2,16,1024]{2,1,0:T(8,128)S(1)} %slice_bitcast_fusion.10), channel_id=1, source_target_pairs={{0,64},{8,72},{16,80},{24,88},{32,96},{40,104},{48,112},{56,120},{... | collective-permute-start | bytes 393224 | tf_op jit(solution)/shard_map/ppermute | solution.py:24
  198.1 2.0 collective-permute-start.22
  200.1 3.6 %collective-permute-start.23 = (f32[2,16,1024]{2,1,0:T(8,128)S(1)}, f32[2,16,1024]{2,1,0:T(8,128)S(1)}, u32[]{:S(2)}, u32[]{:S(2)}) collective-permute-start(f32[2,16,1024]{2,1,0:T(8,128)S(1)} %get-tuple-element.59), channel_id=1, source_target_pairs={{0,192},{8,200},{16,208},{24,216},{32,224},{40,232},{48,240},{56,2... | collective-permute-start | bytes 393224 | tf_op jit(solution)/shard_map/ppermute | solution.py:24
  203.7 6.4 %collective-permute-start.20 = (f32[2,16,1024]{2,1,0:T(8,128)S(1)}, f32[2,16,1024]{2,1,0:T(8,128)S(1)}, u32[]{:S(2)}, u32[]{:S(2)}) collective-permute-start(f32[2,16,1024]{2,1,0:T(8,128)S(1)} %slice_bitcast_fusion.6), channel_id=1, source_target_pairs={{0,64},{8,72},{16,80},{24,88},{32,96},{40,104},{48,112},{56,120},{... | collective-permute-start | bytes 393224 | tf_op jit(solution)/shard_map/ppermute | solution.py:24
  210.2 2.0 collective-permute-start.30
  212.2 1.0 collective-permute-done.23
  213.2 2.7 collective-permute-start.31
  215.8 0.7 collective-permute-start.28
  216.6 2.8 collective-permute-done.31
  219.4 3.2 %collective-permute-done.28 = f32[2,16,1024]{2,1,0:T(8,128)S(1)} collective-permute-done((f32[2,16,1024]{2,1,0:T(8,128)S(1)}, f32[2,16,1024]{2,1,0:T(8,128)S(1)}, u32[]{:S(2)}, u32[]{:S(2)}) %collective-permute-start.28) | collective-permute-done | bytes 131104 | tf_op jit(solution)/shard_map/ppermute | solution.py:24
  222.7 2.1 collective-permute-start.32
  224.9 1.9 collective-permute-start.33
  226.9 3.6 %collective-permute-start.34 = (f32[2,64,1024]{2,1,0:T(8,128)S(1)}, f32[2,64,1024]{2,1,0:T(8,128)S(1)}, u32[]{:S(2)}, u32[]{:S(2)}) collective-permute-start(f32[2,64,1024]{2,1,0:T(8,128)S(1)} %pad_maximum_fusion), channel_id=1, source_target_pairs={{8,0},{16,8},{24,16},{32,24},{40,32},{48,40},{56,48},{64,56},{72,6... | collective-permute-start | bytes 1572872 | tf_op jit(solution)/shard_map/ppermute | solution.py:30
  230.6 3.7 %collective-permute-start.35 = (f32[2,64,1024]{2,1,0:T(8,128)S(1)}, f32[2,64,1024]{2,1,0:T(8,128)S(1)}, u32[]{:S(2)}, u32[]{:S(2)}) collective-permute-start(f32[2,64,1024]{2,1,0:T(8,128)S(1)} %pad_maximum_fusion), channel_id=1, source_target_pairs={{16,0},{24,8},{32,16},{40,24},{48,32},{56,40},{64,48},{72,56},{80,... | collective-permute-start | bytes 1572872 | tf_op jit(solution)/shard_map/ppermute | solution.py:30
  234.4 6.8 %collective-permute-start.42 = (f32[10,4,1024]{2,1,0:T(4,128)S(1)}, f32[10,4,1024]{2,1,0:T(4,128)S(1)}, u32[]{:S(2)}, u32[]{:S(2)}) collective-permute-start(f32[10,4,1024]{2,1,0:T(4,128)S(1)} %get-tuple-element.43), channel_id=1, source_target_pairs={{0,1},{1,2},{2,3},{3,4},{4,5},{5,6},{6,7},{8,9},{9,10},{10,11},{11... | collective-permute-start | bytes 491528 | tf_op jit(solution)/shard_map/ppermute | solution.py:30
  241.2 1.9 collective-permute-start.43
  243.3 13.7 %collective-permute-done.35 = f32[2,64,1024]{2,1,0:T(8,128)S(1)} collective-permute-done((f32[2,64,1024]{2,1,0:T(8,128)S(1)}, f32[2,64,1024]{2,1,0:T(8,128)S(1)}, u32[]{:S(2)}, u32[]{:S(2)}) %collective-permute-start.35) | collective-permute-done | bytes 524320 | tf_op jit(solution)/shard_map/ppermute | solution.py:30
  257.2 4.1 %collective-permute-start.36 = (f32[10,4,1024]{2,1,0:T(4,128)S(1)}, f32[10,4,1024]{2,1,0:T(4,128)S(1)}, u32[]{:S(2)}, u32[]{:S(2)}) collective-permute-start(f32[10,4,1024]{2,1,0:T(4,128)S(1)} %get-tuple-element.45), channel_id=1, source_target_pairs={{0,1},{1,2},{2,3},{3,4},{4,5},{5,6},{6,7},{8,9},{9,10},{10,11},{11... | collective-permute-start | bytes 491528 | tf_op jit(solution)/shard_map/ppermute | solution.py:30
  261.3 1.9 collective-permute-start.37
  263.3 1.1 collective-permute-done.36.heat_low
  264.4 10.2 %collective-permute-done.37.heat_high = f32[10,4,1024]{2,1,0:T(4,128)S(1)} collective-permute-done((f32[10,4,1024]{2,1,0:T(4,128)S(1)}, f32[10,4,1024]{2,1,0:T(4,128)S(1)}, u32[]{:S(2)}, u32[]{:S(2)}) %collective-permute-start.37) | collective-permute-done | bytes 163872 | tf_op jit(solution)/shard_map/ppermute | solution.py:30
  274.6 0.7 copy-done.17
  275.2 14.6 %shard_map.86 = f32[2,64,1024]{2,1,0:T(8,128)} custom-call(f32[10,64,1024]{2,1,0:T(8,128)} %copy-done.1, f32[10,4,1024]{2,1,0:T(4,128)} %copy-done.16, f32[10,4,1024]{2,1,0:T(4,128)} %copy-done.17, f32[10,64,1024]{2,1,0:T(8,128)} %copy-done, f32[10,4,1024]{2,1,0:T(4,128)} %copy-done.14, f32[10,4,1024]{2,1,0:T(4,128)} %copy-done.15), custom_call_target="tpu_custom_call" | custom-call | flops 209715200 | bytes 6291456 | tf_op jit(solution)/shard_map/pallas_call | solution.py:241
  (111 shorter events, 4.5 us)
Async XLA Ops:
  15.3 40.6 %collective-permute-start = (f32[4,4,2,16,1024]{4,3,2,1,0:T(8,128)}, f32[4,4,2,16,1024]{4,3,2,1,0:T(8,128)}, u32[]{:S(2)}, u32[]{:S(2)}) collective-permute-start(f32[4,4,2,16,1024]{4,3,2,1,0:T(8,128)} %shard_map.77), channel_id=1, source_target_pairs={{0,8},{8,0},{16,24},{24,16},{32,40},{40,32},{48,56},{56,48},{64,72... | collective-permute-start | bytes 6291464 | tf_op jit(solution)/shard_map/ppermute | solution.py:24
  25.5 51.0 %collective-permute-start.8 = (f32[4,4,2,16,1024]{4,3,2,1,0:T(8,128)}, f32[4,4,2,16,1024]{4,3,2,1,0:T(8,128)}, u32[]{:S(2)}, u32[]{:S(2)}) collective-permute-start(f32[4,4,2,16,1024]{4,3,2,1,0:T(8,128)} %shard_map.79), channel_id=1, source_target_pairs={{0,8},{8,0},{16,24},{24,16},{32,40},{40,32},{48,56},{56,48},{64,72... | collective-permute-start | bytes 6291464 | tf_op jit(solution)/shard_map/ppermute | solution.py:24
  36.1 52.0 %collective-permute-start.16 = (f32[4,4,2,16,1024]{4,3,2,1,0:T(8,128)}, f32[4,4,2,16,1024]{4,3,2,1,0:T(8,128)}, u32[]{:S(2)}, u32[]{:S(2)}) collective-permute-start(f32[4,4,2,16,1024]{4,3,2,1,0:T(8,128)} %shard_map.81), channel_id=1, source_target_pairs={{0,8},{8,0},{16,24},{24,16},{32,40},{40,32},{48,56},{56,48},{64,72... | collective-permute-start | bytes 6291464 | tf_op jit(solution)/shard_map/ppermute | solution.py:24
  46.3 55.0 %collective-permute-start.24 = (f32[4,4,2,16,1024]{4,3,2,1,0:T(8,128)}, f32[4,4,2,16,1024]{4,3,2,1,0:T(8,128)S(1)}, u32[]{:S(2)}, u32[]{:S(2)}) collective-permute-start(f32[4,4,2,16,1024]{4,3,2,1,0:T(8,128)} %shard_map.83), channel_id=1, source_target_pairs={{0,8},{8,0},{16,24},{24,16},{32,40},{40,32},{48,56},{56,48},{64,72... | collective-permute-start | bytes 6291464 | tf_op jit(solution)/shard_map/ppermute | solution.py:24
  52.0 22.5 %copy-start.3 = (f32[2,64,1024]{2,1,0:T(8,128)S(1)}, f32[2,64,1024]{2,1,0:T(8,128)}, u32[]{:S(2)}) copy-start(f32[2,64,1024]{2,1,0:T(8,128)} %shard_map.85) | copy-start | bytes 1572868
  52.0 17.0 %collective-permute-start.38 = (f32[2,64,1024]{2,1,0:T(8,128)}, f32[2,64,1024]{2,1,0:T(8,128)S(1)}, u32[]{:S(2)}, u32[]{:S(2)}) collective-permute-start(f32[2,64,1024]{2,1,0:T(8,128)} %shard_map.85), channel_id=1, source_target_pairs={{0,16},{8,24},{16,32},{24,40},{32,48},{40,56},{48,64},{56,72},{64,... | collective-permute-start | bytes 1572872 | tf_op jit(solution)/shard_map/ppermute | solution.py:30
  55.9 18.6 %collective-permute-start.39 = (f32[2,64,1024]{2,1,0:T(8,128)}, f32[2,64,1024]{2,1,0:T(8,128)S(1)}, u32[]{:S(2)}, u32[]{:S(2)}) collective-permute-start(f32[2,64,1024]{2,1,0:T(8,128)} %shard_map.85), channel_id=1, source_target_pairs={{0,8},{8,16},{16,24},{24,32},{32,40},{40,48},{48,56},{56,64},{64,7... | collective-permute-start | bytes 1572872 | tf_op jit(solution)/shard_map/ppermute | solution.py:30
  69.0 44.3 %collective-permute-start.1 = (f32[4,2,16,1024]{3,2,1,0:T(8,128)}, f32[4,2,16,1024]{3,2,1,0:T(8,128)S(1)}, u32[]{:S(2)}, u32[]{:S(2)}) collective-permute-start(f32[4,2,16,1024]{3,2,1,0:T(8,128)} %get-tuple-element.24), channel_id=1, source_target_pairs={{0,16},{8,24},{16,32},{24,40},{32,48},{40,56},{48,0},{56,8},{64,80... | collective-permute-start | bytes 1572872 | tf_op jit(solution)/shard_map/ppermute | solution.py:24
  74.5 152.3 %collective-permute-start.40 = (f32[2,64,1024]{2,1,0:T(8,128)S(1)}, f32[2,64,1024]{2,1,0:T(8,128)S(1)}, u32[]{:S(2)}, u32[]{:S(2)}) collective-permute-start(f32[2,64,1024]{2,1,0:T(8,128)S(1)} %copy-done.3), channel_id=1, source_target_pairs={{8,0},{16,8},{24,16},{32,24},{40,32},{48,40},{56,48},{64,56},{72,6... | collective-permute-start | bytes 1572872 | tf_op jit(solution)/shard_map/ppermute | solution.py:30
  76.5 38.7 %collective-permute-start.3 = (f32[4,2,16,1024]{3,2,1,0:T(8,128)}, f32[4,2,16,1024]{3,2,1,0:T(8,128)S(1)}, u32[]{:S(2)}, u32[]{:S(2)}) collective-permute-start(f32[4,2,16,1024]{3,2,1,0:T(8,128)} %get-tuple-element.25), channel_id=1, source_target_pairs={{0,48},{8,56},{16,0},{24,8},{32,16},{40,24},{48,32},{56,40},{64,11... | collective-permute-start | bytes 1572872 | tf_op jit(solution)/shard_map/ppermute | solution.py:24
  88.1 138.7 %collective-permute-start.41 = (f32[2,64,1024]{2,1,0:T(8,128)S(1)}, f32[2,64,1024]{2,1,0:T(8,128)S(1)}, u32[]{:S(2)}, u32[]{:S(2)}) collective-permute-start(f32[2,64,1024]{2,1,0:T(8,128)S(1)} %copy-done.3), channel_id=1, source_target_pairs={{16,0},{24,8},{32,16},{40,24},{48,32},{56,40},{64,48},{72,56},{80,... | collective-permute-start | bytes 1572872 | tf_op jit(solution)/shard_map/ppermute | solution.py:30
  101.3 1.4 copy-start.2
  101.3 16.5 %copy-start.9 = (f32[2,2,16,1024]{3,2,1,0:T(8,128)S(1)}, f32[2,2,16,1024]{3,2,1,0:T(8,128)}, u32[]{:S(2)}) copy-start(f32[2,2,16,1024]{3,2,1,0:T(8,128)} %get-tuple-element.26) | copy-start | bytes 786436
  101.3 16.6 %collective-permute-start.9 = (f32[4,2,16,1024]{3,2,1,0:T(8,128)}, f32[4,2,16,1024]{3,2,1,0:T(8,128)S(1)}, u32[]{:S(2)}, u32[]{:S(2)}) collective-permute-start(f32[4,2,16,1024]{3,2,1,0:T(8,128)} %get-tuple-element.29), channel_id=1, source_target_pairs={{0,16},{8,24},{16,32},{24,40},{32,48},{40,56},{48,0},{56,8},{64,80... | collective-permute-start | bytes 1572872 | tf_op jit(solution)/shard_map/ppermute | solution.py:24
  113.3 27.6 %copy-start.18 = (f32[4,2,16,1024]{3,2,1,0:T(8,128)S(1)}, f32[4,2,16,1024]{3,2,1,0:T(8,128)}, u32[]{:S(2)}) copy-start(f32[4,2,16,1024]{3,2,1,0:T(8,128)} %get-tuple-element.39) | copy-start | bytes 1572868
  113.3 29.0 %copy-start.13 = (f32[2,2,16,1024]{3,2,1,0:T(8,128)S(1)}, f32[2,2,16,1024]{3,2,1,0:T(8,128)}, u32[]{:S(2)}) copy-start(f32[2,2,16,1024]{3,2,1,0:T(8,128)} %get-tuple-element.36) | copy-start | bytes 786436
  113.3 30.4 %copy-start.11 = (f32[2,2,16,1024]{3,2,1,0:T(8,128)S(1)}, f32[2,2,16,1024]{3,2,1,0:T(8,128)}, u32[]{:S(2)}) copy-start(f32[2,2,16,1024]{3,2,1,0:T(8,128)} %get-tuple-element.33) | copy-start | bytes 786436
  113.3 37.8 %copy-start.12 = (f32[2,2,16,1024]{3,2,1,0:T(8,128)S(1)}, f32[2,2,16,1024]{3,2,1,0:T(8,128)}, u32[]{:S(2)}) copy-start(f32[2,2,16,1024]{3,2,1,0:T(8,128)} %get-tuple-element.41) | copy-start | bytes 786436
  113.3 16.3 %collective-permute-start.11 = (f32[4,2,16,1024]{3,2,1,0:T(8,128)}, f32[4,2,16,1024]{3,2,1,0:T(8,128)S(1)}, u32[]{:S(2)}, u32[]{:S(2)}) collective-permute-start(f32[4,2,16,1024]{3,2,1,0:T(8,128)} %get-tuple-element.30), channel_id=1, source_target_pairs={{0,48},{8,56},{16,0},{24,8},{32,16},{40,24},{48,32},{56,40},{64,11... | collective-permute-start | bytes 1572872 | tf_op jit(solution)/shard_map/ppermute | solution.py:24
  114.2 43.9 %copy-start.10 = (f32[2,2,16,1024]{3,2,1,0:T(8,128)S(1)}, f32[2,2,16,1024]{3,2,1,0:T(8,128)}, u32[]{:S(2)}) copy-start(f32[2,2,16,1024]{3,2,1,0:T(8,128)} %get-tuple-element.38) | copy-start | bytes 786436
  115.2 25.7 %collective-permute-start.19 = (f32[4,2,16,1024]{3,2,1,0:T(8,128)}, f32[4,2,16,1024]{3,2,1,0:T(8,128)S(1)}, u32[]{:S(2)}, u32[]{:S(2)}) collective-permute-start(f32[4,2,16,1024]{3,2,1,0:T(8,128)} %get-tuple-element.35), channel_id=1, source_target_pairs={{0,48},{8,56},{16,0},{24,8},{32,16},{40,24},{48,32},{56,40},{64,11... | collective-permute-start | bytes 1572872 | tf_op jit(solution)/shard_map/ppermute | solution.py:24
  117.8 45.5 %copy-start.7 = (f32[4,2,16,1024]{3,2,1,0:T(8,128)S(1)}, f32[4,2,16,1024]{3,2,1,0:T(8,128)}, u32[]{:S(2)}) copy-start(f32[4,2,16,1024]{3,2,1,0:T(8,128)} %get-tuple-element.22) | copy-start | bytes 1572868
  117.9 24.5 %collective-permute-start.17 = (f32[4,2,16,1024]{3,2,1,0:T(8,128)}, f32[4,2,16,1024]{3,2,1,0:T(8,128)S(1)}, u32[]{:S(2)}, u32[]{:S(2)}) collective-permute-start(f32[4,2,16,1024]{3,2,1,0:T(8,128)} %get-tuple-element.34), channel_id=1, source_target_pairs={{0,16},{8,24},{16,32},{24,40},{32,48},{40,56},{48,0},{56,8},{64,80... | collective-permute-start | bytes 1572872 | tf_op jit(solution)/shard_map/ppermute | solution.py:24
  129.6 21.4 %collective-permute-start.27 = (f32[4,2,16,1024]{3,2,1,0:T(8,128)}, f32[4,2,16,1024]{3,2,1,0:T(8,128)S(1)}, u32[]{:S(2)}, u32[]{:S(2)}) collective-permute-start(f32[4,2,16,1024]{3,2,1,0:T(8,128)} %get-tuple-element.40), channel_id=1, source_target_pairs={{0,48},{8,56},{16,0},{24,8},{32,16},{40,24},{48,32},{56,40},{64,11... | collective-permute-start | bytes 1572872 | tf_op jit(solution)/shard_map/ppermute | solution.py:24
  140.9 14.9 %collective-permute-start.25 = (f32[4,2,16,1024]{3,2,1,0:T(8,128)S(1)}, f32[4,2,16,1024]{3,2,1,0:T(8,128)S(1)}, u32[]{:S(2)}, u32[]{:S(2)}) collective-permute-start(f32[4,2,16,1024]{3,2,1,0:T(8,128)S(1)} %copy-done.18), channel_id=1, source_target_pairs={{0,16},{8,24},{16,32},{24,40},{32,48},{40,56},{48,0},{56,8},{64,80... | collective-permute-start | bytes 1572872 | tf_op jit(solution)/shard_map/ppermute | solution.py:24
  142.4 18.8 %collective-permute-start.2 = (f32[2,2,16,1024]{3,2,1,0:T(8,128)S(1)}, f32[2,2,16,1024]{3,2,1,0:T(8,128)S(1)}, u32[]{:S(2)}, u32[]{:S(2)}) collective-permute-start(f32[2,2,16,1024]{3,2,1,0:T(8,128)S(1)} %slice_add_fusion.15), channel_id=1, source_target_pairs={{0,16},{8,24},{16,32},{24,40},{32,48},{40,56},{48,0},{56,8},{64,80... | collective-permute-start | bytes 786440 | tf_op jit(solution)/shard_map/ppermute | solution.py:24
  143.7 27.6 %copy-start.8 = (f32[4,2,16,1024]{3,2,1,0:T(8,128)S(1)}, f32[4,2,16,1024]{3,2,1,0:T(8,128)}, u32[]{:S(2)}) copy-start(f32[4,2,16,1024]{3,2,1,0:T(8,128)} %get-tuple-element.27) | copy-start | bytes 1572868
  151.1 10.3 %collective-permute-start.5 = (f32[2,2,16,1024]{3,2,1,0:T(8,128)S(1)}, f32[2,2,16,1024]{3,2,1,0:T(8,128)S(1)}, u32[]{:S(2)}, u32[]{:S(2)}) collective-permute-start(f32[2,2,16,1024]{3,2,1,0:T(8,128)S(1)} %slice_add_fusion.13), channel_id=1, source_target_pairs={{0,48},{8,56},{16,0},{24,8},{32,16},{40,24},{48,32},{56,40},{64,11... | collective-permute-start | bytes 786440 | tf_op jit(solution)/shard_map/ppermute | solution.py:24
  155.7 8.5 %collective-permute-start.10 = (f32[2,2,16,1024]{3,2,1,0:T(8,128)S(1)}, f32[2,2,16,1024]{3,2,1,0:T(8,128)S(1)}, u32[]{:S(2)}, u32[]{:S(2)}) collective-permute-start(f32[2,2,16,1024]{3,2,1,0:T(8,128)S(1)} %slice_add_fusion.11), channel_id=1, source_target_pairs={{0,16},{8,24},{16,32},{24,40},{32,48},{40,56},{48,0},{56,8},{64,80... | collective-permute-start | bytes 786440 | tf_op jit(solution)/shard_map/ppermute | solution.py:24
  161.2 10.1 %collective-permute-start.13 = (f32[2,2,16,1024]{3,2,1,0:T(8,128)S(1)}, f32[2,2,16,1024]{3,2,1,0:T(8,128)S(1)}, u32[]{:S(2)}, u32[]{:S(2)}) collective-permute-start(f32[2,2,16,1024]{3,2,1,0:T(8,128)S(1)} %slice_add_fusion.9), channel_id=1, source_target_pairs={{0,48},{8,56},{16,0},{24,8},{32,16},{40,24},{48,32},{56,40},{64,11... | collective-permute-start | bytes 786440 | tf_op jit(solution)/shard_map/ppermute | solution.py:24
  161.4 13.0 %collective-permute-start.21 = (f32[2,2,16,1024]{3,2,1,0:T(8,128)S(1)}, f32[2,2,16,1024]{3,2,1,0:T(8,128)S(1)}, u32[]{:S(2)}, u32[]{:S(2)}) collective-permute-start(f32[2,2,16,1024]{3,2,1,0:T(8,128)S(1)} %slice_add_fusion.5), channel_id=1, source_target_pairs={{0,48},{8,56},{16,0},{24,8},{32,16},{40,24},{48,32},{56,40},{64,11... | collective-permute-start | bytes 786440 | tf_op jit(solution)/shard_map/ppermute | solution.py:24
  163.3 15.1 %copy-start.6 = (f32[4,2,16,1024]{3,2,1,0:T(8,128)S(1)}, f32[4,2,16,1024]{3,2,1,0:T(8,128)}, u32[]{:S(2)}) copy-start(f32[4,2,16,1024]{3,2,1,0:T(8,128)} %get-tuple-element.32) | copy-start | bytes 1572868
  164.2 10.5 %collective-permute-start.18 = (f32[2,2,16,1024]{3,2,1,0:T(8,128)S(1)}, f32[2,2,16,1024]{3,2,1,0:T(8,128)S(1)}, u32[]{:S(2)}, u32[]{:S(2)}) collective-permute-start(f32[2,2,16,1024]{3,2,1,0:T(8,128)S(1)} %slice_add_fusion.7), channel_id=1, source_target_pairs={{0,16},{8,24},{16,32},{24,40},{32,48},{40,56},{48,0},{56,8},{64,80... | collective-permute-start | bytes 786440 | tf_op jit(solution)/shard_map/ppermute | solution.py:24
  171.3 7.6 %collective-permute-start.29 = (f32[2,2,16,1024]{3,2,1,0:T(8,128)S(1)}, f32[2,2,16,1024]{3,2,1,0:T(8,128)S(1)}, u32[]{:S(2)}, u32[]{:S(2)}) collective-permute-start(f32[2,2,16,1024]{3,2,1,0:T(8,128)S(1)} %slice_add_fusion.1), channel_id=1, source_target_pairs={{0,48},{8,56},{16,0},{24,8},{32,16},{40,24},{48,32},{56,40},{64,11... | collective-permute-start | bytes 786440 | tf_op jit(solution)/shard_map/ppermute | solution.py:24
  171.3 12.6 %copy-start.5 = (f32[4,2,16,1024]{3,2,1,0:T(8,128)S(1)}, f32[4,2,16,1024]{3,2,1,0:T(8,128)}, u32[]{:S(2)}) copy-start(f32[4,2,16,1024]{3,2,1,0:T(8,128)} %get-tuple-element.37) | copy-start | bytes 1572868
  174.4 9.4 %collective-permute-start.26 = (f32[2,2,16,1024]{3,2,1,0:T(8,128)S(1)}, f32[2,2,16,1024]{3,2,1,0:T(8,128)S(1)}, u32[]{:S(2)}, u32[]{:S(2)}) collective-permute-start(f32[2,2,16,1024]{3,2,1,0:T(8,128)S(1)} %slice_add_fusion.3), channel_id=1, source_target_pairs={{0,16},{8,24},{16,32},{24,40},{32,48},{40,56},{48,0},{56,8},{64,80... | collective-permute-start | bytes 786440 | tf_op jit(solution)/shard_map/ppermute | solution.py:24
  174.7 11.7 %collective-permute-start.6 = (f32[2,16,1024]{2,1,0:T(8,128)S(1)}, f32[2,16,1024]{2,1,0:T(8,128)S(1)}, u32[]{:S(2)}, u32[]{:S(2)}) collective-permute-start(f32[2,16,1024]{2,1,0:T(8,128)S(1)} %get-tuple-element.54), channel_id=1, source_target_pairs={{0,128},{8,136},{16,144},{24,152},{32,160},{40,168},{48,176},{56,1... | collective-permute-start | bytes 393224 | tf_op jit(solution)/shard_map/ppermute | solution.py:24
  178.9 8.2 %collective-permute-start.7 = (f32[2,16,1024]{2,1,0:T(8,128)S(1)}, f32[2,16,1024]{2,1,0:T(8,128)S(1)}, u32[]{:S(2)}, u32[]{:S(2)}) collective-permute-start(f32[2,16,1024]{2,1,0:T(8,128)S(1)} %get-tuple-element.55), channel_id=1, source_target_pairs={{0,192},{8,200},{16,208},{24,216},{32,224},{40,232},{48,240},{56,2... | collective-permute-start | bytes 393224 | tf_op jit(solution)/shard_map/ppermute | solution.py:24
  183.9 9.0 %collective-permute-start.4 = (f32[2,16,1024]{2,1,0:T(8,128)S(1)}, f32[2,16,1024]{2,1,0:T(8,128)S(1)}, u32[]{:S(2)}, u32[]{:S(2)}) collective-permute-start(f32[2,16,1024]{2,1,0:T(8,128)S(1)} %slice_bitcast_fusion.14), channel_id=1, source_target_pairs={{0,64},{8,72},{16,80},{24,88},{32,96},{40,104},{48,112},{56,120},{... | collective-permute-start | bytes 393224 | tf_op jit(solution)/shard_map/ppermute | solution.py:24
  186.5 11.7 %collective-permute-start.14 = (f32[2,16,1024]{2,1,0:T(8,128)S(1)}, f32[2,16,1024]{2,1,0:T(8,128)S(1)}, u32[]{:S(2)}, u32[]{:S(2)}) collective-permute-start(f32[2,16,1024]{2,1,0:T(8,128)S(1)} %get-tuple-element.56), channel_id=1, source_target_pairs={{0,128},{8,136},{16,144},{24,152},{32,160},{40,168},{48,176},{56,1... | collective-permute-start | bytes 393224 | tf_op jit(solution)/shard_map/ppermute | solution.py:24
  187.1 13.0 %collective-permute-start.15 = (f32[2,16,1024]{2,1,0:T(8,128)S(1)}, f32[2,16,1024]{2,1,0:T(8,128)S(1)}, u32[]{:S(2)}, u32[]{:S(2)}) collective-permute-start(f32[2,16,1024]{2,1,0:T(8,128)S(1)} %get-tuple-element.57), channel_id=1, source_target_pairs={{0,192},{8,200},{16,208},{24,216},{32,224},{40,232},{48,240},{56,2... | collective-permute-start | bytes 393224 | tf_op jit(solution)/shard_map/ppermute | solution.py:24
  192.9 10.8 %collective-permute-start.12 = (f32[2,16,1024]{2,1,0:T(8,128)S(1)}, f32[2,16,1024]{2,1,0:T(8,128)S(1)}, u32[]{:S(2)}, u32[]{:S(2)}) collective-permute-start(f32[2,16,1024]{2,1,0:T(8,128)S(1)} %slice_bitcast_fusion.10), channel_id=1, source_target_pairs={{0,64},{8,72},{16,80},{24,88},{32,96},{40,104},{48,112},{56,120},{... | collective-permute-start | bytes 393224 | tf_op jit(solution)/shard_map/ppermute | solution.py:24
  198.1 12.0 %collective-permute-start.22 = (f32[2,16,1024]{2,1,0:T(8,128)S(1)}, f32[2,16,1024]{2,1,0:T(8,128)S(1)}, u32[]{:S(2)}, u32[]{:S(2)}) collective-permute-start(f32[2,16,1024]{2,1,0:T(8,128)S(1)} %get-tuple-element.58), channel_id=1, source_target_pairs={{0,128},{8,136},{16,144},{24,152},{32,160},{40,168},{48,176},{56,1... | collective-permute-start | bytes 393224 | tf_op jit(solution)/shard_map/ppermute | solution.py:24
  200.1 13.0 %collective-permute-start.23 = (f32[2,16,1024]{2,1,0:T(8,128)S(1)}, f32[2,16,1024]{2,1,0:T(8,128)S(1)}, u32[]{:S(2)}, u32[]{:S(2)}) collective-permute-start(f32[2,16,1024]{2,1,0:T(8,128)S(1)} %get-tuple-element.59), channel_id=1, source_target_pairs={{0,192},{8,200},{16,208},{24,216},{32,224},{40,232},{48,240},{56,2... | collective-permute-start | bytes 393224 | tf_op jit(solution)/shard_map/ppermute | solution.py:24
  203.7 12.1 %collective-permute-start.20 = (f32[2,16,1024]{2,1,0:T(8,128)S(1)}, f32[2,16,1024]{2,1,0:T(8,128)S(1)}, u32[]{:S(2)}, u32[]{:S(2)}) collective-permute-start(f32[2,16,1024]{2,1,0:T(8,128)S(1)} %slice_bitcast_fusion.6), channel_id=1, source_target_pairs={{0,64},{8,72},{16,80},{24,88},{32,96},{40,104},{48,112},{56,120},{... | collective-permute-start | bytes 393224 | tf_op jit(solution)/shard_map/ppermute | solution.py:24
  210.2 6.4 %collective-permute-start.30 = (f32[2,16,1024]{2,1,0:T(8,128)S(1)}, f32[2,16,1024]{2,1,0:T(8,128)S(1)}, u32[]{:S(2)}, u32[]{:S(2)}) collective-permute-start(f32[2,16,1024]{2,1,0:T(8,128)S(1)} %get-tuple-element.60), channel_id=1, source_target_pairs={{0,128},{8,136},{16,144},{24,152},{32,160},{40,168},{48,176},{56,1... | collective-permute-start | bytes 393224 | tf_op jit(solution)/shard_map/ppermute | solution.py:24
  213.2 6.3 %collective-permute-start.31 = (f32[2,16,1024]{2,1,0:T(8,128)S(1)}, f32[2,16,1024]{2,1,0:T(8,128)S(1)}, u32[]{:S(2)}, u32[]{:S(2)}) collective-permute-start(f32[2,16,1024]{2,1,0:T(8,128)S(1)} %get-tuple-element.61), channel_id=1, source_target_pairs={{0,192},{8,200},{16,208},{24,216},{32,224},{40,232},{48,240},{56,2... | collective-permute-start | bytes 393224 | tf_op jit(solution)/shard_map/ppermute | solution.py:24
  215.8 6.8 %collective-permute-start.28 = (f32[2,16,1024]{2,1,0:T(8,128)S(1)}, f32[2,16,1024]{2,1,0:T(8,128)S(1)}, u32[]{:S(2)}, u32[]{:S(2)}) collective-permute-start(f32[2,16,1024]{2,1,0:T(8,128)S(1)} %slice_bitcast_fusion.2), channel_id=1, source_target_pairs={{0,64},{8,72},{16,80},{24,88},{32,96},{40,104},{48,112},{56,120},{... | collective-permute-start | bytes 393224 | tf_op jit(solution)/shard_map/ppermute | solution.py:24
  222.7 20.5 %copy-start.4 = (f32[2,64,1024]{2,1,0:T(8,128)}, f32[2,64,1024]{2,1,0:T(8,128)S(1)}, u32[]{:S(2)}) copy-start(f32[2,64,1024]{2,1,0:T(8,128)S(1)} %pad_maximum_fusion) | copy-start | bytes 1572868
  222.7 18.5 %collective-permute-start.32 = (f32[2,64,1024]{2,1,0:T(8,128)S(1)}, f32[2,64,1024]{2,1,0:T(8,128)S(1)}, u32[]{:S(2)}, u32[]{:S(2)}) collective-permute-start(f32[2,64,1024]{2,1,0:T(8,128)S(1)} %pad_maximum_fusion), channel_id=1, source_target_pairs={{0,16},{8,24},{16,32},{24,40},{32,48},{40,56},{48,64},{56,72},{64,... | collective-permute-start | bytes 1572872 | tf_op jit(solution)/shard_map/ppermute | solution.py:30
  224.9 18.3 %collective-permute-start.33 = (f32[2,64,1024]{2,1,0:T(8,128)S(1)}, f32[2,64,1024]{2,1,0:T(8,128)S(1)}, u32[]{:S(2)}, u32[]{:S(2)}) collective-permute-start(f32[2,64,1024]{2,1,0:T(8,128)S(1)} %pad_maximum_fusion), channel_id=1, source_target_pairs={{0,8},{8,16},{16,24},{24,32},{32,40},{40,48},{48,56},{56,64},{64,7... | collective-permute-start | bytes 1572872 | tf_op jit(solution)/shard_map/ppermute | solution.py:30
  226.9 30.2 %copy-start = (f32[10,64,1024]{2,1,0:T(8,128)}, f32[10,64,1024]{2,1,0:T(8,128)S(1)}, u32[]{:S(2)}) copy-start(f32[10,64,1024]{2,1,0:T(8,128)S(1)} %constant_dynamic-update-slice_fusion.5.cond) | copy-start | bytes 7864324
  226.9 16.3 %collective-permute-start.34 = (f32[2,64,1024]{2,1,0:T(8,128)S(1)}, f32[2,64,1024]{2,1,0:T(8,128)S(1)}, u32[]{:S(2)}, u32[]{:S(2)}) collective-permute-start(f32[2,64,1024]{2,1,0:T(8,128)S(1)} %pad_maximum_fusion), channel_id=1, source_target_pairs={{8,0},{16,8},{24,16},{32,24},{40,32},{48,40},{56,48},{64,56},{72,6... | collective-permute-start | bytes 1572872 | tf_op jit(solution)/shard_map/ppermute | solution.py:30
  230.6 26.4 %collective-permute-start.35 = (f32[2,64,1024]{2,1,0:T(8,128)S(1)}, f32[2,64,1024]{2,1,0:T(8,128)S(1)}, u32[]{:S(2)}, u32[]{:S(2)}) collective-permute-start(f32[2,64,1024]{2,1,0:T(8,128)S(1)} %pad_maximum_fusion), channel_id=1, source_target_pairs={{16,0},{24,8},{32,16},{40,24},{48,32},{56,40},{64,48},{72,56},{80,... | collective-permute-start | bytes 1572872 | tf_op jit(solution)/shard_map/ppermute | solution.py:30
  234.4 28.9 %collective-permute-start.42 = (f32[10,4,1024]{2,1,0:T(4,128)S(1)}, f32[10,4,1024]{2,1,0:T(4,128)S(1)}, u32[]{:S(2)}, u32[]{:S(2)}) collective-permute-start(f32[10,4,1024]{2,1,0:T(4,128)S(1)} %get-tuple-element.43), channel_id=1, source_target_pairs={{0,1},{1,2},{2,3},{3,4},{4,5},{5,6},{6,7},{8,9},{9,10},{10,11},{11... | collective-permute-start | bytes 491528 | tf_op jit(solution)/shard_map/ppermute | solution.py:30
  241.2 22.1 %collective-permute-start.43 = (f32[10,4,1024]{2,1,0:T(4,128)S(1)}, f32[10,4,1024]{2,1,0:T(4,128)S(1)}, u32[]{:S(2)}, u32[]{:S(2)}) collective-permute-start(f32[10,4,1024]{2,1,0:T(4,128)S(1)} %get-tuple-element.42), channel_id=1, source_target_pairs={{1,0},{2,1},{3,2},{4,3},{5,4},{6,5},{7,6},{9,8},{10,9},{11,10},{12... | collective-permute-start | bytes 491528 | tf_op jit(solution)/shard_map/ppermute | solution.py:30
  257.1 17.4 %copy-start.1 = (f32[10,64,1024]{2,1,0:T(8,128)}, f32[10,64,1024]{2,1,0:T(8,128)S(1)}, u32[]{:S(2)}) copy-start(f32[10,64,1024]{2,1,0:T(8,128)S(1)} %constant_dynamic-update-slice_fusion.heat) | copy-start | bytes 7864324
  257.2 7.2 %collective-permute-start.36 = (f32[10,4,1024]{2,1,0:T(4,128)S(1)}, f32[10,4,1024]{2,1,0:T(4,128)S(1)}, u32[]{:S(2)}, u32[]{:S(2)}) collective-permute-start(f32[10,4,1024]{2,1,0:T(4,128)S(1)} %get-tuple-element.45), channel_id=1, source_target_pairs={{0,1},{1,2},{2,3},{3,4},{4,5},{5,6},{6,7},{8,9},{9,10},{10,11},{11... | collective-permute-start | bytes 491528 | tf_op jit(solution)/shard_map/ppermute | solution.py:30
  261.3 13.2 %collective-permute-start.37 = (f32[10,4,1024]{2,1,0:T(4,128)S(1)}, f32[10,4,1024]{2,1,0:T(4,128)S(1)}, u32[]{:S(2)}, u32[]{:S(2)}) collective-permute-start(f32[10,4,1024]{2,1,0:T(4,128)S(1)} %get-tuple-element.44), channel_id=1, source_target_pairs={{1,0},{2,1},{3,2},{4,3},{5,4},{6,5},{7,6},{9,8},{10,9},{11,10},{12... | collective-permute-start | bytes 491528 | tf_op jit(solution)/shard_map/ppermute | solution.py:30
  263.2 11.3 %copy-start.14 = (f32[10,4,1024]{2,1,0:T(4,128)}, f32[10,4,1024]{2,1,0:T(4,128)S(1)}, u32[]{:S(2)}) copy-start(f32[10,4,1024]{2,1,0:T(4,128)S(1)} %collective-permute-done.42.cond_low) | copy-start | bytes 491524
  263.3 11.3 %copy-start.15 = (f32[10,4,1024]{2,1,0:T(4,128)}, f32[10,4,1024]{2,1,0:T(4,128)S(1)}, u32[]{:S(2)}) copy-start(f32[10,4,1024]{2,1,0:T(4,128)S(1)} %collective-permute-done.43.cond_high) | copy-start | bytes 491524
  264.4 10.2 %copy-start.16 = (f32[10,4,1024]{2,1,0:T(4,128)}, f32[10,4,1024]{2,1,0:T(4,128)S(1)}, u32[]{:S(2)}) copy-start(f32[10,4,1024]{2,1,0:T(4,128)S(1)} %collective-permute-done.36.heat_low) | copy-start | bytes 491524
  274.6 0.7 copy-start.17

commit v2 on v1

v2 whole, which is shorter than its diff:
```python
import functools
import jax
import jax.numpy as jnp
from jax import lax
from jax.experimental import pallas as pl
from jax.experimental.pallas import tpu as pltpu
from jax.sharding import PartitionSpec as P

STEPS = 4
STEP_SIZE = 0.15
CHUNKS = ((0, 16), (32, 32), (16, 16))
ZL, X, C = 4, 4, 2
VMEM_LIMIT = 26 * 1024 * 1024


def shift_ang(value, dz=0, dx=0, dc=0):
    perm = []
    for z in range(ZL):
        for x in range(X):
            for c in range(C):
                src = (z * X + x) * C + c
                dst = (((z + dz) % ZL) * X + (x + dx) % X) * C + (c ^ dc)
                perm.append((src, dst))
    return lax.ppermute(value, "ang", perm)


def shift_line(value, axis, step):
    count = lax.axis_size(axis)
    perm = [(i, i + step) for i in range(count) if 0 <= i + step < count]
    return lax.ppermute(value, axis, perm)


def gather_and_multiply(pos, offsets, proj, weights, wide, bands, flat, sems, core, store):
    angles, depth, columns = proj.shape
    copies = [
        pltpu.make_async_copy(weights.at[a], flat.at[:, a * 128:(a + 1) * 128], sems.at[a])
        for a in range(angles)
    ]
    for copy in copies:
        copy.start()
    wide[:, :, columns:] = jnp.zeros((angles, depth, 128), jnp.float32)
    for a in range(angles):
        wide[a, :, :columns] = proj[a].astype(jnp.float32)
    lane = lax.broadcasted_iota(jnp.int32, (depth, 128), 1)

    def row_body(row, carry):
        dx, dz, i = row >> 3, (row >> 1) & 3, row & 1
        owner = (
            ((pos[0] + dz) & (ZL - 1)) * (X * C * 2)
            + ((pos[1] + dx) & (X - 1)) * (C * 2)
            + core * 2
            + i
        )
        for a in range(angles):
            off = offsets[a, owner]
            base = pl.multiple_of((off >> 7) << 7, 128)
            rem = off & 127
            low = wide[a, :, pl.ds(base, 128)]
            high = wide[a, :, pl.ds(pl.multiple_of(base + 128, 128), 128)]
            band = pltpu.roll(jnp.where(lane < rem, high, low), (128 - rem) & 127, 1)
            bands[pl.ds(pl.multiple_of(row * depth, depth), depth), a * 128:(a + 1) * 128] = (
                band.astype(jnp.bfloat16)
            )
        return carry

    lax.fori_loop(0, bands.shape[0] // depth, row_body, 0, unroll=4)
    for copy in copies:
        copy.wait()
    tile = 256
    for n in range(0, flat.shape[0], tile):
        out = lax.dot_general(
            bands[...],
            flat[n:n + tile, :],
            (((1,), (1,)), ((), ())),
            preferred_element_type=jnp.float32,
        )
        store(out.reshape(4, 4, 2, depth, tile), slice(n, n + tile))


def other_kernel(pos, offsets, proj, weights, out, *scratch):
    def store(value, cols):
        out[:, :, :, :, cols] = value

    gather_and_multiply(pos, offsets, proj, weights, *scratch, 1 - pos[2], store)


def mine_kernel(pos, offsets, proj, weights, recv, sendp, sendm, holdp, holdm, home, *scratch):
    def store(value, cols):
        value = value + recv[:, :, :, :, cols]
        sendp[:2, :, :, cols] = value[2, :2]
        sendp[2:, :, :, cols] = value[1, 2:]
        sendm[:2, :, :, cols] = value[2, 2:]
        sendm[2:, :, :, cols] = value[3, :2]
        holdp[:, :, :, cols] = value[1, :2]
        holdm[:, :, :, cols] = value[3, 2:]
        home[:, :, :, cols] = value[0]

    gather_and_multiply(pos, offsets, proj, weights, *scratch, pos[2], store)


SMEM = pl.BlockSpec(memory_space=pltpu.SMEM)
VMEM = pl.BlockSpec(memory_space=pltpu.VMEM)
ANY = pl.BlockSpec(memory_space=pl.ANY)


def cost(us):
    return pl.CostEstimate(flops=int(us * 1.1e9), bytes_accessed=2**20, transcendentals=0)


def backproject(pos, offsets, proj, weights, start, depth, recv=None):
    angles, _, columns = proj.shape
    wide_y, band = weights.shape[1:]
    full = lambda shape: pl.BlockSpec(shape, lambda i: (0,) * len(shape))
    params = dict(
        scratch_shapes=[
            pltpu.VMEM((angles, depth, columns + 128), jnp.float32),
            pltpu.VMEM((32 * depth, angles * band), jnp.bfloat16),
            pltpu.VMEM((wide_y, angles * band), jnp.bfloat16),
            pltpu.SemaphoreType.DMA((angles,)),
        ],
        grid=(1,),
        compiler_params=pltpu.CompilerParams(vmem_limit_bytes=VMEM_LIMIT),
        cost_estimate=cost(4.0 if depth == 16 else 6.0),
    )
    proj_spec = pl.BlockSpec((angles, depth, columns), lambda i: (0, start // depth, 0))
    specs = [SMEM, SMEM, proj_spec, ANY]
    f32 = lambda *shape: jax.ShapeDtypeStruct(shape, jnp.float32)
    if recv is None:
        shape = (4, 4, 2, depth, wide_y)
        return pl.pallas_call(
            other_kernel, out_shape=f32(*shape), in_specs=specs, out_specs=full(shape), **params
        )(pos, offsets, proj, weights)
    shapes = [(n, 2, depth, wide_y) for n in (4, 4, 2, 2, 4)]
    return pl.pallas_call(
        mine_kernel,
        out_shape=[f32(*s) for s in shapes],
        in_specs=specs + [full(recv.shape)],
        out_specs=[full(s) for s in shapes],
        **params,
    )(pos, offsets, proj, weights, recv)


def conduct_kernel(table, phase, contact, out):
    for r in range(phase.shape[0]):
        for z in range(0, phase.shape[1], 8):
            label = phase[r, z:z + 8, :]
            other = contact[r, z:z + 8, :]
            odd, upper = (other & 1) == 1, other >= 2
            odd_row, upper_row = (label & 1) == 1, label >= 2
            rows = [
                jnp.where(
                    upper,
                    jnp.where(odd, table[p, 3], table[p, 2]),
                    jnp.where(odd, table[p, 1], table[p, 0]),
                )
                for p in range(4)
            ]
            out[r, z:z + 8, :] = jnp.where(
                upper_row,
                jnp.where(odd_row, rows[3], rows[2]),
                jnp.where(odd_row, rows[1], rows[0]),
            )


def conductivities(table, phase, contact):
    return pl.pallas_call(
        conduct_kernel,
        out_shape=jax.ShapeDtypeStruct(phase.shape, jnp.float32),
        in_specs=[SMEM, VMEM, VMEM],
        out_specs=VMEM,
        cost_estimate=cost(2.0),
    )(table, phase, contact)


def widened(core, value):
    left = shift_line(value, "ang", 2)
    right = shift_line(value, "ang", -2)
    first = core == 0
    given = jnp.concatenate([jnp.where(first, value, left), jnp.where(first, right, value)], axis=0)
    got = shift_ang(given, dc=1)
    return [left, got, value, right]


def ends(pieces_low, pieces_high):
    def rows(pieces, z):
        left, got, value, right = (p[:, z] for p in pieces)
        return jnp.concatenate([left, got[:2], value, got[2:], right], axis=0)

    low = shift_line(rows(pieces_high, slice(-4, None)), "gz", 1)
    high = shift_line(rows(pieces_low, slice(0, 4)), "gz", -1)
    return low, high


def fill(scratch, groups, low, high):
    rows, tall, columns = scratch.shape
    zeros = jnp.zeros((rows, 8, columns), jnp.float32)
    scratch[:, :8] = zeros
    scratch[:, tall - 8:] = zeros
    scratch[:, 4:8] = low[...]
    scratch[:, tall - 8:tall - 4] = high[...]
    for start, (left, got, value, right) in groups:
        z = slice(8 + start, 8 + start + value.shape[1])
        scratch[0:2, z] = left[...]
        scratch[2:4, z] = got[:2]
        scratch[4:6, z] = value[...]
        scratch[6:8, z] = got[2:]
        scratch[8:10, z] = right[...]


def face_of(a, b):
    total = a + b
    positive = total > 0.0
    return jnp.where(positive, 2.0 * a * b / jnp.where(positive, total, 1.0), 0.0)


def next_z(sub, here, above):
    return jnp.where(sub == 7, pltpu.roll(above, 7, 0), pltpu.roll(here, 7, 0))


def faces_kernel(left, got, value, right, low, high, fx, fy, fz, con):
    fill(con, [(0, (left, got, value, right))], low, high)
    rows, tall, columns = con.shape
    tiles = tall // 8
    lane = lax.broadcasted_iota(jnp.int32, (8, columns), 1)
    sub = lax.broadcasted_iota(jnp.int32, (8, columns), 0)

    def face_body(r, carry):
        here = con[r, 0:8, :]
        for t in range(tiles):
            z = slice(8 * t, 8 * t + 8)
            above = con[r, 8 * t + 8:8 * t + 16, :] if t + 1 < tiles else jnp.zeros_like(here)
            along_y = pltpu.roll(here, columns - 1, 1)
            fy[r, z, :] = jnp.where(lane == columns - 1, 0.0, face_of(here, along_y))
            fz[r, z, :] = face_of(here, next_z(sub, here, above))
            fx[r, z, :] = face_of(here, con[jnp.minimum(r + 1, rows - 1), z, :])
            here = above
        return carry

    lax.fori_loop(0, rows, face_body, 0)


def faces(cond, low, high):
    _, depth, columns = cond[2].shape
    shape = (2 * STEPS + 2, depth + 16, columns)
    return pl.pallas_call(
        faces_kernel,
        out_shape=[jax.ShapeDtypeStruct(shape, jnp.float32)] * 3,
        in_specs=[VMEM] * 6,
        out_specs=[VMEM] * 3,
        scratch_shapes=[pltpu.VMEM(shape, jnp.float32)],
        compiler_params=pltpu.CompilerParams(vmem_limit_bytes=VMEM_LIMIT),
        cost_estimate=cost(6.0),
    )(*cond, low, high)


def heat_kernel(starts, *refs):
    count = 4 * len(starts)
    parts, (low, high, fx, fy, fz, out, field, other) = refs[:count], refs[count:]
    fill(field, [(s, parts[4 * n:4 * n + 4]) for n, s in enumerate(starts)], low, high)
    rows, tall, columns = field.shape
    tiles = tall // 8
    sub = lax.broadcasted_iota(jnp.int32, (8, columns), 0)
    source, target = field, other
    for step in range(1, STEPS + 1):
        last = step == STEPS
        first_tile, end_tile = (1, tiles - 1) if last else (0, tiles)

        def row_body(r, carry, source=source, target=target, last=last, first_tile=first_tile, end_tile=end_tile):
            if first_tile:
                before = source[r, 8 * first_tile - 8:8 * first_tile, :]
                here = source[r, 8 * first_tile:8 * first_tile + 8, :]
                flux_before = fz[r, 8 * first_tile - 8:8 * first_tile, :] * (
                    next_z(sub, before, here) - before
                )
            else:
                here = source[r, 0:8, :]
                flux_before = jnp.zeros_like(here)
            for t in range(first_tile, end_tile):
                z = slice(8 * t, 8 * t + 8)
                above = source[r, 8 * t + 8:8 * t + 16, :] if t + 1 < tiles else jnp.zeros_like(here)
                flux_x = fx[r, z, :] * (source[r + 1, z, :] - here)
                flux_x -= fx[r - 1, z, :] * (here - source[r - 1, z, :])
                flux_y = fy[r, z, :] * (pltpu.roll(here, columns - 1, 1) - here)
                flux_y -= pltpu.roll(flux_y, 1, 1)
                flux = fz[r, z, :] * (next_z(sub, here, above) - here)
                flux_z = flux - jnp.where(sub == 0, pltpu.roll(flux_before, 1, 0), pltpu.roll(flux, 1, 0))
                value = here + STEP_SIZE * (flux_x + flux_y + flux_z)
                if last:
                    out[r - STEPS, 8 * t - 8:8 * t, :] = value
                else:
                    target[r, z, :] = value
                here, flux_before = above, flux
            return carry

        lax.fori_loop(step, rows - step, row_body, 0)
        source, target = target, source


def conduct_heat(groups, low, high, face_arrays):
    rows, tall, columns = face_arrays[0].shape
    parts = [p for _, group in groups for p in group]
    return pl.pallas_call(
        functools.partial(heat_kernel, [s for s, _ in groups]),
        out_shape=jax.ShapeDtypeStruct((rows - 2 * STEPS, tall - 16, columns), jnp.float32),
        in_specs=[VMEM] * (len(parts) + 5),
        out_specs=VMEM,
        scratch_shapes=[pltpu.VMEM((rows, tall, columns), jnp.float32)] * 2,
        compiler_params=pltpu.CompilerParams(vmem_limit_bytes=VMEM_LIMIT),
        cost_estimate=cost(9.0),
    )(*parts, low, high, *face_arrays)


def reduced(pos, offsets, proj, weights, start, depth):
    theirs = backproject(pos, offsets, proj, weights, start, depth)
    recv = shift_ang(theirs, dc=1)
    sendp, sendm, holdp, holdm, home = backproject(pos, offsets, proj, weights, start, depth, recv)
    fromp = shift_ang(sendp, dx=1)
    fromm = shift_ang(sendm, dx=-1)
    lastp = shift_ang(holdp + fromp[:2], dx=1)
    lastm = shift_ang(holdm + fromm[:2], dx=-1)
    ring_low = home[:2] + lastp + fromm[2:]
    ring_high = home[2:] + lastm + fromp[2:]
    one = shift_ang(ring_low[1], dz=1)
    two = shift_ang(ring_high[0], dz=2)
    three = shift_ang(ring_high[1], dz=3)
    return ring_low[0] + one + two + three


def local(projections, band_weights, band_offsets, phase, contact, conductivity_table):
    ang = lax.axis_index("ang")
    core = ang & 1
    pos = jnp.stack([ang >> 3, (ang >> 1) & 3, core]).astype(jnp.int32)
    conduct = conductivities(conductivity_table, phase, contact)
    cond = widened(core, conduct)
    face_arrays = faces(cond, *ends(cond, cond))
    args = (pos, band_offsets, projections, band_weights)
    volumes = [reduced(*args, start, depth) for start, depth in CHUNKS]
    groups = [(start, widened(core, v)) for (start, _), v in zip(CHUNKS, volumes)]
    lowest = min(groups, key=lambda g: g[0])[1]
    highest = max(groups, key=lambda g: g[0])[1]
    temperature = conduct_heat(groups, *ends(lowest, highest), face_arrays)
    ordered = sorted(zip((s for s, _ in CHUNKS), volumes), key=lambda g: g[0])
    return jnp.concatenate([v for _, v in ordered], axis=1), temperature


def solution(mesh):
    in_specs = (
        P("ang", "gz", None),
        P("ang", None, None),
        P("ang", None),
        P("ang", "gz", None),
        P("ang", "gz", None),
        P(),
    )
    out_specs = (P("ang", "gz", None), P("ang", "gz", None))
    return jax.shard_map(local, mesh=mesh, in_specs=in_specs, out_specs=out_specs, check_vma=False)
```

time: 291 us -> 197 us (0.68)
  the two profiles are of different devices: /device:TPU:30 before, /device:TPU:224 now
where the time goes in v2:
time: 197 us
  starting transfers between devices  78.8 us (40%)
  waiting for transfers between devices  65.1 us (33%)
  Pallas kernels  47.3 us (24%)
  other arithmetic  2.2 us (1%)
  local copies, waits for them, and re-layouts  1.97 us (1%)
    ppermute x12, starting transfers between devices, shift_line(): return lax.ppermute(value, axis, perm)  46.6 us
    ppermute x28, waiting for transfers between devices, shift_ang(): return lax.ppermute(value, 'ang', perm)  40.8 us
    ppermute x28, starting transfers between devices, shift_ang(): return lax.ppermute(value, 'ang', perm)  32.2 us
    ppermute x12, waiting for transfers between devices, shift_line(): return lax.ppermute(value, axis, perm)  24.3 us
    pallas_call x3, Pallas kernels, backproject(): pl.pallas_call(other_kernel, out_shape=f32(*shape), in_specs=specs, out_s...  16.8 us
    pallas_call x3, Pallas kernels, backproject(): pl.pallas_call(mine_kernel, out_shape=[f32(*s) for s in shapes], in_specs...  16.1 us
    pallas_call x1, Pallas kernels, conduct_heat(): pl.pallas_call(functools.partial(heat_kernel, [s for s, _ in groups]), ou...  8.74 us
  transfers between devices with their start and end apart: 40, of which 13 were waited for; matrix products, arithmetic and copies ran while one was open for 1% of the time, Pallas kernels for 18%

profile of v2, /device:TPU:224, one launch (start us, length us, event | category | flops | bytes accessed | tf_op | source)
XLA Modules:
  0.0 196.6 jit_solution(6880060842027036587)
XLA Ops:
  0.7 2.5 %shard_map.83.value = f32[2,64,1024]{2,1,0:T(8,128)} custom-call(f32[4,4]{1,0:T(4,128)} %table.1, s32[2,64,1024]{2,1,0:T(8,128)} %phase.1, s32[2,64,1024]{2,1,0:T(8,128)} %contact.1), custom_call_target="tpu_custom_call" | custom-call | flops 2200000000 | bytes 1048576 | tf_op jit(solution)/shard_map/pallas_call | solution.py:166
  3.1 5.1 %collective-permute-start.36 = (f32[2,64,1024]{2,1,0:T(8,128)}, f32[2,64,1024]{2,1,0:T(8,128)S(1)}, u32[]{:S(2)}, u32[]{:S(2)}) collective-permute-start(f32[2,64,1024]{2,1,0:T(8,128)} %shard_map.83.value), channel_id=1, source_target_pairs={{16,0},{24,8},{32,16},{40,24},{48,32},{56,40},{64,48},{72,56},{80,... | collective-permute-start | bytes 1572872 | tf_op jit(solution)/shard_map/ppermute | solution.py:30
  8.2 1.9 collective-permute-start.35
  10.2 1.6 copy-done.1
  11.8 5.7 %shard_map.77 = f32[4,4,2,16,1024]{4,3,2,1,0:T(8,128)} custom-call(s32[3]{0:T(128)S(1)} %pad_add_fusion.pos, s32[8,64]{1,0:T(8,128)S(1)} %copy-done.4, bf16[8,64,1024]{2,1,0:T(8,128)(2,1)S(1)} %copy-done.3, bf16[8,1024,128]{2,1,0:T(8,128)(2,1)S(1)} %copy-done.1), custom_call_target="tpu_custom_call" | custom-call | flops 4400000000 | bytes 1048576 | tf_op jit(solution)/shard_map/pallas_call | solution.py:130
  17.5 0.1 collective-permute-start
  17.6 5.7 %shard_map.79 = f32[4,4,2,16,1024]{4,3,2,1,0:T(8,128)} custom-call(s32[3]{0:T(128)S(1)} %pad_add_fusion.pos, s32[8,64]{1,0:T(8,128)S(1)} %copy-done.4, bf16[8,64,1024]{2,1,0:T(8,128)(2,1)S(1)} %copy-done.3, bf16[8,1024,128]{2,1,0:T(8,128)(2,1)S(1)} %copy-done.1), custom_call_target="tpu_custom_call" | custom-call | flops 4400000000 | bytes 1048576 | tf_op jit(solution)/shard_map/pallas_call | solution.py:130
  23.3 0.6 collective-permute-start.8
  23.9 2.0 collective-permute-done.35.left
  25.8 0.1 broadcast_select_fusion.1
  25.9 0.1 pad_maximum_fusion
  26.0 0.1 collective-permute-start.37
  26.1 5.5 %shard_map.81 = f32[4,4,2,32,1024]{4,3,2,1,0:T(8,128)S(1)} custom-call(s32[3]{0:T(128)S(1)} %pad_add_fusion.pos, s32[8,64]{1,0:T(8,128)S(1)} %copy-done.4, bf16[8,64,1024]{2,1,0:T(8,128)(2,1)S(1)} %copy-done.3, bf16[8,1024,128]{2,1,0:T(8,128)(2,1)S(1)} %copy-done.2), custom_call_target="tpu_custom_call" | custom-call | flops 6600000000 | bytes 1048576 | tf_op jit(solution)/shard_map/pallas_call | solution.py:130
  31.6 0.6 collective-permute-start.16
  32.3 5.3 %shard_map.78 = (f32[4,2,16,1024]{3,2,1,0:T(8,128)S(1)}, f32[4,2,16,1024]{3,2,1,0:T(8,128)S(1)}, f32[2,2,16,1024]{3,2,1,0:T(8,128)S(1)}, f32[2,2,16,1024]{3,2,1,0:T(8,128)S(1)}, f32[4,2,16,1024]{3,2,1,0:T(8,128)S(1)}) custom-call(s32[3]{0:T(128)S(1)} %pad_add_fusion.pos, s32[8,64]{1,0:T(8,128)S(1)} %copy-done.4, bf16[8,64,1024]{2,1,0:T(8,128)(2,1)S(1)} %copy-done.3, ...), custom_call_target="tpu_custom_call" | custom-call | flops 4400000000 | bytes 1048576 | tf_op jit(solution)/shard_map/pallas_call | solution.py:134
  37.7 3.2 %collective-permute-start.3 = (f32[4,2,16,1024]{3,2,1,0:T(8,128)S(1)}, f32[4,2,16,1024]{3,2,1,0:T(8,128)S(1)}, u32[]{:S(2)}, u32[]{:S(2)}) collective-permute-start(f32[4,2,16,1024]{3,2,1,0:T(8,128)S(1)} %get-tuple-element.23), channel_id=1, source_target_pairs={{0,48},{8,56},{16,0},{24,8},{32,16},{40,24},{48,32},{56,40},{64,11... | collective-permute-start | bytes 1572872 | tf_op jit(solution)/shard_map/ppermute | solution.py:24
  41.0 5.3 %shard_map.80 = (f32[4,2,16,1024]{3,2,1,0:T(8,128)S(1)}, f32[4,2,16,1024]{3,2,1,0:T(8,128)S(1)}, f32[2,2,16,1024]{3,2,1,0:T(8,128)S(1)}, f32[2,2,16,1024]{3,2,1,0:T(8,128)S(1)}, f32[4,2,16,1024]{3,2,1,0:T(8,128)S(1)}) custom-call(s32[3]{0:T(128)S(1)} %pad_add_fusion.pos, s32[8,64]{1,0:T(8,128)S(1)} %copy-done.4, bf16[8,64,1024]{2,1,0:T(8,128)(2,1)S(1)} %copy-done.3, ...), custom_call_target="tpu_custom_call" | custom-call | flops 4400000000 | bytes 1048576 | tf_op jit(solution)/shard_map/pallas_call | solution.py:134
  46.4 3.3 %collective-permute-start.11 = (f32[4,2,16,1024]{3,2,1,0:T(8,128)S(1)}, f32[4,2,16,1024]{3,2,1,0:T(8,128)S(1)}, u32[]{:S(2)}, u32[]{:S(2)}) collective-permute-start(f32[4,2,16,1024]{3,2,1,0:T(8,128)S(1)} %get-tuple-element.28), channel_id=1, source_target_pairs={{0,48},{8,56},{16,0},{24,8},{32,16},{40,24},{48,32},{56,40},{64,11... | collective-permute-start | bytes 1572872 | tf_op jit(solution)/shard_map/ppermute | solution.py:24
  49.7 4.0 %collective-permute-done.1 = f32[4,2,16,1024]{3,2,1,0:T(8,128)S(1)} collective-permute-done((f32[4,2,16,1024]{3,2,1,0:T(8,128)S(1)}, f32[4,2,16,1024]{3,2,1,0:T(8,128)S(1)}, u32[]{:S(2)}, u32[]{:S(2)}) %collective-permute-start.1) | collective-permute-done | bytes 524320 | tf_op jit(solution)/shard_map/ppermute | solution.py:24
  53.8 0.1 collective-permute-start.2
  53.9 3.3 %collective-permute-start.5 = (f32[2,2,16,1024]{3,2,1,0:T(8,128)S(1)}, f32[2,2,16,1024]{3,2,1,0:T(8,128)S(1)}, u32[]{:S(2)}, u32[]{:S(2)}) collective-permute-start(f32[2,2,16,1024]{3,2,1,0:T(8,128)S(1)} %slice_add_fusion.9), channel_id=1, source_target_pairs={{0,48},{8,56},{16,0},{24,8},{32,16},{40,24},{48,32},{56,40},{64,11... | collective-permute-start | bytes 786440 | tf_op jit(solution)/shard_map/ppermute | solution.py:24
  57.2 7.8 %collective-permute-done.9 = f32[4,2,16,1024]{3,2,1,0:T(8,128)S(1)} collective-permute-done((f32[4,2,16,1024]{3,2,1,0:T(8,128)S(1)}, f32[4,2,16,1024]{3,2,1,0:T(8,128)S(1)}, u32[]{:S(2)}, u32[]{:S(2)}) %collective-permute-start.9) | collective-permute-done | bytes 524320 | tf_op jit(solution)/shard_map/ppermute | solution.py:24
  65.0 0.1 collective-permute-start.10
  65.1 3.3 %collective-permute-start.13 = (f32[2,2,16,1024]{3,2,1,0:T(8,128)S(1)}, f32[2,2,16,1024]{3,2,1,0:T(8,128)S(1)}, u32[]{:S(2)}, u32[]{:S(2)}) collective-permute-start(f32[2,2,16,1024]{3,2,1,0:T(8,128)S(1)} %slice_add_fusion.5), channel_id=1, source_target_pairs={{0,48},{8,56},{16,0},{24,8},{32,16},{40,24},{48,32},{56,40},{64,11... | collective-permute-start | bytes 786440 | tf_op jit(solution)/shard_map/ppermute | solution.py:24
  68.4 2.1 %collective-permute-done.2 = f32[2,2,16,1024]{3,2,1,0:T(8,128)S(1)} collective-permute-done((f32[2,2,16,1024]{3,2,1,0:T(8,128)S(1)}, f32[2,2,16,1024]{3,2,1,0:T(8,128)S(1)}, u32[]{:S(2)}, u32[]{:S(2)}) %collective-permute-start.2) | collective-permute-done | bytes 262176 | tf_op jit(solution)/shard_map/ppermute | solution.py:24
  70.6 0.1 slice_add_fusion.10
  70.7 1.3 collective-permute-start.4
  72.0 1.4 collective-permute-start.6
  73.4 1.0 collective-permute-start.7
  74.4 5.5 %shard_map.82 = (f32[4,2,32,1024]{3,2,1,0:T(8,128)S(1)}, f32[4,2,32,1024]{3,2,1,0:T(8,128)S(1)}, f32[2,2,32,1024]{3,2,1,0:T(8,128)S(1)}, f32[2,2,32,1024]{3,2,1,0:T(8,128)S(1)}, f32[4,2,32,1024]{3,2,1,0:T(8,128)S(1)}) custom-call(s32[3]{0:T(128)S(1)} %pad_add_fusion.pos, s32[8,64]{1,0:T(8,128)S(1)} %copy-done.4, bf16[8,64,1024]{2,1,0:T(8,128)(2,1)S(1)} %copy-done.3, ...), custom_call_target="tpu_custom_call" | custom-call | flops 6600000000 | bytes 1048576 | tf_op jit(solution)/shard_map/pallas_call | solution.py:134
  79.9 0.7 collective-permute-start.17
  80.6 0.1 slice_add_fusion.6
  80.7 2.9 %collective-permute-start.19 = (f32[4,2,32,1024]{3,2,1,0:T(8,128)S(1)}, f32[4,2,32,1024]{3,2,1,0:T(8,128)S(1)}, u32[]{:S(2)}, u32[]{:S(2)}) collective-permute-start(f32[4,2,32,1024]{3,2,1,0:T(8,128)S(1)} %get-tuple-element.33), channel_id=1, source_target_pairs={{0,48},{8,56},{16,0},{24,8},{32,16},{40,24},{48,32},{56,40},{64,11... | collective-permute-start | bytes 3145736 | tf_op jit(solution)/shard_map/ppermute | solution.py:24
  83.7 2.9 %collective-permute-start.12 = (f32[2,16,1024]{2,1,0:T(8,128)S(1)}, f32[2,16,1024]{2,1,0:T(8,128)S(1)}, u32[]{:S(2)}, u32[]{:S(2)}) collective-permute-start(f32[2,16,1024]{2,1,0:T(8,128)S(1)} %slice_bitcast_fusion.6), channel_id=1, source_target_pairs={{0,64},{8,72},{16,80},{24,88},{32,96},{40,104},{48,112},{56,120},{... | collective-permute-start | bytes 393224 | tf_op jit(solution)/shard_map/ppermute | solution.py:24
  86.6 0.7 collective-permute-start.15
  87.3 2.8 %collective-permute-done.12 = f32[2,16,1024]{2,1,0:T(8,128)S(1)} collective-permute-done((f32[2,16,1024]{2,1,0:T(8,128)S(1)}, f32[2,16,1024]{2,1,0:T(8,128)S(1)}, u32[]{:S(2)}, u32[]{:S(2)}) %collective-permute-start.12) | collective-permute-done | bytes 131104 | tf_op jit(solution)/shard_map/ppermute | solution.py:24
  90.1 4.8 %collective-permute-start.39 = (f32[10,4,1024]{2,1,0:T(4,128)S(1)}, f32[10,4,1024]{2,1,0:T(4,128)S(1)}, u32[]{:S(2)}, u32[]{:S(2)}) collective-permute-start(f32[10,4,1024]{2,1,0:T(4,128)S(1)} %get-tuple-element.44), channel_id=1, source_target_pairs={{1,0},{2,1},{3,2},{4,3},{5,4},{6,5},{7,6},{9,8},{10,9},{11,10},{12... | collective-permute-start | bytes 491528 | tf_op jit(solution)/shard_map/ppermute | solution.py:30
  94.9 3.5 %collective-permute-done.14 = f32[2,16,1024]{2,1,0:T(8,128)S(1)} collective-permute-done((f32[2,16,1024]{2,1,0:T(8,128)S(1)}, f32[2,16,1024]{2,1,0:T(8,128)S(1)}, u32[]{:S(2)}, u32[]{:S(2)}) %collective-permute-start.14) | collective-permute-done | bytes 131104 | tf_op jit(solution)/shard_map/ppermute | solution.py:24
  98.4 5.2 %collective-permute-start.25 = (f32[2,16,1024]{2,1,0:T(8,128)S(1)}, f32[2,16,1024]{2,1,0:T(8,128)S(1)}, u32[]{:S(2)}, u32[]{:S(2)}) collective-permute-start(f32[2,16,1024]{2,1,0:T(8,128)S(1)} %fusion.8.refs_2_), channel_id=1, source_target_pairs={{16,0},{24,8},{32,16},{40,24},{48,32},{56,40},{64,48},{72,56},{80,... | collective-permute-start | bytes 393224 | tf_op jit(solution)/shard_map/ppermute | solution.py:30
  103.7 1.9 collective-permute-start.24
  105.6 6.0 %collective-permute-start.31 = (f32[2,16,1024]{2,1,0:T(8,128)S(1)}, f32[2,16,1024]{2,1,0:T(8,128)S(1)}, u32[]{:S(2)}, u32[]{:S(2)}) collective-permute-start(f32[2,16,1024]{2,1,0:T(8,128)S(1)} %fusion.5.refs_10_), channel_id=1, source_target_pairs={{16,0},{24,8},{32,16},{40,24},{48,32},{56,40},{64,48},{72,56},{80,... | collective-permute-start | bytes 393224 | tf_op jit(solution)/shard_map/ppermute | solution.py:30
  111.8 1.9 collective-permute-start.30
  113.9 3.2 %collective-permute-start.21 = (f32[2,2,32,1024]{3,2,1,0:T(8,128)S(1)}, f32[2,2,32,1024]{3,2,1,0:T(8,128)S(1)}, u32[]{:S(2)}, u32[]{:S(2)}) collective-permute-start(f32[2,2,32,1024]{3,2,1,0:T(8,128)S(1)} %slice_add_fusion.1), channel_id=1, source_target_pairs={{0,48},{8,56},{16,0},{24,8},{32,16},{40,24},{48,32},{56,40},{64,11... | collective-permute-start | bytes 1572872 | tf_op jit(solution)/shard_map/ppermute | solution.py:24
  117.1 0.1 collective-permute-start.26
  117.2 3.6 %collective-permute-done.30.refs_8_ = f32[2,16,1024]{2,1,0:T(8,128)S(1)} collective-permute-done((f32[2,16,1024]{2,1,0:T(8,128)S(1)}, f32[2,16,1024]{2,1,0:T(8,128)S(1)}, u32[]{:S(2)}, u32[]{:S(2)}) %collective-permute-start.30) | collective-permute-done | bytes 131104 | tf_op jit(solution)/shard_map/ppermute | solution.py:30
  120.9 5.9 %collective-permute-done.18 = f32[2,2,32,1024]{3,2,1,0:T(8,128)S(1)} collective-permute-done((f32[2,2,32,1024]{3,2,1,0:T(8,128)S(1)}, f32[2,2,32,1024]{3,2,1,0:T(8,128)S(1)}, u32[]{:S(2)}, u32[]{:S(2)}) %collective-permute-start.18) | collective-permute-done | bytes 524320 | tf_op jit(solution)/shard_map/ppermute | solution.py:24
  126.7 0.3 slice_add_fusion.2
  127.1 0.1 collective-permute-start.20
  127.2 2.2 %collective-permute-start.22 = (f32[2,32,1024]{2,1,0:T(8,128)S(1)}, f32[2,32,1024]{2,1,0:T(8,128)S(1)}, u32[]{:S(2)}, u32[]{:S(2)}) collective-permute-start(f32[2,32,1024]{2,1,0:T(8,128)S(1)} %get-tuple-element.56), channel_id=1, source_target_pairs={{0,128},{8,136},{16,144},{24,152},{32,160},{40,168},{48,176},{56,1... | collective-permute-start | bytes 786440 | tf_op jit(solution)/shard_map/ppermute | solution.py:24
  129.4 0.7 collective-permute-start.23
  130.2 7.3 %collective-permute-done.20 = f32[2,32,1024]{2,1,0:T(8,128)S(1)} collective-permute-done((f32[2,32,1024]{2,1,0:T(8,128)S(1)}, f32[2,32,1024]{2,1,0:T(8,128)S(1)}, u32[]{:S(2)}, u32[]{:S(2)}) %collective-permute-start.20) | collective-permute-done | bytes 262176 | tf_op jit(solution)/shard_map/ppermute | solution.py:24
  137.5 3.8 %collective-permute-start.38 = (f32[10,4,1024]{2,1,0:T(4,128)S(1)}, f32[10,4,1024]{2,1,0:T(4,128)S(1)}, u32[]{:S(2)}, u32[]{:S(2)}) collective-permute-start(f32[10,4,1024]{2,1,0:T(4,128)S(1)} %get-tuple-element.45), channel_id=1, source_target_pairs={{0,1},{1,2},{2,3},{3,4},{4,5},{5,6},{6,7},{8,9},{9,10},{10,11},{11... | collective-permute-start | bytes 491528 | tf_op jit(solution)/shard_map/ppermute | solution.py:30
  141.3 7.4 %collective-permute-done.22 = f32[2,32,1024]{2,1,0:T(8,128)S(1)} collective-permute-done((f32[2,32,1024]{2,1,0:T(8,128)S(1)}, f32[2,32,1024]{2,1,0:T(8,128)S(1)}, u32[]{:S(2)}, u32[]{:S(2)}) %collective-permute-start.22) | collective-permute-done | bytes 262176 | tf_op jit(solution)/shard_map/ppermute | solution.py:24
  148.8 4.1 %collective-permute-start.28 = (f32[2,32,1024]{2,1,0:T(8,128)S(1)}, f32[2,32,1024]{2,1,0:T(8,128)S(1)}, u32[]{:S(2)}, u32[]{:S(2)}) collective-permute-start(f32[2,32,1024]{2,1,0:T(8,128)S(1)} %fusion.2.refs_6_), channel_id=1, source_target_pairs={{16,0},{24,8},{32,16},{40,24},{48,32},{56,40},{64,48},{72,56},{80,... | collective-permute-start | bytes 786440 | tf_op jit(solution)/shard_map/ppermute | solution.py:30
  152.9 1.9 collective-permute-start.27
  154.9 4.5 %collective-permute-done.28.refs_7_ = f32[2,32,1024]{2,1,0:T(8,128)S(1)} collective-permute-done((f32[2,32,1024]{2,1,0:T(8,128)S(1)}, f32[2,32,1024]{2,1,0:T(8,128)S(1)}, u32[]{:S(2)}, u32[]{:S(2)}) %collective-permute-start.28) | collective-permute-done | bytes 262176 | tf_op jit(solution)/shard_map/ppermute | solution.py:30
  159.4 6.0 %collective-permute-done.27.refs_4_ = f32[2,32,1024]{2,1,0:T(8,128)S(1)} collective-permute-done((f32[2,32,1024]{2,1,0:T(8,128)S(1)}, f32[2,32,1024]{2,1,0:T(8,128)S(1)}, u32[]{:S(2)}, u32[]{:S(2)}) %collective-permute-start.27) | collective-permute-done | bytes 262176 | tf_op jit(solution)/shard_map/ppermute | solution.py:30
  165.5 0.1 collective-permute-start.29
  165.6 7.9 %collective-permute-start.34 = (f32[10,4,1024]{2,1,0:T(4,128)S(1)}, f32[10,4,1024]{2,1,0:T(4,128)S(1)}, u32[]{:S(2)}, u32[]{:S(2)}) collective-permute-start(f32[10,4,1024]{2,1,0:T(4,128)S(1)} %constant_dynamic-update-slice_fusion.5), channel_id=1, source_target_pairs={{1,0},{2,1},{3,2},{4,3},{5,4},{6,5},{7,6},{9,8},{10,9},{11,10},{12... | collective-permute-start | bytes 491528 | tf_op jit(solution)/shard_map/ppermute | solution.py:30
  173.6 1.9 collective-permute-start.33
  175.6 3.2 %shard_map.84 = (f32[10,80,1024]{2,1,0:T(8,128)S(1)}, f32[10,80,1024]{2,1,0:T(8,128)S(1)}, f32[10,80,1024]{2,1,0:T(8,128)S(1)}) custom-call(f32[2,64,1024]{2,1,0:T(8,128)S(1)} %collective-permute-done.35.left, f32[4,64,1024]{2,1,0:T(8,128)S(1)} %collective-permute-done.37.got, f32[2,64,1024]{2,1,0:T(8,128)S(1)} %copy-done, ...), custom_call_target="tpu_custom_call" | custom-call | flops 6600000000 | bytes 1048576 | tf_op jit(solution)/shard_map/pallas_call | solution.py:245
  178.8 0.8 pad_maximum_fusion.1
  179.6 8.3 %collective-permute-done.33.refs_12_ = f32[10,4,1024]{2,1,0:T(4,128)S(1)} collective-permute-done((f32[10,4,1024]{2,1,0:T(4,128)S(1)}, f32[10,4,1024]{2,1,0:T(4,128)S(1)}, u32[]{:S(2)}, u32[]{:S(2)}) %collective-permute-start.33) | collective-permute-done | bytes 163872 | tf_op jit(solution)/shard_map/ppermute | solution.py:30
  187.9 8.7 %shard_map.85 = f32[2,64,1024]{2,1,0:T(8,128)} custom-call(f32[2,16,1024]{2,1,0:T(8,128)S(1)} %collective-permute-done.24.refs_0_, f32[4,16,1024]{2,1,0:T(8,128)S(1)} %collective-permute-done.26.refs_1_, f32[2,16,1024]{2,1,0:T(8,128)S(1)} %fusion.8.refs_2_, f32[2,16,1024]{2,1,0:T(8,128)S(1)} %collective-permute-done.25.refs_3_, ...), custom_call_target="tpu_custom_call" | custom-call | flops 9900000256 | bytes 1048576 | tf_op jit(solution)/shard_map/pallas_call | solution.py:302
  (78 shorter events, 1.4 us)
Async XLA Ops:
  0.6 9.6 %copy-start.4 = (s32[8,64]{1,0:T(8,128)S(1)}, s32[8,64]{1,0:T(8,128)}, u32[]{:S(2)}) copy-start(s32[8,64]{1,0:T(8,128)} %offsets.11) | copy-start | bytes 6148
  0.6 9.6 %copy-start.3 = (bf16[8,64,1024]{2,1,0:T(8,128)(2,1)S(1)}, bf16[8,64,1024]{2,1,0:T(8,128)(2,1)}, u32[]{:S(2)}) copy-start(bf16[8,64,1024]{2,1,0:T(8,128)(2,1)} %proj.11) | copy-start | bytes 3145732
  3.1 20.7 %collective-permute-start.36 = (f32[2,64,1024]{2,1,0:T(8,128)}, f32[2,64,1024]{2,1,0:T(8,128)S(1)}, u32[]{:S(2)}, u32[]{:S(2)}) collective-permute-start(f32[2,64,1024]{2,1,0:T(8,128)} %shard_map.83.value), channel_id=1, source_target_pairs={{16,0},{24,8},{32,16},{40,24},{48,32},{56,40},{64,48},{72,56},{80,... | collective-permute-start | bytes 1572872 | tf_op jit(solution)/shard_map/ppermute | solution.py:30
  8.2 17.6 %collective-permute-start.35 = (f32[2,64,1024]{2,1,0:T(8,128)}, f32[2,64,1024]{2,1,0:T(8,128)S(1)}, u32[]{:S(2)}, u32[]{:S(2)}) collective-permute-start(f32[2,64,1024]{2,1,0:T(8,128)} %shard_map.83.value), channel_id=1, source_target_pairs={{0,16},{8,24},{16,32},{24,40},{32,48},{40,56},{48,64},{56,72},{64,... | collective-permute-start | bytes 1572872 | tf_op jit(solution)/shard_map/ppermute | solution.py:30
  10.2 1.6 copy-start.1
  17.5 8.3 %copy-start = (f32[2,64,1024]{2,1,0:T(8,128)S(1)}, f32[2,64,1024]{2,1,0:T(8,128)}, u32[]{:S(2)}) copy-start(f32[2,64,1024]{2,1,0:T(8,128)} %shard_map.83.value) | copy-start | bytes 1572868
  17.5 14.8 %collective-permute-start = (f32[4,4,2,16,1024]{4,3,2,1,0:T(8,128)}, f32[4,4,2,16,1024]{4,3,2,1,0:T(8,128)}, u32[]{:S(2)}, u32[]{:S(2)}) collective-permute-start(f32[4,4,2,16,1024]{4,3,2,1,0:T(8,128)} %shard_map.77), channel_id=1, source_target_pairs={{0,8},{8,0},{16,24},{24,16},{32,40},{40,32},{48,56},{56,48},{64,72... | collective-permute-start | bytes 6291464 | tf_op jit(solution)/shard_map/ppermute | solution.py:24
  23.3 17.7 %collective-permute-start.8 = (f32[4,4,2,16,1024]{4,3,2,1,0:T(8,128)}, f32[4,4,2,16,1024]{4,3,2,1,0:T(8,128)}, u32[]{:S(2)}, u32[]{:S(2)}) collective-permute-start(f32[4,4,2,16,1024]{4,3,2,1,0:T(8,128)} %shard_map.79), channel_id=1, source_target_pairs={{0,8},{8,0},{16,24},{24,16},{32,40},{40,32},{48,56},{56,48},{64,72... | collective-permute-start | bytes 6291464 | tf_op jit(solution)/shard_map/ppermute | solution.py:24
  23.9 2.3 %copy-start.2 = (bf16[8,1024,128]{2,1,0:T(8,128)(2,1)S(1)}, bf16[8,1024,128]{2,1,0:T(8,128)(2,1)}, u32[]{:S(2)}) copy-start(bf16[8,1024,128]{2,1,0:T(8,128)(2,1)} %weights.11) | copy-start | bytes 6291460
  26.0 6.2 %collective-permute-start.37 = (f32[4,64,1024]{2,1,0:T(8,128)S(1)}, f32[4,64,1024]{2,1,0:T(8,128)S(1)}, u32[]{:S(2)}, u32[]{:S(2)}) collective-permute-start(f32[4,64,1024]{2,1,0:T(8,128)S(1)} %pad_maximum_fusion), channel_id=1, source_target_pairs={{0,8},{8,0},{16,24},{24,16},{32,40},{40,32},{48,56},{56,48},{64,72... | collective-permute-start | bytes 3145736 | tf_op jit(solution)/shard_map/ppermute | solution.py:24
  31.6 41.7 %collective-permute-start.16 = (f32[4,4,2,32,1024]{4,3,2,1,0:T(8,128)S(1)}, f32[4,4,2,32,1024]{4,3,2,1,0:T(8,128)S(1)}, u32[]{:S(2)}, u32[]{:S(2)}) collective-permute-start(f32[4,4,2,32,1024]{4,3,2,1,0:T(8,128)S(1)} %shard_map.81), channel_id=1, source_target_pairs={{0,8},{8,0},{16,24},{24,16},{32,40},{40,32},{48,56},{56,48},{64,72... | collective-permute-start | bytes 12582920 | tf_op jit(solution)/shard_map/ppermute | solution.py:24
  37.7 16.1 %collective-permute-start.1 = (f32[4,2,16,1024]{3,2,1,0:T(8,128)S(1)}, f32[4,2,16,1024]{3,2,1,0:T(8,128)S(1)}, u32[]{:S(2)}, u32[]{:S(2)}) collective-permute-start(f32[4,2,16,1024]{3,2,1,0:T(8,128)S(1)} %get-tuple-element.22), channel_id=1, source_target_pairs={{0,16},{8,24},{16,32},{24,40},{32,48},{40,56},{48,0},{56,8},{64,80... | collective-permute-start | bytes 1572872 | tf_op jit(solution)/shard_map/ppermute | solution.py:24
  37.7 16.1 %collective-permute-start.3 = (f32[4,2,16,1024]{3,2,1,0:T(8,128)S(1)}, f32[4,2,16,1024]{3,2,1,0:T(8,128)S(1)}, u32[]{:S(2)}, u32[]{:S(2)}) collective-permute-start(f32[4,2,16,1024]{3,2,1,0:T(8,128)S(1)} %get-tuple-element.23), channel_id=1, source_target_pairs={{0,48},{8,56},{16,0},{24,8},{32,16},{40,24},{48,32},{56,40},{64,11... | collective-permute-start | bytes 1572872 | tf_op jit(solution)/shard_map/ppermute | solution.py:24
  46.3 18.7 %collective-permute-start.9 = (f32[4,2,16,1024]{3,2,1,0:T(8,128)S(1)}, f32[4,2,16,1024]{3,2,1,0:T(8,128)S(1)}, u32[]{:S(2)}, u32[]{:S(2)}) collective-permute-start(f32[4,2,16,1024]{3,2,1,0:T(8,128)S(1)} %get-tuple-element.27), channel_id=1, source_target_pairs={{0,16},{8,24},{16,32},{24,40},{32,48},{40,56},{48,0},{56,8},{64,80... | collective-permute-start | bytes 1572872 | tf_op jit(solution)/shard_map/ppermute | solution.py:24
  46.4 18.7 %collective-permute-start.11 = (f32[4,2,16,1024]{3,2,1,0:T(8,128)S(1)}, f32[4,2,16,1024]{3,2,1,0:T(8,128)S(1)}, u32[]{:S(2)}, u32[]{:S(2)}) collective-permute-start(f32[4,2,16,1024]{3,2,1,0:T(8,128)S(1)} %get-tuple-element.28), channel_id=1, source_target_pairs={{0,48},{8,56},{16,0},{24,8},{32,16},{40,24},{48,32},{56,40},{64,11... | collective-permute-start | bytes 1572872 | tf_op jit(solution)/shard_map/ppermute | solution.py:24
  53.8 16.8 %collective-permute-start.2 = (f32[2,2,16,1024]{3,2,1,0:T(8,128)S(1)}, f32[2,2,16,1024]{3,2,1,0:T(8,128)S(1)}, u32[]{:S(2)}, u32[]{:S(2)}) collective-permute-start(f32[2,2,16,1024]{3,2,1,0:T(8,128)S(1)} %slice_add_fusion.11), channel_id=1, source_target_pairs={{0,16},{8,24},{16,32},{24,40},{32,48},{40,56},{48,0},{56,8},{64,80... | collective-permute-start | bytes 786440 | tf_op jit(solution)/shard_map/ppermute | solution.py:24
  53.9 16.7 %collective-permute-start.5 = (f32[2,2,16,1024]{3,2,1,0:T(8,128)S(1)}, f32[2,2,16,1024]{3,2,1,0:T(8,128)S(1)}, u32[]{:S(2)}, u32[]{:S(2)}) collective-permute-start(f32[2,2,16,1024]{3,2,1,0:T(8,128)S(1)} %slice_add_fusion.9), channel_id=1, source_target_pairs={{0,48},{8,56},{16,0},{24,8},{32,16},{40,24},{48,32},{56,40},{64,11... | collective-permute-start | bytes 786440 | tf_op jit(solution)/shard_map/ppermute | solution.py:24
  65.0 14.9 %collective-permute-start.10 = (f32[2,2,16,1024]{3,2,1,0:T(8,128)S(1)}, f32[2,2,16,1024]{3,2,1,0:T(8,128)S(1)}, u32[]{:S(2)}, u32[]{:S(2)}) collective-permute-start(f32[2,2,16,1024]{3,2,1,0:T(8,128)S(1)} %slice_add_fusion.7), channel_id=1, source_target_pairs={{0,16},{8,24},{16,32},{24,40},{32,48},{40,56},{48,0},{56,8},{64,80... | collective-permute-start | bytes 786440 | tf_op jit(solution)/shard_map/ppermute | solution.py:24
  65.1 15.5 %collective-permute-start.13 = (f32[2,2,16,1024]{3,2,1,0:T(8,128)S(1)}, f32[2,2,16,1024]{3,2,1,0:T(8,128)S(1)}, u32[]{:S(2)}, u32[]{:S(2)}) collective-permute-start(f32[2,2,16,1024]{3,2,1,0:T(8,128)S(1)} %slice_add_fusion.5), channel_id=1, source_target_pairs={{0,48},{8,56},{16,0},{24,8},{32,16},{40,24},{48,32},{56,40},{64,11... | collective-permute-start | bytes 786440 | tf_op jit(solution)/shard_map/ppermute | solution.py:24
  70.7 13.0 %collective-permute-start.4 = (f32[2,16,1024]{2,1,0:T(8,128)S(1)}, f32[2,16,1024]{2,1,0:T(8,128)S(1)}, u32[]{:S(2)}, u32[]{:S(2)}) collective-permute-start(f32[2,16,1024]{2,1,0:T(8,128)S(1)} %slice_bitcast_fusion.10), channel_id=1, source_target_pairs={{0,64},{8,72},{16,80},{24,88},{32,96},{40,104},{48,112},{56,120},{... | collective-permute-start | bytes 393224 | tf_op jit(solution)/shard_map/ppermute | solution.py:24
  72.0 14.6 %collective-permute-start.6 = (f32[2,16,1024]{2,1,0:T(8,128)S(1)}, f32[2,16,1024]{2,1,0:T(8,128)S(1)}, u32[]{:S(2)}, u32[]{:S(2)}) collective-permute-start(f32[2,16,1024]{2,1,0:T(8,128)S(1)} %get-tuple-element.60), channel_id=1, source_target_pairs={{0,128},{8,136},{16,144},{24,152},{32,160},{40,168},{48,176},{56,1... | collective-permute-start | bytes 393224 | tf_op jit(solution)/shard_map/ppermute | solution.py:24
  73.4 13.3 %collective-permute-start.7 = (f32[2,16,1024]{2,1,0:T(8,128)S(1)}, f32[2,16,1024]{2,1,0:T(8,128)S(1)}, u32[]{:S(2)}, u32[]{:S(2)}) collective-permute-start(f32[2,16,1024]{2,1,0:T(8,128)S(1)} %get-tuple-element.61), channel_id=1, source_target_pairs={{0,192},{8,200},{16,208},{24,216},{32,224},{40,232},{48,240},{56,2... | collective-permute-start | bytes 393224 | tf_op jit(solution)/shard_map/ppermute | solution.py:24
  79.9 25.7 %collective-permute-start.17 = (f32[4,2,32,1024]{3,2,1,0:T(8,128)S(1)}, f32[4,2,32,1024]{3,2,1,0:T(8,128)S(1)}, u32[]{:S(2)}, u32[]{:S(2)}) collective-permute-start(f32[4,2,32,1024]{3,2,1,0:T(8,128)S(1)} %get-tuple-element.32), channel_id=1, source_target_pairs={{0,16},{8,24},{16,32},{24,40},{32,48},{40,56},{48,0},{56,8},{64,80... | collective-permute-start | bytes 3145736 | tf_op jit(solution)/shard_map/ppermute | solution.py:24
  80.7 31.0 %collective-permute-start.19 = (f32[4,2,32,1024]{3,2,1,0:T(8,128)S(1)}, f32[4,2,32,1024]{3,2,1,0:T(8,128)S(1)}, u32[]{:S(2)}, u32[]{:S(2)}) collective-permute-start(f32[4,2,32,1024]{3,2,1,0:T(8,128)S(1)} %get-tuple-element.33), channel_id=1, source_target_pairs={{0,48},{8,56},{16,0},{24,8},{32,16},{40,24},{48,32},{56,40},{64,11... | collective-permute-start | bytes 3145736 | tf_op jit(solution)/shard_map/ppermute | solution.py:24
  83.7 6.4 %collective-permute-start.12 = (f32[2,16,1024]{2,1,0:T(8,128)S(1)}, f32[2,16,1024]{2,1,0:T(8,128)S(1)}, u32[]{:S(2)}, u32[]{:S(2)}) collective-permute-start(f32[2,16,1024]{2,1,0:T(8,128)S(1)} %slice_bitcast_fusion.6), channel_id=1, source_target_pairs={{0,64},{8,72},{16,80},{24,88},{32,96},{40,104},{48,112},{56,120},{... | collective-permute-start | bytes 393224 | tf_op jit(solution)/shard_map/ppermute | solution.py:24
  86.6 11.8 %collective-permute-start.14 = (f32[2,16,1024]{2,1,0:T(8,128)S(1)}, f32[2,16,1024]{2,1,0:T(8,128)S(1)}, u32[]{:S(2)}, u32[]{:S(2)}) collective-permute-start(f32[2,16,1024]{2,1,0:T(8,128)S(1)} %get-tuple-element.62), channel_id=1, source_target_pairs={{0,128},{8,136},{16,144},{24,152},{32,160},{40,168},{48,176},{56,1... | collective-permute-start | bytes 393224 | tf_op jit(solution)/shard_map/ppermute | solution.py:24
  86.6 17.0 %collective-permute-start.15 = (f32[2,16,1024]{2,1,0:T(8,128)S(1)}, f32[2,16,1024]{2,1,0:T(8,128)S(1)}, u32[]{:S(2)}, u32[]{:S(2)}) collective-permute-start(f32[2,16,1024]{2,1,0:T(8,128)S(1)} %get-tuple-element.63), channel_id=1, source_target_pairs={{0,192},{8,200},{16,208},{24,216},{32,224},{40,232},{48,240},{56,2... | collective-permute-start | bytes 393224 | tf_op jit(solution)/shard_map/ppermute | solution.py:24
  90.1 85.5 %collective-permute-start.39 = (f32[10,4,1024]{2,1,0:T(4,128)S(1)}, f32[10,4,1024]{2,1,0:T(4,128)S(1)}, u32[]{:S(2)}, u32[]{:S(2)}) collective-permute-start(f32[10,4,1024]{2,1,0:T(4,128)S(1)} %get-tuple-element.44), channel_id=1, source_target_pairs={{1,0},{2,1},{3,2},{4,3},{5,4},{6,5},{7,6},{9,8},{10,9},{11,10},{12... | collective-permute-start | bytes 491528 | tf_op jit(solution)/shard_map/ppermute | solution.py:30
  98.4 15.3 %collective-permute-start.25 = (f32[2,16,1024]{2,1,0:T(8,128)S(1)}, f32[2,16,1024]{2,1,0:T(8,128)S(1)}, u32[]{:S(2)}, u32[]{:S(2)}) collective-permute-start(f32[2,16,1024]{2,1,0:T(8,128)S(1)} %fusion.8.refs_2_), channel_id=1, source_target_pairs={{16,0},{24,8},{32,16},{40,24},{48,32},{56,40},{64,48},{72,56},{80,... | collective-permute-start | bytes 393224 | tf_op jit(solution)/shard_map/ppermute | solution.py:30
  103.7 10.2 %collective-permute-start.24 = (f32[2,16,1024]{2,1,0:T(8,128)S(1)}, f32[2,16,1024]{2,1,0:T(8,128)S(1)}, u32[]{:S(2)}, u32[]{:S(2)}) collective-permute-start(f32[2,16,1024]{2,1,0:T(8,128)S(1)} %fusion.8.refs_2_), channel_id=1, source_target_pairs={{0,16},{8,24},{16,32},{24,40},{32,48},{40,56},{48,64},{56,72},{64,... | collective-permute-start | bytes 393224 | tf_op jit(solution)/shard_map/ppermute | solution.py:30
  105.6 11.5 %collective-permute-start.31 = (f32[2,16,1024]{2,1,0:T(8,128)S(1)}, f32[2,16,1024]{2,1,0:T(8,128)S(1)}, u32[]{:S(2)}, u32[]{:S(2)}) collective-permute-start(f32[2,16,1024]{2,1,0:T(8,128)S(1)} %fusion.5.refs_10_), channel_id=1, source_target_pairs={{16,0},{24,8},{32,16},{40,24},{48,32},{56,40},{64,48},{72,56},{80,... | collective-permute-start | bytes 393224 | tf_op jit(solution)/shard_map/ppermute | solution.py:30
  111.8 9.1 %collective-permute-start.30 = (f32[2,16,1024]{2,1,0:T(8,128)S(1)}, f32[2,16,1024]{2,1,0:T(8,128)S(1)}, u32[]{:S(2)}, u32[]{:S(2)}) collective-permute-start(f32[2,16,1024]{2,1,0:T(8,128)S(1)} %fusion.5.refs_10_), channel_id=1, source_target_pairs={{0,16},{8,24},{16,32},{24,40},{32,48},{40,56},{48,64},{56,72},{64,... | collective-permute-start | bytes 393224 | tf_op jit(solution)/shard_map/ppermute | solution.py:30
  113.8 13.0 %collective-permute-start.18 = (f32[2,2,32,1024]{3,2,1,0:T(8,128)S(1)}, f32[2,2,32,1024]{3,2,1,0:T(8,128)S(1)}, u32[]{:S(2)}, u32[]{:S(2)}) collective-permute-start(f32[2,2,32,1024]{3,2,1,0:T(8,128)S(1)} %slice_add_fusion.3), channel_id=1, source_target_pairs={{0,16},{8,24},{16,32},{24,40},{32,48},{40,56},{48,0},{56,8},{64,80... | collective-permute-start | bytes 1572872 | tf_op jit(solution)/shard_map/ppermute | solution.py:24
  113.9 12.9 %collective-permute-start.21 = (f32[2,2,32,1024]{3,2,1,0:T(8,128)S(1)}, f32[2,2,32,1024]{3,2,1,0:T(8,128)S(1)}, u32[]{:S(2)}, u32[]{:S(2)}) collective-permute-start(f32[2,2,32,1024]{3,2,1,0:T(8,128)S(1)} %slice_add_fusion.1), channel_id=1, source_target_pairs={{0,48},{8,56},{16,0},{24,8},{32,16},{40,24},{48,32},{56,40},{64,11... | collective-permute-start | bytes 1572872 | tf_op jit(solution)/shard_map/ppermute | solution.py:24
  117.1 35.8 %collective-permute-start.26 = (f32[4,16,1024]{2,1,0:T(8,128)S(1)}, f32[4,16,1024]{2,1,0:T(8,128)S(1)}, u32[]{:S(2)}, u32[]{:S(2)}) collective-permute-start(f32[4,16,1024]{2,1,0:T(8,128)S(1)} %pad_maximum_fusion.3), channel_id=1, source_target_pairs={{0,8},{8,0},{16,24},{24,16},{32,40},{40,32},{48,56},{56,48},{64,72... | collective-permute-start | bytes 786440 | tf_op jit(solution)/shard_map/ppermute | solution.py:24
  127.1 10.4 %collective-permute-start.20 = (f32[2,32,1024]{2,1,0:T(8,128)S(1)}, f32[2,32,1024]{2,1,0:T(8,128)S(1)}, u32[]{:S(2)}, u32[]{:S(2)}) collective-permute-start(f32[2,32,1024]{2,1,0:T(8,128)S(1)} %slice_bitcast_fusion.2), channel_id=1, source_target_pairs={{0,64},{8,72},{16,80},{24,88},{32,96},{40,104},{48,112},{56,120},{... | collective-permute-start | bytes 786440 | tf_op jit(solution)/shard_map/ppermute | solution.py:24
  127.2 21.5 %collective-permute-start.22 = (f32[2,32,1024]{2,1,0:T(8,128)S(1)}, f32[2,32,1024]{2,1,0:T(8,128)S(1)}, u32[]{:S(2)}, u32[]{:S(2)}) collective-permute-start(f32[2,32,1024]{2,1,0:T(8,128)S(1)} %get-tuple-element.56), channel_id=1, source_target_pairs={{0,128},{8,136},{16,144},{24,152},{32,160},{40,168},{48,176},{56,1... | collective-permute-start | bytes 786440 | tf_op jit(solution)/shard_map/ppermute | solution.py:24
  129.4 19.3 %collective-permute-start.23 = (f32[2,32,1024]{2,1,0:T(8,128)S(1)}, f32[2,32,1024]{2,1,0:T(8,128)S(1)}, u32[]{:S(2)}, u32[]{:S(2)}) collective-permute-start(f32[2,32,1024]{2,1,0:T(8,128)S(1)} %get-tuple-element.57), channel_id=1, source_target_pairs={{0,192},{8,200},{16,208},{24,216},{32,224},{40,232},{48,240},{56,2... | collective-permute-start | bytes 786440 | tf_op jit(solution)/shard_map/ppermute | solution.py:24
  137.5 38.1 %collective-permute-start.38 = (f32[10,4,1024]{2,1,0:T(4,128)S(1)}, f32[10,4,1024]{2,1,0:T(4,128)S(1)}, u32[]{:S(2)}, u32[]{:S(2)}) collective-permute-start(f32[10,4,1024]{2,1,0:T(4,128)S(1)} %get-tuple-element.45), channel_id=1, source_target_pairs={{0,1},{1,2},{2,3},{3,4},{4,5},{5,6},{6,7},{8,9},{9,10},{10,11},{11... | collective-permute-start | bytes 491528 | tf_op jit(solution)/shard_map/ppermute | solution.py:30
  148.7 30.9 %collective-permute-start.32 = (f32[4,16,1024]{2,1,0:T(8,128)S(1)}, f32[4,16,1024]{2,1,0:T(8,128)S(1)}, u32[]{:S(2)}, u32[]{:S(2)}) collective-permute-start(f32[4,16,1024]{2,1,0:T(8,128)S(1)} %pad_maximum_fusion.4), channel_id=1, source_target_pairs={{0,8},{8,0},{16,24},{24,16},{32,40},{40,32},{48,56},{56,48},{64,72... | collective-permute-start | bytes 786440 | tf_op jit(solution)/shard_map/ppermute | solution.py:24
  148.8 10.6 %collective-permute-start.28 = (f32[2,32,1024]{2,1,0:T(8,128)S(1)}, f32[2,32,1024]{2,1,0:T(8,128)S(1)}, u32[]{:S(2)}, u32[]{:S(2)}) collective-permute-start(f32[2,32,1024]{2,1,0:T(8,128)S(1)} %fusion.2.refs_6_), channel_id=1, source_target_pairs={{16,0},{24,8},{32,16},{40,24},{48,32},{56,40},{64,48},{72,56},{80,... | collective-permute-start | bytes 786440 | tf_op jit(solution)/shard_map/ppermute | solution.py:30
  152.9 12.4 %collective-permute-start.27 = (f32[2,32,1024]{2,1,0:T(8,128)S(1)}, f32[2,32,1024]{2,1,0:T(8,128)S(1)}, u32[]{:S(2)}, u32[]{:S(2)}) collective-permute-start(f32[2,32,1024]{2,1,0:T(8,128)S(1)} %fusion.2.refs_6_), channel_id=1, source_target_pairs={{0,16},{8,24},{16,32},{24,40},{32,48},{40,56},{48,64},{56,72},{64,... | collective-permute-start | bytes 786440 | tf_op jit(solution)/shard_map/ppermute | solution.py:30
  165.5 8.1 %collective-permute-start.29 = (f32[4,32,1024]{2,1,0:T(8,128)S(1)}, f32[4,32,1024]{2,1,0:T(8,128)S(1)}, u32[]{:S(2)}, u32[]{:S(2)}) collective-permute-start(f32[4,32,1024]{2,1,0:T(8,128)S(1)} %pad_maximum_fusion.2), channel_id=1, source_target_pairs={{0,8},{8,0},{16,24},{24,16},{32,40},{40,32},{48,56},{56,48},{64,72... | collective-permute-start | bytes 1572872 | tf_op jit(solution)/shard_map/ppermute | solution.py:24
  165.6 14.0 %collective-permute-start.34 = (f32[10,4,1024]{2,1,0:T(4,128)S(1)}, f32[10,4,1024]{2,1,0:T(4,128)S(1)}, u32[]{:S(2)}, u32[]{:S(2)}) collective-permute-start(f32[10,4,1024]{2,1,0:T(4,128)S(1)} %constant_dynamic-update-slice_fusion.5), channel_id=1, source_target_pairs={{1,0},{2,1},{3,2},{4,3},{5,4},{6,5},{7,6},{9,8},{10,9},{11,10},{12... | collective-permute-start | bytes 491528 | tf_op jit(solution)/shard_map/ppermute | solution.py:30
  173.6 14.2 %collective-permute-start.33 = (f32[10,4,1024]{2,1,0:T(4,128)S(1)}, f32[10,4,1024]{2,1,0:T(4,128)S(1)}, u32[]{:S(2)}, u32[]{:S(2)}) collective-permute-start(f32[10,4,1024]{2,1,0:T(4,128)S(1)} %constant_dynamic-update-slice_fusion), channel_id=1, source_target_pairs={{0,1},{1,2},{2,3},{3,4},{4,5},{5,6},{6,7},{8,9},{9,10},{10,11},{11... | collective-permute-start | bytes 491528 | tf_op jit(solution)/shard_map/ppermute | solution.py:30

commit v3 on v2

v3 whole, which is shorter than its diff:
```python
import functools
import jax
import jax.numpy as jnp
from jax import lax
from jax.experimental import pallas as pl
from jax.experimental.pallas import tpu as pltpu
from jax.sharding import PartitionSpec as P

STEPS = 4
STEP_SIZE = 0.15
CHUNKS = (((0, 16), (48, 16)), ((16, 32),))
TILE = 256
NEAR_US = 9.0
SWAP_US = 14.0
ZL, X, C = 4, 4, 2
VMEM_LIMIT = 26 * 1024 * 1024


def shift_ang(value, dz=0, dx=0, dc=0):
    perm = []
    for z in range(ZL):
        for x in range(X):
            for c in range(C):
                src = (z * X + x) * C + c
                dst = ((z ^ dz) * X + (x + dx) % X) * C + (c ^ dc)
                perm.append((src, dst))
    return lax.ppermute(value, "ang", perm)


def shift_line(value, axis, step):
    count = lax.axis_size(axis)
    perm = [(i, i + step) for i in range(count) if 0 <= i + step < count]
    return lax.ppermute(value, axis, perm)


def gather(ranges, pos, offsets, proj, weights, wide, bands, flat, sems, core):
    angles, _, columns = proj.shape
    depth = wide.shape[1]
    copies = [
        pltpu.make_async_copy(weights.at[a], flat.at[:, a * 128:(a + 1) * 128], sems.at[a])
        for a in range(angles)
    ]
    for copy in copies:
        copy.start()
    wide[:, :, columns:] = jnp.zeros((angles, depth, 128), jnp.float32)
    for a in range(angles):
        at = 0
        for first, count in ranges:
            wide[a, at:at + count, :columns] = proj[a, first:first + count, :].astype(jnp.float32)
            at += count
    lane = lax.broadcasted_iota(jnp.int32, (depth, 128), 1)

    def row_body(row, carry):
        dx, dz, i = row >> 3, (row >> 1) & 3, row & 1
        owner = (
            (pos[0] ^ dz) * (X * C * 2)
            + ((pos[1] + dx) & (X - 1)) * (C * 2)
            + core * 2
            + i
        )
        for a in range(angles):
            off = offsets[a, owner]
            base = pl.multiple_of((off >> 7) << 7, 128)
            rem = off & 127
            low = wide[a, :, pl.ds(base, 128)]
            high = wide[a, :, pl.ds(pl.multiple_of(base + 128, 128), 128)]
            band = pltpu.roll(jnp.where(lane < rem, high, low), (128 - rem) & 127, 1)
            bands[pl.ds(pl.multiple_of(row * depth, depth), depth), a * 128:(a + 1) * 128] = (
                band.astype(jnp.bfloat16)
            )
        return carry

    lax.fori_loop(0, bands.shape[0] // depth, row_body, 0, unroll=4)
    for copy in copies:
        copy.wait()


def product(bands, flat, store):
    for n in range(0, flat.shape[0], TILE):
        out = lax.dot_general(
            bands[...],
            flat[n:n + TILE, :],
            (((1,), (1,)), ((), ())),
            preferred_element_type=jnp.float32,
        )
        store(out.reshape(4, 4, 2, bands.shape[0] // 32, TILE), slice(n, n + TILE))


def other_kernel(ranges, pos, offsets, proj, weights, token, out, wide, bands, flat, sems):
    def store(value, cols):
        out[:, :, :, :, cols] = value

    gather(ranges, pos, offsets, proj, weights, wide, bands, flat, sems, 1 - pos[2])
    product(bands, flat, store)


def mine_kernel(
    ranges,
    pos,
    offsets,
    proj,
    weights,
    token,
    recv,
    sendp,
    sendm,
    holdp,
    holdm,
    home,
    wide,
    bands,
    flat,
    sems,
):
    def store(value, cols):
        value = value + recv[:, :, :, :, cols]
        sendp[:2, :, :, cols] = value[2, :2]
        sendp[2:, :, :, cols] = value[1, 2:]
        sendm[:2, :, :, cols] = value[2, 2:]
        sendm[2:, :, :, cols] = value[3, :2]
        holdp[:, :, :, cols] = value[1, :2]
        holdm[:, :, :, cols] = value[3, 2:]
        home[:, :, :, cols] = value[0]

    gather(ranges, pos, offsets, proj, weights, wide, bands, flat, sems, pos[2])
    product(bands, flat, store)


SMEM = pl.BlockSpec(memory_space=pltpu.SMEM)
VMEM = pl.BlockSpec(memory_space=pltpu.VMEM)
ANY = pl.BlockSpec(memory_space=pl.ANY)


def cost(us):
    return pl.CostEstimate(flops=int(us * 1.1e9), bytes_accessed=2**20, transcendentals=0)


def backproject(pos, offsets, proj, weights, ranges, token, recv=None):
    angles, _, columns = proj.shape
    wide_y, band = weights.shape[1:]
    depth = sum(count for _, count in ranges)
    full = lambda shape: pl.BlockSpec(shape, lambda n: (0,) * len(shape))
    params = dict(
        scratch_shapes=[
            pltpu.VMEM((angles, depth, columns + 128), jnp.float32),
            pltpu.VMEM((32 * depth, angles * band), jnp.bfloat16),
            pltpu.VMEM((wide_y, angles * band), jnp.bfloat16),
            pltpu.SemaphoreType.DMA((angles,)),
        ],
        grid=(1,),
        compiler_params=pltpu.CompilerParams(vmem_limit_bytes=VMEM_LIMIT),
        cost_estimate=cost(2.0 + depth / 8),
    )
    specs = [SMEM, SMEM, full(proj.shape), ANY, ANY]
    f32 = lambda *shape: jax.ShapeDtypeStruct(shape, jnp.float32)
    if recv is None:
        shape = (4, 4, 2, depth, wide_y)
        return pl.pallas_call(
            functools.partial(other_kernel, ranges),
            out_shape=f32(*shape),
            in_specs=specs,
            out_specs=full(shape),
            **params,
        )(pos, offsets, proj, weights, token)
    shapes = [(n, 2, depth, wide_y) for n in (4, 4, 2, 2, 4)]
    return pl.pallas_call(
        functools.partial(mine_kernel, ranges),
        out_shape=[f32(*s) for s in shapes],
        in_specs=specs + [full(recv.shape)],
        out_specs=[full(s) for s in shapes],
        **params,
    )(pos, offsets, proj, weights, token, recv)


def conduct_kernel(table, phase, contact, token, out):
    for r in range(phase.shape[0]):
        for z in range(0, phase.shape[1], 8):
            label = phase[r, z:z + 8, :]
            other = contact[r, z:z + 8, :]
            odd, upper = (other & 1) == 1, other >= 2
            odd_row, upper_row = (label & 1) == 1, label >= 2
            rows = [
                jnp.where(
                    upper,
                    jnp.where(odd, table[p, 3], table[p, 2]),
                    jnp.where(odd, table[p, 1], table[p, 0]),
                )
                for p in range(4)
            ]
            out[r, z:z + 8, :] = jnp.where(
                upper_row,
                jnp.where(odd_row, rows[3], rows[2]),
                jnp.where(odd_row, rows[1], rows[0]),
            )


def conductivities(table, phase, contact, token):
    return pl.pallas_call(
        conduct_kernel,
        out_shape=jax.ShapeDtypeStruct(phase.shape, jnp.float32),
        in_specs=[SMEM, VMEM, VMEM, ANY],
        out_specs=VMEM,
        cost_estimate=cost(2.0),
    )(table, phase, contact, token)


def swap_kernel(core, left, value, right, token, given):
    @pl.when(core[0] == 0)
    def _():
        given[:2] = value[...]
        given[2:] = right[...]

    @pl.when(core[0] != 0)
    def _():
        given[:2] = left[...]
        given[2:] = value[...]


def widened(core, value, token, us=1.0):
    left = shift_line(value, "ang", 2)
    right = shift_line(value, "ang", -2)
    _, depth, columns = value.shape
    given = pl.pallas_call(
        swap_kernel,
        out_shape=jax.ShapeDtypeStruct((4, depth, columns), jnp.float32),
        in_specs=[SMEM] + [VMEM] * 3 + [ANY],
        out_specs=VMEM,
        compiler_params=pltpu.CompilerParams(vmem_limit_bytes=VMEM_LIMIT),
        cost_estimate=cost(us),
    )(core.reshape(1), left, value, right, token)
    got = shift_ang(given, dc=1)
    return [left, got, value, right], given


def ends_kernel(*refs):
    top, bottom = refs[8:]
    for n in range(2):
        left, got, value, right = refs[4 * n:4 * n + 4]
        depth = value.shape[1]
        for out, z in ((top, slice(depth - 4, depth)), (bottom, slice(0, 4))):
            out[n, 0:2] = left[:, z]
            out[n, 2:4] = got[:2, z]
            out[n, 4:6] = value[:, z]
            out[n, 6:8] = got[2:, z]
            out[n, 8:10] = right[:, z]


def ends(cond, outer):
    shape = (2, 10, 4, outer[0].shape[2])
    top, bottom = small(ends_kernel, [shape] * 2, [*cond, *outer], us=3.0)
    return shift_line(top, "gz", 1), shift_line(bottom, "gz", -1)


def fill(scratch, groups, low, high, kind):
    rows, tall, columns = scratch.shape
    zeros = jnp.zeros((rows, 8, columns), jnp.float32)
    scratch[:, :8] = zeros
    scratch[:, tall - 8:] = zeros
    scratch[:, 4:8] = low[kind]
    scratch[:, tall - 8:tall - 4] = high[kind]
    for ranges, (left, got, value, right) in groups:
        at = 0
        for first, count in ranges:
            z, own = slice(8 + first, 8 + first + count), slice(at, at + count)
            scratch[0:2, z] = left[:, own]
            scratch[2:4, z] = got[:2, own]
            scratch[4:6, z] = value[:, own]
            scratch[6:8, z] = got[2:, own]
            scratch[8:10, z] = right[:, own]
            at += count


def face_of(a, b):
    total = a + b
    positive = total > 0.0
    return jnp.where(positive, 2.0 * a * b / jnp.where(positive, total, 1.0), 0.0)


def next_z(sub, here, above):
    return jnp.where(sub == 7, pltpu.roll(above, 7, 0), pltpu.roll(here, 7, 0))


def faces_kernel(left, got, value, right, low, high, token, fx, fy, fz, con):
    fill(con, [(((0, value.shape[1]),), (left, got, value, right))], low, high, 0)
    rows, tall, columns = con.shape
    tiles = tall // 8
    lane = lax.broadcasted_iota(jnp.int32, (8, columns), 1)
    sub = lax.broadcasted_iota(jnp.int32, (8, columns), 0)

    def face_body(r, carry):
        here = con[r, 0:8, :]
        for t in range(tiles):
            z = slice(8 * t, 8 * t + 8)
            above = con[r, 8 * t + 8:8 * t + 16, :] if t + 1 < tiles else jnp.zeros_like(here)
            along_y = pltpu.roll(here, columns - 1, 1)
            fy[r, z, :] = jnp.where(lane == columns - 1, 0.0, face_of(here, along_y))
            fz[r, z, :] = face_of(here, next_z(sub, here, above))
            fx[r, z, :] = face_of(here, con[jnp.minimum(r + 1, rows - 1), z, :])
            here = above
        return carry

    lax.fori_loop(0, rows, face_body, 0)


def faces(cond, low, high, token):
    _, depth, columns = cond[2].shape
    shape = (2 * STEPS + 2, depth + 16, columns)
    return pl.pallas_call(
        faces_kernel,
        out_shape=[jax.ShapeDtypeStruct(shape, jnp.float32)] * 3,
        in_specs=[VMEM] * 6 + [ANY],
        out_specs=[VMEM] * 3,
        scratch_shapes=[pltpu.VMEM(shape, jnp.float32)],
        compiler_params=pltpu.CompilerParams(vmem_limit_bytes=VMEM_LIMIT),
        cost_estimate=cost(6.0),
    )(*cond, low, high, token)


def heat_kernel(chunks, *refs):
    count = 4 * len(chunks)
    parts, (low, high, fx, fy, fz, volume, out, field, other) = refs[:count], refs[count:]
    groups = [(c, parts[4 * n:4 * n + 4]) for n, c in enumerate(chunks)]
    fill(field, groups, low, high, 1)
    volume[...] = field[STEPS:STEPS + volume.shape[0], 8:8 + volume.shape[1], :]
    rows, tall, columns = field.shape
    tiles = tall // 8
    sub = lax.broadcasted_iota(jnp.int32, (8, columns), 0)
    source, target = field, other
    for step in range(1, STEPS + 1):
        last = step == STEPS
        first_tile, end_tile = (1, tiles - 1) if last else (0, tiles)

        def row_body(r, carry, source=source, target=target, last=last, first_tile=first_tile, end_tile=end_tile):
            if first_tile:
                before = source[r, 8 * first_tile - 8:8 * first_tile, :]
                here = source[r, 8 * first_tile:8 * first_tile + 8, :]
                flux_before = fz[r, 8 * first_tile - 8:8 * first_tile, :] * (
                    next_z(sub, before, here) - before
                )
            else:
                here = source[r, 0:8, :]
                flux_before = jnp.zeros_like(here)
            for t in range(first_tile, end_tile):
                z = slice(8 * t, 8 * t + 8)
                above = source[r, 8 * t + 8:8 * t + 16, :] if t + 1 < tiles else jnp.zeros_like(here)
                flux_x = fx[r, z, :] * (source[r + 1, z, :] - here)
                flux_x -= fx[r - 1, z, :] * (here - source[r - 1, z, :])
                flux_y = fy[r, z, :] * (pltpu.roll(here, columns - 1, 1) - here)
                flux_y -= pltpu.roll(flux_y, 1, 1)
                flux = fz[r, z, :] * (next_z(sub, here, above) - here)
                flux_z = flux - jnp.where(sub == 0, pltpu.roll(flux_before, 1, 0), pltpu.roll(flux, 1, 0))
                value = here + STEP_SIZE * (flux_x + flux_y + flux_z)
                if last:
                    out[r - STEPS, 8 * t - 8:8 * t, :] = value
                else:
                    target[r, z, :] = value
                here, flux_before = above, flux
            return carry

        lax.fori_loop(step, rows - step, row_body, 0)
        source, target = target, source


def conduct_heat(groups, low, high, face_arrays):
    rows, tall, columns = face_arrays[0].shape
    parts = [p for _, group in groups for p in group]
    return pl.pallas_call(
        functools.partial(heat_kernel, [c for c, _ in groups]),
        out_shape=[jax.ShapeDtypeStruct((rows - 2 * STEPS, tall - 16, columns), jnp.float32)] * 2,
        in_specs=[VMEM] * (len(parts) + 5),
        out_specs=[VMEM] * 2,
        scratch_shapes=[pltpu.VMEM((rows, tall, columns), jnp.float32)] * 2,
        compiler_params=pltpu.CompilerParams(vmem_limit_bytes=VMEM_LIMIT),
        cost_estimate=cost(9.0),
    )(*parts, low, high, *face_arrays)


def second_kernel(holdp, fromp, holdm, fromm, token, outp, outm):
    outp[...] = holdp[...] + fromp[:2]
    outm[...] = holdm[...] + fromm[:2]


def ring_kernel(home, lastp, fromp, lastm, fromm, token, near, far):
    near[0] = home[0] + lastp[0] + fromm[2]
    far[0] = home[1] + lastp[1] + fromm[3]
    near[1] = home[2] + lastm[0] + fromp[2]
    far[1] = home[3] + lastm[1] + fromp[3]


def middle_kernel(near, got, token, out):
    out[...] = near[1] + got[1]


def volume_kernel(near, got, last, token, out):
    out[...] = near[0] + got[0] + last[...]


def small(body, outs, inputs, tokens=(), us=1.0):
    return pl.pallas_call(
        body,
        out_shape=[jax.ShapeDtypeStruct(o, jnp.float32) for o in outs],
        in_specs=[VMEM] * len(inputs) + [ANY] * len(tokens),
        out_specs=[VMEM] * len(outs),
        compiler_params=pltpu.CompilerParams(vmem_limit_bytes=VMEM_LIMIT),
        cost_estimate=cost(us),
    )(*inputs, *tokens)


class Chunk:
    def __init__(self, args, ranges, token):
        self.args, self.ranges = args, ranges
        self.recv = shift_ang(backproject(*args, ranges, token), dc=1)

    def first(self, token):
        *send, holdp, holdm, self.home = backproject(
            *self.args, self.ranges, token, self.recv
        )
        self.hold = holdp, holdm
        self.fromp = shift_ang(send[0], dx=1)
        self.fromm = shift_ang(send[1], dx=-1)
        return self.home

    def second(self, token):
        holdp, holdm = self.hold
        outs = small(
            second_kernel, [holdp.shape] * 2, [holdp, self.fromp, holdm, self.fromm], [token]
        )
        self.lastp = shift_ang(outs[0], dx=1)
        self.lastm = shift_ang(outs[1], dx=-1)
        return outs[0]

    def near_z(self, token, us=1.5):
        inputs = [self.home, self.lastp, self.fromp, self.lastm, self.fromm]
        shape = (2, *self.home.shape[1:])
        self.near, far = small(ring_kernel, [shape] * 2, inputs, [token], us=us)
        self.got = shift_ang(far, dz=1)
        return self.near

    def far_z(self, token):
        (out,) = small(middle_kernel, [self.home.shape[1:]], [self.near, self.got], [token])
        self.last = shift_ang(out, dz=2)
        return out

    def volume(self, token, us=1.0):
        parts = [self.near, self.got, self.last]
        return small(volume_kernel, [self.home.shape[1:]], parts, [token], us=us)[0]


def local(projections, band_weights, band_offsets, phase, contact, conductivity_table):
    ang = lax.axis_index("ang")
    core = ang & 1
    pos = jnp.stack([ang >> 3, (ang >> 1) & 3, core]).astype(jnp.int32)
    args = (pos, band_offsets, projections, band_weights)
    conduct = conductivities(conductivity_table, phase, contact, pos)
    outer = Chunk(args, CHUNKS[0], conduct)
    cond, token = widened(core, conduct, pos, us=SWAP_US)
    outer.first(pos)
    middle = Chunk(args, CHUNKS[1], pos)
    middle.first(outer.second(token))
    outer.near_z(pos, us=NEAR_US)
    token = outer.far_z(middle.second(pos))
    token = middle.near_z(token)
    outer_volume = outer.volume(token)
    token = middle.far_z(outer_volume)
    outer_rows, _ = widened(core, outer_volume, token)
    low, high = ends(cond, outer_rows)
    middle_volume = middle.volume(outer_volume, us=4.0)
    face_arrays = faces(cond, low, high, middle_volume)
    middle_rows, _ = widened(core, middle_volume, face_arrays[0])
    return conduct_heat(list(zip(CHUNKS, (outer_rows, middle_rows))), low, high, face_arrays)


def solution(mesh):
    in_specs = (
        P("ang", "gz", None),
        P("ang", None, None),
        P("ang", None),
        P("ang", "gz", None),
        P("ang", "gz", None),
        P(),
    )
    out_specs = (P("ang", "gz", None), P("ang", "gz", None))
    return jax.shard_map(local, mesh=mesh, in_specs=in_specs, out_specs=out_specs, check_vma=False)
```

time: 197 us -> 182 us (0.924)
  the two profiles are of different devices: /device:TPU:224 before, /device:TPU:30 now
where the time goes in v3:
time: 182 us; the launch traced here: 179 us
  waiting for transfers between devices  98.7 us (54%)
  starting transfers between devices  40.2 us (22%)
  Pallas kernels  37.8 us (21%)
    ppermute x17, waiting for transfers between devices, shift_ang(): return lax.ppermute(value, 'ang', perm)  75 us
    ppermute x8, waiting for transfers between devices, shift_line(): return lax.ppermute(value, axis, perm)  23.8 us
    ppermute x8, starting transfers between devices, shift_line(): return lax.ppermute(value, axis, perm)  23.4 us
    ppermute x17, starting transfers between devices, shift_ang(): return lax.ppermute(value, 'ang', perm)  16.9 us
    pallas_call x2, Pallas kernels, backproject(): pl.pallas_call(functools.partial(mine_kernel, ranges), out_shape=[f32(*s)...  11 us
    pallas_call x2, Pallas kernels, backproject(): pl.pallas_call(functools.partial(other_kernel, ranges), out_shape=f32(*sh...  10.9 us
    pallas_call x1, Pallas kernels, conduct_heat(): pl.pallas_call(functools.partial(heat_kernel, [c for c, _ in groups]), ou...  9.04 us
  transfers between devices with their start and end apart: 25, of which 19 were waited for; matrix products, arithmetic and copies ran while one was open for 0% of the time, Pallas kernels for 11%

profile of v3, /device:TPU:30, one launch (start us, length us, event | category | flops | bytes accessed | tf_op | source)
XLA Modules:
  0.0 179.3 jit_solution(325432986014025955)
XLA Ops:
  0.7 0.6 pad_add_fusion.token.pos
  1.3 2.7 %shard_map.77.token.value.refs_2_ = f32[2,64,1024]{2,1,0:T(8,128)} custom-call(f32[4,4]{1,0:T(4,128)} %table.1, s32[2,64,1024]{2,1,0:T(8,128)} %phase.1, s32[2,64,1024]{2,1,0:T(8,128)} %contact.1, s32[3]{0:T(128)} %pad_add_fusion.token.pos), custom_call_target="tpu_custom_call" | custom-call | flops 2200000000 | bytes 1048576 | tf_op jit(solution)/shard_map/pallas_call | solution.py:198
  4.0 0.0 copy-start.3
  4.0 1.0 copy-done.3
  5.0 5.5 %shard_map.78 = f32[4,4,2,32,1024]{4,3,2,1,0:T(8,128)S(1)} custom-call(s32[3]{0:T(128)S(1)} %copy-done, s32[8,64]{1,0:T(8,128)S(1)} %copy-done.5, bf16[8,64,1024]{2,1,0:T(8,128)(2,1)S(1)} %copy-done.2, bf16[8,1024,128]{2,1,0:T(8,128)(2,1)S(1)} %copy-done.1, f32[2,64,1024]{2,1,0:T(8,128)S(1)} %copy-done.3), custom_call_target="tpu_custom_call" | custom-call | flops 6600000000 | bytes 1048576 | tf_op jit(solution)/shard_map/pallas_call | solution.py:158
  10.5 0.0 copy-start.4
  10.5 0.1 collective-permute-start
  10.6 5.5 %shard_map.83 = f32[4,4,2,32,1024]{4,3,2,1,0:T(8,128)S(1)} custom-call(s32[3]{0:T(128)S(1)} %copy-done, s32[8,64]{1,0:T(8,128)S(1)} %copy-done.5, bf16[8,64,1024]{2,1,0:T(8,128)(2,1)S(1)} %copy-done.2, bf16[8,1024,128]{2,1,0:T(8,128)(2,1)S(1)} %copy-done.1, s32[3]{0:T(128)S(1)} %copy-done), custom_call_target="tpu_custom_call" | custom-call | flops 6600000000 | bytes 1048576 | tf_op jit(solution)/shard_map/pallas_call | solution.py:158
  16.1 0.6 collective-permute-start.8
  16.6 3.7 %collective-permute-start.3 = (f32[2,64,1024]{2,1,0:T(8,128)S(1)}, f32[2,64,1024]{2,1,0:T(8,128)S(1)}, u32[]{:S(2)}, u32[]{:S(2)}) collective-permute-start(f32[2,64,1024]{2,1,0:T(8,128)S(1)} %copy-done.4), channel_id=1, source_target_pairs={{0,16},{8,24},{16,32},{24,40},{32,48},{40,56},{48,64},{56,72},{64,... | collective-permute-start | bytes 1572872 | tf_op jit(solution)/shard_map/ppermute | solution.py:33
  20.4 2.1 %collective-permute-start.4 = (f32[2,64,1024]{2,1,0:T(8,128)S(1)}, f32[2,64,1024]{2,1,0:T(8,128)S(1)}, u32[]{:S(2)}, u32[]{:S(2)}) collective-permute-start(f32[2,64,1024]{2,1,0:T(8,128)S(1)} %copy-done.4), channel_id=1, source_target_pairs={{16,0},{24,8},{32,16},{40,24},{48,32},{56,40},{64,48},{72,56},{80,... | collective-permute-start | bytes 1572872 | tf_op jit(solution)/shard_map/ppermute | solution.py:33
  22.5 5.5 %shard_map.79 = (f32[4,2,32,1024]{3,2,1,0:T(8,128)S(1)}, f32[4,2,32,1024]{3,2,1,0:T(8,128)S(1)}, f32[2,2,32,1024]{3,2,1,0:T(8,128)S(1)}, f32[2,2,32,1024]{3,2,1,0:T(8,128)S(1)}, f32[4,2,32,1024]{3,2,1,0:T(8,128)S(1)}) custom-call(s32[3]{0:T(128)S(1)} %copy-done, s32[8,64]{1,0:T(8,128)S(1)} %copy-done.5, bf16[8,64,1024]{2,1,0:T(8,128)(2,1)S(1)} %copy-done.2, ...), custom_call_target="tpu_custom_call" | custom-call | flops 6600000000 | bytes 1048576 | tf_op jit(solution)/shard_map/pallas_call | solution.py:166
  28.0 0.1 collective-permute-start.1
  28.1 2.0 %collective-permute-start.2 = (f32[4,2,32,1024]{3,2,1,0:T(8,128)S(1)}, f32[4,2,32,1024]{3,2,1,0:T(8,128)S(1)}, u32[]{:S(2)}, u32[]{:S(2)}) collective-permute-start(f32[4,2,32,1024]{3,2,1,0:T(8,128)S(1)} %get-tuple-element.29), channel_id=1, source_target_pairs={{0,48},{8,56},{16,0},{24,8},{32,16},{40,24},{48,32},{56,40},{64,11... | collective-permute-start | bytes 3145736 | tf_op jit(solution)/shard_map/ppermute | solution.py:27
  30.1 3.2 %collective-permute-done.3.left.refs_0_ = f32[2,64,1024]{2,1,0:T(8,128)S(1)} collective-permute-done((f32[2,64,1024]{2,1,0:T(8,128)S(1)}, f32[2,64,1024]{2,1,0:T(8,128)S(1)}, u32[]{:S(2)}, u32[]{:S(2)}) %collective-permute-start.3) | collective-permute-done | bytes 524320 | tf_op jit(solution)/shard_map/ppermute | solution.py:33
  33.3 4.8 %collective-permute-done.4.right.refs_3_ = f32[2,64,1024]{2,1,0:T(8,128)S(1)} collective-permute-done((f32[2,64,1024]{2,1,0:T(8,128)S(1)}, f32[2,64,1024]{2,1,0:T(8,128)S(1)}, u32[]{:S(2)}, u32[]{:S(2)}) %collective-permute-start.4) | collective-permute-done | bytes 524320 | tf_op jit(solution)/shard_map/ppermute | solution.py:33
  38.1 0.1 shard_map.80.token
  38.2 16.7 %collective-permute-done.1.fromp = f32[4,2,32,1024]{3,2,1,0:T(8,128)S(1)} collective-permute-done((f32[4,2,32,1024]{3,2,1,0:T(8,128)S(1)}, f32[4,2,32,1024]{3,2,1,0:T(8,128)S(1)}, u32[]{:S(2)}, u32[]{:S(2)}) %collective-permute-start.1) | collective-permute-done | bytes 1048608 | tf_op jit(solution)/shard_map/ppermute | solution.py:27
  54.9 5.6 %collective-permute-done.2.fromm = f32[4,2,32,1024]{3,2,1,0:T(8,128)S(1)} collective-permute-done((f32[4,2,32,1024]{3,2,1,0:T(8,128)S(1)}, f32[4,2,32,1024]{3,2,1,0:T(8,128)S(1)}, u32[]{:S(2)}, u32[]{:S(2)}) %collective-permute-start.2) | collective-permute-done | bytes 1048608 | tf_op jit(solution)/shard_map/ppermute | solution.py:27
  60.4 0.1 shard_map.81
  60.6 0.3 collective-permute-start.5
  60.8 2.0 %collective-permute-start.6 = (f32[2,2,32,1024]{3,2,1,0:T(8,128)S(1)}, f32[2,2,32,1024]{3,2,1,0:T(8,128)S(1)}, u32[]{:S(2)}, u32[]{:S(2)}) collective-permute-start(f32[2,2,32,1024]{3,2,1,0:T(8,128)S(1)} %get-tuple-element.31), channel_id=1, source_target_pairs={{0,48},{8,56},{16,0},{24,8},{32,16},{40,24},{48,32},{56,40},{64,11... | collective-permute-start | bytes 1572872 | tf_op jit(solution)/shard_map/ppermute | solution.py:27
  62.8 0.0 collective-permute-done.8.recv
  62.8 5.5 %shard_map.84 = (f32[4,2,32,1024]{3,2,1,0:T(8,128)S(1)}, f32[4,2,32,1024]{3,2,1,0:T(8,128)S(1)}, f32[2,2,32,1024]{3,2,1,0:T(8,128)S(1)}, f32[2,2,32,1024]{3,2,1,0:T(8,128)S(1)}, f32[4,2,32,1024]{3,2,1,0:T(8,128)S(1)}) custom-call(s32[3]{0:T(128)S(1)} %copy-done, s32[8,64]{1,0:T(8,128)S(1)} %copy-done.5, bf16[8,64,1024]{2,1,0:T(8,128)(2,1)S(1)} %copy-done.2, ...), custom_call_target="tpu_custom_call" | custom-call | flops 6600000000 | bytes 1048576 | tf_op jit(solution)/shard_map/pallas_call | solution.py:166
  68.3 1.4 collective-permute-start.9
  69.7 0.7 collective-permute-start.10
  70.5 5.1 %collective-permute-done.5.lastp = f32[2,2,32,1024]{3,2,1,0:T(8,128)S(1)} collective-permute-done((f32[2,2,32,1024]{3,2,1,0:T(8,128)S(1)}, f32[2,2,32,1024]{3,2,1,0:T(8,128)S(1)}, u32[]{:S(2)}, u32[]{:S(2)}) %collective-permute-start.5) | collective-permute-done | bytes 524320 | tf_op jit(solution)/shard_map/ppermute | solution.py:27
  75.6 1.3 collective-permute-done.6.lastm
  76.9 0.2 shard_map.82
  77.1 2.0 %collective-permute-start.7 = (f32[2,2,32,1024]{3,2,1,0:T(8,128)S(1)}, f32[2,2,32,1024]{3,2,1,0:T(8,128)S(1)}, u32[]{:S(2)}, u32[]{:S(2)}) collective-permute-start(f32[2,2,32,1024]{3,2,1,0:T(8,128)S(1)} %get-tuple-element.33), channel_id=1, source_target_pairs={{0,64},{8,72},{16,80},{24,88},{32,96},{40,104},{48,112},{56,120},{... | collective-permute-start | bytes 1572872 | tf_op jit(solution)/shard_map/ppermute | solution.py:27
  79.1 18.0 %collective-permute-done.9.fromp = f32[4,2,32,1024]{3,2,1,0:T(8,128)S(1)} collective-permute-done((f32[4,2,32,1024]{3,2,1,0:T(8,128)S(1)}, f32[4,2,32,1024]{3,2,1,0:T(8,128)S(1)}, u32[]{:S(2)}, u32[]{:S(2)}) %collective-permute-start.9) | collective-permute-done | bytes 1048608 | tf_op jit(solution)/shard_map/ppermute | solution.py:27
  97.1 1.3 collective-permute-done.10.fromm
  98.4 0.1 shard_map.85
  98.6 0.3 collective-permute-start.12
  98.8 1.8 %collective-permute-start.13 = (f32[2,2,32,1024]{3,2,1,0:T(8,128)S(1)}, f32[2,2,32,1024]{3,2,1,0:T(8,128)S(1)}, u32[]{:S(2)}, u32[]{:S(2)}) collective-permute-start(f32[2,2,32,1024]{3,2,1,0:T(8,128)S(1)} %get-tuple-element.40), channel_id=1, source_target_pairs={{0,48},{8,56},{16,0},{24,8},{32,16},{40,24},{48,32},{56,40},{64,11... | collective-permute-start | bytes 1572872 | tf_op jit(solution)/shard_map/ppermute | solution.py:27
  100.7 0.0 collective-permute-done.7.got
  100.7 3.4 %collective-permute-start.11 = (f32[2,32,1024]{2,1,0:T(8,128)S(1)}, f32[2,32,1024]{2,1,0:T(8,128)S(1)}, u32[]{:S(2)}, u32[]{:S(2)}) collective-permute-start(f32[2,32,1024]{2,1,0:T(8,128)S(1)} %shard_map.86.token), channel_id=1, source_target_pairs={{0,128},{8,136},{16,144},{24,152},{32,160},{40,168},{48,176},{56,1... | collective-permute-start | bytes 786440 | tf_op jit(solution)/shard_map/ppermute | solution.py:27
  104.1 7.6 %collective-permute-done.12.lastp = f32[2,2,32,1024]{3,2,1,0:T(8,128)S(1)} collective-permute-done((f32[2,2,32,1024]{3,2,1,0:T(8,128)S(1)}, f32[2,2,32,1024]{3,2,1,0:T(8,128)S(1)}, u32[]{:S(2)}, u32[]{:S(2)}) %collective-permute-start.12) | collective-permute-done | bytes 524320 | tf_op jit(solution)/shard_map/ppermute | solution.py:27
  111.6 1.4 collective-permute-done.13.lastm
  113.1 0.2 shard_map.87
  113.3 2.0 %collective-permute-start.16 = (f32[2,2,32,1024]{3,2,1,0:T(8,128)S(1)}, f32[2,2,32,1024]{3,2,1,0:T(8,128)S(1)}, u32[]{:S(2)}, u32[]{:S(2)}) collective-permute-start(f32[2,2,32,1024]{3,2,1,0:T(8,128)S(1)} %get-tuple-element.42), channel_id=1, source_target_pairs={{0,64},{8,72},{16,80},{24,88},{32,96},{40,104},{48,112},{56,120},{... | collective-permute-start | bytes 1572872 | tf_op jit(solution)/shard_map/ppermute | solution.py:27
  115.3 0.0 collective-permute-start.21
  115.3 0.0 collective-permute-done.11.last
  115.3 1.9 %collective-permute-start.14 = (f32[2,32,1024]{2,1,0:T(8,128)S(1)}, f32[2,32,1024]{2,1,0:T(8,128)S(1)}, u32[]{:S(2)}, u32[]{:S(2)}) collective-permute-start(f32[2,32,1024]{2,1,0:T(8,128)S(1)} %shard_map.88.token.value.refs_6_.refs_2_), channel_id=1, source_target_pairs={{0,16},{8,24},{16,32},{24,40},{32,48},{40,56},{48,64},{56,72},{64,... | collective-permute-start | bytes 786440 | tf_op jit(solution)/shard_map/ppermute | solution.py:33
  117.3 3.9 %collective-permute-start.15 = (f32[2,32,1024]{2,1,0:T(8,128)S(1)}, f32[2,32,1024]{2,1,0:T(8,128)S(1)}, u32[]{:S(2)}, u32[]{:S(2)}) collective-permute-start(f32[2,32,1024]{2,1,0:T(8,128)S(1)} %shard_map.88.token.value.refs_6_.refs_2_), channel_id=1, source_target_pairs={{16,0},{24,8},{32,16},{40,24},{48,32},{56,40},{64,48},{72,56},{80,... | collective-permute-start | bytes 786440 | tf_op jit(solution)/shard_map/ppermute | solution.py:33
  121.2 6.5 %collective-permute-done.16.got = f32[2,2,32,1024]{3,2,1,0:T(8,128)S(1)} collective-permute-done((f32[2,2,32,1024]{3,2,1,0:T(8,128)S(1)}, f32[2,2,32,1024]{3,2,1,0:T(8,128)S(1)}, u32[]{:S(2)}, u32[]{:S(2)}) %collective-permute-start.16) | collective-permute-done | bytes 524320 | tf_op jit(solution)/shard_map/ppermute | solution.py:27
  127.7 2.8 %collective-permute-done.14.left.refs_4_.refs_0_ = f32[2,32,1024]{2,1,0:T(8,128)S(1)} collective-permute-done((f32[2,32,1024]{2,1,0:T(8,128)S(1)}, f32[2,32,1024]{2,1,0:T(8,128)S(1)}, u32[]{:S(2)}, u32[]{:S(2)}) %collective-permute-start.14) | collective-permute-done | bytes 262176 | tf_op jit(solution)/shard_map/ppermute | solution.py:33
  130.5 7.9 %collective-permute-done.15.right.refs_7_.refs_3_ = f32[2,32,1024]{2,1,0:T(8,128)S(1)} collective-permute-done((f32[2,32,1024]{2,1,0:T(8,128)S(1)}, f32[2,32,1024]{2,1,0:T(8,128)S(1)}, u32[]{:S(2)}, u32[]{:S(2)}) %collective-permute-start.15) | collective-permute-done | bytes 262176 | tf_op jit(solution)/shard_map/ppermute | solution.py:33
  138.4 0.1 collective-permute-start.17
  138.5 0.1 collective-permute-start.18
  138.7 1.8 collective-permute-done.17.refs_5_.refs_1_
  140.5 1.9 %collective-permute-start.22 = (f32[2,10,4,1024]{3,2,1,0:T(4,128)S(1)}, f32[2,10,4,1024]{3,2,1,0:T(4,128)S(1)}, u32[]{:S(2)}, u32[]{:S(2)}) collective-permute-start(f32[2,10,4,1024]{3,2,1,0:T(4,128)S(1)} %get-tuple-element.43), channel_id=1, source_target_pairs={{0,1},{1,2},{2,3},{3,4},{4,5},{5,6},{6,7},{8,9},{9,10},{10,11},{11... | collective-permute-start | bytes 983048 | tf_op jit(solution)/shard_map/ppermute | solution.py:33
  142.4 3.9 %collective-permute-start.23 = (f32[2,10,4,1024]{3,2,1,0:T(4,128)S(1)}, f32[2,10,4,1024]{3,2,1,0:T(4,128)S(1)}, u32[]{:S(2)}, u32[]{:S(2)}) collective-permute-start(f32[2,10,4,1024]{3,2,1,0:T(4,128)S(1)} %get-tuple-element.44), channel_id=1, source_target_pairs={{1,0},{2,1},{3,2},{4,3},{5,4},{6,5},{7,6},{9,8},{10,9},{11,10},{12... | collective-permute-start | bytes 983048 | tf_op jit(solution)/shard_map/ppermute | solution.py:33
  146.4 7.7 %collective-permute-done.18.last = f32[2,32,1024]{2,1,0:T(8,128)S(1)} collective-permute-done((f32[2,32,1024]{2,1,0:T(8,128)S(1)}, f32[2,32,1024]{2,1,0:T(8,128)S(1)}, u32[]{:S(2)}, u32[]{:S(2)}) %collective-permute-start.18) | collective-permute-done | bytes 262176 | tf_op jit(solution)/shard_map/ppermute | solution.py:27
  154.1 0.1 shard_map.91.token.value.refs_6_
  154.1 1.9 %collective-permute-start.19 = (f32[2,32,1024]{2,1,0:T(8,128)S(1)}, f32[2,32,1024]{2,1,0:T(8,128)S(1)}, u32[]{:S(2)}, u32[]{:S(2)}) collective-permute-start(f32[2,32,1024]{2,1,0:T(8,128)S(1)} %shard_map.91.token.value.refs_6_), channel_id=1, source_target_pairs={{0,16},{8,24},{16,32},{24,40},{32,48},{40,56},{48,64},{56,72},{64,... | collective-permute-start | bytes 786440 | tf_op jit(solution)/shard_map/ppermute | solution.py:33
  156.0 3.9 %collective-permute-start.20 = (f32[2,32,1024]{2,1,0:T(8,128)S(1)}, f32[2,32,1024]{2,1,0:T(8,128)S(1)}, u32[]{:S(2)}, u32[]{:S(2)}) collective-permute-start(f32[2,32,1024]{2,1,0:T(8,128)S(1)} %shard_map.91.token.value.refs_6_), channel_id=1, source_target_pairs={{16,0},{24,8},{32,16},{40,24},{48,32},{56,40},{64,48},{72,56},{80,... | collective-permute-start | bytes 786440 | tf_op jit(solution)/shard_map/ppermute | solution.py:33
  160.0 1.0 collective-permute-done.23.high.refs_9_
  160.9 3.2 %shard_map.93 = (f32[10,80,1024]{2,1,0:T(8,128)S(1)}, f32[10,80,1024]{2,1,0:T(8,128)S(1)}, f32[10,80,1024]{2,1,0:T(8,128)S(1)}) custom-call(f32[2,64,1024]{2,1,0:T(8,128)S(1)} %collective-permute-done.3.left.refs_0_, f32[4,64,1024]{2,1,0:T(8,128)S(1)} %collective-permute-done.21.refs_1_.got, f32[2,64,1024]{2,1,0:T(8,128)S(1)} %copy-done.4, ...), custom_call_target="tpu_custom_call" | custom-call | flops 6600000000 | bytes 1048576 | tf_op jit(solution)/shard_map/pallas_call | solution.py:308
  164.1 0.1 collective-permute-done.19.left.refs_4_
  164.2 4.0 %collective-permute-done.20.right.refs_7_ = f32[2,32,1024]{2,1,0:T(8,128)S(1)} collective-permute-done((f32[2,32,1024]{2,1,0:T(8,128)S(1)}, f32[2,32,1024]{2,1,0:T(8,128)S(1)}, u32[]{:S(2)}, u32[]{:S(2)}) %collective-permute-start.20) | collective-permute-done | bytes 262176 | tf_op jit(solution)/shard_map/ppermute | solution.py:33
  168.3 0.1 collective-permute-start.24
  168.4 1.9 %collective-permute-done.24.refs_5_ = f32[4,32,1024]{2,1,0:T(8,128)S(1)} collective-permute-done((f32[4,32,1024]{2,1,0:T(8,128)S(1)}, f32[4,32,1024]{2,1,0:T(8,128)S(1)}, u32[]{:S(2)}, u32[]{:S(2)}) %collective-permute-start.24) | collective-permute-done | bytes 524320 | tf_op jit(solution)/shard_map/ppermute | solution.py:27
  170.3 9.0 %shard_map.95 = (f32[2,64,1024]{2,1,0:T(8,128)}, f32[2,64,1024]{2,1,0:T(8,128)}) custom-call(f32[2,32,1024]{2,1,0:T(8,128)S(1)} %collective-permute-done.14.left.refs_4_.refs_0_, f32[4,32,1024]{2,1,0:T(8,128)S(1)} %collective-permute-done.17.refs_5_.refs_1_, f32[2,32,1024]{2,1,0:T(8,128)S(1)} %shard_map.88.token.value.refs_6_.refs_2_, ...), custom_call_target="tpu_custom_call" | custom-call | flops 9900000256 | bytes 1048576 | tf_op jit(solution)/shard_map/pallas_call | solution.py:367
  (18 shorter events, 0.3 us)
Async XLA Ops:
  0.6 3.3 %copy-start.5 = (s32[8,64]{1,0:T(8,128)S(1)}, s32[8,64]{1,0:T(8,128)}, u32[]{:S(2)}) copy-start(s32[8,64]{1,0:T(8,128)} %offsets.7) | copy-start | bytes 6148
  0.6 3.3 %copy-start.2 = (bf16[8,64,1024]{2,1,0:T(8,128)(2,1)S(1)}, bf16[8,64,1024]{2,1,0:T(8,128)(2,1)}, u32[]{:S(2)}) copy-start(bf16[8,64,1024]{2,1,0:T(8,128)(2,1)} %proj.7) | copy-start | bytes 3145732
  0.6 3.3 %copy-start.1 = (bf16[8,1024,128]{2,1,0:T(8,128)(2,1)S(1)}, bf16[8,1024,128]{2,1,0:T(8,128)(2,1)}, u32[]{:S(2)}) copy-start(bf16[8,1024,128]{2,1,0:T(8,128)(2,1)} %weights.7) | copy-start | bytes 6291460
  1.3 2.7 %copy-start = (s32[3]{0:T(128)S(1)}, s32[3]{0:T(128)}, u32[]{:S(2)}) copy-start(s32[3]{0:T(128)} %pad_add_fusion.token.pos) | copy-start | bytes 40
  4.0 1.0 copy-start.3
  10.5 6.2 %copy-start.4 = (f32[2,64,1024]{2,1,0:T(8,128)S(1)}, f32[2,64,1024]{2,1,0:T(8,128)}, u32[]{:S(2)}) copy-start(f32[2,64,1024]{2,1,0:T(8,128)} %shard_map.77.token.value.refs_2_) | copy-start | bytes 1572868
  10.5 12.0 %collective-permute-start = (f32[4,4,2,32,1024]{4,3,2,1,0:T(8,128)S(1)}, f32[4,4,2,32,1024]{4,3,2,1,0:T(8,128)S(1)}, u32[]{:S(2)}, u32[]{:S(2)}) collective-permute-start(f32[4,4,2,32,1024]{4,3,2,1,0:T(8,128)S(1)} %shard_map.78), channel_id=1, source_target_pairs={{0,8},{8,0},{16,24},{24,16},{32,40},{40,32},{48,56},{56,48},{64,72... | collective-permute-start | bytes 12582920 | tf_op jit(solution)/shard_map/ppermute | solution.py:27
  16.1 46.8 %collective-permute-start.8 = (f32[4,4,2,32,1024]{4,3,2,1,0:T(8,128)S(1)}, f32[4,4,2,32,1024]{4,3,2,1,0:T(8,128)S(1)}, u32[]{:S(2)}, u32[]{:S(2)}) collective-permute-start(f32[4,4,2,32,1024]{4,3,2,1,0:T(8,128)S(1)} %shard_map.83), channel_id=1, source_target_pairs={{0,8},{8,0},{16,24},{24,16},{32,40},{40,32},{48,56},{56,48},{64,72... | collective-permute-start | bytes 12582920 | tf_op jit(solution)/shard_map/ppermute | solution.py:27
  16.6 16.7 %collective-permute-start.3 = (f32[2,64,1024]{2,1,0:T(8,128)S(1)}, f32[2,64,1024]{2,1,0:T(8,128)S(1)}, u32[]{:S(2)}, u32[]{:S(2)}) collective-permute-start(f32[2,64,1024]{2,1,0:T(8,128)S(1)} %copy-done.4), channel_id=1, source_target_pairs={{0,16},{8,24},{16,32},{24,40},{32,48},{40,56},{48,64},{56,72},{64,... | collective-permute-start | bytes 1572872 | tf_op jit(solution)/shard_map/ppermute | solution.py:33
  20.4 17.7 %collective-permute-start.4 = (f32[2,64,1024]{2,1,0:T(8,128)S(1)}, f32[2,64,1024]{2,1,0:T(8,128)S(1)}, u32[]{:S(2)}, u32[]{:S(2)}) collective-permute-start(f32[2,64,1024]{2,1,0:T(8,128)S(1)} %copy-done.4), channel_id=1, source_target_pairs={{16,0},{24,8},{32,16},{40,24},{48,32},{56,40},{64,48},{72,56},{80,... | collective-permute-start | bytes 1572872 | tf_op jit(solution)/shard_map/ppermute | solution.py:33
  28.0 26.8 %collective-permute-start.1 = (f32[4,2,32,1024]{3,2,1,0:T(8,128)S(1)}, f32[4,2,32,1024]{3,2,1,0:T(8,128)S(1)}, u32[]{:S(2)}, u32[]{:S(2)}) collective-permute-start(f32[4,2,32,1024]{3,2,1,0:T(8,128)S(1)} %get-tuple-element.27), channel_id=1, source_target_pairs={{0,16},{8,24},{16,32},{24,40},{32,48},{40,56},{48,0},{56,8},{64,80... | collective-permute-start | bytes 3145736 | tf_op jit(solution)/shard_map/ppermute | solution.py:27
  28.1 32.3 %collective-permute-start.2 = (f32[4,2,32,1024]{3,2,1,0:T(8,128)S(1)}, f32[4,2,32,1024]{3,2,1,0:T(8,128)S(1)}, u32[]{:S(2)}, u32[]{:S(2)}) collective-permute-start(f32[4,2,32,1024]{3,2,1,0:T(8,128)S(1)} %get-tuple-element.29), channel_id=1, source_target_pairs={{0,48},{8,56},{16,0},{24,8},{32,16},{40,24},{48,32},{56,40},{64,11... | collective-permute-start | bytes 3145736 | tf_op jit(solution)/shard_map/ppermute | solution.py:27
  60.6 15.0 %collective-permute-start.5 = (f32[2,2,32,1024]{3,2,1,0:T(8,128)S(1)}, f32[2,2,32,1024]{3,2,1,0:T(8,128)S(1)}, u32[]{:S(2)}, u32[]{:S(2)}) collective-permute-start(f32[2,2,32,1024]{3,2,1,0:T(8,128)S(1)} %get-tuple-element.30.token), channel_id=1, source_target_pairs={{0,16},{8,24},{16,32},{24,40},{32,48},{40,56},{48,0},{56,8},{64,80... | collective-permute-start | bytes 1572872 | tf_op jit(solution)/shard_map/ppermute | solution.py:27
  60.8 16.1 %collective-permute-start.6 = (f32[2,2,32,1024]{3,2,1,0:T(8,128)S(1)}, f32[2,2,32,1024]{3,2,1,0:T(8,128)S(1)}, u32[]{:S(2)}, u32[]{:S(2)}) collective-permute-start(f32[2,2,32,1024]{3,2,1,0:T(8,128)S(1)} %get-tuple-element.31), channel_id=1, source_target_pairs={{0,48},{8,56},{16,0},{24,8},{32,16},{40,24},{48,32},{56,40},{64,11... | collective-permute-start | bytes 1572872 | tf_op jit(solution)/shard_map/ppermute | solution.py:27
  68.3 28.8 %collective-permute-start.9 = (f32[4,2,32,1024]{3,2,1,0:T(8,128)S(1)}, f32[4,2,32,1024]{3,2,1,0:T(8,128)S(1)}, u32[]{:S(2)}, u32[]{:S(2)}) collective-permute-start(f32[4,2,32,1024]{3,2,1,0:T(8,128)S(1)} %get-tuple-element.35), channel_id=1, source_target_pairs={{0,16},{8,24},{16,32},{24,40},{32,48},{40,56},{48,0},{56,8},{64,80... | collective-permute-start | bytes 3145736 | tf_op jit(solution)/shard_map/ppermute | solution.py:27
  69.7 28.7 %collective-permute-start.10 = (f32[4,2,32,1024]{3,2,1,0:T(8,128)S(1)}, f32[4,2,32,1024]{3,2,1,0:T(8,128)S(1)}, u32[]{:S(2)}, u32[]{:S(2)}) collective-permute-start(f32[4,2,32,1024]{3,2,1,0:T(8,128)S(1)} %get-tuple-element.37), channel_id=1, source_target_pairs={{0,48},{8,56},{16,0},{24,8},{32,16},{40,24},{48,32},{56,40},{64,11... | collective-permute-start | bytes 3145736 | tf_op jit(solution)/shard_map/ppermute | solution.py:27
  77.1 23.6 %collective-permute-start.7 = (f32[2,2,32,1024]{3,2,1,0:T(8,128)S(1)}, f32[2,2,32,1024]{3,2,1,0:T(8,128)S(1)}, u32[]{:S(2)}, u32[]{:S(2)}) collective-permute-start(f32[2,2,32,1024]{3,2,1,0:T(8,128)S(1)} %get-tuple-element.33), channel_id=1, source_target_pairs={{0,64},{8,72},{16,80},{24,88},{32,96},{40,104},{48,112},{56,120},{... | collective-permute-start | bytes 1572872 | tf_op jit(solution)/shard_map/ppermute | solution.py:27
  98.6 13.1 %collective-permute-start.12 = (f32[2,2,32,1024]{3,2,1,0:T(8,128)S(1)}, f32[2,2,32,1024]{3,2,1,0:T(8,128)S(1)}, u32[]{:S(2)}, u32[]{:S(2)}) collective-permute-start(f32[2,2,32,1024]{3,2,1,0:T(8,128)S(1)} %get-tuple-element.38.token), channel_id=1, source_target_pairs={{0,16},{8,24},{16,32},{24,40},{32,48},{40,56},{48,0},{56,8},{64,80... | collective-permute-start | bytes 1572872 | tf_op jit(solution)/shard_map/ppermute | solution.py:27
  98.8 14.2 %collective-permute-start.13 = (f32[2,2,32,1024]{3,2,1,0:T(8,128)S(1)}, f32[2,2,32,1024]{3,2,1,0:T(8,128)S(1)}, u32[]{:S(2)}, u32[]{:S(2)}) collective-permute-start(f32[2,2,32,1024]{3,2,1,0:T(8,128)S(1)} %get-tuple-element.40), channel_id=1, source_target_pairs={{0,48},{8,56},{16,0},{24,8},{32,16},{40,24},{48,32},{56,40},{64,11... | collective-permute-start | bytes 1572872 | tf_op jit(solution)/shard_map/ppermute | solution.py:27
  100.7 14.6 %collective-permute-start.11 = (f32[2,32,1024]{2,1,0:T(8,128)S(1)}, f32[2,32,1024]{2,1,0:T(8,128)S(1)}, u32[]{:S(2)}, u32[]{:S(2)}) collective-permute-start(f32[2,32,1024]{2,1,0:T(8,128)S(1)} %shard_map.86.token), channel_id=1, source_target_pairs={{0,128},{8,136},{16,144},{24,152},{32,160},{40,168},{48,176},{56,1... | collective-permute-start | bytes 786440 | tf_op jit(solution)/shard_map/ppermute | solution.py:27
  113.3 14.4 %collective-permute-start.16 = (f32[2,2,32,1024]{3,2,1,0:T(8,128)S(1)}, f32[2,2,32,1024]{3,2,1,0:T(8,128)S(1)}, u32[]{:S(2)}, u32[]{:S(2)}) collective-permute-start(f32[2,2,32,1024]{3,2,1,0:T(8,128)S(1)} %get-tuple-element.42), channel_id=1, source_target_pairs={{0,64},{8,72},{16,80},{24,88},{32,96},{40,104},{48,112},{56,120},{... | collective-permute-start | bytes 1572872 | tf_op jit(solution)/shard_map/ppermute | solution.py:27
  115.3 23.4 %collective-permute-start.21 = (f32[4,64,1024]{2,1,0:T(8,128)S(1)}, f32[4,64,1024]{2,1,0:T(8,128)S(1)}, u32[]{:S(2)}, u32[]{:S(2)}) collective-permute-start(f32[4,64,1024]{2,1,0:T(8,128)S(1)} %shard_map.80.token), channel_id=1, source_target_pairs={{0,8},{8,0},{16,24},{24,16},{32,40},{40,32},{48,56},{56,48},{64,72... | collective-permute-start | bytes 3145736 | tf_op jit(solution)/shard_map/ppermute | solution.py:27
  115.3 15.2 %collective-permute-start.14 = (f32[2,32,1024]{2,1,0:T(8,128)S(1)}, f32[2,32,1024]{2,1,0:T(8,128)S(1)}, u32[]{:S(2)}, u32[]{:S(2)}) collective-permute-start(f32[2,32,1024]{2,1,0:T(8,128)S(1)} %shard_map.88.token.value.refs_6_.refs_2_), channel_id=1, source_target_pairs={{0,16},{8,24},{16,32},{24,40},{32,48},{40,56},{48,64},{56,72},{64,... | collective-permute-start | bytes 786440 | tf_op jit(solution)/shard_map/ppermute | solution.py:33
  117.3 21.1 %collective-permute-start.15 = (f32[2,32,1024]{2,1,0:T(8,128)S(1)}, f32[2,32,1024]{2,1,0:T(8,128)S(1)}, u32[]{:S(2)}, u32[]{:S(2)}) collective-permute-start(f32[2,32,1024]{2,1,0:T(8,128)S(1)} %shard_map.88.token.value.refs_6_.refs_2_), channel_id=1, source_target_pairs={{16,0},{24,8},{32,16},{40,24},{48,32},{56,40},{64,48},{72,56},{80,... | collective-permute-start | bytes 786440 | tf_op jit(solution)/shard_map/ppermute | solution.py:33
  138.4 2.0 %collective-permute-start.17 = (f32[4,32,1024]{2,1,0:T(8,128)S(1)}, f32[4,32,1024]{2,1,0:T(8,128)S(1)}, u32[]{:S(2)}, u32[]{:S(2)}) collective-permute-start(f32[4,32,1024]{2,1,0:T(8,128)S(1)} %shard_map.90), channel_id=1, source_target_pairs={{0,8},{8,0},{16,24},{24,16},{32,40},{40,32},{48,56},{56,48},{64,72... | collective-permute-start | bytes 1572872 | tf_op jit(solution)/shard_map/ppermute | solution.py:27
  138.5 15.5 %collective-permute-start.18 = (f32[2,32,1024]{2,1,0:T(8,128)S(1)}, f32[2,32,1024]{2,1,0:T(8,128)S(1)}, u32[]{:S(2)}, u32[]{:S(2)}) collective-permute-start(f32[2,32,1024]{2,1,0:T(8,128)S(1)} %shard_map.89.token), channel_id=1, source_target_pairs={{0,128},{8,136},{16,144},{24,152},{32,160},{40,168},{48,176},{56,1... | collective-permute-start | bytes 786440 | tf_op jit(solution)/shard_map/ppermute | solution.py:27
  140.5 19.5 %collective-permute-start.22 = (f32[2,10,4,1024]{3,2,1,0:T(4,128)S(1)}, f32[2,10,4,1024]{3,2,1,0:T(4,128)S(1)}, u32[]{:S(2)}, u32[]{:S(2)}) collective-permute-start(f32[2,10,4,1024]{3,2,1,0:T(4,128)S(1)} %get-tuple-element.43), channel_id=1, source_target_pairs={{0,1},{1,2},{2,3},{3,4},{4,5},{5,6},{6,7},{8,9},{9,10},{10,11},{11... | collective-permute-start | bytes 983048 | tf_op jit(solution)/shard_map/ppermute | solution.py:33
  142.4 18.5 %collective-permute-start.23 = (f32[2,10,4,1024]{3,2,1,0:T(4,128)S(1)}, f32[2,10,4,1024]{3,2,1,0:T(4,128)S(1)}, u32[]{:S(2)}, u32[]{:S(2)}) collective-permute-start(f32[2,10,4,1024]{3,2,1,0:T(4,128)S(1)} %get-tuple-element.44), channel_id=1, source_target_pairs={{1,0},{2,1},{3,2},{4,3},{5,4},{6,5},{7,6},{9,8},{10,9},{11,10},{12... | collective-permute-start | bytes 983048 | tf_op jit(solution)/shard_map/ppermute | solution.py:33
  154.1 10.1 %collective-permute-start.19 = (f32[2,32,1024]{2,1,0:T(8,128)S(1)}, f32[2,32,1024]{2,1,0:T(8,128)S(1)}, u32[]{:S(2)}, u32[]{:S(2)}) collective-permute-start(f32[2,32,1024]{2,1,0:T(8,128)S(1)} %shard_map.91.token.value.refs_6_), channel_id=1, source_target_pairs={{0,16},{8,24},{16,32},{24,40},{32,48},{40,56},{48,64},{56,72},{64,... | collective-permute-start | bytes 786440 | tf_op jit(solution)/shard_map/ppermute | solution.py:33
  156.0 12.2 %collective-permute-start.20 = (f32[2,32,1024]{2,1,0:T(8,128)S(1)}, f32[2,32,1024]{2,1,0:T(8,128)S(1)}, u32[]{:S(2)}, u32[]{:S(2)}) collective-permute-start(f32[2,32,1024]{2,1,0:T(8,128)S(1)} %shard_map.91.token.value.refs_6_), channel_id=1, source_target_pairs={{16,0},{24,8},{32,16},{40,24},{48,32},{56,40},{64,48},{72,56},{80,... | collective-permute-start | bytes 786440 | tf_op jit(solution)/shard_map/ppermute | solution.py:33
  168.3 2.0 %collective-permute-start.24 = (f32[4,32,1024]{2,1,0:T(8,128)S(1)}, f32[4,32,1024]{2,1,0:T(8,128)S(1)}, u32[]{:S(2)}, u32[]{:S(2)}) collective-permute-start(f32[4,32,1024]{2,1,0:T(8,128)S(1)} %shard_map.94), channel_id=1, source_target_pairs={{0,8},{8,0},{16,24},{24,16},{32,40},{40,32},{48,56},{56,48},{64,72... | collective-permute-start | bytes 1572872 | tf_op jit(solution)/shard_map/ppermute | solution.py:27

commit v4 on v3

--- a/solution.py
+++ b/solution.py
@@ -11,7 +11,8 @@
 CHUNKS = (((0, 16), (48, 16)), ((16, 32),))
 TILE = 256
 NEAR_US = 9.0
-SWAP_US = 14.0
+TOKEN = (8, 128)
+SWAP_US = 40.0
 ZL, X, C = 4, 4, 2
 VMEM_LIMIT = 26 * 1024 * 1024
 
@@ -86,7 +87,9 @@
         store(out.reshape(4, 4, 2, bands.shape[0] // 32, TILE), slice(n, n + TILE))
 
 
-def other_kernel(ranges, pos, offsets, proj, weights, token, out, wide, bands, flat, sems):
+def other_kernel(ranges, pos, offsets, proj, weights, token, out, done, wide, bands, flat, sems):
+    done[...] = jnp.zeros(done.shape, jnp.float32)
+
     def store(value, cols):
         out[:, :, :, :, cols] = value
 
@@ -135,7 +138,7 @@
     return pl.CostEstimate(flops=int(us * 1.1e9), bytes_accessed=2**20, transcendentals=0)
 
 
-def backproject(pos, offsets, proj, weights, ranges, token, recv=None):
+def backproject(pos, offsets, proj, weights, ranges, token, recv=None, us=6.0):
     angles, _, columns = proj.shape
     wide_y, band = weights.shape[1:]
     depth = sum(count for _, count in ranges)
@@ -149,7 +152,7 @@
         ],
         grid=(1,),
         compiler_params=pltpu.CompilerParams(vmem_limit_bytes=VMEM_LIMIT),
-        cost_estimate=cost(2.0 + depth / 8),
+        cost_estimate=cost(us),
     )
     specs = [SMEM, SMEM, full(proj.shape), ANY, ANY]
     f32 = lambda *shape: jax.ShapeDtypeStruct(shape, jnp.float32)
@@ -157,9 +160,9 @@
         shape = (4, 4, 2, depth, wide_y)
         return pl.pallas_call(
             functools.partial(other_kernel, ranges),
-            out_shape=f32(*shape),
+            out_shape=[f32(*shape), f32(*TOKEN)],
             in_specs=specs,
-            out_specs=full(shape),
+            out_specs=[full(shape), full(TOKEN)],
             **params,
         )(pos, offsets, proj, weights, token)
     shapes = [(n, 2, depth, wide_y) for n in (4, 4, 2, 2, 4)]
@@ -409,11 +412,12 @@
 class Chunk:
     def __init__(self, args, ranges, token):
         self.args, self.ranges = args, ranges
-        self.recv = shift_ang(backproject(*args, ranges, token), dc=1)
-
-    def first(self, token):
+        theirs, self.started = backproject(*args, ranges, token)
+        self.recv = shift_ang(theirs, dc=1)
+
+    def first(self, token, us=6.0):
         *send, holdp, holdm, self.home = backproject(
-            *self.args, self.ranges, token, self.recv
+            *self.args, self.ranges, token, self.recv, us=us
         )
         self.hold = holdp, holdm
         self.fromp = shift_ang(send[0], dx=1)
@@ -454,8 +458,8 @@
     conduct = conductivities(conductivity_table, phase, contact, pos)
     outer = Chunk(args, CHUNKS[0], conduct)
     cond, token = widened(core, conduct, pos, us=SWAP_US)
-    outer.first(pos)
     middle = Chunk(args, CHUNKS[1], pos)
+    outer.first(middle.started, us=1.0)
     middle.first(outer.second(token))
     outer.near_z(pos, us=NEAR_US)
     token = outer.far_z(middle.second(pos))

time: 182 us -> 178 us (0.978)
  waiting for transfers between devices: 98.7 us -> 86.8 us
  starting transfers between devices: 40.2 us -> 48.7 us
    ppermute x8, waiting for transfers between devices: 23.8 us -> 13.5 us  [shift_line(): return lax.ppermute(value, axis, perm)]
    ppermute x17, starting transfers between devices: 16.9 us -> 22.2 us  [shift_ang(): return lax.ppermute(value, 'ang', perm)]
    ppermute x8, starting transfers between devices: 23.4 us -> 26.5 us  [shift_line(): return lax.ppermute(value, axis, perm)]
  transfers between devices with their start and end apart: 25 -> 25, of which waited for: 19 -> 17; matrix products, arithmetic and copies ran while one was open for 0% -> 0% of each run, Pallas kernels for 11% -> 12%
where the time goes in v4:
time: 178 us; the launch traced here: 176 us
  waiting for transfers between devices  86.8 us (49%)
  starting transfers between devices  48.7 us (27%)
  Pallas kernels  37.7 us (21%)
    ppermute x17, waiting for transfers between devices, shift_ang(): return lax.ppermute(value, 'ang', perm)  73.2 us
    ppermute x8, starting transfers between devices, shift_line(): return lax.ppermute(value, axis, perm)  26.5 us
    ppermute x17, starting transfers between devices, shift_ang(): return lax.ppermute(value, 'ang', perm)  22.2 us
    ppermute x8, waiting for transfers between devices, shift_line(): return lax.ppermute(value, axis, perm)  13.5 us
    pallas_call x2, Pallas kernels, backproject(): pl.pallas_call(functools.partial(mine_kernel, ranges), out_shape=[f32(*s)...  11 us
    pallas_call x2, Pallas kernels, backproject(): pl.pallas_call(functools.partial(other_kernel, ranges), out_shape=[f32(*s...  10.9 us
    pallas_call x1, Pallas kernels, conduct_heat(): pl.pallas_call(functools.partial(heat_kernel, [c for c, _ in groups]), ou...  9.04 us
  transfers between devices with their start and end apart: 25, of which 17 were waited for; matrix products, arithmetic and copies ran while one was open for 0% of the time, Pallas kernels for 12%

profile of v4, /device:TPU:30, one launch (start us, length us, event | category | flops | bytes accessed | tf_op | source)
XLA Modules:
  0.0 175.8 jit_solution(11812953309869599602)
XLA Ops:
  0.7 0.6 pad_add_fusion.pos.token
  1.3 2.7 %shard_map.78.token.value.refs_2_ = f32[2,64,1024]{2,1,0:T(8,128)} custom-call(f32[4,4]{1,0:T(4,128)} %table.1, s32[2,64,1024]{2,1,0:T(8,128)} %phase.1, s32[2,64,1024]{2,1,0:T(8,128)} %contact.1, s32[3]{0:T(128)} %pad_add_fusion.pos.token), custom_call_target="tpu_custom_call" | custom-call | flops 2200000000 | bytes 1048576 | tf_op jit(solution)/shard_map/pallas_call | solution.py:201
  4.0 0.0 copy-start.4
  4.0 1.0 copy-done.4
  5.0 5.5 %shard_map.79 = (f32[4,4,2,32,1024]{4,3,2,1,0:T(8,128)S(1)}, f32[8,128]{1,0:T(8,128)}) custom-call(s32[3]{0:T(128)S(1)} %copy-done.3, s32[8,64]{1,0:T(8,128)S(1)} %copy-done.2, bf16[8,64,1024]{2,1,0:T(8,128)(2,1)S(1)} %copy-done.1, bf16[8,1024,128]{2,1,0:T(8,128)(2,1)S(1)} %copy-done, f32[2,64,1024]{2,1,0:T(8,128)S(1)} %copy-done.4), custom_call_target="tpu_custom_call" | custom-call | flops 6600000000 | bytes 1048576 | tf_op jit(solution)/shard_map/pallas_call | solution.py:161
  10.5 0.1 collective-permute-start
  10.6 3.7 %collective-permute-start.3 = (f32[2,64,1024]{2,1,0:T(8,128)S(1)}, f32[2,64,1024]{2,1,0:T(8,128)S(1)}, u32[]{:S(2)}, u32[]{:S(2)}) collective-permute-start(f32[2,64,1024]{2,1,0:T(8,128)S(1)} %copy-done.4), channel_id=1, source_target_pairs={{0,16},{8,24},{16,32},{24,40},{32,48},{40,56},{48,64},{56,72},{64,... | collective-permute-start | bytes 1572872 | tf_op jit(solution)/shard_map/ppermute | solution.py:34
  14.3 2.1 %collective-permute-start.4 = (f32[2,64,1024]{2,1,0:T(8,128)S(1)}, f32[2,64,1024]{2,1,0:T(8,128)S(1)}, u32[]{:S(2)}, u32[]{:S(2)}) collective-permute-start(f32[2,64,1024]{2,1,0:T(8,128)S(1)} %copy-done.4), channel_id=1, source_target_pairs={{16,0},{24,8},{32,16},{40,24},{48,32},{56,40},{64,48},{72,56},{80,... | collective-permute-start | bytes 1572872 | tf_op jit(solution)/shard_map/ppermute | solution.py:34
  16.5 5.5 %shard_map.77 = (f32[4,4,2,32,1024]{4,3,2,1,0:T(8,128)S(1)}, f32[8,128]{1,0:T(8,128)S(1)}) custom-call(s32[3]{0:T(128)S(1)} %copy-done.3, s32[8,64]{1,0:T(8,128)S(1)} %copy-done.2, bf16[8,64,1024]{2,1,0:T(8,128)(2,1)S(1)} %copy-done.1, bf16[8,1024,128]{2,1,0:T(8,128)(2,1)S(1)} %copy-done, s32[3]{0:T(128)S(1)} %copy-done.3), custom_call_target="tpu_custom_call" | custom-call | flops 6600000000 | bytes 1048576 | tf_op jit(solution)/shard_map/pallas_call | solution.py:161
  21.9 0.1 collective-permute-start.8
  22.0 0.0 collective-permute-done.recv
  22.0 5.5 %shard_map.80 = (f32[4,2,32,1024]{3,2,1,0:T(8,128)S(1)}, f32[4,2,32,1024]{3,2,1,0:T(8,128)S(1)}, f32[2,2,32,1024]{3,2,1,0:T(8,128)S(1)}, f32[2,2,32,1024]{3,2,1,0:T(8,128)S(1)}, f32[4,2,32,1024]{3,2,1,0:T(8,128)S(1)}) custom-call(s32[3]{0:T(128)S(1)} %copy-done.3, s32[8,64]{1,0:T(8,128)S(1)} %copy-done.2, bf16[8,64,1024]{2,1,0:T(8,128)(2,1)S(1)} %copy-done.1, ...), custom_call_target="tpu_custom_call" | custom-call | flops 1100000000 | bytes 1048576 | tf_op jit(solution)/shard_map/pallas_call | solution.py:169
  27.5 0.1 collective-permute-start.1
  27.6 2.0 %collective-permute-start.2 = (f32[4,2,32,1024]{3,2,1,0:T(8,128)S(1)}, f32[4,2,32,1024]{3,2,1,0:T(8,128)S(1)}, u32[]{:S(2)}, u32[]{:S(2)}) collective-permute-start(f32[4,2,32,1024]{3,2,1,0:T(8,128)S(1)} %get-tuple-element.34), channel_id=1, source_target_pairs={{0,48},{8,56},{16,0},{24,8},{32,16},{40,24},{48,32},{56,40},{64,11... | collective-permute-start | bytes 3145736 | tf_op jit(solution)/shard_map/ppermute | solution.py:28
  29.6 0.0 collective-permute-done.3.left.refs_0_
  29.6 2.8 %collective-permute-done.4.right.refs_3_ = f32[2,64,1024]{2,1,0:T(8,128)S(1)} collective-permute-done((f32[2,64,1024]{2,1,0:T(8,128)S(1)}, f32[2,64,1024]{2,1,0:T(8,128)S(1)}, u32[]{:S(2)}, u32[]{:S(2)}) %collective-permute-start.4) | collective-permute-done | bytes 524320 | tf_op jit(solution)/shard_map/ppermute | solution.py:34
  32.4 0.1 shard_map.81.token
  32.5 20.7 %collective-permute-done.1.fromp = f32[4,2,32,1024]{3,2,1,0:T(8,128)S(1)} collective-permute-done((f32[4,2,32,1024]{3,2,1,0:T(8,128)S(1)}, f32[4,2,32,1024]{3,2,1,0:T(8,128)S(1)}, u32[]{:S(2)}, u32[]{:S(2)}) %collective-permute-start.1) | collective-permute-done | bytes 1048608 | tf_op jit(solution)/shard_map/ppermute | solution.py:28
  53.2 1.7 collective-permute-done.2.fromm
  54.9 0.1 shard_map.82
  55.0 0.3 collective-permute-start.5
  55.3 2.0 %collective-permute-start.6 = (f32[2,2,32,1024]{3,2,1,0:T(8,128)S(1)}, f32[2,2,32,1024]{3,2,1,0:T(8,128)S(1)}, u32[]{:S(2)}, u32[]{:S(2)}) collective-permute-start(f32[2,2,32,1024]{3,2,1,0:T(8,128)S(1)} %get-tuple-element.36), channel_id=1, source_target_pairs={{0,48},{8,56},{16,0},{24,8},{32,16},{40,24},{48,32},{56,40},{64,11... | collective-permute-start | bytes 1572872 | tf_op jit(solution)/shard_map/ppermute | solution.py:28
  57.2 0.0 collective-permute-done.8.recv
  57.2 5.5 %shard_map.84 = (f32[4,2,32,1024]{3,2,1,0:T(8,128)S(1)}, f32[4,2,32,1024]{3,2,1,0:T(8,128)S(1)}, f32[2,2,32,1024]{3,2,1,0:T(8,128)S(1)}, f32[2,2,32,1024]{3,2,1,0:T(8,128)S(1)}, f32[4,2,32,1024]{3,2,1,0:T(8,128)S(1)}) custom-call(s32[3]{0:T(128)S(1)} %copy-done.3, s32[8,64]{1,0:T(8,128)S(1)} %copy-done.2, bf16[8,64,1024]{2,1,0:T(8,128)(2,1)S(1)} %copy-done.1, ...), custom_call_target="tpu_custom_call" | custom-call | flops 6600000000 | bytes 1048576 | tf_op jit(solution)/shard_map/pallas_call | solution.py:169
  62.8 1.4 collective-permute-start.9
  64.1 0.7 collective-permute-start.10
  64.9 5.1 %collective-permute-done.5.lastp = f32[2,2,32,1024]{3,2,1,0:T(8,128)S(1)} collective-permute-done((f32[2,2,32,1024]{3,2,1,0:T(8,128)S(1)}, f32[2,2,32,1024]{3,2,1,0:T(8,128)S(1)}, u32[]{:S(2)}, u32[]{:S(2)}) %collective-permute-start.5) | collective-permute-done | bytes 524320 | tf_op jit(solution)/shard_map/ppermute | solution.py:28
  70.0 1.3 collective-permute-done.6.lastm
  71.3 0.2 shard_map.83
  71.5 4.1 %collective-permute-start.7 = (f32[2,2,32,1024]{3,2,1,0:T(8,128)S(1)}, f32[2,2,32,1024]{3,2,1,0:T(8,128)S(1)}, u32[]{:S(2)}, u32[]{:S(2)}) collective-permute-start(f32[2,2,32,1024]{3,2,1,0:T(8,128)S(1)} %get-tuple-element.38), channel_id=1, source_target_pairs={{0,64},{8,72},{16,80},{24,88},{32,96},{40,104},{48,112},{56,120},{... | collective-permute-start | bytes 1572872 | tf_op jit(solution)/shard_map/ppermute | solution.py:28
  75.6 16.0 %collective-permute-done.9.fromp = f32[4,2,32,1024]{3,2,1,0:T(8,128)S(1)} collective-permute-done((f32[4,2,32,1024]{3,2,1,0:T(8,128)S(1)}, f32[4,2,32,1024]{3,2,1,0:T(8,128)S(1)}, u32[]{:S(2)}, u32[]{:S(2)}) %collective-permute-start.9) | collective-permute-done | bytes 1048608 | tf_op jit(solution)/shard_map/ppermute | solution.py:28
  91.5 1.3 collective-permute-done.10.fromm
  92.8 0.1 shard_map.85
  93.0 0.3 collective-permute-start.12
  93.2 1.8 %collective-permute-start.13 = (f32[2,2,32,1024]{3,2,1,0:T(8,128)S(1)}, f32[2,2,32,1024]{3,2,1,0:T(8,128)S(1)}, u32[]{:S(2)}, u32[]{:S(2)}) collective-permute-start(f32[2,2,32,1024]{3,2,1,0:T(8,128)S(1)} %get-tuple-element.46), channel_id=1, source_target_pairs={{0,48},{8,56},{16,0},{24,8},{32,16},{40,24},{48,32},{56,40},{64,11... | collective-permute-start | bytes 1572872 | tf_op jit(solution)/shard_map/ppermute | solution.py:28
  95.1 0.0 collective-permute-done.7.got
  95.1 4.8 %collective-permute-start.11 = (f32[2,32,1024]{2,1,0:T(8,128)S(1)}, f32[2,32,1024]{2,1,0:T(8,128)S(1)}, u32[]{:S(2)}, u32[]{:S(2)}) collective-permute-start(f32[2,32,1024]{2,1,0:T(8,128)S(1)} %shard_map.86.token), channel_id=1, source_target_pairs={{0,128},{8,136},{16,144},{24,152},{32,160},{40,168},{48,176},{56,1... | collective-permute-start | bytes 786440 | tf_op jit(solution)/shard_map/ppermute | solution.py:28
  99.9 6.1 %collective-permute-done.12.lastp = f32[2,2,32,1024]{3,2,1,0:T(8,128)S(1)} collective-permute-done((f32[2,2,32,1024]{3,2,1,0:T(8,128)S(1)}, f32[2,2,32,1024]{3,2,1,0:T(8,128)S(1)}, u32[]{:S(2)}, u32[]{:S(2)}) %collective-permute-start.12) | collective-permute-done | bytes 524320 | tf_op jit(solution)/shard_map/ppermute | solution.py:28
  106.0 1.4 collective-permute-done.13.lastm
  107.5 0.2 shard_map.87
  107.6 2.9 %collective-permute-start.16 = (f32[2,2,32,1024]{3,2,1,0:T(8,128)S(1)}, f32[2,2,32,1024]{3,2,1,0:T(8,128)S(1)}, u32[]{:S(2)}, u32[]{:S(2)}) collective-permute-start(f32[2,2,32,1024]{3,2,1,0:T(8,128)S(1)} %get-tuple-element.48), channel_id=1, source_target_pairs={{0,64},{8,72},{16,80},{24,88},{32,96},{40,104},{48,112},{56,120},{... | collective-permute-start | bytes 1572872 | tf_op jit(solution)/shard_map/ppermute | solution.py:28
  110.6 0.0 copy-start.5
  110.6 3.4 %collective-permute-start.14 = (f32[2,32,1024]{2,1,0:T(8,128)S(1)}, f32[2,32,1024]{2,1,0:T(8,128)S(1)}, u32[]{:S(2)}, u32[]{:S(2)}) collective-permute-start(f32[2,32,1024]{2,1,0:T(8,128)S(1)} %shard_map.88.token.value.refs_6_.refs_2_), channel_id=1, source_target_pairs={{0,16},{8,24},{16,32},{24,40},{32,48},{40,56},{48,64},{56,72},{64,... | collective-permute-start | bytes 786440 | tf_op jit(solution)/shard_map/ppermute | solution.py:34
  114.0 2.6 %collective-permute-start.15 = (f32[2,32,1024]{2,1,0:T(8,128)S(1)}, f32[2,32,1024]{2,1,0:T(8,128)S(1)}, u32[]{:S(2)}, u32[]{:S(2)}) collective-permute-start(f32[2,32,1024]{2,1,0:T(8,128)S(1)} %shard_map.88.token.value.refs_6_.refs_2_), channel_id=1, source_target_pairs={{16,0},{24,8},{32,16},{40,24},{48,32},{56,40},{64,48},{72,56},{80,... | collective-permute-start | bytes 786440 | tf_op jit(solution)/shard_map/ppermute | solution.py:34
  116.6 5.7 %collective-permute-done.16.got = f32[2,2,32,1024]{3,2,1,0:T(8,128)S(1)} collective-permute-done((f32[2,2,32,1024]{3,2,1,0:T(8,128)S(1)}, f32[2,2,32,1024]{3,2,1,0:T(8,128)S(1)}, u32[]{:S(2)}, u32[]{:S(2)}) %collective-permute-start.16) | collective-permute-done | bytes 524320 | tf_op jit(solution)/shard_map/ppermute | solution.py:28
  122.3 2.8 %collective-permute-done.14.left.refs_4_.refs_0_ = f32[2,32,1024]{2,1,0:T(8,128)S(1)} collective-permute-done((f32[2,32,1024]{2,1,0:T(8,128)S(1)}, f32[2,32,1024]{2,1,0:T(8,128)S(1)}, u32[]{:S(2)}, u32[]{:S(2)}) %collective-permute-start.14) | collective-permute-done | bytes 262176 | tf_op jit(solution)/shard_map/ppermute | solution.py:34
  125.1 2.9 %collective-permute-done.15.right.refs_7_.refs_3_ = f32[2,32,1024]{2,1,0:T(8,128)S(1)} collective-permute-done((f32[2,32,1024]{2,1,0:T(8,128)S(1)}, f32[2,32,1024]{2,1,0:T(8,128)S(1)}, u32[]{:S(2)}, u32[]{:S(2)}) %collective-permute-start.15) | collective-permute-done | bytes 262176 | tf_op jit(solution)/shard_map/ppermute | solution.py:34
  128.1 0.1 collective-permute-start.17
  128.2 1.4 collective-permute-start.18
  129.6 0.0 collective-permute-done.21.refs_1_.got
  129.6 0.5 collective-permute-done.17.refs_5_.refs_1_
  130.1 7.0 %collective-permute-start.22 = (f32[2,10,4,1024]{3,2,1,0:T(4,128)S(1)}, f32[2,10,4,1024]{3,2,1,0:T(4,128)S(1)}, u32[]{:S(2)}, u32[]{:S(2)}) collective-permute-start(f32[2,10,4,1024]{3,2,1,0:T(4,128)S(1)} %get-tuple-element.49), channel_id=1, source_target_pairs={{0,1},{1,2},{2,3},{3,4},{4,5},{5,6},{6,7},{8,9},{9,10},{10,11},{11... | collective-permute-start | bytes 983048 | tf_op jit(solution)/shard_map/ppermute | solution.py:34
  137.1 1.9 %collective-permute-start.23 = (f32[2,10,4,1024]{3,2,1,0:T(4,128)S(1)}, f32[2,10,4,1024]{3,2,1,0:T(4,128)S(1)}, u32[]{:S(2)}, u32[]{:S(2)}) collective-permute-start(f32[2,10,4,1024]{3,2,1,0:T(4,128)S(1)} %get-tuple-element.50), channel_id=1, source_target_pairs={{1,0},{2,1},{3,2},{4,3},{5,4},{6,5},{7,6},{9,8},{10,9},{11,10},{12... | collective-permute-start | bytes 983048 | tf_op jit(solution)/shard_map/ppermute | solution.py:34
  139.0 11.5 %collective-permute-done.18.last = f32[2,32,1024]{2,1,0:T(8,128)S(1)} collective-permute-done((f32[2,32,1024]{2,1,0:T(8,128)S(1)}, f32[2,32,1024]{2,1,0:T(8,128)S(1)}, u32[]{:S(2)}, u32[]{:S(2)}) %collective-permute-start.18) | collective-permute-done | bytes 262176 | tf_op jit(solution)/shard_map/ppermute | solution.py:28
  150.6 0.1 shard_map.91.token.value.refs_6_
  150.6 1.9 %collective-permute-start.19 = (f32[2,32,1024]{2,1,0:T(8,128)S(1)}, f32[2,32,1024]{2,1,0:T(8,128)S(1)}, u32[]{:S(2)}, u32[]{:S(2)}) collective-permute-start(f32[2,32,1024]{2,1,0:T(8,128)S(1)} %shard_map.91.token.value.refs_6_), channel_id=1, source_target_pairs={{0,16},{8,24},{16,32},{24,40},{32,48},{40,56},{48,64},{56,72},{64,... | collective-permute-start | bytes 786440 | tf_op jit(solution)/shard_map/ppermute | solution.py:34
  152.5 3.9 %collective-permute-start.20 = (f32[2,32,1024]{2,1,0:T(8,128)S(1)}, f32[2,32,1024]{2,1,0:T(8,128)S(1)}, u32[]{:S(2)}, u32[]{:S(2)}) collective-permute-start(f32[2,32,1024]{2,1,0:T(8,128)S(1)} %shard_map.91.token.value.refs_6_), channel_id=1, source_target_pairs={{16,0},{24,8},{32,16},{40,24},{48,32},{56,40},{64,48},{72,56},{80,... | collective-permute-start | bytes 786440 | tf_op jit(solution)/shard_map/ppermute | solution.py:34
  156.5 0.0 collective-permute-done.22.low.refs_8_
  156.5 3.2 %shard_map.93 = (f32[10,80,1024]{2,1,0:T(8,128)S(1)}, f32[10,80,1024]{2,1,0:T(8,128)S(1)}, f32[10,80,1024]{2,1,0:T(8,128)S(1)}) custom-call(f32[2,64,1024]{2,1,0:T(8,128)S(1)} %collective-permute-done.3.left.refs_0_, f32[4,64,1024]{2,1,0:T(8,128)S(1)} %collective-permute-done.21.refs_1_.got, f32[2,64,1024]{2,1,0:T(8,128)S(1)} %copy-done.5, ...), custom_call_target="tpu_custom_call" | custom-call | flops 6600000000 | bytes 1048576 | tf_op jit(solution)/shard_map/pallas_call | solution.py:311
  159.7 1.0 collective-permute-done.19.left.refs_4_
  160.7 4.0 %collective-permute-done.20.right.refs_7_ = f32[2,32,1024]{2,1,0:T(8,128)S(1)} collective-permute-done((f32[2,32,1024]{2,1,0:T(8,128)S(1)}, f32[2,32,1024]{2,1,0:T(8,128)S(1)}, u32[]{:S(2)}, u32[]{:S(2)}) %collective-permute-start.20) | collective-permute-done | bytes 262176 | tf_op jit(solution)/shard_map/ppermute | solution.py:34
  164.7 0.1 collective-permute-start.24
  164.8 1.9 %collective-permute-done.24.refs_5_ = f32[4,32,1024]{2,1,0:T(8,128)S(1)} collective-permute-done((f32[4,32,1024]{2,1,0:T(8,128)S(1)}, f32[4,32,1024]{2,1,0:T(8,128)S(1)}, u32[]{:S(2)}, u32[]{:S(2)}) %collective-permute-start.24) | collective-permute-done | bytes 524320 | tf_op jit(solution)/shard_map/ppermute | solution.py:28
  166.7 9.0 %shard_map.95 = (f32[2,64,1024]{2,1,0:T(8,128)}, f32[2,64,1024]{2,1,0:T(8,128)}) custom-call(f32[2,32,1024]{2,1,0:T(8,128)S(1)} %collective-permute-done.14.left.refs_4_.refs_0_, f32[4,32,1024]{2,1,0:T(8,128)S(1)} %collective-permute-done.17.refs_5_.refs_1_, f32[2,32,1024]{2,1,0:T(8,128)S(1)} %shard_map.88.token.value.refs_6_.refs_2_, ...), custom_call_target="tpu_custom_call" | custom-call | flops 9900000256 | bytes 1048576 | tf_op jit(solution)/shard_map/pallas_call | solution.py:370
  (18 shorter events, 0.2 us)
Async XLA Ops:
  0.6 3.3 %copy-start.2 = (s32[8,64]{1,0:T(8,128)S(1)}, s32[8,64]{1,0:T(8,128)}, u32[]{:S(2)}) copy-start(s32[8,64]{1,0:T(8,128)} %offsets.7) | copy-start | bytes 6148
  0.6 3.3 %copy-start.1 = (bf16[8,64,1024]{2,1,0:T(8,128)(2,1)S(1)}, bf16[8,64,1024]{2,1,0:T(8,128)(2,1)}, u32[]{:S(2)}) copy-start(bf16[8,64,1024]{2,1,0:T(8,128)(2,1)} %proj.7) | copy-start | bytes 3145732
  0.6 3.3 %copy-start = (bf16[8,1024,128]{2,1,0:T(8,128)(2,1)S(1)}, bf16[8,1024,128]{2,1,0:T(8,128)(2,1)}, u32[]{:S(2)}) copy-start(bf16[8,1024,128]{2,1,0:T(8,128)(2,1)} %weights.7) | copy-start | bytes 6291460
  1.3 2.7 %copy-start.3 = (s32[3]{0:T(128)S(1)}, s32[3]{0:T(128)}, u32[]{:S(2)}) copy-start(s32[3]{0:T(128)} %pad_add_fusion.pos.token) | copy-start | bytes 40
  4.0 1.0 copy-start.4
  10.5 11.5 %collective-permute-start = (f32[4,4,2,32,1024]{4,3,2,1,0:T(8,128)S(1)}, f32[4,4,2,32,1024]{4,3,2,1,0:T(8,128)S(1)}, u32[]{:S(2)}, u32[]{:S(2)}) collective-permute-start(f32[4,4,2,32,1024]{4,3,2,1,0:T(8,128)S(1)} %get-tuple-element.29), channel_id=1, source_target_pairs={{0,8},{8,0},{16,24},{24,16},{32,40},{40,32},{48,56},{56,48},{64,72... | collective-permute-start | bytes 12582920 | tf_op jit(solution)/shard_map/ppermute | solution.py:28
  10.6 19.1 %collective-permute-start.3 = (f32[2,64,1024]{2,1,0:T(8,128)S(1)}, f32[2,64,1024]{2,1,0:T(8,128)S(1)}, u32[]{:S(2)}, u32[]{:S(2)}) collective-permute-start(f32[2,64,1024]{2,1,0:T(8,128)S(1)} %copy-done.4), channel_id=1, source_target_pairs={{0,16},{8,24},{16,32},{24,40},{32,48},{40,56},{48,64},{56,72},{64,... | collective-permute-start | bytes 1572872 | tf_op jit(solution)/shard_map/ppermute | solution.py:34
  14.3 18.1 %collective-permute-start.4 = (f32[2,64,1024]{2,1,0:T(8,128)S(1)}, f32[2,64,1024]{2,1,0:T(8,128)S(1)}, u32[]{:S(2)}, u32[]{:S(2)}) collective-permute-start(f32[2,64,1024]{2,1,0:T(8,128)S(1)} %copy-done.4), channel_id=1, source_target_pairs={{16,0},{24,8},{32,16},{40,24},{48,32},{56,40},{64,48},{72,56},{80,... | collective-permute-start | bytes 1572872 | tf_op jit(solution)/shard_map/ppermute | solution.py:34
  21.9 35.3 %collective-permute-start.8 = (f32[4,4,2,32,1024]{4,3,2,1,0:T(8,128)S(1)}, f32[4,4,2,32,1024]{4,3,2,1,0:T(8,128)S(1)}, u32[]{:S(2)}, u32[]{:S(2)}) collective-permute-start(f32[4,4,2,32,1024]{4,3,2,1,0:T(8,128)S(1)} %get-tuple-element.39), channel_id=1, source_target_pairs={{0,8},{8,0},{16,24},{24,16},{32,40},{40,32},{48,56},{56,48},{64,72... | collective-permute-start | bytes 12582920 | tf_op jit(solution)/shard_map/ppermute | solution.py:28
  27.5 25.6 %collective-permute-start.1 = (f32[4,2,32,1024]{3,2,1,0:T(8,128)S(1)}, f32[4,2,32,1024]{3,2,1,0:T(8,128)S(1)}, u32[]{:S(2)}, u32[]{:S(2)}) collective-permute-start(f32[4,2,32,1024]{3,2,1,0:T(8,128)S(1)} %get-tuple-element.32), channel_id=1, source_target_pairs={{0,16},{8,24},{16,32},{24,40},{32,48},{40,56},{48,0},{56,8},{64,80... | collective-permute-start | bytes 3145736 | tf_op jit(solution)/shard_map/ppermute | solution.py:28
  27.6 27.2 %collective-permute-start.2 = (f32[4,2,32,1024]{3,2,1,0:T(8,128)S(1)}, f32[4,2,32,1024]{3,2,1,0:T(8,128)S(1)}, u32[]{:S(2)}, u32[]{:S(2)}) collective-permute-start(f32[4,2,32,1024]{3,2,1,0:T(8,128)S(1)} %get-tuple-element.34), channel_id=1, source_target_pairs={{0,48},{8,56},{16,0},{24,8},{32,16},{40,24},{48,32},{56,40},{64,11... | collective-permute-start | bytes 3145736 | tf_op jit(solution)/shard_map/ppermute | solution.py:28
  55.0 15.0 %collective-permute-start.5 = (f32[2,2,32,1024]{3,2,1,0:T(8,128)S(1)}, f32[2,2,32,1024]{3,2,1,0:T(8,128)S(1)}, u32[]{:S(2)}, u32[]{:S(2)}) collective-permute-start(f32[2,2,32,1024]{3,2,1,0:T(8,128)S(1)} %get-tuple-element.35.token), channel_id=1, source_target_pairs={{0,16},{8,24},{16,32},{24,40},{32,48},{40,56},{48,0},{56,8},{64,80... | collective-permute-start | bytes 1572872 | tf_op jit(solution)/shard_map/ppermute | solution.py:28
  55.3 16.1 %collective-permute-start.6 = (f32[2,2,32,1024]{3,2,1,0:T(8,128)S(1)}, f32[2,2,32,1024]{3,2,1,0:T(8,128)S(1)}, u32[]{:S(2)}, u32[]{:S(2)}) collective-permute-start(f32[2,2,32,1024]{3,2,1,0:T(8,128)S(1)} %get-tuple-element.36), channel_id=1, source_target_pairs={{0,48},{8,56},{16,0},{24,8},{32,16},{40,24},{48,32},{56,40},{64,11... | collective-permute-start | bytes 1572872 | tf_op jit(solution)/shard_map/ppermute | solution.py:28
  62.8 28.8 %collective-permute-start.9 = (f32[4,2,32,1024]{3,2,1,0:T(8,128)S(1)}, f32[4,2,32,1024]{3,2,1,0:T(8,128)S(1)}, u32[]{:S(2)}, u32[]{:S(2)}) collective-permute-start(f32[4,2,32,1024]{3,2,1,0:T(8,128)S(1)} %get-tuple-element.41), channel_id=1, source_target_pairs={{0,16},{8,24},{16,32},{24,40},{32,48},{40,56},{48,0},{56,8},{64,80... | collective-permute-start | bytes 3145736 | tf_op jit(solution)/shard_map/ppermute | solution.py:28
  64.1 28.7 %collective-permute-start.10 = (f32[4,2,32,1024]{3,2,1,0:T(8,128)S(1)}, f32[4,2,32,1024]{3,2,1,0:T(8,128)S(1)}, u32[]{:S(2)}, u32[]{:S(2)}) collective-permute-start(f32[4,2,32,1024]{3,2,1,0:T(8,128)S(1)} %get-tuple-element.43), channel_id=1, source_target_pairs={{0,48},{8,56},{16,0},{24,8},{32,16},{40,24},{48,32},{56,40},{64,11... | collective-permute-start | bytes 3145736 | tf_op jit(solution)/shard_map/ppermute | solution.py:28
  71.5 23.6 %collective-permute-start.7 = (f32[2,2,32,1024]{3,2,1,0:T(8,128)S(1)}, f32[2,2,32,1024]{3,2,1,0:T(8,128)S(1)}, u32[]{:S(2)}, u32[]{:S(2)}) collective-permute-start(f32[2,2,32,1024]{3,2,1,0:T(8,128)S(1)} %get-tuple-element.38), channel_id=1, source_target_pairs={{0,64},{8,72},{16,80},{24,88},{32,96},{40,104},{48,112},{56,120},{... | collective-permute-start | bytes 1572872 | tf_op jit(solution)/shard_map/ppermute | solution.py:28
  93.0 13.1 %collective-permute-start.12 = (f32[2,2,32,1024]{3,2,1,0:T(8,128)S(1)}, f32[2,2,32,1024]{3,2,1,0:T(8,128)S(1)}, u32[]{:S(2)}, u32[]{:S(2)}) collective-permute-start(f32[2,2,32,1024]{3,2,1,0:T(8,128)S(1)} %get-tuple-element.44.token), channel_id=1, source_target_pairs={{0,16},{8,24},{16,32},{24,40},{32,48},{40,56},{48,0},{56,8},{64,80... | collective-permute-start | bytes 1572872 | tf_op jit(solution)/shard_map/ppermute | solution.py:28
  93.2 14.2 %collective-permute-start.13 = (f32[2,2,32,1024]{3,2,1,0:T(8,128)S(1)}, f32[2,2,32,1024]{3,2,1,0:T(8,128)S(1)}, u32[]{:S(2)}, u32[]{:S(2)}) collective-permute-start(f32[2,2,32,1024]{3,2,1,0:T(8,128)S(1)} %get-tuple-element.46), channel_id=1, source_target_pairs={{0,48},{8,56},{16,0},{24,8},{32,16},{40,24},{48,32},{56,40},{64,11... | collective-permute-start | bytes 1572872 | tf_op jit(solution)/shard_map/ppermute | solution.py:28
  95.1 15.4 %collective-permute-start.11 = (f32[2,32,1024]{2,1,0:T(8,128)S(1)}, f32[2,32,1024]{2,1,0:T(8,128)S(1)}, u32[]{:S(2)}, u32[]{:S(2)}) collective-permute-start(f32[2,32,1024]{2,1,0:T(8,128)S(1)} %shard_map.86.token), channel_id=1, source_target_pairs={{0,128},{8,136},{16,144},{24,152},{32,160},{40,168},{48,176},{56,1... | collective-permute-start | bytes 786440 | tf_op jit(solution)/shard_map/ppermute | solution.py:28
  107.6 14.7 %collective-permute-start.16 = (f32[2,2,32,1024]{3,2,1,0:T(8,128)S(1)}, f32[2,2,32,1024]{3,2,1,0:T(8,128)S(1)}, u32[]{:S(2)}, u32[]{:S(2)}) collective-permute-start(f32[2,2,32,1024]{3,2,1,0:T(8,128)S(1)} %get-tuple-element.48), channel_id=1, source_target_pairs={{0,64},{8,72},{16,80},{24,88},{32,96},{40,104},{48,112},{56,120},{... | collective-permute-start | bytes 1572872 | tf_op jit(solution)/shard_map/ppermute | solution.py:28
  110.5 19.1 %collective-permute-start.21 = (f32[4,64,1024]{2,1,0:T(8,128)S(1)}, f32[4,64,1024]{2,1,0:T(8,128)S(1)}, u32[]{:S(2)}, u32[]{:S(2)}) collective-permute-start(f32[4,64,1024]{2,1,0:T(8,128)S(1)} %shard_map.81.token), channel_id=1, source_target_pairs={{0,8},{8,0},{16,24},{24,16},{32,40},{40,32},{48,56},{56,48},{64,72... | collective-permute-start | bytes 3145736 | tf_op jit(solution)/shard_map/ppermute | solution.py:28
  110.6 19.5 %copy-start.5 = (f32[2,64,1024]{2,1,0:T(8,128)S(1)}, f32[2,64,1024]{2,1,0:T(8,128)}, u32[]{:S(2)}) copy-start(f32[2,64,1024]{2,1,0:T(8,128)} %shard_map.78.token.value.refs_2_) | copy-start | bytes 1572868
  110.6 14.5 %collective-permute-start.14 = (f32[2,32,1024]{2,1,0:T(8,128)S(1)}, f32[2,32,1024]{2,1,0:T(8,128)S(1)}, u32[]{:S(2)}, u32[]{:S(2)}) collective-permute-start(f32[2,32,1024]{2,1,0:T(8,128)S(1)} %shard_map.88.token.value.refs_6_.refs_2_), channel_id=1, source_target_pairs={{0,16},{8,24},{16,32},{24,40},{32,48},{40,56},{48,64},{56,72},{64,... | collective-permute-start | bytes 786440 | tf_op jit(solution)/shard_map/ppermute | solution.py:34
  114.0 14.0 %collective-permute-start.15 = (f32[2,32,1024]{2,1,0:T(8,128)S(1)}, f32[2,32,1024]{2,1,0:T(8,128)S(1)}, u32[]{:S(2)}, u32[]{:S(2)}) collective-permute-start(f32[2,32,1024]{2,1,0:T(8,128)S(1)} %shard_map.88.token.value.refs_6_.refs_2_), channel_id=1, source_target_pairs={{16,0},{24,8},{32,16},{40,24},{48,32},{56,40},{64,48},{72,56},{80,... | collective-permute-start | bytes 786440 | tf_op jit(solution)/shard_map/ppermute | solution.py:34
  128.1 2.0 %collective-permute-start.17 = (f32[4,32,1024]{2,1,0:T(8,128)S(1)}, f32[4,32,1024]{2,1,0:T(8,128)S(1)}, u32[]{:S(2)}, u32[]{:S(2)}) collective-permute-start(f32[4,32,1024]{2,1,0:T(8,128)S(1)} %shard_map.90), channel_id=1, source_target_pairs={{0,8},{8,0},{16,24},{24,16},{32,40},{40,32},{48,56},{56,48},{64,72... | collective-permute-start | bytes 1572872 | tf_op jit(solution)/shard_map/ppermute | solution.py:28
  128.2 22.4 %collective-permute-start.18 = (f32[2,32,1024]{2,1,0:T(8,128)S(1)}, f32[2,32,1024]{2,1,0:T(8,128)S(1)}, u32[]{:S(2)}, u32[]{:S(2)}) collective-permute-start(f32[2,32,1024]{2,1,0:T(8,128)S(1)} %shard_map.89.token), channel_id=1, source_target_pairs={{0,128},{8,136},{16,144},{24,152},{32,160},{40,168},{48,176},{56,1... | collective-permute-start | bytes 786440 | tf_op jit(solution)/shard_map/ppermute | solution.py:28
  130.1 26.3 %collective-permute-start.22 = (f32[2,10,4,1024]{3,2,1,0:T(4,128)S(1)}, f32[2,10,4,1024]{3,2,1,0:T(4,128)S(1)}, u32[]{:S(2)}, u32[]{:S(2)}) collective-permute-start(f32[2,10,4,1024]{3,2,1,0:T(4,128)S(1)} %get-tuple-element.49), channel_id=1, source_target_pairs={{0,1},{1,2},{2,3},{3,4},{4,5},{5,6},{6,7},{8,9},{9,10},{10,11},{11... | collective-permute-start | bytes 983048 | tf_op jit(solution)/shard_map/ppermute | solution.py:34
  137.1 19.4 %collective-permute-start.23 = (f32[2,10,4,1024]{3,2,1,0:T(4,128)S(1)}, f32[2,10,4,1024]{3,2,1,0:T(4,128)S(1)}, u32[]{:S(2)}, u32[]{:S(2)}) collective-permute-start(f32[2,10,4,1024]{3,2,1,0:T(4,128)S(1)} %get-tuple-element.50), channel_id=1, source_target_pairs={{1,0},{2,1},{3,2},{4,3},{5,4},{6,5},{7,6},{9,8},{10,9},{11,10},{12... | collective-permute-start | bytes 983048 | tf_op jit(solution)/shard_map/ppermute | solution.py:34
  150.6 10.0 %collective-permute-start.19 = (f32[2,32,1024]{2,1,0:T(8,128)S(1)}, f32[2,32,1024]{2,1,0:T(8,128)S(1)}, u32[]{:S(2)}, u32[]{:S(2)}) collective-permute-start(f32[2,32,1024]{2,1,0:T(8,128)S(1)} %shard_map.91.token.value.refs_6_), channel_id=1, source_target_pairs={{0,16},{8,24},{16,32},{24,40},{32,48},{40,56},{48,64},{56,72},{64,... | collective-permute-start | bytes 786440 | tf_op jit(solution)/shard_map/ppermute | solution.py:34
  152.5 12.1 %collective-permute-start.20 = (f32[2,32,1024]{2,1,0:T(8,128)S(1)}, f32[2,32,1024]{2,1,0:T(8,128)S(1)}, u32[]{:S(2)}, u32[]{:S(2)}) collective-permute-start(f32[2,32,1024]{2,1,0:T(8,128)S(1)} %shard_map.91.token.value.refs_6_), channel_id=1, source_target_pairs={{16,0},{24,8},{32,16},{40,24},{48,32},{56,40},{64,48},{72,56},{80,... | collective-permute-start | bytes 786440 | tf_op jit(solution)/shard_map/ppermute | solution.py:34
  164.7 2.0 %collective-permute-start.24 = (f32[4,32,1024]{2,1,0:T(8,128)S(1)}, f32[4,32,1024]{2,1,0:T(8,128)S(1)}, u32[]{:S(2)}, u32[]{:S(2)}) collective-permute-start(f32[4,32,1024]{2,1,0:T(8,128)S(1)} %shard_map.94), channel_id=1, source_target_pairs={{0,8},{8,0},{16,24},{24,16},{32,40},{40,32},{48,56},{56,48},{64,72... | collective-permute-start | bytes 1572872 | tf_op jit(solution)/shard_map/ppermute | solution.py:28

commit v5 on v4

--- a/solution.py
+++ b/solution.py
@@ -175,7 +175,8 @@
     )(pos, offsets, proj, weights, token, recv)
 
 
-def conduct_kernel(table, phase, contact, token, out):
+def conduct_kernel(table, phase, contact, token, out, done):
+    done[...] = jnp.zeros(done.shape, jnp.float32)
     for r in range(phase.shape[0]):
         for z in range(0, phase.shape[1], 8):
             label = phase[r, z:z + 8, :]
@@ -200,9 +201,9 @@
 def conductivities(table, phase, contact, token):
     return pl.pallas_call(
         conduct_kernel,
-        out_shape=jax.ShapeDtypeStruct(phase.shape, jnp.float32),
+        out_shape=[jax.ShapeDtypeStruct(v, jnp.float32) for v in (phase.shape, TOKEN)],
         in_specs=[SMEM, VMEM, VMEM, ANY],
-        out_specs=VMEM,
+        out_specs=[VMEM, VMEM],
         cost_estimate=cost(2.0),
     )(table, phase, contact, token)
 
@@ -455,8 +456,8 @@
     core = ang & 1
     pos = jnp.stack([ang >> 3, (ang >> 1) & 3, core]).astype(jnp.int32)
     args = (pos, band_offsets, projections, band_weights)
-    conduct = conductivities(conductivity_table, phase, contact, pos)
-    outer = Chunk(args, CHUNKS[0], conduct)
+    conduct, token = conductivities(conductivity_table, phase, contact, pos)
+    outer = Chunk(args, CHUNKS[0], token)
     cond, token = widened(core, conduct, pos, us=SWAP_US)
     middle = Chunk(args, CHUNKS[1], pos)
     outer.first(middle.started, us=1.0)

time: 178 us -> 178 us (level)
  no operation moved by 1% of the time
where the time goes in v5:
time: 178 us; the launch traced here: 175 us
  waiting for transfers between devices  87 us (49%)
  starting transfers between devices  48.5 us (27%)
  Pallas kernels  37.7 us (21%)
    ppermute x17, waiting for transfers between devices, shift_ang(): return lax.ppermute(value, 'ang', perm)  73.4 us
    ppermute x8, starting transfers between devices, shift_line(): return lax.ppermute(value, axis, perm)  26.4 us
    ppermute x17, starting transfers between devices, shift_ang(): return lax.ppermute(value, 'ang', perm)  22.1 us
    ppermute x8, waiting for transfers between devices, shift_line(): return lax.ppermute(value, axis, perm)  13.6 us
    pallas_call x2, Pallas kernels, backproject(): pl.pallas_call(functools.partial(mine_kernel, ranges), out_shape=[f32(*s)...  11 us
    pallas_call x2, Pallas kernels, backproject(): pl.pallas_call(functools.partial(other_kernel, ranges), out_shape=[f32(*s...  10.9 us
    pallas_call x1, Pallas kernels, conduct_heat(): pl.pallas_call(functools.partial(heat_kernel, [c for c, _ in groups]), ou...  9.04 us
  transfers between devices with their start and end apart: 25, of which 17 were waited for; matrix products, arithmetic and copies ran while one was open for 0% of the time, Pallas kernels for 12%

profile of v5, /device:TPU:30, one launch (start us, length us, event | category | flops | bytes accessed | tf_op | source)
XLA Modules:
  0.0 175.4 jit_solution(6829588667674173252)
XLA Ops:
  0.7 0.6 pad_add_fusion.pos.token
  1.3 2.7 %shard_map.78 = (f32[2,64,1024]{2,1,0:T(8,128)}, f32[8,128]{1,0:T(8,128)}) custom-call(f32[4,4]{1,0:T(4,128)} %table.1, s32[2,64,1024]{2,1,0:T(8,128)} %phase.1, s32[2,64,1024]{2,1,0:T(8,128)} %contact.1, s32[3]{0:T(128)} %pad_add_fusion.pos.token), custom_call_target="tpu_custom_call" | custom-call | flops 2200000000 | bytes 1048576 | tf_op jit(solution)/shard_map/pallas_call | solution.py:202
  4.0 0.0 copy-start.5
  4.0 0.7 copy-done.5
  4.7 5.5 %shard_map.79 = (f32[4,4,2,32,1024]{4,3,2,1,0:T(8,128)S(1)}, f32[8,128]{1,0:T(8,128)}) custom-call(s32[3]{0:T(128)S(1)} %copy-done.3, s32[8,64]{1,0:T(8,128)S(1)} %copy-done.2, bf16[8,64,1024]{2,1,0:T(8,128)(2,1)S(1)} %copy-done.1, bf16[8,1024,128]{2,1,0:T(8,128)(2,1)S(1)} %copy-done, f32[8,128]{1,0:T(8,128)S(1)} %copy-done.5), custom_call_target="tpu_custom_call" | custom-call | flops 6600000000 | bytes 1048576 | tf_op jit(solution)/shard_map/pallas_call | solution.py:161
  10.1 0.1 collective-permute-start
  10.2 3.7 %collective-permute-start.3 = (f32[2,64,1024]{2,1,0:T(8,128)S(1)}, f32[2,64,1024]{2,1,0:T(8,128)S(1)}, u32[]{:S(2)}, u32[]{:S(2)}) collective-permute-start(f32[2,64,1024]{2,1,0:T(8,128)S(1)} %copy-done.4), channel_id=1, source_target_pairs={{0,16},{8,24},{16,32},{24,40},{32,48},{40,56},{48,64},{56,72},{64,... | collective-permute-start | bytes 1572872 | tf_op jit(solution)/shard_map/ppermute | solution.py:34
  14.0 2.1 %collective-permute-start.4 = (f32[2,64,1024]{2,1,0:T(8,128)S(1)}, f32[2,64,1024]{2,1,0:T(8,128)S(1)}, u32[]{:S(2)}, u32[]{:S(2)}) collective-permute-start(f32[2,64,1024]{2,1,0:T(8,128)S(1)} %copy-done.4), channel_id=1, source_target_pairs={{16,0},{24,8},{32,16},{40,24},{48,32},{56,40},{64,48},{72,56},{80,... | collective-permute-start | bytes 1572872 | tf_op jit(solution)/shard_map/ppermute | solution.py:34
  16.1 5.5 %shard_map.77 = (f32[4,4,2,32,1024]{4,3,2,1,0:T(8,128)S(1)}, f32[8,128]{1,0:T(8,128)S(1)}) custom-call(s32[3]{0:T(128)S(1)} %copy-done.3, s32[8,64]{1,0:T(8,128)S(1)} %copy-done.2, bf16[8,64,1024]{2,1,0:T(8,128)(2,1)S(1)} %copy-done.1, bf16[8,1024,128]{2,1,0:T(8,128)(2,1)S(1)} %copy-done, s32[3]{0:T(128)S(1)} %copy-done.3), custom_call_target="tpu_custom_call" | custom-call | flops 6600000000 | bytes 1048576 | tf_op jit(solution)/shard_map/pallas_call | solution.py:161
  21.6 0.1 collective-permute-start.8
  21.7 0.0 collective-permute-done.recv
  21.7 5.5 %shard_map.80 = (f32[4,2,32,1024]{3,2,1,0:T(8,128)S(1)}, f32[4,2,32,1024]{3,2,1,0:T(8,128)S(1)}, f32[2,2,32,1024]{3,2,1,0:T(8,128)S(1)}, f32[2,2,32,1024]{3,2,1,0:T(8,128)S(1)}, f32[4,2,32,1024]{3,2,1,0:T(8,128)S(1)}) custom-call(s32[3]{0:T(128)S(1)} %copy-done.3, s32[8,64]{1,0:T(8,128)S(1)} %copy-done.2, bf16[8,64,1024]{2,1,0:T(8,128)(2,1)S(1)} %copy-done.1, ...), custom_call_target="tpu_custom_call" | custom-call | flops 1100000000 | bytes 1048576 | tf_op jit(solution)/shard_map/pallas_call | solution.py:169
  27.2 0.1 collective-permute-start.1
  27.3 2.0 %collective-permute-start.2 = (f32[4,2,32,1024]{3,2,1,0:T(8,128)S(1)}, f32[4,2,32,1024]{3,2,1,0:T(8,128)S(1)}, u32[]{:S(2)}, u32[]{:S(2)}) collective-permute-start(f32[4,2,32,1024]{3,2,1,0:T(8,128)S(1)} %get-tuple-element.37), channel_id=1, source_target_pairs={{0,48},{8,56},{16,0},{24,8},{32,16},{40,24},{48,32},{56,40},{64,11... | collective-permute-start | bytes 3145736 | tf_op jit(solution)/shard_map/ppermute | solution.py:28
  29.3 0.0 collective-permute-done.3.left.refs_0_
  29.3 2.8 %collective-permute-done.4.right.refs_3_ = f32[2,64,1024]{2,1,0:T(8,128)S(1)} collective-permute-done((f32[2,64,1024]{2,1,0:T(8,128)S(1)}, f32[2,64,1024]{2,1,0:T(8,128)S(1)}, u32[]{:S(2)}, u32[]{:S(2)}) %collective-permute-start.4) | collective-permute-done | bytes 524320 | tf_op jit(solution)/shard_map/ppermute | solution.py:34
  32.1 0.1 shard_map.81.token
  32.1 20.7 %collective-permute-done.1.fromp = f32[4,2,32,1024]{3,2,1,0:T(8,128)S(1)} collective-permute-done((f32[4,2,32,1024]{3,2,1,0:T(8,128)S(1)}, f32[4,2,32,1024]{3,2,1,0:T(8,128)S(1)}, u32[]{:S(2)}, u32[]{:S(2)}) %collective-permute-start.1) | collective-permute-done | bytes 1048608 | tf_op jit(solution)/shard_map/ppermute | solution.py:28
  52.8 1.7 collective-permute-done.2.fromm
  54.5 0.1 shard_map.82
  54.6 0.3 collective-permute-start.5
  54.9 2.0 %collective-permute-start.6 = (f32[2,2,32,1024]{3,2,1,0:T(8,128)S(1)}, f32[2,2,32,1024]{3,2,1,0:T(8,128)S(1)}, u32[]{:S(2)}, u32[]{:S(2)}) collective-permute-start(f32[2,2,32,1024]{3,2,1,0:T(8,128)S(1)} %get-tuple-element.40), channel_id=1, source_target_pairs={{0,48},{8,56},{16,0},{24,8},{32,16},{40,24},{48,32},{56,40},{64,11... | collective-permute-start | bytes 1572872 | tf_op jit(solution)/shard_map/ppermute | solution.py:28
  56.9 0.0 collective-permute-done.8.recv
  56.9 5.5 %shard_map.84 = (f32[4,2,32,1024]{3,2,1,0:T(8,128)S(1)}, f32[4,2,32,1024]{3,2,1,0:T(8,128)S(1)}, f32[2,2,32,1024]{3,2,1,0:T(8,128)S(1)}, f32[2,2,32,1024]{3,2,1,0:T(8,128)S(1)}, f32[4,2,32,1024]{3,2,1,0:T(8,128)S(1)}) custom-call(s32[3]{0:T(128)S(1)} %copy-done.3, s32[8,64]{1,0:T(8,128)S(1)} %copy-done.2, bf16[8,64,1024]{2,1,0:T(8,128)(2,1)S(1)} %copy-done.1, ...), custom_call_target="tpu_custom_call" | custom-call | flops 6600000000 | bytes 1048576 | tf_op jit(solution)/shard_map/pallas_call | solution.py:169
  62.4 1.4 collective-permute-start.9
  63.8 0.7 collective-permute-start.10
  64.5 5.2 %collective-permute-done.5.lastp = f32[2,2,32,1024]{3,2,1,0:T(8,128)S(1)} collective-permute-done((f32[2,2,32,1024]{3,2,1,0:T(8,128)S(1)}, f32[2,2,32,1024]{3,2,1,0:T(8,128)S(1)}, u32[]{:S(2)}, u32[]{:S(2)}) %collective-permute-start.5) | collective-permute-done | bytes 524320 | tf_op jit(solution)/shard_map/ppermute | solution.py:28
  69.7 1.3 collective-permute-done.6.lastm
  71.0 0.2 shard_map.83
  71.1 4.1 %collective-permute-start.7 = (f32[2,2,32,1024]{3,2,1,0:T(8,128)S(1)}, f32[2,2,32,1024]{3,2,1,0:T(8,128)S(1)}, u32[]{:S(2)}, u32[]{:S(2)}) collective-permute-start(f32[2,2,32,1024]{3,2,1,0:T(8,128)S(1)} %get-tuple-element.42), channel_id=1, source_target_pairs={{0,64},{8,72},{16,80},{24,88},{32,96},{40,104},{48,112},{56,120},{... | collective-permute-start | bytes 1572872 | tf_op jit(solution)/shard_map/ppermute | solution.py:28
  75.2 15.9 %collective-permute-done.9.fromp = f32[4,2,32,1024]{3,2,1,0:T(8,128)S(1)} collective-permute-done((f32[4,2,32,1024]{3,2,1,0:T(8,128)S(1)}, f32[4,2,32,1024]{3,2,1,0:T(8,128)S(1)}, u32[]{:S(2)}, u32[]{:S(2)}) %collective-permute-start.9) | collective-permute-done | bytes 1048608 | tf_op jit(solution)/shard_map/ppermute | solution.py:28
  91.2 1.3 collective-permute-done.10.fromm
  92.5 0.1 shard_map.85
  92.6 0.3 collective-permute-start.12
  92.9 1.8 %collective-permute-start.13 = (f32[2,2,32,1024]{3,2,1,0:T(8,128)S(1)}, f32[2,2,32,1024]{3,2,1,0:T(8,128)S(1)}, u32[]{:S(2)}, u32[]{:S(2)}) collective-permute-start(f32[2,2,32,1024]{3,2,1,0:T(8,128)S(1)} %get-tuple-element.50), channel_id=1, source_target_pairs={{0,48},{8,56},{16,0},{24,8},{32,16},{40,24},{48,32},{56,40},{64,11... | collective-permute-start | bytes 1572872 | tf_op jit(solution)/shard_map/ppermute | solution.py:28
  94.7 4.8 %collective-permute-start.11 = (f32[2,32,1024]{2,1,0:T(8,128)S(1)}, f32[2,32,1024]{2,1,0:T(8,128)S(1)}, u32[]{:S(2)}, u32[]{:S(2)}) collective-permute-start(f32[2,32,1024]{2,1,0:T(8,128)S(1)} %shard_map.86.token), channel_id=1, source_target_pairs={{0,128},{8,136},{16,144},{24,152},{32,160},{40,168},{48,176},{56,1... | collective-permute-start | bytes 786440 | tf_op jit(solution)/shard_map/ppermute | solution.py:28
  99.6 6.1 %collective-permute-done.12.lastp = f32[2,2,32,1024]{3,2,1,0:T(8,128)S(1)} collective-permute-done((f32[2,2,32,1024]{3,2,1,0:T(8,128)S(1)}, f32[2,2,32,1024]{3,2,1,0:T(8,128)S(1)}, u32[]{:S(2)}, u32[]{:S(2)}) %collective-permute-start.12) | collective-permute-done | bytes 524320 | tf_op jit(solution)/shard_map/ppermute | solution.py:28
  105.7 1.4 collective-permute-done.13.lastm
  107.1 0.2 shard_map.87
  107.2 2.9 %collective-permute-start.16 = (f32[2,2,32,1024]{3,2,1,0:T(8,128)S(1)}, f32[2,2,32,1024]{3,2,1,0:T(8,128)S(1)}, u32[]{:S(2)}, u32[]{:S(2)}) collective-permute-start(f32[2,2,32,1024]{3,2,1,0:T(8,128)S(1)} %get-tuple-element.52), channel_id=1, source_target_pairs={{0,64},{8,72},{16,80},{24,88},{32,96},{40,104},{48,112},{56,120},{... | collective-permute-start | bytes 1572872 | tf_op jit(solution)/shard_map/ppermute | solution.py:28
  110.2 0.0 collective-permute-start.21
  110.2 0.0 collective-permute-done.11.last
  110.2 3.3 %collective-permute-start.14 = (f32[2,32,1024]{2,1,0:T(8,128)S(1)}, f32[2,32,1024]{2,1,0:T(8,128)S(1)}, u32[]{:S(2)}, u32[]{:S(2)}) collective-permute-start(f32[2,32,1024]{2,1,0:T(8,128)S(1)} %shard_map.88.token.value.refs_6_.refs_2_), channel_id=1, source_target_pairs={{0,16},{8,24},{16,32},{24,40},{32,48},{40,56},{48,64},{56,72},{64,... | collective-permute-start | bytes 786440 | tf_op jit(solution)/shard_map/ppermute | solution.py:34
  113.5 2.6 %collective-permute-start.15 = (f32[2,32,1024]{2,1,0:T(8,128)S(1)}, f32[2,32,1024]{2,1,0:T(8,128)S(1)}, u32[]{:S(2)}, u32[]{:S(2)}) collective-permute-start(f32[2,32,1024]{2,1,0:T(8,128)S(1)} %shard_map.88.token.value.refs_6_.refs_2_), channel_id=1, source_target_pairs={{16,0},{24,8},{32,16},{40,24},{48,32},{56,40},{64,48},{72,56},{80,... | collective-permute-start | bytes 786440 | tf_op jit(solution)/shard_map/ppermute | solution.py:34
  116.1 5.9 %collective-permute-done.16.got = f32[2,2,32,1024]{3,2,1,0:T(8,128)S(1)} collective-permute-done((f32[2,2,32,1024]{3,2,1,0:T(8,128)S(1)}, f32[2,2,32,1024]{3,2,1,0:T(8,128)S(1)}, u32[]{:S(2)}, u32[]{:S(2)}) %collective-permute-start.16) | collective-permute-done | bytes 524320 | tf_op jit(solution)/shard_map/ppermute | solution.py:28
  122.0 2.8 %collective-permute-done.14.left.refs_4_.refs_0_ = f32[2,32,1024]{2,1,0:T(8,128)S(1)} collective-permute-done((f32[2,32,1024]{2,1,0:T(8,128)S(1)}, f32[2,32,1024]{2,1,0:T(8,128)S(1)}, u32[]{:S(2)}, u32[]{:S(2)}) %collective-permute-start.14) | collective-permute-done | bytes 262176 | tf_op jit(solution)/shard_map/ppermute | solution.py:34
  124.8 2.9 %collective-permute-done.15.right.refs_7_.refs_3_ = f32[2,32,1024]{2,1,0:T(8,128)S(1)} collective-permute-done((f32[2,32,1024]{2,1,0:T(8,128)S(1)}, f32[2,32,1024]{2,1,0:T(8,128)S(1)}, u32[]{:S(2)}, u32[]{:S(2)}) %collective-permute-start.15) | collective-permute-done | bytes 262176 | tf_op jit(solution)/shard_map/ppermute | solution.py:34
  127.7 0.1 collective-permute-start.17
  127.8 1.2 collective-permute-start.18
  129.1 0.0 collective-permute-done.21.refs_1_.got
  129.1 0.6 collective-permute-done.17.refs_5_.refs_1_
  129.8 7.0 %collective-permute-start.22 = (f32[2,10,4,1024]{3,2,1,0:T(4,128)S(1)}, f32[2,10,4,1024]{3,2,1,0:T(4,128)S(1)}, u32[]{:S(2)}, u32[]{:S(2)}) collective-permute-start(f32[2,10,4,1024]{3,2,1,0:T(4,128)S(1)} %get-tuple-element.53), channel_id=1, source_target_pairs={{0,1},{1,2},{2,3},{3,4},{4,5},{5,6},{6,7},{8,9},{9,10},{10,11},{11... | collective-permute-start | bytes 983048 | tf_op jit(solution)/shard_map/ppermute | solution.py:34
  136.7 1.9 %collective-permute-start.23 = (f32[2,10,4,1024]{3,2,1,0:T(4,128)S(1)}, f32[2,10,4,1024]{3,2,1,0:T(4,128)S(1)}, u32[]{:S(2)}, u32[]{:S(2)}) collective-permute-start(f32[2,10,4,1024]{3,2,1,0:T(4,128)S(1)} %get-tuple-element.54), channel_id=1, source_target_pairs={{1,0},{2,1},{3,2},{4,3},{5,4},{6,5},{7,6},{9,8},{10,9},{11,10},{12... | collective-permute-start | bytes 983048 | tf_op jit(solution)/shard_map/ppermute | solution.py:34
  138.7 11.4 %collective-permute-done.18.last = f32[2,32,1024]{2,1,0:T(8,128)S(1)} collective-permute-done((f32[2,32,1024]{2,1,0:T(8,128)S(1)}, f32[2,32,1024]{2,1,0:T(8,128)S(1)}, u32[]{:S(2)}, u32[]{:S(2)}) %collective-permute-start.18) | collective-permute-done | bytes 262176 | tf_op jit(solution)/shard_map/ppermute | solution.py:28
  150.1 0.1 shard_map.91.token.value.refs_6_
  150.2 1.9 %collective-permute-start.19 = (f32[2,32,1024]{2,1,0:T(8,128)S(1)}, f32[2,32,1024]{2,1,0:T(8,128)S(1)}, u32[]{:S(2)}, u32[]{:S(2)}) collective-permute-start(f32[2,32,1024]{2,1,0:T(8,128)S(1)} %shard_map.91.token.value.refs_6_), channel_id=1, source_target_pairs={{0,16},{8,24},{16,32},{24,40},{32,48},{40,56},{48,64},{56,72},{64,... | collective-permute-start | bytes 786440 | tf_op jit(solution)/shard_map/ppermute | solution.py:34
  152.1 3.9 %collective-permute-start.20 = (f32[2,32,1024]{2,1,0:T(8,128)S(1)}, f32[2,32,1024]{2,1,0:T(8,128)S(1)}, u32[]{:S(2)}, u32[]{:S(2)}) collective-permute-start(f32[2,32,1024]{2,1,0:T(8,128)S(1)} %shard_map.91.token.value.refs_6_), channel_id=1, source_target_pairs={{16,0},{24,8},{32,16},{40,24},{48,32},{56,40},{64,48},{72,56},{80,... | collective-permute-start | bytes 786440 | tf_op jit(solution)/shard_map/ppermute | solution.py:34
  156.0 0.0 collective-permute-done.23.high.refs_9_
  156.0 3.2 %shard_map.93 = (f32[10,80,1024]{2,1,0:T(8,128)S(1)}, f32[10,80,1024]{2,1,0:T(8,128)S(1)}, f32[10,80,1024]{2,1,0:T(8,128)S(1)}) custom-call(f32[2,64,1024]{2,1,0:T(8,128)S(1)} %collective-permute-done.3.left.refs_0_, f32[4,64,1024]{2,1,0:T(8,128)S(1)} %collective-permute-done.21.refs_1_.got, f32[2,64,1024]{2,1,0:T(8,128)S(1)} %copy-done.4, ...), custom_call_target="tpu_custom_call" | custom-call | flops 6600000000 | bytes 1048576 | tf_op jit(solution)/shard_map/pallas_call | solution.py:312
  159.2 1.1 collective-permute-done.19.left.refs_4_
  160.3 4.0 %collective-permute-done.20.right.refs_7_ = f32[2,32,1024]{2,1,0:T(8,128)S(1)} collective-permute-done((f32[2,32,1024]{2,1,0:T(8,128)S(1)}, f32[2,32,1024]{2,1,0:T(8,128)S(1)}, u32[]{:S(2)}, u32[]{:S(2)}) %collective-permute-start.20) | collective-permute-done | bytes 262176 | tf_op jit(solution)/shard_map/ppermute | solution.py:34
  164.4 0.1 collective-permute-start.24
  164.5 1.9 %collective-permute-done.24.refs_5_ = f32[4,32,1024]{2,1,0:T(8,128)S(1)} collective-permute-done((f32[4,32,1024]{2,1,0:T(8,128)S(1)}, f32[4,32,1024]{2,1,0:T(8,128)S(1)}, u32[]{:S(2)}, u32[]{:S(2)}) %collective-permute-start.24) | collective-permute-done | bytes 524320 | tf_op jit(solution)/shard_map/ppermute | solution.py:28
  166.4 9.0 %shard_map.95 = (f32[2,64,1024]{2,1,0:T(8,128)}, f32[2,64,1024]{2,1,0:T(8,128)}) custom-call(f32[2,32,1024]{2,1,0:T(8,128)S(1)} %collective-permute-done.14.left.refs_4_.refs_0_, f32[4,32,1024]{2,1,0:T(8,128)S(1)} %collective-permute-done.17.refs_5_.refs_1_, f32[2,32,1024]{2,1,0:T(8,128)S(1)} %shard_map.88.token.value.refs_6_.refs_2_, ...), custom_call_target="tpu_custom_call" | custom-call | flops 9900000256 | bytes 1048576 | tf_op jit(solution)/shard_map/pallas_call | solution.py:371
  (18 shorter events, 0.2 us)
Async XLA Ops:
  0.6 3.3 %copy-start.2 = (s32[8,64]{1,0:T(8,128)S(1)}, s32[8,64]{1,0:T(8,128)}, u32[]{:S(2)}) copy-start(s32[8,64]{1,0:T(8,128)} %offsets.7) | copy-start | bytes 6148
  0.6 3.3 %copy-start.1 = (bf16[8,64,1024]{2,1,0:T(8,128)(2,1)S(1)}, bf16[8,64,1024]{2,1,0:T(8,128)(2,1)}, u32[]{:S(2)}) copy-start(bf16[8,64,1024]{2,1,0:T(8,128)(2,1)} %proj.7) | copy-start | bytes 3145732
  0.6 3.3 %copy-start = (bf16[8,1024,128]{2,1,0:T(8,128)(2,1)S(1)}, bf16[8,1024,128]{2,1,0:T(8,128)(2,1)}, u32[]{:S(2)}) copy-start(bf16[8,1024,128]{2,1,0:T(8,128)(2,1)} %weights.7) | copy-start | bytes 6291460
  1.3 2.7 %copy-start.3 = (s32[3]{0:T(128)S(1)}, s32[3]{0:T(128)}, u32[]{:S(2)}) copy-start(s32[3]{0:T(128)} %pad_add_fusion.pos.token) | copy-start | bytes 40
  4.0 0.7 copy-start.5
  4.7 5.6 %copy-start.4 = (f32[2,64,1024]{2,1,0:T(8,128)S(1)}, f32[2,64,1024]{2,1,0:T(8,128)}, u32[]{:S(2)}) copy-start(f32[2,64,1024]{2,1,0:T(8,128)} %get-tuple-element.38.value.refs_2_) | copy-start | bytes 1572868
  10.1 11.5 %collective-permute-start = (f32[4,4,2,32,1024]{4,3,2,1,0:T(8,128)S(1)}, f32[4,4,2,32,1024]{4,3,2,1,0:T(8,128)S(1)}, u32[]{:S(2)}, u32[]{:S(2)}) collective-permute-start(f32[4,4,2,32,1024]{4,3,2,1,0:T(8,128)S(1)} %get-tuple-element.32), channel_id=1, source_target_pairs={{0,8},{8,0},{16,24},{24,16},{32,40},{40,32},{48,56},{56,48},{64,72... | collective-permute-start | bytes 12582920 | tf_op jit(solution)/shard_map/ppermute | solution.py:28
  10.2 19.1 %collective-permute-start.3 = (f32[2,64,1024]{2,1,0:T(8,128)S(1)}, f32[2,64,1024]{2,1,0:T(8,128)S(1)}, u32[]{:S(2)}, u32[]{:S(2)}) collective-permute-start(f32[2,64,1024]{2,1,0:T(8,128)S(1)} %copy-done.4), channel_id=1, source_target_pairs={{0,16},{8,24},{16,32},{24,40},{32,48},{40,56},{48,64},{56,72},{64,... | collective-permute-start | bytes 1572872 | tf_op jit(solution)/shard_map/ppermute | solution.py:34
  14.0 18.1 %collective-permute-start.4 = (f32[2,64,1024]{2,1,0:T(8,128)S(1)}, f32[2,64,1024]{2,1,0:T(8,128)S(1)}, u32[]{:S(2)}, u32[]{:S(2)}) collective-permute-start(f32[2,64,1024]{2,1,0:T(8,128)S(1)} %copy-done.4), channel_id=1, source_target_pairs={{16,0},{24,8},{32,16},{40,24},{48,32},{56,40},{64,48},{72,56},{80,... | collective-permute-start | bytes 1572872 | tf_op jit(solution)/shard_map/ppermute | solution.py:34
  21.6 35.3 %collective-permute-start.8 = (f32[4,4,2,32,1024]{4,3,2,1,0:T(8,128)S(1)}, f32[4,4,2,32,1024]{4,3,2,1,0:T(8,128)S(1)}, u32[]{:S(2)}, u32[]{:S(2)}) collective-permute-start(f32[4,4,2,32,1024]{4,3,2,1,0:T(8,128)S(1)} %get-tuple-element.43), channel_id=1, source_target_pairs={{0,8},{8,0},{16,24},{24,16},{32,40},{40,32},{48,56},{56,48},{64,72... | collective-permute-start | bytes 12582920 | tf_op jit(solution)/shard_map/ppermute | solution.py:28
  27.2 25.6 %collective-permute-start.1 = (f32[4,2,32,1024]{3,2,1,0:T(8,128)S(1)}, f32[4,2,32,1024]{3,2,1,0:T(8,128)S(1)}, u32[]{:S(2)}, u32[]{:S(2)}) collective-permute-start(f32[4,2,32,1024]{3,2,1,0:T(8,128)S(1)} %get-tuple-element.35), channel_id=1, source_target_pairs={{0,16},{8,24},{16,32},{24,40},{32,48},{40,56},{48,0},{56,8},{64,80... | collective-permute-start | bytes 3145736 | tf_op jit(solution)/shard_map/ppermute | solution.py:28
  27.3 27.2 %collective-permute-start.2 = (f32[4,2,32,1024]{3,2,1,0:T(8,128)S(1)}, f32[4,2,32,1024]{3,2,1,0:T(8,128)S(1)}, u32[]{:S(2)}, u32[]{:S(2)}) collective-permute-start(f32[4,2,32,1024]{3,2,1,0:T(8,128)S(1)} %get-tuple-element.37), channel_id=1, source_target_pairs={{0,48},{8,56},{16,0},{24,8},{32,16},{40,24},{48,32},{56,40},{64,11... | collective-permute-start | bytes 3145736 | tf_op jit(solution)/shard_map/ppermute | solution.py:28
  54.6 15.0 %collective-permute-start.5 = (f32[2,2,32,1024]{3,2,1,0:T(8,128)S(1)}, f32[2,2,32,1024]{3,2,1,0:T(8,128)S(1)}, u32[]{:S(2)}, u32[]{:S(2)}) collective-permute-start(f32[2,2,32,1024]{3,2,1,0:T(8,128)S(1)} %get-tuple-element.39.token), channel_id=1, source_target_pairs={{0,16},{8,24},{16,32},{24,40},{32,48},{40,56},{48,0},{56,8},{64,80... | collective-permute-start | bytes 1572872 | tf_op jit(solution)/shard_map/ppermute | solution.py:28
  54.9 16.0 %collective-permute-start.6 = (f32[2,2,32,1024]{3,2,1,0:T(8,128)S(1)}, f32[2,2,32,1024]{3,2,1,0:T(8,128)S(1)}, u32[]{:S(2)}, u32[]{:S(2)}) collective-permute-start(f32[2,2,32,1024]{3,2,1,0:T(8,128)S(1)} %get-tuple-element.40), channel_id=1, source_target_pairs={{0,48},{8,56},{16,0},{24,8},{32,16},{40,24},{48,32},{56,40},{64,11... | collective-permute-start | bytes 1572872 | tf_op jit(solution)/shard_map/ppermute | solution.py:28
  62.4 28.8 %collective-permute-start.9 = (f32[4,2,32,1024]{3,2,1,0:T(8,128)S(1)}, f32[4,2,32,1024]{3,2,1,0:T(8,128)S(1)}, u32[]{:S(2)}, u32[]{:S(2)}) collective-permute-start(f32[4,2,32,1024]{3,2,1,0:T(8,128)S(1)} %get-tuple-element.45), channel_id=1, source_target_pairs={{0,16},{8,24},{16,32},{24,40},{32,48},{40,56},{48,0},{56,8},{64,80... | collective-permute-start | bytes 3145736 | tf_op jit(solution)/shard_map/ppermute | solution.py:28
  63.8 28.7 %collective-permute-start.10 = (f32[4,2,32,1024]{3,2,1,0:T(8,128)S(1)}, f32[4,2,32,1024]{3,2,1,0:T(8,128)S(1)}, u32[]{:S(2)}, u32[]{:S(2)}) collective-permute-start(f32[4,2,32,1024]{3,2,1,0:T(8,128)S(1)} %get-tuple-element.47), channel_id=1, source_target_pairs={{0,48},{8,56},{16,0},{24,8},{32,16},{40,24},{48,32},{56,40},{64,11... | collective-permute-start | bytes 3145736 | tf_op jit(solution)/shard_map/ppermute | solution.py:28
  71.1 23.6 %collective-permute-start.7 = (f32[2,2,32,1024]{3,2,1,0:T(8,128)S(1)}, f32[2,2,32,1024]{3,2,1,0:T(8,128)S(1)}, u32[]{:S(2)}, u32[]{:S(2)}) collective-permute-start(f32[2,2,32,1024]{3,2,1,0:T(8,128)S(1)} %get-tuple-element.42), channel_id=1, source_target_pairs={{0,64},{8,72},{16,80},{24,88},{32,96},{40,104},{48,112},{56,120},{... | collective-permute-start | bytes 1572872 | tf_op jit(solution)/shard_map/ppermute | solution.py:28
  92.6 13.1 %collective-permute-start.12 = (f32[2,2,32,1024]{3,2,1,0:T(8,128)S(1)}, f32[2,2,32,1024]{3,2,1,0:T(8,128)S(1)}, u32[]{:S(2)}, u32[]{:S(2)}) collective-permute-start(f32[2,2,32,1024]{3,2,1,0:T(8,128)S(1)} %get-tuple-element.48.token), channel_id=1, source_target_pairs={{0,16},{8,24},{16,32},{24,40},{32,48},{40,56},{48,0},{56,8},{64,80... | collective-permute-start | bytes 1572872 | tf_op jit(solution)/shard_map/ppermute | solution.py:28
  92.9 14.2 %collective-permute-start.13 = (f32[2,2,32,1024]{3,2,1,0:T(8,128)S(1)}, f32[2,2,32,1024]{3,2,1,0:T(8,128)S(1)}, u32[]{:S(2)}, u32[]{:S(2)}) collective-permute-start(f32[2,2,32,1024]{3,2,1,0:T(8,128)S(1)} %get-tuple-element.50), channel_id=1, source_target_pairs={{0,48},{8,56},{16,0},{24,8},{32,16},{40,24},{48,32},{56,40},{64,11... | collective-permute-start | bytes 1572872 | tf_op jit(solution)/shard_map/ppermute | solution.py:28
  94.7 15.4 %collective-permute-start.11 = (f32[2,32,1024]{2,1,0:T(8,128)S(1)}, f32[2,32,1024]{2,1,0:T(8,128)S(1)}, u32[]{:S(2)}, u32[]{:S(2)}) collective-permute-start(f32[2,32,1024]{2,1,0:T(8,128)S(1)} %shard_map.86.token), channel_id=1, source_target_pairs={{0,128},{8,136},{16,144},{24,152},{32,160},{40,168},{48,176},{56,1... | collective-permute-start | bytes 786440 | tf_op jit(solution)/shard_map/ppermute | solution.py:28
  107.2 14.7 %collective-permute-start.16 = (f32[2,2,32,1024]{3,2,1,0:T(8,128)S(1)}, f32[2,2,32,1024]{3,2,1,0:T(8,128)S(1)}, u32[]{:S(2)}, u32[]{:S(2)}) collective-permute-start(f32[2,2,32,1024]{3,2,1,0:T(8,128)S(1)} %get-tuple-element.52), channel_id=1, source_target_pairs={{0,64},{8,72},{16,80},{24,88},{32,96},{40,104},{48,112},{56,120},{... | collective-permute-start | bytes 1572872 | tf_op jit(solution)/shard_map/ppermute | solution.py:28
  110.2 18.9 %collective-permute-start.21 = (f32[4,64,1024]{2,1,0:T(8,128)S(1)}, f32[4,64,1024]{2,1,0:T(8,128)S(1)}, u32[]{:S(2)}, u32[]{:S(2)}) collective-permute-start(f32[4,64,1024]{2,1,0:T(8,128)S(1)} %shard_map.81.token), channel_id=1, source_target_pairs={{0,8},{8,0},{16,24},{24,16},{32,40},{40,32},{48,56},{56,48},{64,72... | collective-permute-start | bytes 3145736 | tf_op jit(solution)/shard_map/ppermute | solution.py:28
  110.2 14.5 %collective-permute-start.14 = (f32[2,32,1024]{2,1,0:T(8,128)S(1)}, f32[2,32,1024]{2,1,0:T(8,128)S(1)}, u32[]{:S(2)}, u32[]{:S(2)}) collective-permute-start(f32[2,32,1024]{2,1,0:T(8,128)S(1)} %shard_map.88.token.value.refs_6_.refs_2_), channel_id=1, source_target_pairs={{0,16},{8,24},{16,32},{24,40},{32,48},{40,56},{48,64},{56,72},{64,... | collective-permute-start | bytes 786440 | tf_op jit(solution)/shard_map/ppermute | solution.py:34
  113.5 14.2 %collective-permute-start.15 = (f32[2,32,1024]{2,1,0:T(8,128)S(1)}, f32[2,32,1024]{2,1,0:T(8,128)S(1)}, u32[]{:S(2)}, u32[]{:S(2)}) collective-permute-start(f32[2,32,1024]{2,1,0:T(8,128)S(1)} %shard_map.88.token.value.refs_6_.refs_2_), channel_id=1, source_target_pairs={{16,0},{24,8},{32,16},{40,24},{48,32},{56,40},{64,48},{72,56},{80,... | collective-permute-start | bytes 786440 | tf_op jit(solution)/shard_map/ppermute | solution.py:34
  127.7 2.0 %collective-permute-start.17 = (f32[4,32,1024]{2,1,0:T(8,128)S(1)}, f32[4,32,1024]{2,1,0:T(8,128)S(1)}, u32[]{:S(2)}, u32[]{:S(2)}) collective-permute-start(f32[4,32,1024]{2,1,0:T(8,128)S(1)} %shard_map.90), channel_id=1, source_target_pairs={{0,8},{8,0},{16,24},{24,16},{32,40},{40,32},{48,56},{56,48},{64,72... | collective-permute-start | bytes 1572872 | tf_op jit(solution)/shard_map/ppermute | solution.py:28
  127.8 22.3 %collective-permute-start.18 = (f32[2,32,1024]{2,1,0:T(8,128)S(1)}, f32[2,32,1024]{2,1,0:T(8,128)S(1)}, u32[]{:S(2)}, u32[]{:S(2)}) collective-permute-start(f32[2,32,1024]{2,1,0:T(8,128)S(1)} %shard_map.89.token), channel_id=1, source_target_pairs={{0,128},{8,136},{16,144},{24,152},{32,160},{40,168},{48,176},{56,1... | collective-permute-start | bytes 786440 | tf_op jit(solution)/shard_map/ppermute | solution.py:28
  129.8 26.2 %collective-permute-start.22 = (f32[2,10,4,1024]{3,2,1,0:T(4,128)S(1)}, f32[2,10,4,1024]{3,2,1,0:T(4,128)S(1)}, u32[]{:S(2)}, u32[]{:S(2)}) collective-permute-start(f32[2,10,4,1024]{3,2,1,0:T(4,128)S(1)} %get-tuple-element.53), channel_id=1, source_target_pairs={{0,1},{1,2},{2,3},{3,4},{4,5},{5,6},{6,7},{8,9},{9,10},{10,11},{11... | collective-permute-start | bytes 983048 | tf_op jit(solution)/shard_map/ppermute | solution.py:34
  136.7 19.3 %collective-permute-start.23 = (f32[2,10,4,1024]{3,2,1,0:T(4,128)S(1)}, f32[2,10,4,1024]{3,2,1,0:T(4,128)S(1)}, u32[]{:S(2)}, u32[]{:S(2)}) collective-permute-start(f32[2,10,4,1024]{3,2,1,0:T(4,128)S(1)} %get-tuple-element.54), channel_id=1, source_target_pairs={{1,0},{2,1},{3,2},{4,3},{5,4},{6,5},{7,6},{9,8},{10,9},{11,10},{12... | collective-permute-start | bytes 983048 | tf_op jit(solution)/shard_map/ppermute | solution.py:34
  150.2 10.1 %collective-permute-start.19 = (f32[2,32,1024]{2,1,0:T(8,128)S(1)}, f32[2,32,1024]{2,1,0:T(8,128)S(1)}, u32[]{:S(2)}, u32[]{:S(2)}) collective-permute-start(f32[2,32,1024]{2,1,0:T(8,128)S(1)} %shard_map.91.token.value.refs_6_), channel_id=1, source_target_pairs={{0,16},{8,24},{16,32},{24,40},{32,48},{40,56},{48,64},{56,72},{64,... | collective-permute-start | bytes 786440 | tf_op jit(solution)/shard_map/ppermute | solution.py:34
  152.1 12.2 %collective-permute-start.20 = (f32[2,32,1024]{2,1,0:T(8,128)S(1)}, f32[2,32,1024]{2,1,0:T(8,128)S(1)}, u32[]{:S(2)}, u32[]{:S(2)}) collective-permute-start(f32[2,32,1024]{2,1,0:T(8,128)S(1)} %shard_map.91.token.value.refs_6_), channel_id=1, source_target_pairs={{16,0},{24,8},{32,16},{40,24},{48,32},{56,40},{64,48},{72,56},{80,... | collective-permute-start | bytes 786440 | tf_op jit(solution)/shard_map/ppermute | solution.py:34
  164.4 2.0 %collective-permute-start.24 = (f32[4,32,1024]{2,1,0:T(8,128)S(1)}, f32[4,32,1024]{2,1,0:T(8,128)S(1)}, u32[]{:S(2)}, u32[]{:S(2)}) collective-permute-start(f32[4,32,1024]{2,1,0:T(8,128)S(1)} %shard_map.94), channel_id=1, source_target_pairs={{0,8},{8,0},{16,24},{24,16},{32,40},{40,32},{48,56},{56,48},{64,72... | collective-permute-start | bytes 1572872 | tf_op jit(solution)/shard_map/ppermute | solution.py:28

commit v6 on v5

--- a/solution.py
+++ b/solution.py
@@ -467,7 +467,7 @@
     token = middle.near_z(token)
     outer_volume = outer.volume(token)
     token = middle.far_z(outer_volume)
-    outer_rows, _ = widened(core, outer_volume, token)
+    outer_rows, _ = widened(core, outer_volume, pos)
     low, high = ends(cond, outer_rows)
     middle_volume = middle.volume(outer_volume, us=4.0)
     face_arrays = faces(cond, low, high, middle_volume)

time: 178 us -> 181 us (1.017); the launches traced: 175 us -> 180 us
  waiting for transfers between devices: 87 us -> 90.2 us
    ppermute x8, waiting for transfers between devices: 13.6 us -> 18.5 us  [shift_line(): return lax.ppermute(value, axis, perm)]
  transfers between devices with their start and end apart: 25 -> 25, of which waited for: 17 -> 16; matrix products, arithmetic and copies ran while one was open for 0% -> 0% of each run, Pallas kernels for 12% -> 11%
where the time goes in v6:
time: 181 us; the launch traced here: 180 us
  waiting for transfers between devices  90.2 us (50%)
  starting transfers between devices  50.2 us (28%)
  Pallas kernels  37.5 us (21%)
    ppermute x17, waiting for transfers between devices, shift_ang(): return lax.ppermute(value, 'ang', perm)  71.8 us
    ppermute x8, starting transfers between devices, shift_line(): return lax.ppermute(value, axis, perm)  28.1 us
    ppermute x17, starting transfers between devices, shift_ang(): return lax.ppermute(value, 'ang', perm)  22.2 us
    ppermute x8, waiting for transfers between devices, shift_line(): return lax.ppermute(value, axis, perm)  18.5 us
    pallas_call x2, Pallas kernels, backproject(): pl.pallas_call(functools.partial(mine_kernel, ranges), out_shape=[f32(*s)...  11 us
    pallas_call x2, Pallas kernels, backproject(): pl.pallas_call(functools.partial(other_kernel, ranges), out_shape=[f32(*s...  10.9 us
    pallas_call x1, Pallas kernels, conduct_heat(): pl.pallas_call(functools.partial(heat_kernel, [c for c, _ in groups]), ou...  8.77 us
  transfers between devices with their start and end apart: 25, of which 16 were waited for; matrix products, arithmetic and copies ran while one was open for 0% of the time, Pallas kernels for 11%

profile of v6, /device:TPU:30, one launch (start us, length us, event | category | flops | bytes accessed | tf_op | source)
XLA Modules:
  0.0 180.2 jit_solution(14724825232415275811)
XLA Ops:
  0.7 0.6 pad_add_fusion.pos.token
  1.3 2.7 %shard_map.78 = (f32[2,64,1024]{2,1,0:T(8,128)}, f32[8,128]{1,0:T(8,128)}) custom-call(f32[4,4]{1,0:T(4,128)} %table.1, s32[2,64,1024]{2,1,0:T(8,128)} %phase.1, s32[2,64,1024]{2,1,0:T(8,128)} %contact.1, s32[3]{0:T(128)} %pad_add_fusion.pos.token), custom_call_target="tpu_custom_call" | custom-call | flops 2200000000 | bytes 1048576 | tf_op jit(solution)/shard_map/pallas_call | solution.py:202
  4.0 0.0 copy-start.5
  4.0 0.7 copy-done.5
  4.7 5.5 %shard_map.79 = (f32[4,4,2,32,1024]{4,3,2,1,0:T(8,128)S(1)}, f32[8,128]{1,0:T(8,128)}) custom-call(s32[3]{0:T(128)S(1)} %copy-done.3, s32[8,64]{1,0:T(8,128)S(1)} %copy-done.2, bf16[8,64,1024]{2,1,0:T(8,128)(2,1)S(1)} %copy-done.1, bf16[8,1024,128]{2,1,0:T(8,128)(2,1)S(1)} %copy-done, f32[8,128]{1,0:T(8,128)S(1)} %copy-done.5), custom_call_target="tpu_custom_call" | custom-call | flops 6600000000 | bytes 1048576 | tf_op jit(solution)/shard_map/pallas_call | solution.py:161
  10.1 0.1 collective-permute-start
  10.2 3.7 %collective-permute-start.3 = (f32[2,64,1024]{2,1,0:T(8,128)S(1)}, f32[2,64,1024]{2,1,0:T(8,128)S(1)}, u32[]{:S(2)}, u32[]{:S(2)}) collective-permute-start(f32[2,64,1024]{2,1,0:T(8,128)S(1)} %copy-done.4), channel_id=1, source_target_pairs={{0,16},{8,24},{16,32},{24,40},{32,48},{40,56},{48,64},{56,72},{64,... | collective-permute-start | bytes 1572872 | tf_op jit(solution)/shard_map/ppermute | solution.py:34
  14.0 2.1 %collective-permute-start.4 = (f32[2,64,1024]{2,1,0:T(8,128)S(1)}, f32[2,64,1024]{2,1,0:T(8,128)S(1)}, u32[]{:S(2)}, u32[]{:S(2)}) collective-permute-start(f32[2,64,1024]{2,1,0:T(8,128)S(1)} %copy-done.4), channel_id=1, source_target_pairs={{16,0},{24,8},{32,16},{40,24},{48,32},{56,40},{64,48},{72,56},{80,... | collective-permute-start | bytes 1572872 | tf_op jit(solution)/shard_map/ppermute | solution.py:34
  16.1 5.5 %shard_map.77 = (f32[4,4,2,32,1024]{4,3,2,1,0:T(8,128)S(1)}, f32[8,128]{1,0:T(8,128)S(1)}) custom-call(s32[3]{0:T(128)S(1)} %copy-done.3, s32[8,64]{1,0:T(8,128)S(1)} %copy-done.2, bf16[8,64,1024]{2,1,0:T(8,128)(2,1)S(1)} %copy-done.1, bf16[8,1024,128]{2,1,0:T(8,128)(2,1)S(1)} %copy-done, s32[3]{0:T(128)S(1)} %copy-done.3), custom_call_target="tpu_custom_call" | custom-call | flops 6600000000 | bytes 1048576 | tf_op jit(solution)/shard_map/pallas_call | solution.py:161
  21.6 0.1 collective-permute-start.8
  21.7 0.0 collective-permute-done.recv
  21.7 5.5 %shard_map.80 = (f32[4,2,32,1024]{3,2,1,0:T(8,128)S(1)}, f32[4,2,32,1024]{3,2,1,0:T(8,128)S(1)}, f32[2,2,32,1024]{3,2,1,0:T(8,128)S(1)}, f32[2,2,32,1024]{3,2,1,0:T(8,128)S(1)}, f32[4,2,32,1024]{3,2,1,0:T(8,128)S(1)}) custom-call(s32[3]{0:T(128)S(1)} %copy-done.3, s32[8,64]{1,0:T(8,128)S(1)} %copy-done.2, bf16[8,64,1024]{2,1,0:T(8,128)(2,1)S(1)} %copy-done.1, ...), custom_call_target="tpu_custom_call" | custom-call | flops 1100000000 | bytes 1048576 | tf_op jit(solution)/shard_map/pallas_call | solution.py:169
  27.2 0.1 collective-permute-start.1
  27.3 2.0 %collective-permute-start.2 = (f32[4,2,32,1024]{3,2,1,0:T(8,128)S(1)}, f32[4,2,32,1024]{3,2,1,0:T(8,128)S(1)}, u32[]{:S(2)}, u32[]{:S(2)}) collective-permute-start(f32[4,2,32,1024]{3,2,1,0:T(8,128)S(1)} %get-tuple-element.37), channel_id=1, source_target_pairs={{0,48},{8,56},{16,0},{24,8},{32,16},{40,24},{48,32},{56,40},{64,11... | collective-permute-start | bytes 3145736 | tf_op jit(solution)/shard_map/ppermute | solution.py:28
  29.3 0.0 collective-permute-done.3.left.refs_0_
  29.3 2.8 %collective-permute-done.4.right.refs_3_ = f32[2,64,1024]{2,1,0:T(8,128)S(1)} collective-permute-done((f32[2,64,1024]{2,1,0:T(8,128)S(1)}, f32[2,64,1024]{2,1,0:T(8,128)S(1)}, u32[]{:S(2)}, u32[]{:S(2)}) %collective-permute-start.4) | collective-permute-done | bytes 524320 | tf_op jit(solution)/shard_map/ppermute | solution.py:34
  32.1 0.1 shard_map.81.token
  32.1 20.7 %collective-permute-done.1.fromp = f32[4,2,32,1024]{3,2,1,0:T(8,128)S(1)} collective-permute-done((f32[4,2,32,1024]{3,2,1,0:T(8,128)S(1)}, f32[4,2,32,1024]{3,2,1,0:T(8,128)S(1)}, u32[]{:S(2)}, u32[]{:S(2)}) %collective-permute-start.1) | collective-permute-done | bytes 1048608 | tf_op jit(solution)/shard_map/ppermute | solution.py:28
  52.8 1.7 collective-permute-done.2.fromm
  54.5 0.1 shard_map.82
  54.6 0.3 collective-permute-start.5
  54.9 2.0 %collective-permute-start.6 = (f32[2,2,32,1024]{3,2,1,0:T(8,128)S(1)}, f32[2,2,32,1024]{3,2,1,0:T(8,128)S(1)}, u32[]{:S(2)}, u32[]{:S(2)}) collective-permute-start(f32[2,2,32,1024]{3,2,1,0:T(8,128)S(1)} %get-tuple-element.40), channel_id=1, source_target_pairs={{0,48},{8,56},{16,0},{24,8},{32,16},{40,24},{48,32},{56,40},{64,11... | collective-permute-start | bytes 1572872 | tf_op jit(solution)/shard_map/ppermute | solution.py:28
  56.9 0.0 collective-permute-done.8.recv
  56.9 5.5 %shard_map.84 = (f32[4,2,32,1024]{3,2,1,0:T(8,128)S(1)}, f32[4,2,32,1024]{3,2,1,0:T(8,128)S(1)}, f32[2,2,32,1024]{3,2,1,0:T(8,128)S(1)}, f32[2,2,32,1024]{3,2,1,0:T(8,128)S(1)}, f32[4,2,32,1024]{3,2,1,0:T(8,128)S(1)}) custom-call(s32[3]{0:T(128)S(1)} %copy-done.3, s32[8,64]{1,0:T(8,128)S(1)} %copy-done.2, bf16[8,64,1024]{2,1,0:T(8,128)(2,1)S(1)} %copy-done.1, ...), custom_call_target="tpu_custom_call" | custom-call | flops 6600000000 | bytes 1048576 | tf_op jit(solution)/shard_map/pallas_call | solution.py:169
  62.4 1.4 collective-permute-start.9
  63.8 0.7 collective-permute-start.10
  64.5 5.2 %collective-permute-done.5.lastp = f32[2,2,32,1024]{3,2,1,0:T(8,128)S(1)} collective-permute-done((f32[2,2,32,1024]{3,2,1,0:T(8,128)S(1)}, f32[2,2,32,1024]{3,2,1,0:T(8,128)S(1)}, u32[]{:S(2)}, u32[]{:S(2)}) %collective-permute-start.5) | collective-permute-done | bytes 524320 | tf_op jit(solution)/shard_map/ppermute | solution.py:28
  69.7 1.3 collective-permute-done.6.lastm
  71.0 0.2 shard_map.83
  71.2 4.1 %collective-permute-start.7 = (f32[2,2,32,1024]{3,2,1,0:T(8,128)S(1)}, f32[2,2,32,1024]{3,2,1,0:T(8,128)S(1)}, u32[]{:S(2)}, u32[]{:S(2)}) collective-permute-start(f32[2,2,32,1024]{3,2,1,0:T(8,128)S(1)} %get-tuple-element.42), channel_id=1, source_target_pairs={{0,64},{8,72},{16,80},{24,88},{32,96},{40,104},{48,112},{56,120},{... | collective-permute-start | bytes 1572872 | tf_op jit(solution)/shard_map/ppermute | solution.py:28
  75.3 15.9 %collective-permute-done.9.fromp = f32[4,2,32,1024]{3,2,1,0:T(8,128)S(1)} collective-permute-done((f32[4,2,32,1024]{3,2,1,0:T(8,128)S(1)}, f32[4,2,32,1024]{3,2,1,0:T(8,128)S(1)}, u32[]{:S(2)}, u32[]{:S(2)}) %collective-permute-start.9) | collective-permute-done | bytes 1048608 | tf_op jit(solution)/shard_map/ppermute | solution.py:28
  91.2 1.3 collective-permute-done.10.fromm
  92.5 0.1 shard_map.85
  92.6 0.3 collective-permute-start.12
  92.9 1.8 %collective-permute-start.13 = (f32[2,2,32,1024]{3,2,1,0:T(8,128)S(1)}, f32[2,2,32,1024]{3,2,1,0:T(8,128)S(1)}, u32[]{:S(2)}, u32[]{:S(2)}) collective-permute-start(f32[2,2,32,1024]{3,2,1,0:T(8,128)S(1)} %get-tuple-element.50), channel_id=1, source_target_pairs={{0,48},{8,56},{16,0},{24,8},{32,16},{40,24},{48,32},{56,40},{64,11... | collective-permute-start | bytes 1572872 | tf_op jit(solution)/shard_map/ppermute | solution.py:28
  94.7 0.0 collective-permute-done.7.got
  94.7 4.8 %collective-permute-start.11 = (f32[2,32,1024]{2,1,0:T(8,128)S(1)}, f32[2,32,1024]{2,1,0:T(8,128)S(1)}, u32[]{:S(2)}, u32[]{:S(2)}) collective-permute-start(f32[2,32,1024]{2,1,0:T(8,128)S(1)} %shard_map.86.token), channel_id=1, source_target_pairs={{0,128},{8,136},{16,144},{24,152},{32,160},{40,168},{48,176},{56,1... | collective-permute-start | bytes 786440 | tf_op jit(solution)/shard_map/ppermute | solution.py:28
  99.5 0.0 collective-permute-start.21
  99.6 6.1 %collective-permute-done.12.lastp = f32[2,2,32,1024]{3,2,1,0:T(8,128)S(1)} collective-permute-done((f32[2,2,32,1024]{3,2,1,0:T(8,128)S(1)}, f32[2,2,32,1024]{3,2,1,0:T(8,128)S(1)}, u32[]{:S(2)}, u32[]{:S(2)}) %collective-permute-start.12) | collective-permute-done | bytes 524320 | tf_op jit(solution)/shard_map/ppermute | solution.py:28
  105.6 1.4 collective-permute-done.13.lastm
  107.0 0.2 shard_map.87
  107.2 2.4 %collective-permute-done.11.last = f32[2,32,1024]{2,1,0:T(8,128)S(1)} collective-permute-done((f32[2,32,1024]{2,1,0:T(8,128)S(1)}, f32[2,32,1024]{2,1,0:T(8,128)S(1)}, u32[]{:S(2)}, u32[]{:S(2)}) %collective-permute-start.11) | collective-permute-done | bytes 262176 | tf_op jit(solution)/shard_map/ppermute | solution.py:28
  109.6 0.1 shard_map.88.value.token.refs_6_.refs_2_
  109.6 3.9 %collective-permute-start.14 = (f32[2,32,1024]{2,1,0:T(8,128)S(1)}, f32[2,32,1024]{2,1,0:T(8,128)S(1)}, u32[]{:S(2)}, u32[]{:S(2)}) collective-permute-start(f32[2,32,1024]{2,1,0:T(8,128)S(1)} %shard_map.88.value.token.refs_6_.refs_2_), channel_id=1, source_target_pairs={{0,16},{8,24},{16,32},{24,40},{32,48},{40,56},{48,64},{56,72},{64,... | collective-permute-start | bytes 786440 | tf_op jit(solution)/shard_map/ppermute | solution.py:34
  113.5 2.0 %collective-permute-start.15 = (f32[2,32,1024]{2,1,0:T(8,128)S(1)}, f32[2,32,1024]{2,1,0:T(8,128)S(1)}, u32[]{:S(2)}, u32[]{:S(2)}) collective-permute-start(f32[2,32,1024]{2,1,0:T(8,128)S(1)} %shard_map.88.value.token.refs_6_.refs_2_), channel_id=1, source_target_pairs={{16,0},{24,8},{32,16},{40,24},{48,32},{56,40},{64,48},{72,56},{80,... | collective-permute-start | bytes 786440 | tf_op jit(solution)/shard_map/ppermute | solution.py:34
  115.5 0.8 collective-permute-start.17
  116.3 3.9 %collective-permute-done.14.left.refs_4_.refs_0_ = f32[2,32,1024]{2,1,0:T(8,128)S(1)} collective-permute-done((f32[2,32,1024]{2,1,0:T(8,128)S(1)}, f32[2,32,1024]{2,1,0:T(8,128)S(1)}, u32[]{:S(2)}, u32[]{:S(2)}) %collective-permute-start.14) | collective-permute-done | bytes 262176 | tf_op jit(solution)/shard_map/ppermute | solution.py:34
  120.2 6.5 %collective-permute-done.15.right.refs_7_.refs_3_ = f32[2,32,1024]{2,1,0:T(8,128)S(1)} collective-permute-done((f32[2,32,1024]{2,1,0:T(8,128)S(1)}, f32[2,32,1024]{2,1,0:T(8,128)S(1)}, u32[]{:S(2)}, u32[]{:S(2)}) %collective-permute-start.15) | collective-permute-done | bytes 262176 | tf_op jit(solution)/shard_map/ppermute | solution.py:34
  126.8 0.1 collective-permute-start.16
  126.9 3.6 %collective-permute-done.17.got = f32[2,2,32,1024]{3,2,1,0:T(8,128)S(1)} collective-permute-done((f32[2,2,32,1024]{3,2,1,0:T(8,128)S(1)}, f32[2,2,32,1024]{3,2,1,0:T(8,128)S(1)}, u32[]{:S(2)}, u32[]{:S(2)}) %collective-permute-start.17) | collective-permute-done | bytes 524320 | tf_op jit(solution)/shard_map/ppermute | solution.py:28
  130.5 3.5 %collective-permute-start.18 = (f32[2,32,1024]{2,1,0:T(8,128)S(1)}, f32[2,32,1024]{2,1,0:T(8,128)S(1)}, u32[]{:S(2)}, u32[]{:S(2)}) collective-permute-start(f32[2,32,1024]{2,1,0:T(8,128)S(1)} %shard_map.90), channel_id=1, source_target_pairs={{0,128},{8,136},{16,144},{24,152},{32,160},{40,168},{48,176},{56,1... | collective-permute-start | bytes 786440 | tf_op jit(solution)/shard_map/ppermute | solution.py:28
  134.0 0.0 collective-permute-done.21.refs_1_.got
  134.0 0.0 collective-permute-done.16.refs_5_.refs_1_
  134.0 6.0 %collective-permute-start.22 = (f32[2,10,4,1024]{3,2,1,0:T(4,128)S(1)}, f32[2,10,4,1024]{3,2,1,0:T(4,128)S(1)}, u32[]{:S(2)}, u32[]{:S(2)}) collective-permute-start(f32[2,10,4,1024]{3,2,1,0:T(4,128)S(1)} %get-tuple-element.53), channel_id=1, source_target_pairs={{0,1},{1,2},{2,3},{3,4},{4,5},{5,6},{6,7},{8,9},{9,10},{10,11},{11... | collective-permute-start | bytes 983048 | tf_op jit(solution)/shard_map/ppermute | solution.py:34
  140.0 1.9 %collective-permute-start.23 = (f32[2,10,4,1024]{3,2,1,0:T(4,128)S(1)}, f32[2,10,4,1024]{3,2,1,0:T(4,128)S(1)}, u32[]{:S(2)}, u32[]{:S(2)}) collective-permute-start(f32[2,10,4,1024]{3,2,1,0:T(4,128)S(1)} %get-tuple-element.54), channel_id=1, source_target_pairs={{1,0},{2,1},{3,2},{4,3},{5,4},{6,5},{7,6},{9,8},{10,9},{11,10},{12... | collective-permute-start | bytes 983048 | tf_op jit(solution)/shard_map/ppermute | solution.py:34
  142.0 10.4 %collective-permute-done.18.last = f32[2,32,1024]{2,1,0:T(8,128)S(1)} collective-permute-done((f32[2,32,1024]{2,1,0:T(8,128)S(1)}, f32[2,32,1024]{2,1,0:T(8,128)S(1)}, u32[]{:S(2)}, u32[]{:S(2)}) %collective-permute-start.18) | collective-permute-done | bytes 262176 | tf_op jit(solution)/shard_map/ppermute | solution.py:28
  152.4 6.6 %collective-permute-start.19 = (f32[2,32,1024]{2,1,0:T(8,128)S(1)}, f32[2,32,1024]{2,1,0:T(8,128)S(1)}, u32[]{:S(2)}, u32[]{:S(2)}) collective-permute-start(f32[2,32,1024]{2,1,0:T(8,128)S(1)} %shard_map.91.token.value.refs_6_), channel_id=1, source_target_pairs={{0,16},{8,24},{16,32},{24,40},{32,48},{40,56},{48,64},{56,72},{64,... | collective-permute-start | bytes 786440 | tf_op jit(solution)/shard_map/ppermute | solution.py:34
  159.0 1.9 %collective-permute-start.20 = (f32[2,32,1024]{2,1,0:T(8,128)S(1)}, f32[2,32,1024]{2,1,0:T(8,128)S(1)}, u32[]{:S(2)}, u32[]{:S(2)}) collective-permute-start(f32[2,32,1024]{2,1,0:T(8,128)S(1)} %shard_map.91.token.value.refs_6_), channel_id=1, source_target_pairs={{16,0},{24,8},{32,16},{40,24},{48,32},{56,40},{64,48},{72,56},{80,... | collective-permute-start | bytes 786440 | tf_op jit(solution)/shard_map/ppermute | solution.py:34
  160.9 0.0 collective-permute-done.23.high.refs_9_
  160.9 3.2 %shard_map.93 = (f32[10,80,1024]{2,1,0:T(8,128)S(1)}, f32[10,80,1024]{2,1,0:T(8,128)S(1)}, f32[10,80,1024]{2,1,0:T(8,128)S(1)}) custom-call(f32[2,64,1024]{2,1,0:T(8,128)S(1)} %collective-permute-done.3.left.refs_0_, f32[4,64,1024]{2,1,0:T(8,128)S(1)} %collective-permute-done.21.refs_1_.got, f32[2,64,1024]{2,1,0:T(8,128)S(1)} %copy-done.4, ...), custom_call_target="tpu_custom_call" | custom-call | flops 6600000000 | bytes 1048576 | tf_op jit(solution)/shard_map/pallas_call | solution.py:312
  164.1 5.3 %collective-permute-done.20.right.refs_7_ = f32[2,32,1024]{2,1,0:T(8,128)S(1)} collective-permute-done((f32[2,32,1024]{2,1,0:T(8,128)S(1)}, f32[2,32,1024]{2,1,0:T(8,128)S(1)}, u32[]{:S(2)}, u32[]{:S(2)}) %collective-permute-start.20) | collective-permute-done | bytes 262176 | tf_op jit(solution)/shard_map/ppermute | solution.py:34
  169.4 0.1 collective-permute-start.24
  169.5 1.9 %collective-permute-done.24.refs_5_ = f32[4,32,1024]{2,1,0:T(8,128)S(1)} collective-permute-done((f32[4,32,1024]{2,1,0:T(8,128)S(1)}, f32[4,32,1024]{2,1,0:T(8,128)S(1)}, u32[]{:S(2)}, u32[]{:S(2)}) %collective-permute-start.24) | collective-permute-done | bytes 524320 | tf_op jit(solution)/shard_map/ppermute | solution.py:28
  171.4 8.8 %shard_map.95 = (f32[2,64,1024]{2,1,0:T(8,128)}, f32[2,64,1024]{2,1,0:T(8,128)}) custom-call(f32[2,32,1024]{2,1,0:T(8,128)S(1)} %collective-permute-done.14.left.refs_4_.refs_0_, f32[4,32,1024]{2,1,0:T(8,128)S(1)} %collective-permute-done.16.refs_5_.refs_1_, f32[2,32,1024]{2,1,0:T(8,128)S(1)} %shard_map.88.value.token.refs_6_.refs_2_, ...), custom_call_target="tpu_custom_call" | custom-call | flops 9900000256 | bytes 1048576 | tf_op jit(solution)/shard_map/pallas_call | solution.py:371
  (18 shorter events, 0.3 us)
Async XLA Ops:
  0.6 3.3 %copy-start.2 = (s32[8,64]{1,0:T(8,128)S(1)}, s32[8,64]{1,0:T(8,128)}, u32[]{:S(2)}) copy-start(s32[8,64]{1,0:T(8,128)} %offsets.7) | copy-start | bytes 6148
  0.6 3.3 %copy-start.1 = (bf16[8,64,1024]{2,1,0:T(8,128)(2,1)S(1)}, bf16[8,64,1024]{2,1,0:T(8,128)(2,1)}, u32[]{:S(2)}) copy-start(bf16[8,64,1024]{2,1,0:T(8,128)(2,1)} %proj.7) | copy-start | bytes 3145732
  0.6 3.3 %copy-start = (bf16[8,1024,128]{2,1,0:T(8,128)(2,1)S(1)}, bf16[8,1024,128]{2,1,0:T(8,128)(2,1)}, u32[]{:S(2)}) copy-start(bf16[8,1024,128]{2,1,0:T(8,128)(2,1)} %weights.7) | copy-start | bytes 6291460
  1.3 2.7 %copy-start.3 = (s32[3]{0:T(128)S(1)}, s32[3]{0:T(128)}, u32[]{:S(2)}) copy-start(s32[3]{0:T(128)} %pad_add_fusion.pos.token) | copy-start | bytes 40
  4.0 0.7 copy-start.5
  4.7 5.6 %copy-start.4 = (f32[2,64,1024]{2,1,0:T(8,128)S(1)}, f32[2,64,1024]{2,1,0:T(8,128)}, u32[]{:S(2)}) copy-start(f32[2,64,1024]{2,1,0:T(8,128)} %get-tuple-element.38.value.refs_2_) | copy-start | bytes 1572868
  10.1 11.5 %collective-permute-start = (f32[4,4,2,32,1024]{4,3,2,1,0:T(8,128)S(1)}, f32[4,4,2,32,1024]{4,3,2,1,0:T(8,128)S(1)}, u32[]{:S(2)}, u32[]{:S(2)}) collective-permute-start(f32[4,4,2,32,1024]{4,3,2,1,0:T(8,128)S(1)} %get-tuple-element.32), channel_id=1, source_target_pairs={{0,8},{8,0},{16,24},{24,16},{32,40},{40,32},{48,56},{56,48},{64,72... | collective-permute-start | bytes 12582920 | tf_op jit(solution)/shard_map/ppermute | solution.py:28
  10.2 19.1 %collective-permute-start.3 = (f32[2,64,1024]{2,1,0:T(8,128)S(1)}, f32[2,64,1024]{2,1,0:T(8,128)S(1)}, u32[]{:S(2)}, u32[]{:S(2)}) collective-permute-start(f32[2,64,1024]{2,1,0:T(8,128)S(1)} %copy-done.4), channel_id=1, source_target_pairs={{0,16},{8,24},{16,32},{24,40},{32,48},{40,56},{48,64},{56,72},{64,... | collective-permute-start | bytes 1572872 | tf_op jit(solution)/shard_map/ppermute | solution.py:34
  14.0 18.1 %collective-permute-start.4 = (f32[2,64,1024]{2,1,0:T(8,128)S(1)}, f32[2,64,1024]{2,1,0:T(8,128)S(1)}, u32[]{:S(2)}, u32[]{:S(2)}) collective-permute-start(f32[2,64,1024]{2,1,0:T(8,128)S(1)} %copy-done.4), channel_id=1, source_target_pairs={{16,0},{24,8},{32,16},{40,24},{48,32},{56,40},{64,48},{72,56},{80,... | collective-permute-start | bytes 1572872 | tf_op jit(solution)/shard_map/ppermute | solution.py:34
  21.6 35.3 %collective-permute-start.8 = (f32[4,4,2,32,1024]{4,3,2,1,0:T(8,128)S(1)}, f32[4,4,2,32,1024]{4,3,2,1,0:T(8,128)S(1)}, u32[]{:S(2)}, u32[]{:S(2)}) collective-permute-start(f32[4,4,2,32,1024]{4,3,2,1,0:T(8,128)S(1)} %get-tuple-element.43), channel_id=1, source_target_pairs={{0,8},{8,0},{16,24},{24,16},{32,40},{40,32},{48,56},{56,48},{64,72... | collective-permute-start | bytes 12582920 | tf_op jit(solution)/shard_map/ppermute | solution.py:28
  27.2 25.6 %collective-permute-start.1 = (f32[4,2,32,1024]{3,2,1,0:T(8,128)S(1)}, f32[4,2,32,1024]{3,2,1,0:T(8,128)S(1)}, u32[]{:S(2)}, u32[]{:S(2)}) collective-permute-start(f32[4,2,32,1024]{3,2,1,0:T(8,128)S(1)} %get-tuple-element.35), channel_id=1, source_target_pairs={{0,16},{8,24},{16,32},{24,40},{32,48},{40,56},{48,0},{56,8},{64,80... | collective-permute-start | bytes 3145736 | tf_op jit(solution)/shard_map/ppermute | solution.py:28
  27.3 27.2 %collective-permute-start.2 = (f32[4,2,32,1024]{3,2,1,0:T(8,128)S(1)}, f32[4,2,32,1024]{3,2,1,0:T(8,128)S(1)}, u32[]{:S(2)}, u32[]{:S(2)}) collective-permute-start(f32[4,2,32,1024]{3,2,1,0:T(8,128)S(1)} %get-tuple-element.37), channel_id=1, source_target_pairs={{0,48},{8,56},{16,0},{24,8},{32,16},{40,24},{48,32},{56,40},{64,11... | collective-permute-start | bytes 3145736 | tf_op jit(solution)/shard_map/ppermute | solution.py:28
  54.6 15.0 %collective-permute-start.5 = (f32[2,2,32,1024]{3,2,1,0:T(8,128)S(1)}, f32[2,2,32,1024]{3,2,1,0:T(8,128)S(1)}, u32[]{:S(2)}, u32[]{:S(2)}) collective-permute-start(f32[2,2,32,1024]{3,2,1,0:T(8,128)S(1)} %get-tuple-element.39.token), channel_id=1, source_target_pairs={{0,16},{8,24},{16,32},{24,40},{32,48},{40,56},{48,0},{56,8},{64,80... | collective-permute-start | bytes 1572872 | tf_op jit(solution)/shard_map/ppermute | solution.py:28
  54.9 16.0 %collective-permute-start.6 = (f32[2,2,32,1024]{3,2,1,0:T(8,128)S(1)}, f32[2,2,32,1024]{3,2,1,0:T(8,128)S(1)}, u32[]{:S(2)}, u32[]{:S(2)}) collective-permute-start(f32[2,2,32,1024]{3,2,1,0:T(8,128)S(1)} %get-tuple-element.40), channel_id=1, source_target_pairs={{0,48},{8,56},{16,0},{24,8},{32,16},{40,24},{48,32},{56,40},{64,11... | collective-permute-start | bytes 1572872 | tf_op jit(solution)/shard_map/ppermute | solution.py:28
  62.4 28.8 %collective-permute-start.9 = (f32[4,2,32,1024]{3,2,1,0:T(8,128)S(1)}, f32[4,2,32,1024]{3,2,1,0:T(8,128)S(1)}, u32[]{:S(2)}, u32[]{:S(2)}) collective-permute-start(f32[4,2,32,1024]{3,2,1,0:T(8,128)S(1)} %get-tuple-element.45), channel_id=1, source_target_pairs={{0,16},{8,24},{16,32},{24,40},{32,48},{40,56},{48,0},{56,8},{64,80... | collective-permute-start | bytes 3145736 | tf_op jit(solution)/shard_map/ppermute | solution.py:28
  63.8 28.7 %collective-permute-start.10 = (f32[4,2,32,1024]{3,2,1,0:T(8,128)S(1)}, f32[4,2,32,1024]{3,2,1,0:T(8,128)S(1)}, u32[]{:S(2)}, u32[]{:S(2)}) collective-permute-start(f32[4,2,32,1024]{3,2,1,0:T(8,128)S(1)} %get-tuple-element.47), channel_id=1, source_target_pairs={{0,48},{8,56},{16,0},{24,8},{32,16},{40,24},{48,32},{56,40},{64,11... | collective-permute-start | bytes 3145736 | tf_op jit(solution)/shard_map/ppermute | solution.py:28
  71.2 23.5 %collective-permute-start.7 = (f32[2,2,32,1024]{3,2,1,0:T(8,128)S(1)}, f32[2,2,32,1024]{3,2,1,0:T(8,128)S(1)}, u32[]{:S(2)}, u32[]{:S(2)}) collective-permute-start(f32[2,2,32,1024]{3,2,1,0:T(8,128)S(1)} %get-tuple-element.42), channel_id=1, source_target_pairs={{0,64},{8,72},{16,80},{24,88},{32,96},{40,104},{48,112},{56,120},{... | collective-permute-start | bytes 1572872 | tf_op jit(solution)/shard_map/ppermute | solution.py:28
  92.6 13.1 %collective-permute-start.12 = (f32[2,2,32,1024]{3,2,1,0:T(8,128)S(1)}, f32[2,2,32,1024]{3,2,1,0:T(8,128)S(1)}, u32[]{:S(2)}, u32[]{:S(2)}) collective-permute-start(f32[2,2,32,1024]{3,2,1,0:T(8,128)S(1)} %get-tuple-element.48.token), channel_id=1, source_target_pairs={{0,16},{8,24},{16,32},{24,40},{32,48},{40,56},{48,0},{56,8},{64,80... | collective-permute-start | bytes 1572872 | tf_op jit(solution)/shard_map/ppermute | solution.py:28
  92.9 14.2 %collective-permute-start.13 = (f32[2,2,32,1024]{3,2,1,0:T(8,128)S(1)}, f32[2,2,32,1024]{3,2,1,0:T(8,128)S(1)}, u32[]{:S(2)}, u32[]{:S(2)}) collective-permute-start(f32[2,2,32,1024]{3,2,1,0:T(8,128)S(1)} %get-tuple-element.50), channel_id=1, source_target_pairs={{0,48},{8,56},{16,0},{24,8},{32,16},{40,24},{48,32},{56,40},{64,11... | collective-permute-start | bytes 1572872 | tf_op jit(solution)/shard_map/ppermute | solution.py:28
  94.7 14.9 %collective-permute-start.11 = (f32[2,32,1024]{2,1,0:T(8,128)S(1)}, f32[2,32,1024]{2,1,0:T(8,128)S(1)}, u32[]{:S(2)}, u32[]{:S(2)}) collective-permute-start(f32[2,32,1024]{2,1,0:T(8,128)S(1)} %shard_map.86.token), channel_id=1, source_target_pairs={{0,128},{8,136},{16,144},{24,152},{32,160},{40,168},{48,176},{56,1... | collective-permute-start | bytes 786440 | tf_op jit(solution)/shard_map/ppermute | solution.py:28
  99.5 34.4 %collective-permute-start.21 = (f32[4,64,1024]{2,1,0:T(8,128)S(1)}, f32[4,64,1024]{2,1,0:T(8,128)S(1)}, u32[]{:S(2)}, u32[]{:S(2)}) collective-permute-start(f32[4,64,1024]{2,1,0:T(8,128)S(1)} %shard_map.81.token), channel_id=1, source_target_pairs={{0,8},{8,0},{16,24},{24,16},{32,40},{40,32},{48,56},{56,48},{64,72... | collective-permute-start | bytes 3145736 | tf_op jit(solution)/shard_map/ppermute | solution.py:28
  109.6 10.5 %collective-permute-start.14 = (f32[2,32,1024]{2,1,0:T(8,128)S(1)}, f32[2,32,1024]{2,1,0:T(8,128)S(1)}, u32[]{:S(2)}, u32[]{:S(2)}) collective-permute-start(f32[2,32,1024]{2,1,0:T(8,128)S(1)} %shard_map.88.value.token.refs_6_.refs_2_), channel_id=1, source_target_pairs={{0,16},{8,24},{16,32},{24,40},{32,48},{40,56},{48,64},{56,72},{64,... | collective-permute-start | bytes 786440 | tf_op jit(solution)/shard_map/ppermute | solution.py:34
  113.5 13.2 %collective-permute-start.15 = (f32[2,32,1024]{2,1,0:T(8,128)S(1)}, f32[2,32,1024]{2,1,0:T(8,128)S(1)}, u32[]{:S(2)}, u32[]{:S(2)}) collective-permute-start(f32[2,32,1024]{2,1,0:T(8,128)S(1)} %shard_map.88.value.token.refs_6_.refs_2_), channel_id=1, source_target_pairs={{16,0},{24,8},{32,16},{40,24},{48,32},{56,40},{64,48},{72,56},{80,... | collective-permute-start | bytes 786440 | tf_op jit(solution)/shard_map/ppermute | solution.py:34
  115.5 15.0 %collective-permute-start.17 = (f32[2,2,32,1024]{3,2,1,0:T(8,128)S(1)}, f32[2,2,32,1024]{3,2,1,0:T(8,128)S(1)}, u32[]{:S(2)}, u32[]{:S(2)}) collective-permute-start(f32[2,2,32,1024]{3,2,1,0:T(8,128)S(1)} %get-tuple-element.52), channel_id=1, source_target_pairs={{0,64},{8,72},{16,80},{24,88},{32,96},{40,104},{48,112},{56,120},{... | collective-permute-start | bytes 1572872 | tf_op jit(solution)/shard_map/ppermute | solution.py:28
  126.8 7.2 %collective-permute-start.16 = (f32[4,32,1024]{2,1,0:T(8,128)S(1)}, f32[4,32,1024]{2,1,0:T(8,128)S(1)}, u32[]{:S(2)}, u32[]{:S(2)}) collective-permute-start(f32[4,32,1024]{2,1,0:T(8,128)S(1)} %shard_map.89), channel_id=1, source_target_pairs={{0,8},{8,0},{16,24},{24,16},{32,40},{40,32},{48,56},{56,48},{64,72... | collective-permute-start | bytes 1572872 | tf_op jit(solution)/shard_map/ppermute | solution.py:28
  130.5 21.9 %collective-permute-start.18 = (f32[2,32,1024]{2,1,0:T(8,128)S(1)}, f32[2,32,1024]{2,1,0:T(8,128)S(1)}, u32[]{:S(2)}, u32[]{:S(2)}) collective-permute-start(f32[2,32,1024]{2,1,0:T(8,128)S(1)} %shard_map.90), channel_id=1, source_target_pairs={{0,128},{8,136},{16,144},{24,152},{32,160},{40,168},{48,176},{56,1... | collective-permute-start | bytes 786440 | tf_op jit(solution)/shard_map/ppermute | solution.py:28
  134.0 26.9 %collective-permute-start.22 = (f32[2,10,4,1024]{3,2,1,0:T(4,128)S(1)}, f32[2,10,4,1024]{3,2,1,0:T(4,128)S(1)}, u32[]{:S(2)}, u32[]{:S(2)}) collective-permute-start(f32[2,10,4,1024]{3,2,1,0:T(4,128)S(1)} %get-tuple-element.53), channel_id=1, source_target_pairs={{0,1},{1,2},{2,3},{3,4},{4,5},{5,6},{6,7},{8,9},{9,10},{10,11},{11... | collective-permute-start | bytes 983048 | tf_op jit(solution)/shard_map/ppermute | solution.py:34
  140.0 20.9 %collective-permute-start.23 = (f32[2,10,4,1024]{3,2,1,0:T(4,128)S(1)}, f32[2,10,4,1024]{3,2,1,0:T(4,128)S(1)}, u32[]{:S(2)}, u32[]{:S(2)}) collective-permute-start(f32[2,10,4,1024]{3,2,1,0:T(4,128)S(1)} %get-tuple-element.54), channel_id=1, source_target_pairs={{1,0},{2,1},{3,2},{4,3},{5,4},{6,5},{7,6},{9,8},{10,9},{11,10},{12... | collective-permute-start | bytes 983048 | tf_op jit(solution)/shard_map/ppermute | solution.py:34
  152.4 11.7 %collective-permute-start.19 = (f32[2,32,1024]{2,1,0:T(8,128)S(1)}, f32[2,32,1024]{2,1,0:T(8,128)S(1)}, u32[]{:S(2)}, u32[]{:S(2)}) collective-permute-start(f32[2,32,1024]{2,1,0:T(8,128)S(1)} %shard_map.91.token.value.refs_6_), channel_id=1, source_target_pairs={{0,16},{8,24},{16,32},{24,40},{32,48},{40,56},{48,64},{56,72},{64,... | collective-permute-start | bytes 786440 | tf_op jit(solution)/shard_map/ppermute | solution.py:34
  159.0 10.4 %collective-permute-start.20 = (f32[2,32,1024]{2,1,0:T(8,128)S(1)}, f32[2,32,1024]{2,1,0:T(8,128)S(1)}, u32[]{:S(2)}, u32[]{:S(2)}) collective-permute-start(f32[2,32,1024]{2,1,0:T(8,128)S(1)} %shard_map.91.token.value.refs_6_), channel_id=1, source_target_pairs={{16,0},{24,8},{32,16},{40,24},{48,32},{56,40},{64,48},{72,56},{80,... | collective-permute-start | bytes 786440 | tf_op jit(solution)/shard_map/ppermute | solution.py:34
  169.4 2.0 %collective-permute-start.24 = (f32[4,32,1024]{2,1,0:T(8,128)S(1)}, f32[4,32,1024]{2,1,0:T(8,128)S(1)}, u32[]{:S(2)}, u32[]{:S(2)}) collective-permute-start(f32[4,32,1024]{2,1,0:T(8,128)S(1)} %shard_map.94), channel_id=1, source_target_pairs={{0,8},{8,0},{16,24},{24,16},{32,40},{40,32},{48,56},{56,48},{64,72... | collective-permute-start | bytes 1572872 | tf_op jit(solution)/shard_map/ppermute | solution.py:28

commit v7 on v5

--- a/solution.py
+++ b/solution.py
@@ -425,10 +425,10 @@
         self.fromm = shift_ang(send[1], dx=-1)
         return self.home
 
-    def second(self, token):
+    def second(self, token, us=1.0):
         holdp, holdm = self.hold
         outs = small(
-            second_kernel, [holdp.shape] * 2, [holdp, self.fromp, holdm, self.fromm], [token]
+            second_kernel, [holdp.shape] * 2, [holdp, self.fromp, holdm, self.fromm], [token], us=us
         )
         self.lastp = shift_ang(outs[0], dx=1)
         self.lastm = shift_ang(outs[1], dx=-1)
@@ -463,9 +463,9 @@
     outer.first(middle.started, us=1.0)
     middle.first(outer.second(token))
     outer.near_z(pos, us=NEAR_US)
-    token = outer.far_z(middle.second(pos))
-    token = middle.near_z(token)
+    token = middle.second(outer.far_z(pos), us=4.0)
     outer_volume = outer.volume(token)
+    middle.near_z(outer_volume, us=4.0)
     token = middle.far_z(outer_volume)
     outer_rows, _ = widened(core, outer_volume, token)
     low, high = ends(cond, outer_rows)

time: 178 us -> 180 us (1.011)
  waiting for transfers between devices: 87 us -> 89.3 us
  transfers between devices with their start and end apart: 25 -> 25, of which waited for: 17 -> 16; matrix products, arithmetic and copies ran while one was open for 0% -> 0% of each run, Pallas kernels for 12% -> 11%
where the time goes in v7:
time: 180 us; the launch traced here: 177 us
  waiting for transfers between devices  89.3 us (50%)
  starting transfers between devices  48.1 us (27%)
  Pallas kernels  37.8 us (21%)
    ppermute x17, waiting for transfers between devices, shift_ang(): return lax.ppermute(value, 'ang', perm)  74.8 us
    ppermute x8, starting transfers between devices, shift_line(): return lax.ppermute(value, axis, perm)  26 us
    ppermute x17, starting transfers between devices, shift_ang(): return lax.ppermute(value, 'ang', perm)  22.1 us
    ppermute x8, waiting for transfers between devices, shift_line(): return lax.ppermute(value, axis, perm)  14.5 us
    pallas_call x2, Pallas kernels, backproject(): pl.pallas_call(functools.partial(mine_kernel, ranges), out_shape=[f32(*s)...  11 us
    pallas_call x2, Pallas kernels, backproject(): pl.pallas_call(functools.partial(other_kernel, ranges), out_shape=[f32(*s...  10.9 us
    pallas_call x1, Pallas kernels, conduct_heat(): pl.pallas_call(functools.partial(heat_kernel, [c for c, _ in groups]), ou...  9.04 us
  transfers between devices with their start and end apart: 25, of which 16 were waited for; matrix products, arithmetic and copies ran while one was open for 0% of the time, Pallas kernels for 11%

profile of v7, /device:TPU:30, one launch (start us, length us, event | category | flops | bytes accessed | tf_op | source)
XLA Modules:
  0.0 177.3 jit_solution(5944359117737541144)
XLA Ops:
  0.7 0.6 pad_add_fusion.pos.token
  1.3 2.7 %shard_map.78 = (f32[2,64,1024]{2,1,0:T(8,128)}, f32[8,128]{1,0:T(8,128)}) custom-call(f32[4,4]{1,0:T(4,128)} %table.1, s32[2,64,1024]{2,1,0:T(8,128)} %phase.1, s32[2,64,1024]{2,1,0:T(8,128)} %contact.1, s32[3]{0:T(128)} %pad_add_fusion.pos.token), custom_call_target="tpu_custom_call" | custom-call | flops 2200000000 | bytes 1048576 | tf_op jit(solution)/shard_map/pallas_call | solution.py:202
  4.0 0.0 copy-start.5
  4.0 0.7 copy-done.5
  4.7 5.5 %shard_map.79 = (f32[4,4,2,32,1024]{4,3,2,1,0:T(8,128)S(1)}, f32[8,128]{1,0:T(8,128)}) custom-call(s32[3]{0:T(128)S(1)} %copy-done.3, s32[8,64]{1,0:T(8,128)S(1)} %copy-done.2, bf16[8,64,1024]{2,1,0:T(8,128)(2,1)S(1)} %copy-done.1, bf16[8,1024,128]{2,1,0:T(8,128)(2,1)S(1)} %copy-done, f32[8,128]{1,0:T(8,128)S(1)} %copy-done.5), custom_call_target="tpu_custom_call" | custom-call | flops 6600000000 | bytes 1048576 | tf_op jit(solution)/shard_map/pallas_call | solution.py:161
  10.1 0.1 collective-permute-start
  10.2 3.7 %collective-permute-start.3 = (f32[2,64,1024]{2,1,0:T(8,128)S(1)}, f32[2,64,1024]{2,1,0:T(8,128)S(1)}, u32[]{:S(2)}, u32[]{:S(2)}) collective-permute-start(f32[2,64,1024]{2,1,0:T(8,128)S(1)} %copy-done.4), channel_id=1, source_target_pairs={{0,16},{8,24},{16,32},{24,40},{32,48},{40,56},{48,64},{56,72},{64,... | collective-permute-start | bytes 1572872 | tf_op jit(solution)/shard_map/ppermute | solution.py:34
  14.0 2.1 %collective-permute-start.4 = (f32[2,64,1024]{2,1,0:T(8,128)S(1)}, f32[2,64,1024]{2,1,0:T(8,128)S(1)}, u32[]{:S(2)}, u32[]{:S(2)}) collective-permute-start(f32[2,64,1024]{2,1,0:T(8,128)S(1)} %copy-done.4), channel_id=1, source_target_pairs={{16,0},{24,8},{32,16},{40,24},{48,32},{56,40},{64,48},{72,56},{80,... | collective-permute-start | bytes 1572872 | tf_op jit(solution)/shard_map/ppermute | solution.py:34
  16.1 5.5 %shard_map.77 = (f32[4,4,2,32,1024]{4,3,2,1,0:T(8,128)S(1)}, f32[8,128]{1,0:T(8,128)S(1)}) custom-call(s32[3]{0:T(128)S(1)} %copy-done.3, s32[8,64]{1,0:T(8,128)S(1)} %copy-done.2, bf16[8,64,1024]{2,1,0:T(8,128)(2,1)S(1)} %copy-done.1, bf16[8,1024,128]{2,1,0:T(8,128)(2,1)S(1)} %copy-done, s32[3]{0:T(128)S(1)} %copy-done.3), custom_call_target="tpu_custom_call" | custom-call | flops 6600000000 | bytes 1048576 | tf_op jit(solution)/shard_map/pallas_call | solution.py:161
  21.6 0.1 collective-permute-start.9
  21.7 0.0 collective-permute-done.recv
  21.7 5.5 %shard_map.80 = (f32[4,2,32,1024]{3,2,1,0:T(8,128)S(1)}, f32[4,2,32,1024]{3,2,1,0:T(8,128)S(1)}, f32[2,2,32,1024]{3,2,1,0:T(8,128)S(1)}, f32[2,2,32,1024]{3,2,1,0:T(8,128)S(1)}, f32[4,2,32,1024]{3,2,1,0:T(8,128)S(1)}) custom-call(s32[3]{0:T(128)S(1)} %copy-done.3, s32[8,64]{1,0:T(8,128)S(1)} %copy-done.2, bf16[8,64,1024]{2,1,0:T(8,128)(2,1)S(1)} %copy-done.1, ...), custom_call_target="tpu_custom_call" | custom-call | flops 1100000000 | bytes 1048576 | tf_op jit(solution)/shard_map/pallas_call | solution.py:169
  27.2 0.1 collective-permute-start.1
  27.3 2.0 %collective-permute-start.2 = (f32[4,2,32,1024]{3,2,1,0:T(8,128)S(1)}, f32[4,2,32,1024]{3,2,1,0:T(8,128)S(1)}, u32[]{:S(2)}, u32[]{:S(2)}) collective-permute-start(f32[4,2,32,1024]{3,2,1,0:T(8,128)S(1)} %get-tuple-element.37), channel_id=1, source_target_pairs={{0,48},{8,56},{16,0},{24,8},{32,16},{40,24},{48,32},{56,40},{64,11... | collective-permute-start | bytes 3145736 | tf_op jit(solution)/shard_map/ppermute | solution.py:28
  29.3 0.0 collective-permute-done.3.left.refs_0_
  29.3 2.8 %collective-permute-done.4.right.refs_3_ = f32[2,64,1024]{2,1,0:T(8,128)S(1)} collective-permute-done((f32[2,64,1024]{2,1,0:T(8,128)S(1)}, f32[2,64,1024]{2,1,0:T(8,128)S(1)}, u32[]{:S(2)}, u32[]{:S(2)}) %collective-permute-start.4) | collective-permute-done | bytes 524320 | tf_op jit(solution)/shard_map/ppermute | solution.py:34
  32.1 0.1 shard_map.81.token
  32.1 20.7 %collective-permute-done.1.fromp = f32[4,2,32,1024]{3,2,1,0:T(8,128)S(1)} collective-permute-done((f32[4,2,32,1024]{3,2,1,0:T(8,128)S(1)}, f32[4,2,32,1024]{3,2,1,0:T(8,128)S(1)}, u32[]{:S(2)}, u32[]{:S(2)}) %collective-permute-start.1) | collective-permute-done | bytes 1048608 | tf_op jit(solution)/shard_map/ppermute | solution.py:28
  52.8 1.7 collective-permute-done.2.fromm
  54.5 0.1 shard_map.82
  54.6 0.3 collective-permute-start.5
  54.9 2.0 %collective-permute-start.6 = (f32[2,2,32,1024]{3,2,1,0:T(8,128)S(1)}, f32[2,2,32,1024]{3,2,1,0:T(8,128)S(1)}, u32[]{:S(2)}, u32[]{:S(2)}) collective-permute-start(f32[2,2,32,1024]{3,2,1,0:T(8,128)S(1)} %get-tuple-element.40), channel_id=1, source_target_pairs={{0,48},{8,56},{16,0},{24,8},{32,16},{40,24},{48,32},{56,40},{64,11... | collective-permute-start | bytes 1572872 | tf_op jit(solution)/shard_map/ppermute | solution.py:28
  56.9 0.0 collective-permute-done.9.recv
  56.9 5.5 %shard_map.85 = (f32[4,2,32,1024]{3,2,1,0:T(8,128)S(1)}, f32[4,2,32,1024]{3,2,1,0:T(8,128)S(1)}, f32[2,2,32,1024]{3,2,1,0:T(8,128)S(1)}, f32[2,2,32,1024]{3,2,1,0:T(8,128)S(1)}, f32[4,2,32,1024]{3,2,1,0:T(8,128)S(1)}) custom-call(s32[3]{0:T(128)S(1)} %copy-done.3, s32[8,64]{1,0:T(8,128)S(1)} %copy-done.2, bf16[8,64,1024]{2,1,0:T(8,128)(2,1)S(1)} %copy-done.1, ...), custom_call_target="tpu_custom_call" | custom-call | flops 6600000000 | bytes 1048576 | tf_op jit(solution)/shard_map/pallas_call | solution.py:169
  62.4 1.4 collective-permute-start.10
  63.8 0.7 collective-permute-start.11
  64.5 5.2 %collective-permute-done.5.lastp = f32[2,2,32,1024]{3,2,1,0:T(8,128)S(1)} collective-permute-done((f32[2,2,32,1024]{3,2,1,0:T(8,128)S(1)}, f32[2,2,32,1024]{3,2,1,0:T(8,128)S(1)}, u32[]{:S(2)}, u32[]{:S(2)}) %collective-permute-start.5) | collective-permute-done | bytes 524320 | tf_op jit(solution)/shard_map/ppermute | solution.py:28
  69.7 1.3 collective-permute-done.6.lastm
  71.0 0.2 shard_map.83
  71.1 4.1 %collective-permute-start.7 = (f32[2,2,32,1024]{3,2,1,0:T(8,128)S(1)}, f32[2,2,32,1024]{3,2,1,0:T(8,128)S(1)}, u32[]{:S(2)}, u32[]{:S(2)}) collective-permute-start(f32[2,2,32,1024]{3,2,1,0:T(8,128)S(1)} %get-tuple-element.42), channel_id=1, source_target_pairs={{0,64},{8,72},{16,80},{24,88},{32,96},{40,104},{48,112},{56,120},{... | collective-permute-start | bytes 1572872 | tf_op jit(solution)/shard_map/ppermute | solution.py:28
  75.2 9.0 %collective-permute-done.7.got = f32[2,2,32,1024]{3,2,1,0:T(8,128)S(1)} collective-permute-done((f32[2,2,32,1024]{3,2,1,0:T(8,128)S(1)}, f32[2,2,32,1024]{3,2,1,0:T(8,128)S(1)}, u32[]{:S(2)}, u32[]{:S(2)}) %collective-permute-start.7) | collective-permute-done | bytes 524320 | tf_op jit(solution)/shard_map/ppermute | solution.py:28
  84.2 6.9 %collective-permute-done.10.fromp = f32[4,2,32,1024]{3,2,1,0:T(8,128)S(1)} collective-permute-done((f32[4,2,32,1024]{3,2,1,0:T(8,128)S(1)}, f32[4,2,32,1024]{3,2,1,0:T(8,128)S(1)}, u32[]{:S(2)}, u32[]{:S(2)}) %collective-permute-start.10) | collective-permute-done | bytes 1048608 | tf_op jit(solution)/shard_map/ppermute | solution.py:28
  91.2 1.3 collective-permute-done.11.fromm
  92.5 0.1 shard_map.86
  92.6 0.3 collective-permute-start.14
  92.9 1.8 %collective-permute-start.15 = (f32[2,2,32,1024]{3,2,1,0:T(8,128)S(1)}, f32[2,2,32,1024]{3,2,1,0:T(8,128)S(1)}, u32[]{:S(2)}, u32[]{:S(2)}) collective-permute-start(f32[2,2,32,1024]{3,2,1,0:T(8,128)S(1)} %get-tuple-element.50), channel_id=1, source_target_pairs={{0,48},{8,56},{16,0},{24,8},{32,16},{40,24},{48,32},{56,40},{64,11... | collective-permute-start | bytes 1572872 | tf_op jit(solution)/shard_map/ppermute | solution.py:28
  94.7 4.7 %collective-permute-start.8 = (f32[2,32,1024]{2,1,0:T(8,128)S(1)}, f32[2,32,1024]{2,1,0:T(8,128)S(1)}, u32[]{:S(2)}, u32[]{:S(2)}) collective-permute-start(f32[2,32,1024]{2,1,0:T(8,128)S(1)} %shard_map.84.token), channel_id=1, source_target_pairs={{0,128},{8,136},{16,144},{24,152},{32,160},{40,168},{48,176},{56,1... | collective-permute-start | bytes 786440 | tf_op jit(solution)/shard_map/ppermute | solution.py:28
  99.4 10.0 %collective-permute-done.8.last = f32[2,32,1024]{2,1,0:T(8,128)S(1)} collective-permute-done((f32[2,32,1024]{2,1,0:T(8,128)S(1)}, f32[2,32,1024]{2,1,0:T(8,128)S(1)}, u32[]{:S(2)}, u32[]{:S(2)}) %collective-permute-start.8) | collective-permute-done | bytes 262176 | tf_op jit(solution)/shard_map/ppermute | solution.py:28
  109.5 0.0 collective-permute-done.14.lastp
  109.5 0.0 collective-permute-done.15.lastm
  109.5 0.2 shard_map.88
  109.7 0.8 collective-permute-start.16
  110.5 0.0 collective-permute-start.21
  110.5 4.4 %collective-permute-start.12 = (f32[2,32,1024]{2,1,0:T(8,128)S(1)}, f32[2,32,1024]{2,1,0:T(8,128)S(1)}, u32[]{:S(2)}, u32[]{:S(2)}) collective-permute-start(f32[2,32,1024]{2,1,0:T(8,128)S(1)} %shard_map.87.token.value.refs_6_.refs_2_), channel_id=1, source_target_pairs={{0,16},{8,24},{16,32},{24,40},{32,48},{40,56},{48,64},{56,72},{64,... | collective-permute-start | bytes 786440 | tf_op jit(solution)/shard_map/ppermute | solution.py:34
  115.0 1.9 %collective-permute-start.13 = (f32[2,32,1024]{2,1,0:T(8,128)S(1)}, f32[2,32,1024]{2,1,0:T(8,128)S(1)}, u32[]{:S(2)}, u32[]{:S(2)}) collective-permute-start(f32[2,32,1024]{2,1,0:T(8,128)S(1)} %shard_map.87.token.value.refs_6_.refs_2_), channel_id=1, source_target_pairs={{16,0},{24,8},{32,16},{40,24},{48,32},{56,40},{64,48},{72,56},{80,... | collective-permute-start | bytes 786440 | tf_op jit(solution)/shard_map/ppermute | solution.py:34
  116.9 5.9 %collective-permute-done.16.got = f32[2,2,32,1024]{3,2,1,0:T(8,128)S(1)} collective-permute-done((f32[2,2,32,1024]{3,2,1,0:T(8,128)S(1)}, f32[2,2,32,1024]{3,2,1,0:T(8,128)S(1)}, u32[]{:S(2)}, u32[]{:S(2)}) %collective-permute-start.16) | collective-permute-done | bytes 524320 | tf_op jit(solution)/shard_map/ppermute | solution.py:28
  122.9 4.5 %collective-permute-done.12.left.refs_4_.refs_0_ = f32[2,32,1024]{2,1,0:T(8,128)S(1)} collective-permute-done((f32[2,32,1024]{2,1,0:T(8,128)S(1)}, f32[2,32,1024]{2,1,0:T(8,128)S(1)}, u32[]{:S(2)}, u32[]{:S(2)}) %collective-permute-start.12) | collective-permute-done | bytes 262176 | tf_op jit(solution)/shard_map/ppermute | solution.py:34
  127.4 2.1 %collective-permute-done.13.right.refs_7_.refs_3_ = f32[2,32,1024]{2,1,0:T(8,128)S(1)} collective-permute-done((f32[2,32,1024]{2,1,0:T(8,128)S(1)}, f32[2,32,1024]{2,1,0:T(8,128)S(1)}, u32[]{:S(2)}, u32[]{:S(2)}) %collective-permute-start.13) | collective-permute-done | bytes 262176 | tf_op jit(solution)/shard_map/ppermute | solution.py:34
  129.5 0.1 collective-permute-start.17
  129.6 3.5 %collective-permute-start.18 = (f32[2,32,1024]{2,1,0:T(8,128)S(1)}, f32[2,32,1024]{2,1,0:T(8,128)S(1)}, u32[]{:S(2)}, u32[]{:S(2)}) collective-permute-start(f32[2,32,1024]{2,1,0:T(8,128)S(1)} %shard_map.89.token), channel_id=1, source_target_pairs={{0,128},{8,136},{16,144},{24,152},{32,160},{40,168},{48,176},{56,1... | collective-permute-start | bytes 786440 | tf_op jit(solution)/shard_map/ppermute | solution.py:28
  133.1 0.0 collective-permute-done.21.refs_1_.got
  133.1 0.0 collective-permute-done.17.refs_5_.refs_1_
  133.2 6.0 %collective-permute-start.22 = (f32[2,10,4,1024]{3,2,1,0:T(4,128)S(1)}, f32[2,10,4,1024]{3,2,1,0:T(4,128)S(1)}, u32[]{:S(2)}, u32[]{:S(2)}) collective-permute-start(f32[2,10,4,1024]{3,2,1,0:T(4,128)S(1)} %get-tuple-element.53), channel_id=1, source_target_pairs={{0,1},{1,2},{2,3},{3,4},{4,5},{5,6},{6,7},{8,9},{9,10},{10,11},{11... | collective-permute-start | bytes 983048 | tf_op jit(solution)/shard_map/ppermute | solution.py:34
  139.2 1.9 %collective-permute-start.23 = (f32[2,10,4,1024]{3,2,1,0:T(4,128)S(1)}, f32[2,10,4,1024]{3,2,1,0:T(4,128)S(1)}, u32[]{:S(2)}, u32[]{:S(2)}) collective-permute-start(f32[2,10,4,1024]{3,2,1,0:T(4,128)S(1)} %get-tuple-element.54), channel_id=1, source_target_pairs={{1,0},{2,1},{3,2},{4,3},{5,4},{6,5},{7,6},{9,8},{10,9},{11,10},{12... | collective-permute-start | bytes 983048 | tf_op jit(solution)/shard_map/ppermute | solution.py:34
  141.1 10.9 %collective-permute-done.18.last = f32[2,32,1024]{2,1,0:T(8,128)S(1)} collective-permute-done((f32[2,32,1024]{2,1,0:T(8,128)S(1)}, f32[2,32,1024]{2,1,0:T(8,128)S(1)}, u32[]{:S(2)}, u32[]{:S(2)}) %collective-permute-start.18) | collective-permute-done | bytes 262176 | tf_op jit(solution)/shard_map/ppermute | solution.py:28
  152.1 1.9 %collective-permute-start.19 = (f32[2,32,1024]{2,1,0:T(8,128)S(1)}, f32[2,32,1024]{2,1,0:T(8,128)S(1)}, u32[]{:S(2)}, u32[]{:S(2)}) collective-permute-start(f32[2,32,1024]{2,1,0:T(8,128)S(1)} %shard_map.91.token.value.refs_6_), channel_id=1, source_target_pairs={{0,16},{8,24},{16,32},{24,40},{32,48},{40,56},{48,64},{56,72},{64,... | collective-permute-start | bytes 786440 | tf_op jit(solution)/shard_map/ppermute | solution.py:34
  154.0 3.9 %collective-permute-start.20 = (f32[2,32,1024]{2,1,0:T(8,128)S(1)}, f32[2,32,1024]{2,1,0:T(8,128)S(1)}, u32[]{:S(2)}, u32[]{:S(2)}) collective-permute-start(f32[2,32,1024]{2,1,0:T(8,128)S(1)} %shard_map.91.token.value.refs_6_), channel_id=1, source_target_pairs={{16,0},{24,8},{32,16},{40,24},{48,32},{56,40},{64,48},{72,56},{80,... | collective-permute-start | bytes 786440 | tf_op jit(solution)/shard_map/ppermute | solution.py:34
  157.9 0.0 collective-permute-done.22.low.refs_8_
  157.9 3.2 %shard_map.93 = (f32[10,80,1024]{2,1,0:T(8,128)S(1)}, f32[10,80,1024]{2,1,0:T(8,128)S(1)}, f32[10,80,1024]{2,1,0:T(8,128)S(1)}) custom-call(f32[2,64,1024]{2,1,0:T(8,128)S(1)} %collective-permute-done.3.left.refs_0_, f32[4,64,1024]{2,1,0:T(8,128)S(1)} %collective-permute-done.21.refs_1_.got, f32[2,64,1024]{2,1,0:T(8,128)S(1)} %copy-done.4, ...), custom_call_target="tpu_custom_call" | custom-call | flops 6600000000 | bytes 1048576 | tf_op jit(solution)/shard_map/pallas_call | solution.py:312
  161.1 1.1 collective-permute-done.19.left.refs_4_
  162.2 4.0 %collective-permute-done.20.right.refs_7_ = f32[2,32,1024]{2,1,0:T(8,128)S(1)} collective-permute-done((f32[2,32,1024]{2,1,0:T(8,128)S(1)}, f32[2,32,1024]{2,1,0:T(8,128)S(1)}, u32[]{:S(2)}, u32[]{:S(2)}) %collective-permute-start.20) | collective-permute-done | bytes 262176 | tf_op jit(solution)/shard_map/ppermute | solution.py:34
  166.3 0.1 collective-permute-start.24
  166.4 1.9 %collective-permute-done.24.refs_5_ = f32[4,32,1024]{2,1,0:T(8,128)S(1)} collective-permute-done((f32[4,32,1024]{2,1,0:T(8,128)S(1)}, f32[4,32,1024]{2,1,0:T(8,128)S(1)}, u32[]{:S(2)}, u32[]{:S(2)}) %collective-permute-start.24) | collective-permute-done | bytes 524320 | tf_op jit(solution)/shard_map/ppermute | solution.py:28
  168.3 9.0 %shard_map.95 = (f32[2,64,1024]{2,1,0:T(8,128)}, f32[2,64,1024]{2,1,0:T(8,128)}) custom-call(f32[2,32,1024]{2,1,0:T(8,128)S(1)} %collective-permute-done.12.left.refs_4_.refs_0_, f32[4,32,1024]{2,1,0:T(8,128)S(1)} %collective-permute-done.17.refs_5_.refs_1_, f32[2,32,1024]{2,1,0:T(8,128)S(1)} %shard_map.87.token.value.refs_6_.refs_2_, ...), custom_call_target="tpu_custom_call" | custom-call | flops 9900000256 | bytes 1048576 | tf_op jit(solution)/shard_map/pallas_call | solution.py:371
  (18 shorter events, 0.3 us)
Async XLA Ops:
  0.6 3.3 %copy-start.2 = (s32[8,64]{1,0:T(8,128)S(1)}, s32[8,64]{1,0:T(8,128)}, u32[]{:S(2)}) copy-start(s32[8,64]{1,0:T(8,128)} %offsets.7) | copy-start | bytes 6148
  0.6 3.3 %copy-start.1 = (bf16[8,64,1024]{2,1,0:T(8,128)(2,1)S(1)}, bf16[8,64,1024]{2,1,0:T(8,128)(2,1)}, u32[]{:S(2)}) copy-start(bf16[8,64,1024]{2,1,0:T(8,128)(2,1)} %proj.7) | copy-start | bytes 3145732
  0.6 3.3 %copy-start = (bf16[8,1024,128]{2,1,0:T(8,128)(2,1)S(1)}, bf16[8,1024,128]{2,1,0:T(8,128)(2,1)}, u32[]{:S(2)}) copy-start(bf16[8,1024,128]{2,1,0:T(8,128)(2,1)} %weights.7) | copy-start | bytes 6291460
  1.3 2.7 %copy-start.3 = (s32[3]{0:T(128)S(1)}, s32[3]{0:T(128)}, u32[]{:S(2)}) copy-start(s32[3]{0:T(128)} %pad_add_fusion.pos.token) | copy-start | bytes 40
  4.0 0.7 copy-start.5
  4.7 5.6 %copy-start.4 = (f32[2,64,1024]{2,1,0:T(8,128)S(1)}, f32[2,64,1024]{2,1,0:T(8,128)}, u32[]{:S(2)}) copy-start(f32[2,64,1024]{2,1,0:T(8,128)} %get-tuple-element.38.value.refs_2_) | copy-start | bytes 1572868
  10.1 11.5 %collective-permute-start = (f32[4,4,2,32,1024]{4,3,2,1,0:T(8,128)S(1)}, f32[4,4,2,32,1024]{4,3,2,1,0:T(8,128)S(1)}, u32[]{:S(2)}, u32[]{:S(2)}) collective-permute-start(f32[4,4,2,32,1024]{4,3,2,1,0:T(8,128)S(1)} %get-tuple-element.32), channel_id=1, source_target_pairs={{0,8},{8,0},{16,24},{24,16},{32,40},{40,32},{48,56},{56,48},{64,72... | collective-permute-start | bytes 12582920 | tf_op jit(solution)/shard_map/ppermute | solution.py:28
  10.2 19.1 %collective-permute-start.3 = (f32[2,64,1024]{2,1,0:T(8,128)S(1)}, f32[2,64,1024]{2,1,0:T(8,128)S(1)}, u32[]{:S(2)}, u32[]{:S(2)}) collective-permute-start(f32[2,64,1024]{2,1,0:T(8,128)S(1)} %copy-done.4), channel_id=1, source_target_pairs={{0,16},{8,24},{16,32},{24,40},{32,48},{40,56},{48,64},{56,72},{64,... | collective-permute-start | bytes 1572872 | tf_op jit(solution)/shard_map/ppermute | solution.py:34
  14.0 18.1 %collective-permute-start.4 = (f32[2,64,1024]{2,1,0:T(8,128)S(1)}, f32[2,64,1024]{2,1,0:T(8,128)S(1)}, u32[]{:S(2)}, u32[]{:S(2)}) collective-permute-start(f32[2,64,1024]{2,1,0:T(8,128)S(1)} %copy-done.4), channel_id=1, source_target_pairs={{16,0},{24,8},{32,16},{40,24},{48,32},{56,40},{64,48},{72,56},{80,... | collective-permute-start | bytes 1572872 | tf_op jit(solution)/shard_map/ppermute | solution.py:34
  21.6 35.3 %collective-permute-start.9 = (f32[4,4,2,32,1024]{4,3,2,1,0:T(8,128)S(1)}, f32[4,4,2,32,1024]{4,3,2,1,0:T(8,128)S(1)}, u32[]{:S(2)}, u32[]{:S(2)}) collective-permute-start(f32[4,4,2,32,1024]{4,3,2,1,0:T(8,128)S(1)} %get-tuple-element.43), channel_id=1, source_target_pairs={{0,8},{8,0},{16,24},{24,16},{32,40},{40,32},{48,56},{56,48},{64,72... | collective-permute-start | bytes 12582920 | tf_op jit(solution)/shard_map/ppermute | solution.py:28
  27.2 25.6 %collective-permute-start.1 = (f32[4,2,32,1024]{3,2,1,0:T(8,128)S(1)}, f32[4,2,32,1024]{3,2,1,0:T(8,128)S(1)}, u32[]{:S(2)}, u32[]{:S(2)}) collective-permute-start(f32[4,2,32,1024]{3,2,1,0:T(8,128)S(1)} %get-tuple-element.35), channel_id=1, source_target_pairs={{0,16},{8,24},{16,32},{24,40},{32,48},{40,56},{48,0},{56,8},{64,80... | collective-permute-start | bytes 3145736 | tf_op jit(solution)/shard_map/ppermute | solution.py:28
  27.3 27.2 %collective-permute-start.2 = (f32[4,2,32,1024]{3,2,1,0:T(8,128)S(1)}, f32[4,2,32,1024]{3,2,1,0:T(8,128)S(1)}, u32[]{:S(2)}, u32[]{:S(2)}) collective-permute-start(f32[4,2,32,1024]{3,2,1,0:T(8,128)S(1)} %get-tuple-element.37), channel_id=1, source_target_pairs={{0,48},{8,56},{16,0},{24,8},{32,16},{40,24},{48,32},{56,40},{64,11... | collective-permute-start | bytes 3145736 | tf_op jit(solution)/shard_map/ppermute | solution.py:28
  54.6 15.0 %collective-permute-start.5 = (f32[2,2,32,1024]{3,2,1,0:T(8,128)S(1)}, f32[2,2,32,1024]{3,2,1,0:T(8,128)S(1)}, u32[]{:S(2)}, u32[]{:S(2)}) collective-permute-start(f32[2,2,32,1024]{3,2,1,0:T(8,128)S(1)} %get-tuple-element.39.token), channel_id=1, source_target_pairs={{0,16},{8,24},{16,32},{24,40},{32,48},{40,56},{48,0},{56,8},{64,80... | collective-permute-start | bytes 1572872 | tf_op jit(solution)/shard_map/ppermute | solution.py:28
  54.9 16.0 %collective-permute-start.6 = (f32[2,2,32,1024]{3,2,1,0:T(8,128)S(1)}, f32[2,2,32,1024]{3,2,1,0:T(8,128)S(1)}, u32[]{:S(2)}, u32[]{:S(2)}) collective-permute-start(f32[2,2,32,1024]{3,2,1,0:T(8,128)S(1)} %get-tuple-element.40), channel_id=1, source_target_pairs={{0,48},{8,56},{16,0},{24,8},{32,16},{40,24},{48,32},{56,40},{64,11... | collective-permute-start | bytes 1572872 | tf_op jit(solution)/shard_map/ppermute | solution.py:28
  62.4 28.8 %collective-permute-start.10 = (f32[4,2,32,1024]{3,2,1,0:T(8,128)S(1)}, f32[4,2,32,1024]{3,2,1,0:T(8,128)S(1)}, u32[]{:S(2)}, u32[]{:S(2)}) collective-permute-start(f32[4,2,32,1024]{3,2,1,0:T(8,128)S(1)} %get-tuple-element.45), channel_id=1, source_target_pairs={{0,16},{8,24},{16,32},{24,40},{32,48},{40,56},{48,0},{56,8},{64,80... | collective-permute-start | bytes 3145736 | tf_op jit(solution)/shard_map/ppermute | solution.py:28
  63.8 28.7 %collective-permute-start.11 = (f32[4,2,32,1024]{3,2,1,0:T(8,128)S(1)}, f32[4,2,32,1024]{3,2,1,0:T(8,128)S(1)}, u32[]{:S(2)}, u32[]{:S(2)}) collective-permute-start(f32[4,2,32,1024]{3,2,1,0:T(8,128)S(1)} %get-tuple-element.47), channel_id=1, source_target_pairs={{0,48},{8,56},{16,0},{24,8},{32,16},{40,24},{48,32},{56,40},{64,11... | collective-permute-start | bytes 3145736 | tf_op jit(solution)/shard_map/ppermute | solution.py:28
  71.1 13.1 %collective-permute-start.7 = (f32[2,2,32,1024]{3,2,1,0:T(8,128)S(1)}, f32[2,2,32,1024]{3,2,1,0:T(8,128)S(1)}, u32[]{:S(2)}, u32[]{:S(2)}) collective-permute-start(f32[2,2,32,1024]{3,2,1,0:T(8,128)S(1)} %get-tuple-element.42), channel_id=1, source_target_pairs={{0,64},{8,72},{16,80},{24,88},{32,96},{40,104},{48,112},{56,120},{... | collective-permute-start | bytes 1572872 | tf_op jit(solution)/shard_map/ppermute | solution.py:28
  92.6 16.9 %collective-permute-start.14 = (f32[2,2,32,1024]{3,2,1,0:T(8,128)S(1)}, f32[2,2,32,1024]{3,2,1,0:T(8,128)S(1)}, u32[]{:S(2)}, u32[]{:S(2)}) collective-permute-start(f32[2,2,32,1024]{3,2,1,0:T(8,128)S(1)} %get-tuple-element.48.token), channel_id=1, source_target_pairs={{0,16},{8,24},{16,32},{24,40},{32,48},{40,56},{48,0},{56,8},{64,80... | collective-permute-start | bytes 1572872 | tf_op jit(solution)/shard_map/ppermute | solution.py:28
  92.9 16.6 %collective-permute-start.15 = (f32[2,2,32,1024]{3,2,1,0:T(8,128)S(1)}, f32[2,2,32,1024]{3,2,1,0:T(8,128)S(1)}, u32[]{:S(2)}, u32[]{:S(2)}) collective-permute-start(f32[2,2,32,1024]{3,2,1,0:T(8,128)S(1)} %get-tuple-element.50), channel_id=1, source_target_pairs={{0,48},{8,56},{16,0},{24,8},{32,16},{40,24},{48,32},{56,40},{64,11... | collective-permute-start | bytes 1572872 | tf_op jit(solution)/shard_map/ppermute | solution.py:28
  94.7 14.8 %collective-permute-start.8 = (f32[2,32,1024]{2,1,0:T(8,128)S(1)}, f32[2,32,1024]{2,1,0:T(8,128)S(1)}, u32[]{:S(2)}, u32[]{:S(2)}) collective-permute-start(f32[2,32,1024]{2,1,0:T(8,128)S(1)} %shard_map.84.token), channel_id=1, source_target_pairs={{0,128},{8,136},{16,144},{24,152},{32,160},{40,168},{48,176},{56,1... | collective-permute-start | bytes 786440 | tf_op jit(solution)/shard_map/ppermute | solution.py:28
  109.7 13.1 %collective-permute-start.16 = (f32[2,2,32,1024]{3,2,1,0:T(8,128)S(1)}, f32[2,2,32,1024]{3,2,1,0:T(8,128)S(1)}, u32[]{:S(2)}, u32[]{:S(2)}) collective-permute-start(f32[2,2,32,1024]{3,2,1,0:T(8,128)S(1)} %get-tuple-element.52), channel_id=1, source_target_pairs={{0,64},{8,72},{16,80},{24,88},{32,96},{40,104},{48,112},{56,120},{... | collective-permute-start | bytes 1572872 | tf_op jit(solution)/shard_map/ppermute | solution.py:28
  110.5 22.6 %collective-permute-start.21 = (f32[4,64,1024]{2,1,0:T(8,128)S(1)}, f32[4,64,1024]{2,1,0:T(8,128)S(1)}, u32[]{:S(2)}, u32[]{:S(2)}) collective-permute-start(f32[4,64,1024]{2,1,0:T(8,128)S(1)} %shard_map.81.token), channel_id=1, source_target_pairs={{0,8},{8,0},{16,24},{24,16},{32,40},{40,32},{48,56},{56,48},{64,72... | collective-permute-start | bytes 3145736 | tf_op jit(solution)/shard_map/ppermute | solution.py:28
  110.5 16.9 %collective-permute-start.12 = (f32[2,32,1024]{2,1,0:T(8,128)S(1)}, f32[2,32,1024]{2,1,0:T(8,128)S(1)}, u32[]{:S(2)}, u32[]{:S(2)}) collective-permute-start(f32[2,32,1024]{2,1,0:T(8,128)S(1)} %shard_map.87.token.value.refs_6_.refs_2_), channel_id=1, source_target_pairs={{0,16},{8,24},{16,32},{24,40},{32,48},{40,56},{48,64},{56,72},{64,... | collective-permute-start | bytes 786440 | tf_op jit(solution)/shard_map/ppermute | solution.py:34
  115.0 14.5 %collective-permute-start.13 = (f32[2,32,1024]{2,1,0:T(8,128)S(1)}, f32[2,32,1024]{2,1,0:T(8,128)S(1)}, u32[]{:S(2)}, u32[]{:S(2)}) collective-permute-start(f32[2,32,1024]{2,1,0:T(8,128)S(1)} %shard_map.87.token.value.refs_6_.refs_2_), channel_id=1, source_target_pairs={{16,0},{24,8},{32,16},{40,24},{48,32},{56,40},{64,48},{72,56},{80,... | collective-permute-start | bytes 786440 | tf_op jit(solution)/shard_map/ppermute | solution.py:34
  129.5 3.6 %collective-permute-start.17 = (f32[4,32,1024]{2,1,0:T(8,128)S(1)}, f32[4,32,1024]{2,1,0:T(8,128)S(1)}, u32[]{:S(2)}, u32[]{:S(2)}) collective-permute-start(f32[4,32,1024]{2,1,0:T(8,128)S(1)} %shard_map.90), channel_id=1, source_target_pairs={{0,8},{8,0},{16,24},{24,16},{32,40},{40,32},{48,56},{56,48},{64,72... | collective-permute-start | bytes 1572872 | tf_op jit(solution)/shard_map/ppermute | solution.py:28
  129.6 22.4 %collective-permute-start.18 = (f32[2,32,1024]{2,1,0:T(8,128)S(1)}, f32[2,32,1024]{2,1,0:T(8,128)S(1)}, u32[]{:S(2)}, u32[]{:S(2)}) collective-permute-start(f32[2,32,1024]{2,1,0:T(8,128)S(1)} %shard_map.89.token), channel_id=1, source_target_pairs={{0,128},{8,136},{16,144},{24,152},{32,160},{40,168},{48,176},{56,1... | collective-permute-start | bytes 786440 | tf_op jit(solution)/shard_map/ppermute | solution.py:28
  133.2 24.8 %collective-permute-start.22 = (f32[2,10,4,1024]{3,2,1,0:T(4,128)S(1)}, f32[2,10,4,1024]{3,2,1,0:T(4,128)S(1)}, u32[]{:S(2)}, u32[]{:S(2)}) collective-permute-start(f32[2,10,4,1024]{3,2,1,0:T(4,128)S(1)} %get-tuple-element.53), channel_id=1, source_target_pairs={{0,1},{1,2},{2,3},{3,4},{4,5},{5,6},{6,7},{8,9},{9,10},{10,11},{11... | collective-permute-start | bytes 983048 | tf_op jit(solution)/shard_map/ppermute | solution.py:34
  139.2 18.8 %collective-permute-start.23 = (f32[2,10,4,1024]{3,2,1,0:T(4,128)S(1)}, f32[2,10,4,1024]{3,2,1,0:T(4,128)S(1)}, u32[]{:S(2)}, u32[]{:S(2)}) collective-permute-start(f32[2,10,4,1024]{3,2,1,0:T(4,128)S(1)} %get-tuple-element.54), channel_id=1, source_target_pairs={{1,0},{2,1},{3,2},{4,3},{5,4},{6,5},{7,6},{9,8},{10,9},{11,10},{12... | collective-permute-start | bytes 983048 | tf_op jit(solution)/shard_map/ppermute | solution.py:34
  152.1 10.1 %collective-permute-start.19 = (f32[2,32,1024]{2,1,0:T(8,128)S(1)}, f32[2,32,1024]{2,1,0:T(8,128)S(1)}, u32[]{:S(2)}, u32[]{:S(2)}) collective-permute-start(f32[2,32,1024]{2,1,0:T(8,128)S(1)} %shard_map.91.token.value.refs_6_), channel_id=1, source_target_pairs={{0,16},{8,24},{16,32},{24,40},{32,48},{40,56},{48,64},{56,72},{64,... | collective-permute-start | bytes 786440 | tf_op jit(solution)/shard_map/ppermute | solution.py:34
  154.0 12.2 %collective-permute-start.20 = (f32[2,32,1024]{2,1,0:T(8,128)S(1)}, f32[2,32,1024]{2,1,0:T(8,128)S(1)}, u32[]{:S(2)}, u32[]{:S(2)}) collective-permute-start(f32[2,32,1024]{2,1,0:T(8,128)S(1)} %shard_map.91.token.value.refs_6_), channel_id=1, source_target_pairs={{16,0},{24,8},{32,16},{40,24},{48,32},{56,40},{64,48},{72,56},{80,... | collective-permute-start | bytes 786440 | tf_op jit(solution)/shard_map/ppermute | solution.py:34
  166.3 2.0 %collective-permute-start.24 = (f32[4,32,1024]{2,1,0:T(8,128)S(1)}, f32[4,32,1024]{2,1,0:T(8,128)S(1)}, u32[]{:S(2)}, u32[]{:S(2)}) collective-permute-start(f32[4,32,1024]{2,1,0:T(8,128)S(1)} %shard_map.94), channel_id=1, source_target_pairs={{0,8},{8,0},{16,24},{24,16},{32,40},{40,32},{48,56},{56,48},{64,72... | collective-permute-start | bytes 1572872 | tf_op jit(solution)/shard_map/ppermute | solution.py:28
